TPU v7x, 32 devices: a whole 2x2x4 slice. The times are simulated.
32 devices in a mesh: groups: 2 (over y), wide: 4 (over z), narrow: 4 (over x, core).
Axes of the slice: x: 2, y: 2, z: 4, core: 2. Of those that a mesh axis runs over, the one named last changes fastest.
Arguments:
- target_states: bfloat16 [256, 8192], P(('groups', 'wide'), 'narrow'), parts along dimension 0, may hold values from -6 to 6
- source_states: bfloat16 [256, 8192], P(('groups', 'wide'), 'narrow'), parts along dimension 0, may hold values from -6 to 6
- target_gate: bfloat16 [8192, 14336], P('narrow', 'wide'), may hold values from -0.0625 to 0.0625
- target_up: bfloat16 [8192, 14336], P('narrow', 'wide'), may hold values from -0.0625 to 0.0625
- source_gate: bfloat16 [8192, 14336], P('narrow', 'wide'), may hold values from -0.0625 to 0.0625
- source_up: bfloat16 [8192, 14336], P('narrow', 'wide'), may hold values from -0.0625 to 0.0625
- token_ids: int32 [256], P(('groups', 'narrow')), parts along dimension 0, may hold values from 0 to 128255
- lengths: int32 [16], P(('groups', 'narrow')), parts along dimension 0, may hold values from 1 to 16
- ratio_weight: float32 [128256], replicated, may hold values from 0.25 to 1
Outputs:
- target_hidden: bfloat16 [256, 14336], P(('groups', 'narrow'), 'wide'), parts along dimension 0
- ratio_hidden: bfloat16 [256, 14336], P(('groups', 'narrow'), 'wide'), parts along dimension 0
There are 2 independent parts, one for each index of `groups`. A program takes and returns all parts, laid end to end along the dimension named above; an argument that names none is the same for every part. Nothing has to cross between parts.
All inputs are finite; a program needn't handle non-finite values.
Results may differ from a plain program's by a relative error of at most 0.02.
Values may be sent and summed in bfloat16 or wider, within the bound.
No kernel may reach another device: no remote copies, remote signals or barrier semaphores. Data moves between devices by JAX's collectives and lax.ppermute only.
A program may use at most 128 MiB of HBM per device.

v0:
```python
import jax
import jax.numpy as jnp
from jax import lax
from jax.sharding import PartitionSpec as P


def matmul(left, right):
    return jnp.dot(left, right, preferred_element_type=jnp.float32)


def pair_project(w_gate, w_upper, piece):
    return jnp.concatenate([matmul(piece, w_gate), matmul(piece, w_upper)], axis=1)


def gated(summed, hidden_cols):
    return jax.nn.silu(summed[:, :hidden_cols]) * summed[:, hidden_cols:]


def local(
    target_states,
    source_states,
    target_gate,
    target_up,
    source_gate,
    source_up,
    token_ids,
    lengths,
    ratio_weight,
):
    hidden_cols = target_gate.shape[1]
    own_rows = token_ids.shape[0]
    target_terms = pair_project(
        target_gate, target_up, lax.all_gather(target_states, "wide", axis=0, tiled=True)
    )
    source_terms = pair_project(
        source_gate, source_up, lax.all_gather(source_states, "wide", axis=0, tiled=True)
    )
    target_sum, source_sum = (
        lax.psum_scatter(
            target_terms.astype(jnp.bfloat16), "narrow", scatter_dimension=0, tiled=True
        ).astype(jnp.float32),
        lax.psum_scatter(
            source_terms.astype(jnp.bfloat16), "narrow", scatter_dimension=0, tiled=True
        ).astype(jnp.float32),
    )
    target_act = gated(target_sum, hidden_cols)
    source_act = gated(source_sum, hidden_cols)
    slot_count = own_rows // lengths.shape[0]
    slots = jnp.arange(slot_count, dtype=jnp.int32)
    live = (slots[None, :] < lengths[:, None]).reshape(-1).astype(jnp.float32)
    weight = ratio_weight[token_ids]
    target_out = (live[:, None] * target_act).astype(jnp.bfloat16)
    ratio_out = (live[:, None] * (target_act - weight[:, None] * source_act)).astype(jnp.bfloat16)
    return (target_out, ratio_out)


def solution(mesh):
    placed = (
        P(("groups", "wide"), "narrow"),
        P(("groups", "wide"), "narrow"),
        P("narrow", "wide"),
        P("narrow", "wide"),
        P("narrow", "wide"),
        P("narrow", "wide"),
        P(("groups", "narrow")),
        P(("groups", "narrow")),
        P(),
    )
    return jax.shard_map(
        local,
        mesh=mesh,
        in_specs=placed,
        out_specs=(P(("groups", "narrow"), "wide"), P(("groups", "narrow"), "wide")),
        check_vma=False,
    )
```

profile of v0, /device:TPU:0, one launch (start us, length us, event | category | flops | bytes accessed | tf_op | source)
XLA Modules:
  0.0 111.2 jit_solution(676333890963916121)
XLA Ops:
  7.2 0.0 copy-start
  7.2 0.0 reduce-scatter.3.cloned.1.call-start
  7.2 17.7 %all_gather.6 = bf16[128,2048]{1,0:T(8,128)(2,1)S(1)} all-gather(bf16[32,2048]{1,0:T(8,128)(2,1)} %param.9), channel_id=1, replica_groups=mesh['groups'=2,'wide'=4,'narrow'=4] {'wide'}, dimensions={0}, use_global_device_ids=true | all-gather | bytes 655360 | tf_op jit(solution)/shard_map/all_gather | solution.py:33
  24.9 0.0 copy-start.1
  24.9 7.4 %convolution_convert_fusion.2 = bf16[128,3584]{1,0:T(8,128)(2,1)S(1)} fusion(bf16[128,2048]{1,0:T(8,128)(2,1)S(1)} %all_gather.6, bf16[2048,3584]{1,0:T(8,128)(2,1)} %param.12), kind=kOutput, calls=%fused_computation.3 | convolution fusion | flops 1879506944 | bytes 16121856 | tf_op jit(solution)/shard_map/dot_general | solution.py:8
  32.3 1.9 %copy-done.1 = bf16[2048,3584]{1,0:T(8,128)(2,1)S(1)} copy-done((bf16[2048,3584]{1,0:T(8,128)(2,1)S(1)}, bf16[2048,3584]{1,0:T(8,128)(2,1)}, u32[]{:S(2)}) %copy-start.1) | copy-done | bytes 14680088
  34.3 2.2 %convolution_convert_fusion.3 = bf16[128,3584]{1,0:T(8,128)(2,1)S(1)} fusion(bf16[128,2048]{1,0:T(8,128)(2,1)S(1)} %all_gather.6, bf16[2048,3584]{1,0:T(8,128)(2,1)S(1)} %copy-done.1), kind=kOutput, calls=%fused_computation.4 | convolution fusion | flops 1879506944 | bytes 16121856 | tf_op jit(solution)/shard_map/dot_general | solution.py:8
  36.4 0.0 copy-start.2
  36.5 1.4 %pad_maximum_fusion = bf16[128,7168]{1,0:T(8,128)(2,1)} fusion(bf16[128,3584]{1,0:T(8,128)(2,1)S(1)} %convolution_convert_fusion.2, bf16[128,3584]{1,0:T(8,128)(2,1)S(1)} %convolution_convert_fusion.3), kind=kLoop, calls=%fused_computation.5 | loop fusion | flops 3670016 | bytes 3670016 | tf_op jit(solution)/shard_map/concatenate | solution.py:12
  37.9 0.0 reduce-scatter.3.cloned.1.call-update
  37.9 0.0 reduce-scatter.5.cloned.1.call-start
  37.9 0.0 copy-done.2
  38.0 16.3 %all_gather.7 = bf16[128,2048]{1,0:T(8,128)(2,1)S(1)} all-gather(bf16[32,2048]{1,0:T(8,128)(2,1)S(1)} %copy-done.2), channel_id=1, replica_groups=mesh['groups'=2,'wide'=4,'narrow'=4] {'wide'}, dimensions={0}, use_global_device_ids=true | all-gather | bytes 655360 | tf_op jit(solution)/shard_map/all_gather | solution.py:36
  54.2 7.6 %convolution_convert_fusion = bf16[128,3584]{1,0:T(8,128)(2,1)S(1)} fusion(bf16[128,2048]{1,0:T(8,128)(2,1)S(1)} %all_gather.7, bf16[2048,3584]{1,0:T(8,128)(2,1)} %param.14), kind=kOutput, calls=%fused_computation.1 | convolution fusion | flops 1879506944 | bytes 16121856 | tf_op jit(solution)/shard_map/dot_general | solution.py:8
  61.8 7.3 %convolution_convert_fusion.1 = bf16[128,3584]{1,0:T(8,128)(2,1)S(1)} fusion(bf16[128,2048]{1,0:T(8,128)(2,1)S(1)} %all_gather.7, bf16[2048,3584]{1,0:T(8,128)(2,1)} %param.13), kind=kOutput, calls=%fused_computation.2 | convolution fusion | flops 1879506944 | bytes 16121856 | tf_op jit(solution)/shard_map/dot_general | solution.py:8
  69.2 0.0 copy-start.3
  69.2 0.0 copy-start.4
  69.2 1.4 %pad_maximum_fusion.1 = bf16[128,7168]{1,0:T(8,128)(2,1)} fusion(bf16[128,3584]{1,0:T(8,128)(2,1)S(1)} %convolution_convert_fusion, bf16[128,3584]{1,0:T(8,128)(2,1)S(1)} %convolution_convert_fusion.1), kind=kLoop, calls=%fused_computation.6 | loop fusion | flops 3670016 | bytes 3670016 | tf_op jit(solution)/shard_map/concatenate | solution.py:12
  70.6 0.0 reduce-scatter.5.cloned.1.call-update
  70.7 0.0 copy-done.3
  70.7 0.1 compare_convert_fusion
  70.7 0.1 reshape.22
  70.8 0.0 copy-done.4
  70.8 0.0 copy-done
  70.8 0.7 gather_fusion
  71.5 0.0 reduce-scatter.3.cloned.1.call-done
  71.6 1.1 convert_element_type.26
  72.6 29.5 %reduce-scatter.5.cloned.1.call-done = bf16[32,7168]{1,0:T(8,128)(2,1)} async-done(((bf16[128,7168]{1,0:T(8,128)(2,1)}), bf16[32,7168]{1,0:T(8,128)(2,1)}) %reduce-scatter.5.cloned.1.call-update) | async-done | bytes 458768 | tf_op jit(solution)/shard_map/reduce_scatter | solution.py:42
  102.2 1.1 convert_element_type.28
  103.2 1.1 fusion.3
  (2 shorter events, 0.0 us)
Async XLA Ops:
  7.2 63.7 %copy-start = (f32[128256]{0:T(1024)S(1)}, f32[128256]{0:T(1024)}, u32[]{:S(2)}) copy-start(f32[128256]{0:T(1024)} %param.17) | copy-start | bytes 1539076
  7.2 64.4 %reduce-scatter.3.cloned.1.call-start = ((), (), s32[]{:S(2)}) async-start(), calls=%async_computation.2 | async-start | bytes 2293760 | tf_op jit(solution)/shard_map/reduce_scatter | solution.py:39
  24.9 9.3 %copy-start.1 = (bf16[2048,3584]{1,0:T(8,128)(2,1)S(1)}, bf16[2048,3584]{1,0:T(8,128)(2,1)}, u32[]{:S(2)}) copy-start(bf16[2048,3584]{1,0:T(8,128)(2,1)} %param.11) | copy-start | bytes 44040196
  36.4 1.5 %copy-start.2 = (bf16[32,2048]{1,0:T(8,128)(2,1)S(1)}, bf16[32,2048]{1,0:T(8,128)(2,1)}, u32[]{:S(2)}) copy-start(bf16[32,2048]{1,0:T(8,128)(2,1)} %param.10) | copy-start | bytes 393220
  37.9 64.3 %reduce-scatter.5.cloned.1.call-start = ((), (), s32[]{:S(2)}) async-start(), calls=%async_computation.3 | async-start | bytes 2293760 | tf_op jit(solution)/shard_map/reduce_scatter | solution.py:42
  69.2 1.5 %copy-start.3 = (s32[2]{0:T(128)S(1)}, s32[2]{0:T(128)}, u32[]{:S(2)}) copy-start(s32[2]{0:T(128)} %param.16) | copy-start | bytes 28
  69.2 1.6 %copy-start.4 = (s32[32]{0:T(128)S(1)}, s32[32]{0:T(128)}, u32[]{:S(2)}) copy-start(s32[32]{0:T(128)} %param.15) | copy-start | bytes 388
Sparse Core Ops, SparseCore 0:
  38.0 31.5 reduce-scatter.2
  72.3 29.8 reduce-scatter.4
where the time goes:
time: 111 us
  blocking collectives  34 us (31%)
  waiting for transfers between devices  29.6 us (27%)
  matrix products  24.5 us (22%)
  between operations  14.1 us (13%)
  other arithmetic  6.17 us (6%)
  local copies, waits for them, and re-layouts  2.74 us (2%)
    reduce_scatter x1, waiting for transfers between devices, local(): lax.psum_scatter(source_terms.astype(jnp.bfloat16), 'narrow', scatter_dim...  29.5 us
    dot_general x4, matrix products, matmul(): return jnp.dot(left, right, preferred_element_type=jnp.float32)  24.5 us
    all_gather x1, blocking collectives, local(): lax.all_gather(target_states, 'wide', axis=0, tiled=True)  17.7 us
    all_gather x1, blocking collectives, local(): lax.all_gather(source_states, 'wide', axis=0, tiled=True)  16.3 us
    concatenate x2, other arithmetic, pair_project(): jnp.concatenate([matmul(piece, w_gate), matmul(piece, w_upper)], axis=1)  2.84 us
  transfers between devices with their start and end apart: 2, of which 1 were waited for; matrix products, arithmetic and copies ran while one was open for 16% of the time, Pallas kernels for 0%

commit v1 on v0

v1 whole, which is shorter than its diff:
```python
import math

import jax
import jax.numpy as jnp
from jax import lax
from jax.sharding import PartitionSpec as P


def ring_gather(piece, axis, size):
    pairs = [(i, (i + 1) % size) for i in range(size)]
    pieces = [piece]
    for _ in range(size - 1):
        pieces.append(lax.ppermute(pieces[-1], axis, pairs))
    return pieces


def halving_order(size):
    bits = size.bit_length() - 1
    reverse = [sum(((p >> b) & 1) << (bits - 1 - b) for b in range(bits)) for p in range(size)]
    return reverse[::-1]


def arrange(pieces, me_wide, me_narrow, wide, narrow):
    piece_rows = pieces[0].shape[0]
    block_rows = piece_rows * wide // narrow
    sub = math.gcd(piece_rows, block_rows)
    place = [0] * narrow
    for position, offset in enumerate(halving_order(narrow)):
        place[offset] = position
    place = jnp.array(place, jnp.int32)
    whole = jnp.zeros((piece_rows * wide, pieces[0].shape[1]), pieces[0].dtype)
    for back, piece in enumerate(pieces):
        for start in range(0, piece_rows, sub):
            row = (me_wide + wide - back) % wide * piece_rows + start
            owner = row // block_rows
            row = place[owner ^ me_narrow] * block_rows + row % block_rows
            whole = lax.dynamic_update_slice_in_dim(whole, piece[start : start + sub], row, axis=0)
    return whole


def halving_sum(terms, axis, size):
    step = 1
    while step < size:
        half = terms.shape[0] // 2
        pairs = [(i, i ^ step) for i in range(size)]
        got = lax.ppermute(terms[:half].astype(jnp.bfloat16), axis, pairs)
        terms = terms[half:] + got.astype(jnp.float32)
        step *= 2
    return terms


def local(mesh_shape, target_states, source_states, target_gate, target_up, source_gate, source_up, token_ids, lengths, ratio_weight):
    wide, narrow = mesh_shape["wide"], mesh_shape["narrow"]
    me_wide, me_narrow = lax.axis_index("wide"), lax.axis_index("narrow")
    own_rows = token_ids.shape[0]

    slot_count = own_rows // lengths.shape[0]
    slots = jnp.arange(slot_count, dtype=jnp.int32)
    live = (slots[None, :] < lengths[:, None]).reshape(-1).astype(jnp.float32)
    weight = ratio_weight[token_ids]

    target_pieces = ring_gather(target_states, "wide", wide)
    source_states, target_pieces = lax.optimization_barrier((source_states, target_pieces))
    source_pieces = ring_gather(source_states, "wide", wide)

    def product(rows, matrix):
        terms = jnp.dot(rows, matrix, preferred_element_type=jnp.float32).astype(jnp.bfloat16)
        return halving_sum(terms.astype(jnp.float32), "narrow", narrow)

    target_rows = arrange(target_pieces, me_wide, me_narrow, wide, narrow)
    target_act = jax.nn.silu(product(target_rows, target_gate)) * product(target_rows, target_up)
    source_rows = arrange(source_pieces, me_wide, me_narrow, wide, narrow)
    source_act = jax.nn.silu(product(source_rows, source_gate)) * product(source_rows, source_up)

    target_out = (live[:, None] * target_act).astype(jnp.bfloat16)
    ratio_out = (live[:, None] * (target_act - weight[:, None] * source_act)).astype(jnp.bfloat16)
    return (target_out, ratio_out)


def solution(mesh):
    placed = (
        P(("groups", "wide"), "narrow"),
        P(("groups", "wide"), "narrow"),
        P("narrow", "wide"),
        P("narrow", "wide"),
        P("narrow", "wide"),
        P("narrow", "wide"),
        P(("groups", "narrow")),
        P(("groups", "narrow")),
        P(),
    )
    mesh_shape = dict(mesh.shape)

    def body(*args):
        return local(mesh_shape, *args)

    return jax.shard_map(
        body,
        mesh=mesh,
        in_specs=placed,
        out_specs=(P(("groups", "narrow"), "wide"), P(("groups", "narrow"), "wide")),
        check_vma=False,
    )
```

time: 111 us -> 92.3 us (0.83)
  blocking collectives: 34 us -> 0 us
  local copies, waits for them, and re-layouts: 2.74 us -> 18.1 us
  between operations: 14.1 us -> 3.49 us
  starting transfers between devices: 0.08 us -> 9.22 us
    all_gather x2 -> x0, blocking collectives: 34 us -> none  [the longest x1 17.7 us: local(): lax.all_gather(target_states, 'wide', axis=0, tiled=True)]
    ppermute x0 -> x14, waiting for transfers between devices: none -> 30.1 us  [the longest x6 16.3 us: ring_gather(): pieces.append(lax.ppermute(pieces[-1], axis, pairs))]
    reduce_scatter x2 -> x0, waiting for transfers between devices: 29.5 us -> none  [the longest x1 29.5 us: local(): lax.psum_scatter(source_terms.astype(jnp.bfloat16), 'narrow', scatter_dim...]
    dynamic_update_slice x0 -> x8, local copies, waits for them, and re-layouts: none -> 11.1 us  [arrange(): lax.dynamic_update_slice_in_dim(whole, piece[start:start + sub], row, axi...]
    ppermute x0 -> x14, starting transfers between devices: none -> 9.22 us  [the longest x8 4.98 us: halving_sum(): got = lax.ppermute(terms[:half].astype(jnp.bfloat16), axis, pairs)]
    slice x0 -> x8, local copies, waits for them, and re-layouts: none -> 3.75 us  [halving_sum(): got = lax.ppermute(terms[:half].astype(jnp.bfloat16), axis, pairs)]
    concatenate x2 -> x0, other arithmetic: 2.84 us -> none  [pair_project(): jnp.concatenate([matmul(piece, w_gate), matmul(piece, w_upper)], axis=1)]
    add x0 -> x4, other arithmetic: none -> 2.52 us  [halving_sum(): terms = terms[half:] + got.astype(jnp.float32)]
  transfers between devices with their start and end apart: 2 -> 14, of which waited for: 1 -> 7; matrix products, arithmetic and copies ran while one was open for 16% -> 49% of each run, Pallas kernels for 0% -> 0%
where the time goes in v1:
time: 92.3 us; the launch traced here: 91.7 us
  waiting for transfers between devices  30.1 us (33%)
  matrix products  24.4 us (26%)
  local copies, waits for them, and re-layouts  18.1 us (20%)
  starting transfers between devices  9.22 us (10%)
  other arithmetic  6.39 us (7%)
  between operations  3.49 us (4%)
    dot_general x4, matrix products, product(): jnp.dot(rows, matrix, preferred_element_type=jnp.float32)  24.4 us
    ppermute x6, waiting for transfers between devices, ring_gather(): pieces.append(lax.ppermute(pieces[-1], axis, pairs))  16.3 us
    ppermute x8, waiting for transfers between devices, halving_sum(): got = lax.ppermute(terms[:half].astype(jnp.bfloat16), axis, pairs)  13.9 us
    dynamic_update_slice x8, local copies, waits for them, and re-layouts, arrange(): lax.dynamic_update_slice_in_dim(whole, piece[start:start + sub], row, axi...  11.1 us
    ppermute x8, starting transfers between devices, halving_sum(): got = lax.ppermute(terms[:half].astype(jnp.bfloat16), axis, pairs)  4.98 us
    ppermute x6, starting transfers between devices, ring_gather(): pieces.append(lax.ppermute(pieces[-1], axis, pairs))  4.23 us
    slice x8, local copies, waits for them, and re-layouts, halving_sum(): got = lax.ppermute(terms[:half].astype(jnp.bfloat16), axis, pairs)  3.75 us
    add x4, other arithmetic, halving_sum(): terms = terms[half:] + got.astype(jnp.float32)  2.52 us
  transfers between devices with their start and end apart: 14, of which 7 were waited for; matrix products, arithmetic and copies ran while one was open for 49% of the time, Pallas kernels for 0%

profile of v1, /device:TPU:0, one launch (start us, length us, event | category | flops | bytes accessed | tf_op | source)
XLA Modules:
  0.0 91.7 jit_solution(13892202399920338471)
XLA Ops:
  0.6 0.0 copy-start
  0.6 3.1 %collective-permute-start = (bf16[32,2048]{1,0:T(8,128)(2,1)}, bf16[32,2048]{1,0:T(8,128)(2,1)S(1)}, u32[]{:S(2)}, u32[]{:S(2)}) collective-permute-start(bf16[32,2048]{1,0:T(8,128)(2,1)} %param.11), channel_id=1, source_target_pairs={{0,4},{4,8},{8,12},{12,0},{1,5},{5,9},{9,13},{13,1},{2,6},{6,10},{... | collective-permute-start | bytes 393224 | tf_op jit(solution)/shard_map/ppermute | solution.py:13
  3.7 5.7 %collective-permute-done = bf16[32,2048]{1,0:T(8,128)(2,1)S(1)} collective-permute-done((bf16[32,2048]{1,0:T(8,128)(2,1)}, bf16[32,2048]{1,0:T(8,128)(2,1)S(1)}, u32[]{:S(2)}, u32[]{:S(2)}) %collective-permute-start) | collective-permute-done | bytes 131104 | tf_op jit(solution)/shard_map/ppermute | solution.py:13
  9.5 0.0 collective-permute-start.1
  9.5 6.8 %collective-permute-done.1 = bf16[32,2048]{1,0:T(8,128)(2,1)S(1)} collective-permute-done((bf16[32,2048]{1,0:T(8,128)(2,1)S(1)}, bf16[32,2048]{1,0:T(8,128)(2,1)S(1)}, u32[]{:S(2)}, u32[]{:S(2)}) %collective-permute-start.1) | collective-permute-done | bytes 131104 | tf_op jit(solution)/shard_map/ppermute | solution.py:13
  16.2 0.0 collective-permute-start.2
  16.2 1.4 %fusion.7 = (s32[1]{0:T(128)}, s32[1]{0:T(128)}, s32[1]{0:T(128)}, s32[1]{0:T(128)}) fusion(s32[4]{0:T(128)} %constant.145.clone, s32[]{:T(128)S(6)} %select_n.128, s32[]{:T(128)S(6)} %select_n.118, s32[]{:T(128)S(6)} %select_n.113, s32[]{:T(128)S(6)} %select_n.123), kind=kLoop, calls=%fused_computation.27 | loop fusion | bytes 48 | tf_op jit(solution)/shard_map/dynamic_slice | solution.py:36
  20.3 2.7 %collective-permute-done.2 = bf16[32,2048]{1,0:T(8,128)(2,1)S(1)} collective-permute-done((bf16[32,2048]{1,0:T(8,128)(2,1)S(1)}, bf16[32,2048]{1,0:T(8,128)(2,1)S(1)}, u32[]{:S(2)}, u32[]{:S(2)}) %collective-permute-start.2) | collective-permute-done | bytes 131104 | tf_op jit(solution)/shard_map/ppermute | solution.py:13
  23.0 0.0 collective-permute-start.7
  23.0 0.7 compare_convert_fusion
  23.7 0.1 reshape.38
  23.9 1.6 %dynamic_update_slice.24 = bf16[128,2048]{1,0:T(8,128)(2,1)S(1)} dynamic-update-slice(bf16[128,2048]{1,0:T(8,128)(2,1)S(1)} %broadcast.22.clone.1, bf16[32,2048]{1,0:T(8,128)(2,1)} %param.11, s32[]{:T(128)S(6)} %select_n.115, s32[]{:T(128)} %constant.133.clone.1) | dynamic-update-slice | bytes 262148 | tf_op jit(solution)/shard_map/dynamic_update_slice | solution.py:37
  25.4 1.2 %dynamic_update_slice.25 = bf16[128,2048]{1,0:T(8,128)(2,1)S(1)} dynamic-update-slice(bf16[128,2048]{1,0:T(8,128)(2,1)S(1)} %dynamic_update_slice.24, bf16[32,2048]{1,0:T(8,128)(2,1)S(1)} %collective-permute-done, s32[]{:T(128)S(6)} %select_n.120, s32[]{:T(128)} %constant.133.clone.1) | dynamic-update-slice | bytes 262148 | tf_op jit(solution)/shard_map/dynamic_update_slice | solution.py:37
  26.6 1.2 %dynamic_update_slice.26 = bf16[128,2048]{1,0:T(8,128)(2,1)S(1)} dynamic-update-slice(bf16[128,2048]{1,0:T(8,128)(2,1)S(1)} %dynamic_update_slice.25, bf16[32,2048]{1,0:T(8,128)(2,1)S(1)} %collective-permute-done.1, s32[]{:T(128)S(6)} %select_n.125, s32[]{:T(128)} %constant.133.clone.1) | dynamic-update-slice | bytes 262148 | tf_op jit(solution)/shard_map/dynamic_update_slice | solution.py:37
  27.8 1.2 %dynamic_update_slice.27 = bf16[128,2048]{1,0:T(8,128)(2,1)S(1)} dynamic-update-slice(bf16[128,2048]{1,0:T(8,128)(2,1)S(1)} %dynamic_update_slice.26, bf16[32,2048]{1,0:T(8,128)(2,1)S(1)} %collective-permute-done.2, s32[]{:T(128)S(6)} %select_n.130, s32[]{:T(128)} %constant.133.clone.1) | dynamic-update-slice | bytes 262148 | tf_op jit(solution)/shard_map/dynamic_update_slice | solution.py:37
  28.9 0.0 copy-start.1
  28.9 1.0 %collective-permute-done.7 = bf16[32,2048]{1,0:T(8,128)(2,1)S(1)} collective-permute-done((bf16[32,2048]{1,0:T(8,128)(2,1)}, bf16[32,2048]{1,0:T(8,128)(2,1)S(1)}, u32[]{:S(2)}, u32[]{:S(2)}) %collective-permute-start.7) | collective-permute-done | bytes 131104 | tf_op jit(solution)/shard_map/ppermute | solution.py:13
  30.0 0.0 collective-permute-start.8
  30.0 7.7 %convolution_convert_fusion.3 = bf16[128,3584]{1,0:T(8,128)(2,1)S(1)} fusion(bf16[128,2048]{1,0:T(8,128)(2,1)S(1)} %dynamic_update_slice.27, bf16[2048,3584]{1,0:T(8,128)(2,1)} %param.13), kind=kOutput, calls=%fused_computation.4 | convolution fusion | flops 1879506944 | bytes 16121856 | tf_op jit(solution)/shard_map/dot_general | solution.py:67
  37.7 0.0 copy-start.3
  37.7 0.1 collective-permute-start.3
  37.8 0.0 collective-permute-done.8
  37.8 0.0 copy-done.4
  37.9 1.1 %collective-permute-start.9 = (bf16[32,2048]{1,0:T(8,128)(2,1)}, bf16[32,2048]{1,0:T(8,128)(2,1)}, u32[]{:S(2)}, u32[]{:S(2)}) collective-permute-start(bf16[32,2048]{1,0:T(8,128)(2,1)} %collective-permute-done.8), channel_id=1, source_target_pairs={{0,4},{4,8},{8,12},{12,0},{1,5},{5,9},{9,13},{13,1},{2,6},{6,10},{... | collective-permute-start | bytes 393224 | tf_op jit(solution)/shard_map/ppermute | solution.py:13
  39.0 0.0 copy-done.1
  39.0 2.2 %convolution_convert_fusion.2 = bf16[128,3584]{1,0:T(8,128)(2,1)S(1)} fusion(bf16[128,2048]{1,0:T(8,128)(2,1)S(1)} %dynamic_update_slice.27, bf16[2048,3584]{1,0:T(8,128)(2,1)S(1)} %copy-done.1), kind=kOutput, calls=%fused_computation.3 | convolution fusion | flops 1879506944 | bytes 16121856 | tf_op jit(solution)/shard_map/dot_general | solution.py:67
  41.2 0.8 slice.95
  42.0 0.0 collective-permute-start.5
  42.0 0.0 copy-done.3
  42.0 0.8 dynamic_update_slice.28
  42.8 1.8 %dynamic_update_slice.29 = bf16[128,2048]{1,0:T(8,128)(2,1)S(1)} dynamic-update-slice(bf16[128,2048]{1,0:T(8,128)(2,1)S(1)} %dynamic_update_slice.28, bf16[32,2048]{1,0:T(8,128)(2,1)} %copy-done.4, s32[]{:T(128)S(6)} %select_n.120, s32[]{:T(128)} %constant.133.clone.1) | dynamic-update-slice | bytes 262148 | tf_op jit(solution)/shard_map/dynamic_update_slice | solution.py:37
  44.6 1.8 %dynamic_update_slice.30 = bf16[128,2048]{1,0:T(8,128)(2,1)S(1)} dynamic-update-slice(bf16[128,2048]{1,0:T(8,128)(2,1)S(1)} %dynamic_update_slice.29, bf16[32,2048]{1,0:T(8,128)(2,1)} %collective-permute-done.8, s32[]{:T(128)S(6)} %select_n.125, s32[]{:T(128)} %constant.133.clone.1) | dynamic-update-slice | bytes 262148 | tf_op jit(solution)/shard_map/dynamic_update_slice | solution.py:37
  46.3 0.0 collective-permute-done.9
  46.4 1.8 %dynamic_update_slice.31 = bf16[128,2048]{1,0:T(8,128)(2,1)S(1)} dynamic-update-slice(bf16[128,2048]{1,0:T(8,128)(2,1)S(1)} %dynamic_update_slice.30, bf16[32,2048]{1,0:T(8,128)(2,1)} %collective-permute-done.9, s32[]{:T(128)S(6)} %select_n.130, s32[]{:T(128)} %constant.133.clone.1) | dynamic-update-slice | bytes 262148 | tf_op jit(solution)/shard_map/dynamic_update_slice | solution.py:37
  48.1 7.3 %convolution_convert_fusion.1 = bf16[128,3584]{1,0:T(8,128)(2,1)S(1)} fusion(bf16[128,2048]{1,0:T(8,128)(2,1)S(1)} %dynamic_update_slice.31, bf16[2048,3584]{1,0:T(8,128)(2,1)} %param.15), kind=kOutput, calls=%fused_computation.2 | convolution fusion | flops 1879506944 | bytes 16121856 | tf_op jit(solution)/shard_map/dot_general | solution.py:67
  55.4 0.0 copy-start.5
  55.4 0.8 collective-permute-start.10
  56.2 7.3 %convolution_convert_fusion = bf16[128,3584]{1,0:T(8,128)(2,1)S(1)} fusion(bf16[128,2048]{1,0:T(8,128)(2,1)S(1)} %dynamic_update_slice.31, bf16[2048,3584]{1,0:T(8,128)(2,1)} %param.16), kind=kOutput, calls=%fused_computation.1 | convolution fusion | flops 1879506944 | bytes 16121856 | tf_op jit(solution)/shard_map/dot_general | solution.py:67
  63.5 0.1 collective-permute-start.12
  63.6 0.0 collective-permute-done.3
  63.6 1.2 %convert_add_fusion.3 = f32[64,3584]{1,0:T(8,128)S(1)} fusion(bf16[64,3584]{1,0:T(8,128)(2,1)} %collective-permute-done.3, bf16[128,3584]{1,0:T(8,128)(2,1)S(1)} %convolution_convert_fusion.3), kind=kLoop, calls=%fused_computation.8 | loop fusion | flops 688128 | bytes 1835008 | tf_op jit(solution)/shard_map/add | solution.py:47
  64.8 0.7 slice.141
  65.5 1.5 %collective-permute-start.4 = (bf16[32,3584]{1,0:T(8,128)(2,1)}, bf16[32,3584]{1,0:T(8,128)(2,1)S(1)}, u32[]{:S(2)}, u32[]{:S(2)}) collective-permute-start(bf16[32,3584]{1,0:T(8,128)(2,1)} %slice.141), channel_id=1, source_target_pairs={{0,2},{1,3},{2,0},{3,1},{4,6},{5,7},{6,4},{7,5},{8,10},{9,11},{10,... | collective-permute-start | bytes 688136 | tf_op jit(solution)/shard_map/ppermute | solution.py:46
  67.0 0.0 collective-permute-done.5
  67.0 1.2 %convert_add_fusion.2 = f32[64,3584]{1,0:T(8,128)S(1)} fusion(bf16[64,3584]{1,0:T(8,128)(2,1)} %collective-permute-done.5, bf16[128,3584]{1,0:T(8,128)(2,1)S(1)} %convolution_convert_fusion.2), kind=kLoop, calls=%fused_computation.7 | loop fusion | flops 688128 | bytes 1835008 | tf_op jit(solution)/shard_map/add | solution.py:47
  68.2 0.7 slice.140
  68.9 0.5 collective-permute-start.6
  69.4 0.0 collective-permute-done.10
  69.4 0.1 convert_add_fusion.1
  69.5 0.7 slice.139
  70.2 1.5 %collective-permute-start.11 = (bf16[32,3584]{1,0:T(8,128)(2,1)}, bf16[32,3584]{1,0:T(8,128)(2,1)}, u32[]{:S(2)}, u32[]{:S(2)}) collective-permute-start(bf16[32,3584]{1,0:T(8,128)(2,1)} %slice.139), channel_id=1, source_target_pairs={{0,2},{1,3},{2,0},{3,1},{4,6},{5,7},{6,4},{7,5},{8,10},{9,11},{10,... | collective-permute-start | bytes 688136 | tf_op jit(solution)/shard_map/ppermute | solution.py:46
  71.7 0.0 collective-permute-done.12
  71.7 0.1 convert_add_fusion
  71.8 0.0 copy-start.2
  71.8 0.9 %copy-done.2 = f32[64,3584]{1,0:T(8,128)} copy-done((f32[64,3584]{1,0:T(8,128)}, f32[64,3584]{1,0:T(8,128)S(1)}, u32[]{:S(2)}) %copy-start.2) | copy-done | bytes 917528
  72.7 0.7 slice.138
  73.4 0.5 collective-permute-start.13
  74.0 0.7 gather_fusion
  74.7 0.0 collective-permute-done.4
  74.7 4.4 %collective-permute-done.6 = bf16[32,3584]{1,0:T(8,128)(2,1)} collective-permute-done((bf16[32,3584]{1,0:T(8,128)(2,1)}, bf16[32,3584]{1,0:T(8,128)(2,1)}, u32[]{:S(2)}, u32[]{:S(2)}) %collective-permute-start.6) | collective-permute-done | bytes 229408 | tf_op jit(solution)/shard_map/ppermute | solution.py:46
  79.1 4.9 %collective-permute-done.11 = bf16[32,3584]{1,0:T(8,128)(2,1)} collective-permute-done((bf16[32,3584]{1,0:T(8,128)(2,1)}, bf16[32,3584]{1,0:T(8,128)(2,1)}, u32[]{:S(2)}, u32[]{:S(2)}) %collective-permute-start.11) | collective-permute-done | bytes 229408 | tf_op jit(solution)/shard_map/ppermute | solution.py:46
  84.0 4.5 %collective-permute-done.13 = bf16[32,3584]{1,0:T(8,128)(2,1)} collective-permute-done((bf16[32,3584]{1,0:T(8,128)(2,1)}, bf16[32,3584]{1,0:T(8,128)(2,1)}, u32[]{:S(2)}, u32[]{:S(2)}) %collective-permute-start.13) | collective-permute-done | bytes 229408 | tf_op jit(solution)/shard_map/ppermute | solution.py:46
  88.6 2.3 %fusion.4 = (bf16[32,3584]{1,0:T(8,128)(2,1)}, f32[32,3584]{1,0:T(8,128)S(1)}) fusion(f32[64,3584]{1,0:T(8,128)} %copy-done.2, bf16[32,3584]{1,0:T(8,128)(2,1)} %collective-permute-done.13, f32[64,3584]{1,0:T(8,128)S(1)} %convert_add_fusion.1, bf16[32,3584]{1,0:T(8,128)(2,1)} %collective-permute-done.11, f32[32]{0:T(128)S(1)} %gather_fusion, ...), kind=kLoop, calls=%fused_computation.15 | loop fusion | flops 2523136 | bytes 3440896 | tf_op jit(solution)/shard_map/convert_element_type | solution.py:76
  90.9 0.8 multiply_convert_fusion
  (10 shorter events, 0.2 us)
Async XLA Ops:
  0.6 73.4 %copy-start = (f32[128256]{0:T(1024)S(1)}, f32[128256]{0:T(1024)}, u32[]{:S(2)}) copy-start(f32[128256]{0:T(1024)} %param.19) | copy-start | bytes 1539076
  0.6 8.8 %collective-permute-start = (bf16[32,2048]{1,0:T(8,128)(2,1)}, bf16[32,2048]{1,0:T(8,128)(2,1)S(1)}, u32[]{:S(2)}, u32[]{:S(2)}) collective-permute-start(bf16[32,2048]{1,0:T(8,128)(2,1)} %param.11), channel_id=1, source_target_pairs={{0,4},{4,8},{8,12},{12,0},{1,5},{5,9},{9,13},{13,1},{2,6},{6,10},{... | collective-permute-start | bytes 393224 | tf_op jit(solution)/shard_map/ppermute | solution.py:13
  9.5 6.8 %collective-permute-start.1 = (bf16[32,2048]{1,0:T(8,128)(2,1)S(1)}, bf16[32,2048]{1,0:T(8,128)(2,1)S(1)}, u32[]{:S(2)}, u32[]{:S(2)}) collective-permute-start(bf16[32,2048]{1,0:T(8,128)(2,1)S(1)} %collective-permute-done), channel_id=1, source_target_pairs={{0,4},{4,8},{8,12},{12,0},{1,5},{5,9},{9,13},{13,1},{2,6},{6,10},{... | collective-permute-start | bytes 393224 | tf_op jit(solution)/shard_map/ppermute | solution.py:13
  16.2 6.8 %collective-permute-start.2 = (bf16[32,2048]{1,0:T(8,128)(2,1)S(1)}, bf16[32,2048]{1,0:T(8,128)(2,1)S(1)}, u32[]{:S(2)}, u32[]{:S(2)}) collective-permute-start(bf16[32,2048]{1,0:T(8,128)(2,1)S(1)} %collective-permute-done.1), channel_id=1, source_target_pairs={{0,4},{4,8},{8,12},{12,0},{1,5},{5,9},{9,13},{13,1},{2,6},{6,10},{... | collective-permute-start | bytes 393224 | tf_op jit(solution)/shard_map/ppermute | solution.py:13
  23.0 7.0 %collective-permute-start.7 = (bf16[32,2048]{1,0:T(8,128)(2,1)}, bf16[32,2048]{1,0:T(8,128)(2,1)S(1)}, u32[]{:S(2)}, u32[]{:S(2)}) collective-permute-start(bf16[32,2048]{1,0:T(8,128)(2,1)} %param.12), channel_id=1, source_target_pairs={{0,4},{4,8},{8,12},{12,0},{1,5},{5,9},{9,13},{13,1},{2,6},{6,10},{... | collective-permute-start | bytes 393224 | tf_op jit(solution)/shard_map/ppermute | solution.py:13
  28.9 10.1 %copy-start.1 = (bf16[2048,3584]{1,0:T(8,128)(2,1)S(1)}, bf16[2048,3584]{1,0:T(8,128)(2,1)}, u32[]{:S(2)}) copy-start(bf16[2048,3584]{1,0:T(8,128)(2,1)} %param.14) | copy-start | bytes 44040196
  30.0 7.9 %copy-start.4 = (bf16[32,2048]{1,0:T(8,128)(2,1)}, bf16[32,2048]{1,0:T(8,128)(2,1)S(1)}, u32[]{:S(2)}) copy-start(bf16[32,2048]{1,0:T(8,128)(2,1)S(1)} %collective-permute-done.7) | copy-start | bytes 393220
  30.0 7.9 %collective-permute-start.8 = (bf16[32,2048]{1,0:T(8,128)(2,1)S(1)}, bf16[32,2048]{1,0:T(8,128)(2,1)}, u32[]{:S(2)}, u32[]{:S(2)}) collective-permute-start(bf16[32,2048]{1,0:T(8,128)(2,1)S(1)} %collective-permute-done.7), channel_id=1, source_target_pairs={{0,4},{4,8},{8,12},{12,0},{1,5},{5,9},{9,13},{13,1},{2,6},{6,10},{... | collective-permute-start | bytes 393224 | tf_op jit(solution)/shard_map/ppermute | solution.py:13
  37.7 4.3 %copy-start.3 = (bf16[32,2048]{1,0:T(8,128)(2,1)S(1)}, bf16[32,2048]{1,0:T(8,128)(2,1)}, u32[]{:S(2)}) copy-start(bf16[32,2048]{1,0:T(8,128)(2,1)} %param.12) | copy-start | bytes 393220
  37.7 25.9 %collective-permute-start.3 = (bf16[64,3584]{1,0:T(8,128)(2,1)S(1)}, bf16[64,3584]{1,0:T(8,128)(2,1)}, u32[]{:S(2)}, u32[]{:S(2)}) collective-permute-start(bf16[64,3584]{1,0:T(8,128)(2,1)S(1)} %slice.91), channel_id=1, source_target_pairs={{0,1},{1,0},{2,3},{3,2},{4,5},{5,4},{6,7},{7,6},{8,9},{9,8},{10,11... | collective-permute-start | bytes 1376264 | tf_op jit(solution)/shard_map/ppermute | solution.py:46
  37.9 8.5 %collective-permute-start.9 = (bf16[32,2048]{1,0:T(8,128)(2,1)}, bf16[32,2048]{1,0:T(8,128)(2,1)}, u32[]{:S(2)}, u32[]{:S(2)}) collective-permute-start(bf16[32,2048]{1,0:T(8,128)(2,1)} %collective-permute-done.8), channel_id=1, source_target_pairs={{0,4},{4,8},{8,12},{12,0},{1,5},{5,9},{9,13},{13,1},{2,6},{6,10},{... | collective-permute-start | bytes 393224 | tf_op jit(solution)/shard_map/ppermute | solution.py:13
  42.0 25.0 %collective-permute-start.5 = (bf16[64,3584]{1,0:T(8,128)(2,1)}, bf16[64,3584]{1,0:T(8,128)(2,1)}, u32[]{:S(2)}, u32[]{:S(2)}) collective-permute-start(bf16[64,3584]{1,0:T(8,128)(2,1)} %slice.95), channel_id=1, source_target_pairs={{0,1},{1,0},{2,3},{3,2},{4,5},{5,4},{6,7},{7,6},{8,9},{9,8},{10,11... | collective-permute-start | bytes 1376264 | tf_op jit(solution)/shard_map/ppermute | solution.py:46
  55.4 18.6 %copy-start.5 = (s32[32]{0:T(128)S(1)}, s32[32]{0:T(128)}, u32[]{:S(2)}) copy-start(s32[32]{0:T(128)} %param.17) | copy-start | bytes 388
  55.4 14.0 %collective-permute-start.10 = (bf16[64,3584]{1,0:T(8,128)(2,1)S(1)}, bf16[64,3584]{1,0:T(8,128)(2,1)S(1)}, u32[]{:S(2)}, u32[]{:S(2)}) collective-permute-start(bf16[64,3584]{1,0:T(8,128)(2,1)S(1)} %slice.99), channel_id=1, source_target_pairs={{0,1},{1,0},{2,3},{3,2},{4,5},{5,4},{6,7},{7,6},{8,9},{9,8},{10,11... | collective-permute-start | bytes 1376264 | tf_op jit(solution)/shard_map/ppermute | solution.py:46
  63.5 8.2 %collective-permute-start.12 = (bf16[64,3584]{1,0:T(8,128)(2,1)S(1)}, bf16[64,3584]{1,0:T(8,128)(2,1)S(1)}, u32[]{:S(2)}, u32[]{:S(2)}) collective-permute-start(bf16[64,3584]{1,0:T(8,128)(2,1)S(1)} %slice.103), channel_id=1, source_target_pairs={{0,1},{1,0},{2,3},{3,2},{4,5},{5,4},{6,7},{7,6},{8,9},{9,8},{10,11... | collective-permute-start | bytes 1376264 | tf_op jit(solution)/shard_map/ppermute | solution.py:46
  65.5 9.2 %collective-permute-start.4 = (bf16[32,3584]{1,0:T(8,128)(2,1)}, bf16[32,3584]{1,0:T(8,128)(2,1)S(1)}, u32[]{:S(2)}, u32[]{:S(2)}) collective-permute-start(bf16[32,3584]{1,0:T(8,128)(2,1)} %slice.141), channel_id=1, source_target_pairs={{0,2},{1,3},{2,0},{3,1},{4,6},{5,7},{6,4},{7,5},{8,10},{9,11},{10,... | collective-permute-start | bytes 688136 | tf_op jit(solution)/shard_map/ppermute | solution.py:46
  68.9 10.3 %collective-permute-start.6 = (bf16[32,3584]{1,0:T(8,128)(2,1)}, bf16[32,3584]{1,0:T(8,128)(2,1)}, u32[]{:S(2)}, u32[]{:S(2)}) collective-permute-start(bf16[32,3584]{1,0:T(8,128)(2,1)} %slice.140), channel_id=1, source_target_pairs={{0,2},{1,3},{2,0},{3,1},{4,6},{5,7},{6,4},{7,5},{8,10},{9,11},{10,... | collective-permute-start | bytes 688136 | tf_op jit(solution)/shard_map/ppermute | solution.py:46
  70.2 13.8 %collective-permute-start.11 = (bf16[32,3584]{1,0:T(8,128)(2,1)}, bf16[32,3584]{1,0:T(8,128)(2,1)}, u32[]{:S(2)}, u32[]{:S(2)}) collective-permute-start(bf16[32,3584]{1,0:T(8,128)(2,1)} %slice.139), channel_id=1, source_target_pairs={{0,2},{1,3},{2,0},{3,1},{4,6},{5,7},{6,4},{7,5},{8,10},{9,11},{10,... | collective-permute-start | bytes 688136 | tf_op jit(solution)/shard_map/ppermute | solution.py:46
  71.8 0.9 %copy-start.2 = (f32[64,3584]{1,0:T(8,128)}, f32[64,3584]{1,0:T(8,128)S(1)}, u32[]{:S(2)}) copy-start(f32[64,3584]{1,0:T(8,128)S(1)} %convert_add_fusion) | copy-start | bytes 2752516
  73.4 15.1 %collective-permute-start.13 = (bf16[32,3584]{1,0:T(8,128)(2,1)}, bf16[32,3584]{1,0:T(8,128)(2,1)}, u32[]{:S(2)}, u32[]{:S(2)}) collective-permute-start(bf16[32,3584]{1,0:T(8,128)(2,1)} %slice.138), channel_id=1, source_target_pairs={{0,2},{1,3},{2,0},{3,1},{4,6},{5,7},{6,4},{7,5},{8,10},{9,11},{10,... | collective-permute-start | bytes 688136 | tf_op jit(solution)/shard_map/ppermute | solution.py:46

commit v2 on v1

v2 whole, which is shorter than its diff:
```python
import functools
import math

import jax
import jax.numpy as jnp
from jax import lax
from jax.experimental import pallas as pl
from jax.experimental.pallas import tpu as pltpu
from jax.sharding import PartitionSpec as P

IN_VMEM = pl.BlockSpec(memory_space=pltpu.VMEM)
ANYWHERE = pl.BlockSpec(memory_space=pl.ANY)


def gather_pieces(piece, axis, size, relayed):
    pieces = [piece]
    for offset in range(1, size):
        low = offset & -offset if relayed else offset
        pairs = [(i, i ^ low) for i in range(size)]
        pieces.append(lax.ppermute(pieces[offset ^ low], axis, pairs))
    return pieces


def halving_order(size):
    bits = size.bit_length() - 1
    reverse = [sum(((p >> b) & 1) << (bits - 1 - b) for b in range(bits)) for p in range(size)]
    return reverse[::-1]


def spots(piece_rows, wide, narrow):
    me_wide, me_narrow = lax.axis_index("wide"), lax.axis_index("narrow")
    block_rows = piece_rows * wide // narrow
    sub = math.gcd(piece_rows, block_rows)
    found = []
    for offset in range(wide):
        for start in range(0, piece_rows, sub):
            row = (me_wide ^ offset) * piece_rows + start
            block = (row // block_rows) ^ me_narrow
            place = sum(
                jnp.where(block == known, position, 0)
                for position, known in enumerate(halving_order(narrow))
            )
            found.append((offset, start, sub, place * block_rows + row % block_rows))
    return found


def load_kernel(count, *refs):
    outs = refs[-1 - count : -1]
    copies = [pltpu.make_async_copy(refs[i], outs[i], refs[-1].at[i]) for i in range(count)]
    for copy in copies:
        copy.start()
    for copy in copies:
        copy.wait()


def load(arrays, after=()):
    return pl.pallas_call(
        functools.partial(load_kernel, len(arrays)),
        out_shape=tuple(pltpu.VMEM(a.shape, a.dtype) for a in arrays),
        in_specs=[ANYWHERE] * (len(arrays) + len(after)),
        out_specs=tuple(IN_VMEM for _ in arrays),
        scratch_shapes=[pltpu.SemaphoreType.DMA((len(arrays),))],
        compiler_params=pltpu.CompilerParams(vmem_limit_bytes=1 << 20),
        cost_estimate=pl.CostEstimate(
            flops=0, transcendentals=0, bytes_accessed=sum(a.size * a.dtype.itemsize for a in arrays)
        ),
    )(*(pltpu.with_memory_space_constraint(a, pltpu.HBM) for a in arrays), *after)


def place_rows(pieces, narrow, rows):
    for i, start, size, spot in spots(pieces[0].shape[0], len(pieces), narrow):
        rows[pl.ds(pl.multiple_of(spot, size), size), :] = pieces[i][start : start + size, :]


def store_parts(outs, value, cols):
    start = 0
    for out in outs:
        out[:, cols] = value[start : start + out.shape[0]].astype(out.dtype)
        start += out.shape[0]


def tile_of(cols):
    for tile in (512, 256, 128):
        if cols % tile == 0:
            return tile
    return cols


def held_kernel(count, narrow, *refs):
    pieces, matrix, outs, rows = refs[:count], refs[count], refs[count + 2 : -1], refs[-1]
    place_rows(pieces, narrow, rows)
    tile = tile_of(matrix.shape[1])
    for start in range(0, matrix.shape[1], tile):
        cols = slice(start, start + tile)
        store_parts(outs, jnp.dot(rows[...], matrix[:, cols], preferred_element_type=jnp.float32), cols)


def streamed_kernel(count, narrow, *refs):
    pieces, matrix, outs, rows = refs[:count], refs[count], refs[count + 2 : -1], refs[-1]

    @pl.when(pl.program_id(0) == 0)
    def _():
        place_rows(pieces, narrow, rows)

    store_parts(outs, jnp.dot(rows[...], matrix[...], preferred_element_type=jnp.float32), slice(None))


def product(pieces, matrix, narrow, held, after):
    total = pieces[0].shape[0] * len(pieces)
    depth, width = matrix.shape
    sizes, left = [], total
    while left > total // narrow:
        left //= 2
        sizes.append(left)
    sizes.append(left)
    tile = tile_of(width)
    shapes = [jax.ShapeDtypeStruct((size, width), jnp.bfloat16) for size in sizes]
    scratch = [pltpu.VMEM((total, depth), jnp.bfloat16)]
    cost = pl.CostEstimate(
        flops=2 * total * depth * width,
        transcendentals=0,
        bytes_accessed=matrix.size * matrix.dtype.itemsize,
    )
    params = pltpu.CompilerParams(vmem_limit_bytes=(8 if held else 16) << 20)
    if held:
        return pl.pallas_call(
            functools.partial(held_kernel, len(pieces), narrow),
            out_shape=shapes,
            in_specs=[IN_VMEM] * (len(pieces) + 1) + [ANYWHERE],
            out_specs=[IN_VMEM] * len(sizes),
            scratch_shapes=scratch,
            compiler_params=params,
            cost_estimate=cost,
        )(*pieces, pltpu.with_memory_space_constraint(matrix, pltpu.VMEM), after)
    return pl.pallas_call(
        functools.partial(streamed_kernel, len(pieces), narrow),
        out_shape=shapes,
        grid=(width // tile,),
        in_specs=[IN_VMEM] * len(pieces)
        + [pl.BlockSpec((depth, tile), lambda i: (0, i)), ANYWHERE],
        out_specs=[pl.BlockSpec((size, tile), lambda i: (0, i)) for size in sizes],
        scratch_shapes=scratch,
        compiler_params=params,
        cost_estimate=cost,
    )(*pieces, pltpu.with_memory_space_constraint(matrix, pltpu.HBM), after)


def halving_step(parts, given, step, size):
    got = lax.ppermute(parts[0], "narrow", [(i, i ^ step) for i in range(size)])
    parts = list(parts[1:])
    sums, start = [], 0
    for part in parts:
        sums.append(part.astype(jnp.float32) + got[start : start + part.shape[0]].astype(jnp.float32))
        start += part.shape[0]
    if len(sums) > 1:
        sums[0] = sums[0].astype(jnp.bfloat16)
    return sums


def halving_sum(parts, step, size):
    while step < size:
        parts = halving_step(parts, None, step, size)
        step *= 2
    return parts[0]


def local(mesh_shape, target_states, source_states, target_gate, target_up, source_gate, source_up, token_ids, lengths, ratio_weight):
    wide, narrow = mesh_shape["wide"], mesh_shape["narrow"]
    own_rows = token_ids.shape[0]

    slot_count = own_rows // lengths.shape[0]
    slots = jnp.arange(slot_count, dtype=jnp.int32)
    live = (slots[None, :] < lengths[:, None]).reshape(-1).astype(jnp.float32)
    weight = ratio_weight[token_ids]

    target_pieces = gather_pieces(target_states, "wide", wide, False)
    (source_states,) = load((source_states,))
    source_pieces = gather_pieces(source_states, "wide", wide, True)
    target_gate, target_up = load((target_gate, target_up), (live, weight))

    gate = product(target_pieces, target_gate, narrow, True, live)
    upper = product(target_pieces, target_up, narrow, True, gate[0])
    gate = halving_step(gate, None, 1, narrow)
    source_g = product(source_pieces, source_gate, narrow, False, gate[0])
    upper = halving_step(upper, None, 1, narrow)
    source_u = product(source_pieces, source_up, narrow, False, upper[0])

    target_act = jax.nn.silu(halving_sum(gate, 2, narrow)) * halving_sum(upper, 2, narrow)
    target_out = (live[:, None] * target_act).astype(jnp.bfloat16)
    source_act = jax.nn.silu(halving_sum(source_g, 1, narrow)) * halving_sum(source_u, 1, narrow)
    ratio_out = (live[:, None] * (target_act - weight[:, None] * source_act)).astype(jnp.bfloat16)
    return (target_out, ratio_out)


def solution(mesh):
    placed = (
        P(("groups", "wide"), "narrow"),
        P(("groups", "wide"), "narrow"),
        P("narrow", "wide"),
        P("narrow", "wide"),
        P("narrow", "wide"),
        P("narrow", "wide"),
        P(("groups", "narrow")),
        P(("groups", "narrow")),
        P(),
    )
    mesh_shape = dict(mesh.shape)

    def body(*args):
        return local(mesh_shape, *args)

    return jax.shard_map(
        body,
        mesh=mesh,
        in_specs=placed,
        out_specs=(P(("groups", "narrow"), "wide"), P(("groups", "narrow"), "wide")),
        check_vma=False,
    )
```

time: 92.3 us -> 70.5 us (0.76)
  Pallas kernels: 0 us -> 31.7 us
  matrix products: 24.4 us -> 0 us
  local copies, waits for them, and re-layouts: 18.1 us -> 0.8 us
  waiting for transfers between devices: 30.1 us -> 18.1 us
  starting transfers between devices: 9.22 us -> 15.2 us
  other arithmetic: 6.39 us -> 3.64 us
  between operations: 3.49 us -> 0.78 us
    pallas_call x0 -> x6, Pallas kernels: none -> 31.7 us  [the longest x2 17.1 us: product(): pl.pallas_call(functools.partial(streamed_kernel, len(pieces), narrow), o...]
    dot_general x4 -> x0, matrix products: 24.4 us -> none  [product(): jnp.dot(rows, matrix, preferred_element_type=jnp.float32)]
    ppermute x14, waiting for transfers between devices: 30.1 us -> 18.1 us  [the longest x8 11.7 us: halving_step(): got = lax.ppermute(parts[0], 'narrow', [(i, i ^ step) for i in range(size)])]
    dynamic_update_slice x8 -> x0, local copies, waits for them, and re-layouts: 11.1 us -> none  [arrange(): lax.dynamic_update_slice_in_dim(whole, piece[start:start + sub], row, axi...]
    ppermute x14, starting transfers between devices: 9.22 us -> 15.2 us  [the longest x6 10.1 us: gather_pieces(): pieces.append(lax.ppermute(pieces[offset ^ low], axis, pairs))]
    slice x8 -> x0, local copies, waits for them, and re-layouts: 3.75 us -> none  [halving_sum(): got = lax.ppermute(terms[:half].astype(jnp.bfloat16), axis, pairs)]
    add x4 -> x0, other arithmetic: 2.52 us -> none  [halving_sum(): terms = terms[half:] + got.astype(jnp.float32)]
    dynamic_slice x1 -> x0, local copies, waits for them, and re-layouts: 1.43 us -> none  [arrange(): row = place[owner ^ me_narrow] * block_rows + row % block_rows]
  transfers between devices with their start and end apart: 14 -> 14, of which waited for: 7 -> 5; matrix products, arithmetic and copies ran while one was open for 49% -> 3% of each run, Pallas kernels for 0% -> 42%
where the time goes in v2:
time: 70.5 us; the launch traced here: 70.2 us
  Pallas kernels  31.7 us (45%)
  waiting for transfers between devices  18.1 us (26%)
  starting transfers between devices  15.2 us (22%)
  other arithmetic  3.64 us (5%)
  local copies, waits for them, and re-layouts  0.8 us (1%)
  between operations  0.78 us (1%)
    pallas_call x2, Pallas kernels, product(): pl.pallas_call(functools.partial(streamed_kernel, len(pieces), narrow), o...  17.1 us
    ppermute x8, waiting for transfers between devices, halving_step(): got = lax.ppermute(parts[0], 'narrow', [(i, i ^ step) for i in range(size)])  11.7 us
    pallas_call x2, Pallas kernels, load(): pl.pallas_call(functools.partial(load_kernel, len(arrays)), out_shape=tup...  10.4 us
    ppermute x6, starting transfers between devices, gather_pieces(): pieces.append(lax.ppermute(pieces[offset ^ low], axis, pairs))  10.1 us
    ppermute x6, waiting for transfers between devices, gather_pieces(): pieces.append(lax.ppermute(pieces[offset ^ low], axis, pairs))  6.35 us
    ppermute x8, starting transfers between devices, halving_step(): got = lax.ppermute(parts[0], 'narrow', [(i, i ^ step) for i in range(size)])  5.03 us
    pallas_call x2, Pallas kernels, product(): pl.pallas_call(functools.partial(held_kernel, len(pieces), narrow), out_s...  4.23 us
  transfers between devices with their start and end apart: 14, of which 5 were waited for; matrix products, arithmetic and copies ran while one was open for 3% of the time, Pallas kernels for 42%

profile of v2, /device:TPU:0, one launch (start us, length us, event | category | flops | bytes accessed | tf_op | source)
XLA Modules:
  0.0 70.2 jit_solution(1819576506086903042)
XLA Ops:
  0.6 0.0 copy-start
  0.6 3.1 %collective-permute-start = (bf16[32,2048]{1,0:T(8,128)(2,1)}, bf16[32,2048]{1,0:T(8,128)(2,1)S(1)}, u32[]{:S(2)}, u32[]{:S(2)}) collective-permute-start(bf16[32,2048]{1,0:T(8,128)(2,1)} %refs_0_.6), channel_id=1, source_target_pairs={{0,4},{4,0},{8,12},{12,8},{1,5},{5,1},{9,13},{13,9},{2,6},{6,2},{1... | collective-permute-start | bytes 393224 | tf_op jit(solution)/shard_map/ppermute | solution.py:20
  3.7 2.6 %collective-permute-start.1 = (bf16[32,2048]{1,0:T(8,128)(2,1)}, bf16[32,2048]{1,0:T(8,128)(2,1)S(1)}, u32[]{:S(2)}, u32[]{:S(2)}) collective-permute-start(bf16[32,2048]{1,0:T(8,128)(2,1)} %refs_0_.6), channel_id=1, source_target_pairs={{0,8},{4,12},{8,0},{12,4},{1,9},{5,13},{9,1},{13,5},{2,10},{6,14},... | collective-permute-start | bytes 393224 | tf_op jit(solution)/shard_map/ppermute | solution.py:20
  6.3 0.0 collective-permute-start.2
  6.3 0.7 %compare_convert_fusion = f32[2,16]{1,0:T(2,128)S(1)} fusion(s32[2]{0:T(128)} %param.16), kind=kLoop, calls=%fused_computation.10 | loop fusion | flops 64 | bytes 136 | tf_op jit(solution)/shard_map/convert_element_type | solution.py:173
  7.1 0.7 compare_select_fusion
  7.7 0.1 reshape.22.refs_2_.refs_5_
  7.8 0.0 copy-done
  7.8 0.7 gather_fusion
  8.5 0.0 copy-start.2
  8.5 9.4 %shard_map.104 = (bf16[2048,3584]{1,0:T(8,128)(2,1)S(1)}, bf16[2048,3584]{1,0:T(8,128)(2,1)S(1)}) custom-call(bf16[2048,3584]{1,0:T(8,128)(2,1)} %refs_0_.4, bf16[2048,3584]{1,0:T(8,128)(2,1)} %refs_1_.1, f32[32]{0:T(128)S(1)} %reshape.22.refs_2_.refs_5_, f32[32]{0:T(128)S(1)} %gather_fusion), custom_call_target="tpu_custom_call" | custom-call | bytes 29360128 | tf_op jit(solution)/shard_map/pallas_call | solution.py:57
  18.0 0.0 collective-permute-done.refs_1_
  18.0 0.0 collective-permute-done.1.refs_2_
  18.0 0.0 collective-permute-done.2.refs_3_
  18.0 0.0 copy-done.2
  18.0 2.1 %shard_map.105 = (bf16[64,3584]{1,0:T(8,128)(2,1)S(1)}, bf16[32,3584]{1,0:T(8,128)(2,1)S(1)}, bf16[32,3584]{1,0:T(8,128)(2,1)S(1)}) custom-call(bf16[32,2048]{1,0:T(8,128)(2,1)S(1)} %copy-done.2, bf16[32,2048]{1,0:T(8,128)(2,1)S(1)} %collective-permute-done.refs_1_, bf16[32,2048]{1,0:T(8,128)(2,1)S(1)} %collective-permute-done.1.refs_2_, ...), custom_call_target="tpu_custom_call" | custom-call | flops 1879048192 | bytes 14680064 | tf_op jit(solution)/shard_map/pallas_call | solution.py:126
  20.1 0.1 collective-permute-start.3
  20.2 0.9 %shard_map.107.refs_0_ = bf16[32,2048]{1,0:T(8,128)(2,1)S(1)} custom-call(bf16[32,2048]{1,0:T(8,128)(2,1)} %refs_0_.7), custom_call_target="tpu_custom_call" | custom-call | bytes 131072 | tf_op jit(solution)/shard_map/pallas_call | solution.py:57
  21.1 2.0 %collective-permute-start.8 = (bf16[32,2048]{1,0:T(8,128)(2,1)S(1)}, bf16[32,2048]{1,0:T(8,128)(2,1)S(1)}, u32[]{:S(2)}, u32[]{:S(2)}) collective-permute-start(bf16[32,2048]{1,0:T(8,128)(2,1)S(1)} %shard_map.107.refs_0_), channel_id=1, source_target_pairs={{0,8},{4,12},{8,0},{12,4},{1,9},{5,13},{9,1},{13,5},{2,10},{6,14},... | collective-permute-start | bytes 393224 | tf_op jit(solution)/shard_map/ppermute | solution.py:20
  23.1 2.5 %collective-permute-start.7 = (bf16[32,2048]{1,0:T(8,128)(2,1)S(1)}, bf16[32,2048]{1,0:T(8,128)(2,1)S(1)}, u32[]{:S(2)}, u32[]{:S(2)}) collective-permute-start(bf16[32,2048]{1,0:T(8,128)(2,1)S(1)} %shard_map.107.refs_0_), channel_id=1, source_target_pairs={{0,4},{4,0},{8,12},{12,8},{1,5},{5,1},{9,13},{13,9},{2,6},{6,2},{1... | collective-permute-start | bytes 393224 | tf_op jit(solution)/shard_map/ppermute | solution.py:20
  25.6 2.1 %shard_map.106 = (bf16[64,3584]{1,0:T(8,128)(2,1)S(1)}, bf16[32,3584]{1,0:T(8,128)(2,1)S(1)}, bf16[32,3584]{1,0:T(8,128)(2,1)S(1)}) custom-call(bf16[32,2048]{1,0:T(8,128)(2,1)S(1)} %copy-done.2, bf16[32,2048]{1,0:T(8,128)(2,1)S(1)} %collective-permute-done.refs_1_, bf16[32,2048]{1,0:T(8,128)(2,1)S(1)} %collective-permute-done.1.refs_2_, ...), custom_call_target="tpu_custom_call" | custom-call | flops 1879048192 | bytes 14680064 | tf_op jit(solution)/shard_map/pallas_call | solution.py:126
  27.7 0.1 collective-permute-start.5
  27.8 3.1 %collective-permute-done.8.refs_2_ = bf16[32,2048]{1,0:T(8,128)(2,1)S(1)} collective-permute-done((bf16[32,2048]{1,0:T(8,128)(2,1)S(1)}, bf16[32,2048]{1,0:T(8,128)(2,1)S(1)}, u32[]{:S(2)}, u32[]{:S(2)}) %collective-permute-start.8) | collective-permute-done | bytes 131104 | tf_op jit(solution)/shard_map/ppermute | solution.py:20
  30.9 0.0 collective-permute-start.9
  30.9 0.0 collective-permute-done.3
  30.9 0.1 add_convert_fusion.3.refs_5_
  31.0 1.8 %collective-permute-start.4 = (bf16[32,3584]{1,0:T(8,128)(2,1)S(1)}, bf16[32,3584]{1,0:T(8,128)(2,1)S(1)}, u32[]{:S(2)}, u32[]{:S(2)}) collective-permute-start(bf16[32,3584]{1,0:T(8,128)(2,1)S(1)} %add_convert_fusion.3.refs_5_), channel_id=1, source_target_pairs={{0,2},{1,3},{2,0},{3,1},{4,6},{5,7},{6,4},{7,5},{8,10},{9,11},{10,... | collective-permute-start | bytes 688136 | tf_op jit(solution)/shard_map/ppermute | solution.py:149
  32.7 0.0 collective-permute-done.7.refs_1_
  32.7 3.2 %collective-permute-done.9.refs_3_ = bf16[32,2048]{1,0:T(8,128)(2,1)S(1)} collective-permute-done((bf16[32,2048]{1,0:T(8,128)(2,1)S(1)}, bf16[32,2048]{1,0:T(8,128)(2,1)S(1)}, u32[]{:S(2)}, u32[]{:S(2)}) %collective-permute-start.9) | collective-permute-done | bytes 131104 | tf_op jit(solution)/shard_map/ppermute | solution.py:20
  36.0 0.0 copy-start.1
  36.0 8.6 %shard_map.108 = (bf16[64,3584]{1,0:T(8,128)(2,1)S(1)}, bf16[32,3584]{1,0:T(8,128)(2,1)S(1)}, bf16[32,3584]{1,0:T(8,128)(2,1)S(1)}) custom-call(bf16[32,2048]{1,0:T(8,128)(2,1)S(1)} %shard_map.107.refs_0_, bf16[32,2048]{1,0:T(8,128)(2,1)S(1)} %collective-permute-done.7.refs_1_, bf16[32,2048]{1,0:T(8,128)(2,1)S(1)} %collective-permute-done.8.refs_2_, ...), custom_call_target="tpu_custom_call" | custom-call | flops 1879048192 | bytes 14680064 | tf_op jit(solution)/shard_map/pallas_call | solution.py:135
  44.6 0.1 collective-permute-start.10
  44.6 0.0 collective-permute-done.5
  44.6 0.1 add_convert_fusion.2.refs_5_
  44.7 1.8 %collective-permute-start.6 = (bf16[32,3584]{1,0:T(8,128)(2,1)S(1)}, bf16[32,3584]{1,0:T(8,128)(2,1)S(1)}, u32[]{:S(2)}, u32[]{:S(2)}) collective-permute-start(bf16[32,3584]{1,0:T(8,128)(2,1)S(1)} %add_convert_fusion.2.refs_5_), channel_id=1, source_target_pairs={{0,2},{1,3},{2,0},{3,1},{4,6},{5,7},{6,4},{7,5},{8,10},{9,11},{10,... | collective-permute-start | bytes 688136 | tf_op jit(solution)/shard_map/ppermute | solution.py:149
  46.5 8.5 %shard_map.109 = (bf16[64,3584]{1,0:T(8,128)(2,1)S(1)}, bf16[32,3584]{1,0:T(8,128)(2,1)S(1)}, bf16[32,3584]{1,0:T(8,128)(2,1)S(1)}) custom-call(bf16[32,2048]{1,0:T(8,128)(2,1)S(1)} %shard_map.107.refs_0_, bf16[32,2048]{1,0:T(8,128)(2,1)S(1)} %collective-permute-done.7.refs_1_, bf16[32,2048]{1,0:T(8,128)(2,1)S(1)} %collective-permute-done.8.refs_2_, ...), custom_call_target="tpu_custom_call" | custom-call | flops 1879048192 | bytes 14680064 | tf_op jit(solution)/shard_map/pallas_call | solution.py:135
  55.0 0.3 collective-permute-start.12
  55.3 0.0 collective-permute-done.10
  55.3 0.1 add_convert_fusion.1
  55.4 0.4 collective-permute-start.11
  55.8 1.2 %collective-permute-done.12 = bf16[64,3584]{1,0:T(8,128)(2,1)S(1)} collective-permute-done((bf16[64,3584]{1,0:T(8,128)(2,1)S(1)}, bf16[64,3584]{1,0:T(8,128)(2,1)S(1)}, u32[]{:S(2)}, u32[]{:S(2)}) %collective-permute-start.12) | collective-permute-done | bytes 458784 | tf_op jit(solution)/shard_map/ppermute | solution.py:149
  56.9 0.1 add_convert_fusion
  57.0 0.6 collective-permute-start.13
  57.6 0.0 collective-permute-done.6
  57.6 0.0 collective-permute-done.4
  57.6 6.3 %collective-permute-done.11 = bf16[32,3584]{1,0:T(8,128)(2,1)S(1)} collective-permute-done((bf16[32,3584]{1,0:T(8,128)(2,1)S(1)}, bf16[32,3584]{1,0:T(8,128)(2,1)S(1)}, u32[]{:S(2)}, u32[]{:S(2)}) %collective-permute-start.11) | collective-permute-done | bytes 229408 | tf_op jit(solution)/shard_map/ppermute | solution.py:149
  63.9 4.3 %collective-permute-done.13 = bf16[32,3584]{1,0:T(8,128)(2,1)S(1)} collective-permute-done((bf16[32,3584]{1,0:T(8,128)(2,1)S(1)}, bf16[32,3584]{1,0:T(8,128)(2,1)S(1)}, u32[]{:S(2)}, u32[]{:S(2)}) %collective-permute-start.13) | collective-permute-done | bytes 229408 | tf_op jit(solution)/shard_map/ppermute | solution.py:149
  68.2 1.2 %multiply_convert_fusion = (bf16[32,3584]{1,0:T(8,128)(2,1)}, f32[32,3584]{1,0:T(8,128)S(1)}) fusion(bf16[32,3584]{1,0:T(8,128)(2,1)S(1)} %collective-permute-done.13, bf16[32,3584]{1,0:T(8,128)(2,1)S(1)} %get-tuple-element.27, bf16[32,3584]{1,0:T(8,128)(2,1)S(1)} %collective-permute-done.11, bf16[32,3584]{1,0:T(8,128)(2,1)S(1)} %get-tuple-element.24, ...), kind=kLoop, calls=%fused_computation.1 | loop fusion | flops 3899392 | bytes 3440896 | tf_op jit(solution)/shard_map/convert_element_type | solution.py:191
  69.4 0.8 %multiply_convert_fusion.1 = bf16[32,3584]{1,0:T(8,128)(2,1)} fusion(f32[32,3584]{1,0:T(8,128)S(1)} %get-tuple-element.31, f32[32]{0:T(128)S(1)} %reshape.22.refs_2_.refs_5_), kind=kLoop, calls=%fused_computation.4 | loop fusion | flops 229376 | bytes 688256 | tf_op jit(solution)/shard_map/convert_element_type | solution.py:189
  70.2 0.0 copy-done.1
  (1 shorter events, 0.0 us)
Async XLA Ops:
  0.6 7.2 %copy-start = (f32[128256]{0:T(1024)S(1)}, f32[128256]{0:T(1024)}, u32[]{:S(2)}) copy-start(f32[128256]{0:T(1024)} %param.17) | copy-start | bytes 1539076
  0.6 17.3 %collective-permute-start = (bf16[32,2048]{1,0:T(8,128)(2,1)}, bf16[32,2048]{1,0:T(8,128)(2,1)S(1)}, u32[]{:S(2)}, u32[]{:S(2)}) collective-permute-start(bf16[32,2048]{1,0:T(8,128)(2,1)} %refs_0_.6), channel_id=1, source_target_pairs={{0,4},{4,0},{8,12},{12,8},{1,5},{5,1},{9,13},{13,9},{2,6},{6,2},{1... | collective-permute-start | bytes 393224 | tf_op jit(solution)/shard_map/ppermute | solution.py:20
  3.7 14.2 %collective-permute-start.1 = (bf16[32,2048]{1,0:T(8,128)(2,1)}, bf16[32,2048]{1,0:T(8,128)(2,1)S(1)}, u32[]{:S(2)}, u32[]{:S(2)}) collective-permute-start(bf16[32,2048]{1,0:T(8,128)(2,1)} %refs_0_.6), channel_id=1, source_target_pairs={{0,8},{4,12},{8,0},{12,4},{1,9},{5,13},{9,1},{13,5},{2,10},{6,14},... | collective-permute-start | bytes 393224 | tf_op jit(solution)/shard_map/ppermute | solution.py:20
  6.3 11.7 %collective-permute-start.2 = (bf16[32,2048]{1,0:T(8,128)(2,1)}, bf16[32,2048]{1,0:T(8,128)(2,1)S(1)}, u32[]{:S(2)}, u32[]{:S(2)}) collective-permute-start(bf16[32,2048]{1,0:T(8,128)(2,1)} %refs_0_.6), channel_id=1, source_target_pairs={{0,12},{4,8},{8,4},{12,0},{1,13},{5,9},{9,5},{13,1},{2,14},{6,10},... | collective-permute-start | bytes 393224 | tf_op jit(solution)/shard_map/ppermute | solution.py:20
  8.5 9.5 %copy-start.2 = (bf16[32,2048]{1,0:T(8,128)(2,1)S(1)}, bf16[32,2048]{1,0:T(8,128)(2,1)}, u32[]{:S(2)}) copy-start(bf16[32,2048]{1,0:T(8,128)(2,1)} %refs_0_.6) | copy-start | bytes 393220
  20.1 10.8 %collective-permute-start.3 = (bf16[64,3584]{1,0:T(8,128)(2,1)S(1)}, bf16[64,3584]{1,0:T(8,128)(2,1)S(1)}, u32[]{:S(2)}, u32[]{:S(2)}) collective-permute-start(bf16[64,3584]{1,0:T(8,128)(2,1)S(1)} %get-tuple-element.18.refs_5_), channel_id=1, source_target_pairs={{0,1},{1,0},{2,3},{3,2},{4,5},{5,4},{6,7},{7,6},{8,9},{9,8},{10,11... | collective-permute-start | bytes 1376264 | tf_op jit(solution)/shard_map/ppermute | solution.py:149
  21.1 9.8 %collective-permute-start.8 = (bf16[32,2048]{1,0:T(8,128)(2,1)S(1)}, bf16[32,2048]{1,0:T(8,128)(2,1)S(1)}, u32[]{:S(2)}, u32[]{:S(2)}) collective-permute-start(bf16[32,2048]{1,0:T(8,128)(2,1)S(1)} %shard_map.107.refs_0_), channel_id=1, source_target_pairs={{0,8},{4,12},{8,0},{12,4},{1,9},{5,13},{9,1},{13,5},{2,10},{6,14},... | collective-permute-start | bytes 393224 | tf_op jit(solution)/shard_map/ppermute | solution.py:20
  23.1 9.6 %collective-permute-start.7 = (bf16[32,2048]{1,0:T(8,128)(2,1)S(1)}, bf16[32,2048]{1,0:T(8,128)(2,1)S(1)}, u32[]{:S(2)}, u32[]{:S(2)}) collective-permute-start(bf16[32,2048]{1,0:T(8,128)(2,1)S(1)} %shard_map.107.refs_0_), channel_id=1, source_target_pairs={{0,4},{4,0},{8,12},{12,8},{1,5},{5,1},{9,13},{13,9},{2,6},{6,2},{1... | collective-permute-start | bytes 393224 | tf_op jit(solution)/shard_map/ppermute | solution.py:20
  27.7 17.0 %collective-permute-start.5 = (bf16[64,3584]{1,0:T(8,128)(2,1)S(1)}, bf16[64,3584]{1,0:T(8,128)(2,1)S(1)}, u32[]{:S(2)}, u32[]{:S(2)}) collective-permute-start(bf16[64,3584]{1,0:T(8,128)(2,1)S(1)} %get-tuple-element.22), channel_id=1, source_target_pairs={{0,1},{1,0},{2,3},{3,2},{4,5},{5,4},{6,7},{7,6},{8,9},{9,8},{10,11... | collective-permute-start | bytes 1376264 | tf_op jit(solution)/shard_map/ppermute | solution.py:149
  30.9 5.1 %collective-permute-start.9 = (bf16[32,2048]{1,0:T(8,128)(2,1)S(1)}, bf16[32,2048]{1,0:T(8,128)(2,1)S(1)}, u32[]{:S(2)}, u32[]{:S(2)}) collective-permute-start(bf16[32,2048]{1,0:T(8,128)(2,1)S(1)} %collective-permute-done.8.refs_2_), channel_id=1, source_target_pairs={{0,4},{4,0},{8,12},{12,8},{1,5},{5,1},{9,13},{13,9},{2,6},{6,2},{1... | collective-permute-start | bytes 393224 | tf_op jit(solution)/shard_map/ppermute | solution.py:20
  31.0 26.6 %collective-permute-start.4 = (bf16[32,3584]{1,0:T(8,128)(2,1)S(1)}, bf16[32,3584]{1,0:T(8,128)(2,1)S(1)}, u32[]{:S(2)}, u32[]{:S(2)}) collective-permute-start(bf16[32,3584]{1,0:T(8,128)(2,1)S(1)} %add_convert_fusion.3.refs_5_), channel_id=1, source_target_pairs={{0,2},{1,3},{2,0},{3,1},{4,6},{5,7},{6,4},{7,5},{8,10},{9,11},{10,... | collective-permute-start | bytes 688136 | tf_op jit(solution)/shard_map/ppermute | solution.py:149
  36.0 34.2 %copy-start.1 = (f32[128256]{0:T(1024)S(1)}, f32[128256]{0:T(1024)}, u32[]{:S(2)}) copy-start(f32[128256]{0:T(1024)} %param.17) | copy-start | bytes 1539076
  44.6 10.8 %collective-permute-start.10 = (bf16[64,3584]{1,0:T(8,128)(2,1)S(1)}, bf16[64,3584]{1,0:T(8,128)(2,1)S(1)}, u32[]{:S(2)}, u32[]{:S(2)}) collective-permute-start(bf16[64,3584]{1,0:T(8,128)(2,1)S(1)} %get-tuple-element.25), channel_id=1, source_target_pairs={{0,1},{1,0},{2,3},{3,2},{4,5},{5,4},{6,7},{7,6},{8,9},{9,8},{10,11... | collective-permute-start | bytes 1376264 | tf_op jit(solution)/shard_map/ppermute | solution.py:149
  44.7 12.9 %collective-permute-start.6 = (bf16[32,3584]{1,0:T(8,128)(2,1)S(1)}, bf16[32,3584]{1,0:T(8,128)(2,1)S(1)}, u32[]{:S(2)}, u32[]{:S(2)}) collective-permute-start(bf16[32,3584]{1,0:T(8,128)(2,1)S(1)} %add_convert_fusion.2.refs_5_), channel_id=1, source_target_pairs={{0,2},{1,3},{2,0},{3,1},{4,6},{5,7},{6,4},{7,5},{8,10},{9,11},{10,... | collective-permute-start | bytes 688136 | tf_op jit(solution)/shard_map/ppermute | solution.py:149
  55.0 1.9 %collective-permute-start.12 = (bf16[64,3584]{1,0:T(8,128)(2,1)S(1)}, bf16[64,3584]{1,0:T(8,128)(2,1)S(1)}, u32[]{:S(2)}, u32[]{:S(2)}) collective-permute-start(bf16[64,3584]{1,0:T(8,128)(2,1)S(1)} %get-tuple-element.28), channel_id=1, source_target_pairs={{0,1},{1,0},{2,3},{3,2},{4,5},{5,4},{6,7},{7,6},{8,9},{9,8},{10,11... | collective-permute-start | bytes 1376264 | tf_op jit(solution)/shard_map/ppermute | solution.py:149
  55.4 8.5 %collective-permute-start.11 = (bf16[32,3584]{1,0:T(8,128)(2,1)S(1)}, bf16[32,3584]{1,0:T(8,128)(2,1)S(1)}, u32[]{:S(2)}, u32[]{:S(2)}) collective-permute-start(bf16[32,3584]{1,0:T(8,128)(2,1)S(1)} %add_convert_fusion.1), channel_id=1, source_target_pairs={{0,2},{1,3},{2,0},{3,1},{4,6},{5,7},{6,4},{7,5},{8,10},{9,11},{10,... | collective-permute-start | bytes 688136 | tf_op jit(solution)/shard_map/ppermute | solution.py:149
  57.0 11.2 %collective-permute-start.13 = (bf16[32,3584]{1,0:T(8,128)(2,1)S(1)}, bf16[32,3584]{1,0:T(8,128)(2,1)S(1)}, u32[]{:S(2)}, u32[]{:S(2)}) collective-permute-start(bf16[32,3584]{1,0:T(8,128)(2,1)S(1)} %add_convert_fusion), channel_id=1, source_target_pairs={{0,2},{1,3},{2,0},{3,1},{4,6},{5,7},{6,4},{7,5},{8,10},{9,11},{10,... | collective-permute-start | bytes 688136 | tf_op jit(solution)/shard_map/ppermute | solution.py:149

commit v3 on v1

v3 whole, which is shorter than its diff:
```python
import functools
import math

import jax
import jax.numpy as jnp
from jax import lax
from jax.experimental import pallas as pl
from jax.experimental.pallas import tpu as pltpu
from jax.sharding import PartitionSpec as P

IN_VMEM = pl.BlockSpec(memory_space=pltpu.VMEM)
IN_SMEM = pl.BlockSpec(memory_space=pltpu.SMEM)
ANYWHERE = pl.BlockSpec(memory_space=pl.ANY)
LANES = 128


def in_hbm(array):
    return pltpu.with_memory_space_constraint(array, pltpu.HBM)


def in_vmem(array):
    return pltpu.with_memory_space_constraint(array, pltpu.VMEM)


def pass_kernel(piece, *refs):
    refs[-1][...] = piece[...]


def passed(piece, after):
    return pl.pallas_call(
        pass_kernel,
        out_shape=jax.ShapeDtypeStruct(piece.shape, piece.dtype),
        in_specs=[IN_VMEM] + [ANYWHERE] * len(after),
        out_specs=IN_VMEM,
        compiler_params=pltpu.CompilerParams(vmem_limit_bytes=1 << 20),
    )(piece, *after)


def gather_pieces(piece, axis, size, after=()):
    pieces = [piece]
    for offset in range(1, size):
        low = offset & -offset
        pairs = [(i, i ^ low) for i in range(size)]
        piece = pieces[offset ^ low]
        if after and offset != low:
            piece = passed(piece, after)
        pieces.append(lax.ppermute(piece, axis, pairs))
    return pieces


def halving_order(size):
    bits = size.bit_length() - 1
    reverse = [sum(((p >> b) & 1) << (bits - 1 - b) for b in range(bits)) for p in range(size)]
    return reverse[::-1]


def place_rows(pieces, rows, narrow):
    me_wide, me_narrow = lax.axis_index("wide"), lax.axis_index("narrow")
    piece_rows = pieces[0].shape[0]
    block_rows = piece_rows * len(pieces) // narrow
    size = math.gcd(piece_rows, block_rows)
    for offset, piece in enumerate(pieces):
        for start in range(0, piece_rows, size):
            row = (me_wide ^ offset) * piece_rows + start
            block = (row // block_rows) ^ me_narrow
            place = sum(
                jnp.where(block == known, position, 0)
                for position, known in enumerate(halving_order(narrow))
            )
            spot = pl.multiple_of(place * block_rows + row % block_rows, size)
            rows[pl.ds(spot, size), :] = piece[start : start + size, :]


def start_loads(sources, spans, dests, sems):
    copies = []
    for i, (source, (start, size)) in enumerate(zip(sources, spans)):
        copies.append(pltpu.make_async_copy(source.at[pl.ds(start, size), :], dests[i], sems.at[i]))
        copies[-1].start()
    return copies


def prepare_kernel(spans, slots, ids, lengths, table, *refs):
    count = len(spans)
    dests, live, weight = refs[count : 2 * count], refs[2 * count], refs[2 * count + 1]
    entries, picked, sems = refs[2 * count + 2 :]
    lookup = pltpu.make_async_copy(table, entries, sems.at[count])
    lookup.start()
    copies = start_loads(refs[:count], spans, dests, sems)
    for i in range(lengths.shape[0]):
        slot = lax.broadcasted_iota(jnp.int32, (slots, LANES), 0)
        live[i * slots : (i + 1) * slots, :] = (slot < lengths[i]).astype(jnp.float32)
    lookup.wait()

    def pick(i, carry):
        entry = ids[i]
        lane = lax.broadcasted_iota(jnp.int32, (1, LANES), 1)
        row = entries[pl.ds(entry // LANES, 1), :]
        picked[pl.ds(i, 1), :] = jnp.where(lane == entry % LANES, row, 0.0)
        return carry

    lax.fori_loop(0, ids.shape[0], pick, 0)
    weight[...] = jnp.broadcast_to(jnp.sum(picked[...], axis=1, keepdims=True), weight.shape)
    for copy in copies:
        copy.wait()


def prepare(loads, ids, lengths, table):
    spans = [span for _, span in loads]
    table = table.reshape(-1, LANES)
    flag = jax.ShapeDtypeStruct((ids.shape[0], LANES), jnp.float32)
    return pl.pallas_call(
        functools.partial(prepare_kernel, spans, ids.shape[0] // lengths.shape[0]),
        out_shape=[pltpu.VMEM((size, m.shape[1]), m.dtype) for m, (_, size) in loads] + [flag, flag],
        in_specs=[IN_SMEM, IN_SMEM, ANYWHERE] + [ANYWHERE] * len(loads),
        out_specs=[IN_VMEM] * (len(loads) + 2),
        scratch_shapes=[
            pltpu.VMEM(table.shape, table.dtype),
            pltpu.VMEM(flag.shape, flag.dtype),
            pltpu.SemaphoreType.DMA((len(loads) + 1,)),
        ],
        compiler_params=pltpu.CompilerParams(vmem_limit_bytes=3 << 20),
    )(*map(in_hbm, (ids, lengths, table, *(m for m, _ in loads))))


def load_kernel(spans, after, *refs):
    dests = refs[len(spans) + after : -1]
    for copy in start_loads(refs[: len(spans)], spans, dests, refs[-1]):
        copy.wait()


def halves(matrix):
    half = matrix.shape[0] // 2
    return [(matrix, (0, half)), (matrix, (half, half))]


def load(loads, after):
    return pl.pallas_call(
        functools.partial(load_kernel, [span for _, span in loads], len(after)),
        out_shape=[pltpu.VMEM((size, m.shape[1]), m.dtype) for m, (_, size) in loads],
        in_specs=[ANYWHERE] * (len(loads) + len(after)),
        out_specs=[IN_VMEM] * len(loads),
        scratch_shapes=[pltpu.SemaphoreType.DMA((len(loads),))],
        compiler_params=pltpu.CompilerParams(vmem_limit_bytes=1 << 20),
    )(*(in_hbm(m) for m, _ in loads), *after)


def tile_of(cols):
    for tile in (512, 256, 128):
        if cols % tile == 0:
            return tile
    return cols


def product_kernel(pieces, parts, spans, after, narrow, placing, *refs):
    tokens, matrices = refs[:pieces], refs[pieces : pieces + parts]
    start = pieces + parts
    sources = refs[start : start + len(spans)]
    start += len(spans) + after
    dests = refs[start : start + len(spans)]
    start += len(spans)
    outs, sems = refs[start:-1], refs[-1]
    copies = start_loads(sources, spans, dests, sems)
    if placing:
        place_rows(tokens, outs[0], narrow)
        tokens, outs = outs[:1], outs[1:]
    width = matrices[0].shape[1]
    tile = tile_of(width)
    for column in range(0, width, tile):
        cols = slice(column, column + tile)
        total, depth = None, 0
        for matrix in matrices:
            rows = tokens[0][:, depth : depth + matrix.shape[0]]
            term = jnp.dot(rows, matrix[:, cols], preferred_element_type=jnp.float32)
            total = term if total is None else total + term
            depth += matrix.shape[0]
        row = 0
        for out in outs:
            out[:, cols] = total[row : row + out.shape[0]].astype(out.dtype)
            row += out.shape[0]
    for copy in copies:
        copy.wait()


def product(tokens, matrices, narrow, after=(), loads=()):
    placing = len(tokens) > 1
    total = sum(t.shape[0] for t in tokens)
    depth, width = tokens[0].shape[1], matrices[0].shape[1]
    sizes, left = [], total
    while left > total // narrow:
        left //= 2
        sizes.append(left)
    sizes.append(left)
    spans = [span for _, span in loads]
    found = pl.pallas_call(
        functools.partial(product_kernel, len(tokens), len(matrices), spans, len(after), narrow, placing),
        out_shape=[pltpu.VMEM((size, m.shape[1]), m.dtype) for m, (_, size) in loads]
        + [jax.ShapeDtypeStruct((total, depth), tokens[0].dtype)] * placing
        + [jax.ShapeDtypeStruct((size, width), jnp.bfloat16) for size in sizes],
        in_specs=[IN_VMEM] * (len(tokens) + len(matrices)) + [ANYWHERE] * (len(loads) + len(after)),
        out_specs=[IN_VMEM] * (len(loads) + placing + len(sizes)),
        scratch_shapes=[pltpu.SemaphoreType.DMA((max(1, len(loads)),))],
        compiler_params=pltpu.CompilerParams(vmem_limit_bytes=6 << 20),
    )(*tokens, *map(in_vmem, matrices), *(in_hbm(m) for m, _ in loads), *after)
    loaded, found = found[: len(loads)], found[len(loads) :]
    return loaded, (found[:1] if placing else tokens), found[placing:]


def next_kernel(behind, count, *refs):
    part, out = refs[0], refs[-1]
    for cols in column_tiles(out.shape[1]):
        total = part[:, cols].astype(jnp.float32)
        for came in refs[1:count]:
            start = came.shape[0] - behind - part.shape[0]
            total += came[start : start + part.shape[0], cols].astype(jnp.float32)
        out[:, cols] = total.astype(out.dtype)


def next_part(parts, got, after):
    step = len(got)
    behind = sum(part.shape[0] for part in parts[step + 1 :])
    return pl.pallas_call(
        functools.partial(next_kernel, behind, 1 + step),
        out_shape=jax.ShapeDtypeStruct(parts[step].shape, jnp.bfloat16),
        in_specs=[IN_VMEM] * (1 + step) + [ANYWHERE] * len(after),
        out_specs=IN_VMEM,
        compiler_params=pltpu.CompilerParams(vmem_limit_bytes=4 << 20),
    )(parts[step], *got, *after)


def exchange(send, step, size):
    return lax.ppermute(send, "narrow", [(i, i ^ (1 << step)) for i in range(size)])


def finish(parts, got, size, after):
    send = parts[0]
    while (1 << len(got)) < size:
        send = next_part(parts, got, after)
        got = got + [exchange(send, len(got), size)]
    return send, [parts[-1]] + got


def own_sum(refs, cols):
    count = refs[0].shape[0]
    return sum(ref[ref.shape[0] - count :, cols].astype(jnp.float32) for ref in refs)


def column_tiles(width):
    tile = tile_of(width)
    return [slice(start, start + tile) for start in range(0, width, tile)]


def target_kernel(count, live, *refs):
    gate, upper, act, out = refs[:count], refs[count : 2 * count], refs[-2], refs[-1]
    for cols in column_tiles(out.shape[1]):
        value = live[:, :1] * (jax.nn.silu(own_sum(gate, cols)) * own_sum(upper, cols))
        act[:, cols] = value
        out[:, cols] = value.astype(out.dtype)


def target_end(live, gate, upper, after):
    shape = gate[0].shape
    return pl.pallas_call(
        functools.partial(target_kernel, len(gate)),
        out_shape=[jax.ShapeDtypeStruct(shape, jnp.float32), jax.ShapeDtypeStruct(shape, jnp.bfloat16)],
        in_specs=[IN_VMEM] * (1 + len(gate) + len(upper)) + [ANYWHERE] * len(after),
        out_specs=[IN_VMEM] * 2,
        compiler_params=pltpu.CompilerParams(vmem_limit_bytes=6 << 20),
    )(live, *gate, *upper, *after)


def source_kernel(live, weight, *refs):
    gate, out = refs[:-1], refs[-1]
    for cols in column_tiles(out.shape[1]):
        out[:, cols] = (live[:, :1] * weight[:, :1]) * jax.nn.silu(own_sum(gate, cols))


def source_middle(live, weight, gate):
    return pl.pallas_call(
        source_kernel,
        out_shape=jax.ShapeDtypeStruct(gate[0].shape, jnp.float32),
        in_specs=[IN_VMEM] * (2 + len(gate)),
        out_specs=IN_VMEM,
        compiler_params=pltpu.CompilerParams(vmem_limit_bytes=6 << 20),
    )(live, weight, *gate)


def ratio_kernel(act, gated, *refs):
    upper, out = refs[:-1], refs[-1]
    for cols in column_tiles(out.shape[1]):
        out[:, cols] = (act[:, cols] - gated[:, cols] * own_sum(upper, cols)).astype(out.dtype)


def ratio_end(act, gated, upper):
    return pl.pallas_call(
        ratio_kernel,
        out_shape=jax.ShapeDtypeStruct(act.shape, jnp.bfloat16),
        in_specs=[IN_VMEM] * (2 + len(upper)),
        out_specs=IN_VMEM,
        compiler_params=pltpu.CompilerParams(vmem_limit_bytes=6 << 20),
    )(act, gated, *upper)


def local(mesh_shape, target_states, source_states, target_gate, target_up, source_gate, source_up, token_ids, lengths, ratio_weight):
    wide, narrow = mesh_shape["wide"], mesh_shape["narrow"]
    gate_top, gate_bottom = halves(source_gate)
    up_top, up_bottom = halves(source_up)

    *target_gate, live, weight = prepare(halves(target_gate), token_ids, lengths, ratio_weight)
    target_pieces = gather_pieces(target_states, "wide", wide, (live,))
    source_pieces = gather_pieces(source_states, "wide", wide)
    target_up = load(halves(target_up), (live, target_pieces[wide // 2]))

    after = (target_up[0], source_pieces[1], source_pieces[wide // 2])
    _, rows, gate = product(target_pieces, target_gate, narrow, after)
    gate_came = [exchange(gate[0], 0, narrow)]
    (gate_top,), _, upper = product(rows, target_up, narrow, (gate[0],), [gate_top])
    upper_came = [exchange(upper[0], 0, narrow)]
    sent, gate = finish(gate, gate_came, narrow, (upper[0],))
    gate_bottom, up_top = load([gate_bottom, up_top], (sent,))
    sent, upper = finish(upper, upper_came, narrow, (gate_bottom, source_pieces[-1]))

    (up_bottom,), rows, source_g = product(
        source_pieces, (gate_top, gate_bottom), narrow, (sent,), [up_bottom]
    )
    gate_came = [exchange(source_g[0], 0, narrow)]
    _, _, source_u = product(rows, (up_top, up_bottom), narrow, (source_g[0], gate[-1], upper[-1]))
    upper_came = [exchange(source_u[0], 0, narrow)]
    sent, source_g = finish(source_g, gate_came, narrow, (source_u[0],))
    act, target_out = target_end(live, gate, upper, (sent,))
    _, source_u = finish(source_u, upper_came, narrow, (act,))
    gated = source_middle(live, weight, source_g)
    ratio_out = ratio_end(act, gated, source_u)
    return (target_out, ratio_out)


def solution(mesh):
    placed = (
        P(("groups", "wide"), "narrow"),
        P(("groups", "wide"), "narrow"),
        P("narrow", "wide"),
        P("narrow", "wide"),
        P("narrow", "wide"),
        P("narrow", "wide"),
        P(("groups", "narrow")),
        P(("groups", "narrow")),
        P(),
    )
    mesh_shape = dict(mesh.shape)

    def body(*args):
        return local(mesh_shape, *args)

    return jax.shard_map(
        body,
        mesh=mesh,
        in_specs=placed,
        out_specs=(P(("groups", "narrow"), "wide"), P(("groups", "narrow"), "wide")),
        check_vma=False,
    )
```

time: 92.3 us -> 57.5 us (0.62)
  Pallas kernels: 0 us -> 29 us
  matrix products: 24.4 us -> 0 us
  local copies, waits for them, and re-layouts: 18.1 us -> 0.22 us
  waiting for transfers between devices: 30.1 us -> 12.9 us
  other arithmetic: 6.39 us -> 0 us
  starting transfers between devices: 9.22 us -> 14.3 us
  between operations: 3.49 us -> 0.85 us
    pallas_call x0 -> x15, Pallas kernels: none -> 29 us  [the longest x4 10.5 us: product(): pl.pallas_call(functools.partial(product_kernel, len(tokens), len(matrice...]
    dot_general x4 -> x0, matrix products: 24.4 us -> none  [product(): jnp.dot(rows, matrix, preferred_element_type=jnp.float32)]
    ppermute x14, waiting for transfers between devices: 30.1 us -> 12.9 us  [the longest x8 12.9 us: exchange(): lax.ppermute(send, 'narrow', [(i, i ^ 1 << step) for i in range(size)])]
    dynamic_update_slice x8 -> x0, local copies, waits for them, and re-layouts: 11.1 us -> none  [arrange(): lax.dynamic_update_slice_in_dim(whole, piece[start:start + sub], row, axi...]
    ppermute x14, starting transfers between devices: 9.22 us -> 14.3 us  [the longest x6 9.43 us: gather_pieces(): pieces.append(lax.ppermute(piece, axis, pairs))]
    convert_element_type x3 -> x0, other arithmetic: 3.86 us -> none  [the longest x1 2.35 us: local(): (live[:, None] * (target_act - weight[:, None] * source_act)).astype(jnp....]
    slice x8 -> x0, local copies, waits for them, and re-layouts: 3.75 us -> none  [halving_sum(): got = lax.ppermute(terms[:half].astype(jnp.bfloat16), axis, pairs)]
    add x4 -> x0, other arithmetic: 2.52 us -> none  [halving_sum(): terms = terms[half:] + got.astype(jnp.float32)]
  transfers between devices with their start and end apart: 14 -> 14, of which waited for: 7 -> 4; matrix products, arithmetic and copies ran while one was open for 49% -> 0% of each run, Pallas kernels for 0% -> 45%
where the time goes in v3:
time: 57.5 us; the launch traced here: 57.3 us
  Pallas kernels  29 us (50%)
  starting transfers between devices  14.3 us (25%)
  waiting for transfers between devices  12.9 us (22%)
  between operations  0.85 us (1%)
    ppermute x8, waiting for transfers between devices, exchange(): lax.ppermute(send, 'narrow', [(i, i ^ 1 << step) for i in range(size)])  12.9 us
    pallas_call x4, Pallas kernels, product(): pl.pallas_call(functools.partial(product_kernel, len(tokens), len(matrice...  10.5 us
    pallas_call x2, Pallas kernels, load(): pl.pallas_call(functools.partial(load_kernel, [span for _, span in loads]...  10.4 us
    ppermute x6, starting transfers between devices, gather_pieces(): pieces.append(lax.ppermute(piece, axis, pairs))  9.43 us
    pallas_call x1, Pallas kernels, prepare(): pl.pallas_call(functools.partial(prepare_kernel, spans, ids.shape[0] // l...  6.05 us
    ppermute x8, starting transfers between devices, exchange(): lax.ppermute(send, 'narrow', [(i, i ^ 1 << step) for i in range(size)])  4.89 us
  transfers between devices with their start and end apart: 14, of which 4 were waited for; matrix products, arithmetic and copies ran while one was open for 0% of the time, Pallas kernels for 45%

profile of v3, /device:TPU:0, one launch (start us, length us, event | category | flops | bytes accessed | tf_op | source)
XLA Modules:
  0.0 57.3 jit_solution(14296965456995162045)
XLA Ops:
  0.6 4.1 %collective-permute-start.1 = (bf16[32,2048]{1,0:T(8,128)(2,1)}, bf16[32,2048]{1,0:T(8,128)(2,1)S(1)}, u32[]{:S(2)}, u32[]{:S(2)}) collective-permute-start(bf16[32,2048]{1,0:T(8,128)(2,1)} %refs_0_.7), channel_id=1, source_target_pairs={{0,8},{4,12},{8,0},{12,4},{1,9},{5,13},{9,1},{13,5},{2,10},{6,14},... | collective-permute-start | bytes 393224 | tf_op jit(solution)/shard_map/ppermute | solution.py:47
  4.7 1.6 %collective-permute-start = (bf16[32,2048]{1,0:T(8,128)(2,1)}, bf16[32,2048]{1,0:T(8,128)(2,1)S(1)}, u32[]{:S(2)}, u32[]{:S(2)}) collective-permute-start(bf16[32,2048]{1,0:T(8,128)(2,1)} %refs_0_.7), channel_id=1, source_target_pairs={{0,4},{4,0},{8,12},{12,8},{1,5},{5,1},{9,13},{13,9},{2,6},{6,2},{1... | collective-permute-start | bytes 393224 | tf_op jit(solution)/shard_map/ppermute | solution.py:47
  6.3 0.4 collective-permute-start.3
  6.8 0.1 collective-permute-start.4
  6.8 6.1 %shard_map.104 = (bf16[1024,3584]{1,0:T(8,128)(2,1)S(1)}, bf16[1024,3584]{1,0:T(8,128)(2,1)S(1)}, f32[32,128]{1,0:T(8,128)S(1)}, f32[32,128]{1,0:T(8,128)S(1)}) custom-call(s32[32]{0:T(128)} %ids.1, s32[2]{0:T(128)} %lengths.1, f32[1002,128]{1,0:T(8,128)} %bitcast.1, bf16[2048,3584]{1,0:T(8,128)(2,1)} %refs_1_.3, bf16[2048,3584]{1,0:T(8,128)(2,1)} %refs_1_.3), custom_call_target="tpu_custom_call" | custom-call | tf_op jit(solution)/shard_map/pallas_call | solution.py:111
  12.9 0.0 collective-permute-done.1.piece.refs_3_.refs_2_
  12.9 0.0 copy-start
  12.9 1.9 %collective-permute-start.2 = (bf16[32,2048]{1,0:T(8,128)(2,1)S(1)}, bf16[32,2048]{1,0:T(8,128)(2,1)S(1)}, u32[]{:S(2)}, u32[]{:S(2)}) collective-permute-start(bf16[32,2048]{1,0:T(8,128)(2,1)S(1)} %shard_map.105), channel_id=1, source_target_pairs={{0,4},{4,0},{8,12},{12,8},{1,5},{5,1},{9,13},{13,9},{2,6},{6,2},{1... | collective-permute-start | bytes 393224 | tf_op jit(solution)/shard_map/ppermute | solution.py:47
  14.8 5.2 %shard_map.106 = (bf16[1024,3584]{1,0:T(8,128)(2,1)S(1)}, bf16[1024,3584]{1,0:T(8,128)(2,1)S(1)}) custom-call(bf16[2048,3584]{1,0:T(8,128)(2,1)} %refs_1_.4, bf16[2048,3584]{1,0:T(8,128)(2,1)} %refs_1_.4, f32[32,128]{1,0:T(8,128)S(1)} %get-tuple-element.28.refs_0_.refs_2_.live, bf16[32,2048]{1,0:T(8,128)(2,1)S(1)} %collective-permute-done.1.piece.refs_3_.refs_2_), custom_call_target="tpu_custom_call" | custom-call | tf_op jit(solution)/shard_map/pallas_call | solution.py:137
  20.0 0.0 collective-permute-done.refs_1_
  20.0 0.0 collective-permute-done.3.refs_7_.refs_1_
  20.1 0.0 collective-permute-done.4.refs_8_.refs_2_
  20.1 0.0 collective-permute-done.2.refs_3_
  20.1 0.0 copy-done
  20.1 2.1 %shard_map.107 = (bf16[128,2048]{1,0:T(8,128)(2,1)S(1)}, bf16[64,3584]{1,0:T(8,128)(2,1)S(1)}, bf16[32,3584]{1,0:T(8,128)(2,1)S(1)}, bf16[32,3584]{1,0:T(8,128)(2,1)S(1)}) custom-call(bf16[32,2048]{1,0:T(8,128)(2,1)S(1)} %copy-done, bf16[32,2048]{1,0:T(8,128)(2,1)S(1)} %collective-permute-done.refs_1_, ...), custom_call_target="tpu_custom_call" | custom-call | tf_op jit(solution)/shard_map/pallas_call | solution.py:194
  22.2 0.1 collective-permute-start.5
  22.3 3.1 %shard_map.108 = (bf16[1024,3584]{1,0:T(8,128)(2,1)S(1)}, bf16[64,3584]{1,0:T(8,128)(2,1)S(1)}, bf16[32,3584]{1,0:T(8,128)(2,1)S(1)}, bf16[32,3584]{1,0:T(8,128)(2,1)S(1)}) custom-call(bf16[128,2048]{1,0:T(8,128)(2,1)S(1)} %get-tuple-element.35.refs_0_, bf16[1024,3584]{1,0:T(8,128)(2,1)S(1)} %get-tuple-element.31.refs_6_.refs_1_, ...), custom_call_target="tpu_custom_call" | custom-call | tf_op jit(solution)/shard_map/pallas_call | solution.py:194
  25.4 0.6 collective-permute-start.7
  26.0 1.3 %collective-permute-start.8 = (bf16[32,2048]{1,0:T(8,128)(2,1)S(1)}, bf16[32,2048]{1,0:T(8,128)(2,1)S(1)}, u32[]{:S(2)}, u32[]{:S(2)}) collective-permute-start(bf16[32,2048]{1,0:T(8,128)(2,1)S(1)} %collective-permute-done.4.refs_8_.refs_2_), channel_id=1, source_target_pairs={{0,4},{4,0},{8,12},{12,8},{1,5},{5,1},{9,13},{13,9},{2,6},{6,2},{1... | collective-permute-start | bytes 393224 | tf_op jit(solution)/shard_map/ppermute | solution.py:47
  27.3 0.0 collective-permute-done.5.refs_1_
  27.3 0.1 shard_map.109.refs_2_
  27.4 1.6 %collective-permute-start.6 = (bf16[32,3584]{1,0:T(8,128)(2,1)S(1)}, bf16[32,3584]{1,0:T(8,128)(2,1)S(1)}, u32[]{:S(2)}, u32[]{:S(2)}) collective-permute-start(bf16[32,3584]{1,0:T(8,128)(2,1)S(1)} %shard_map.109.refs_2_), channel_id=1, source_target_pairs={{0,2},{1,3},{2,0},{3,1},{4,6},{5,7},{6,4},{7,5},{8,10},{9,11},{10,... | collective-permute-start | bytes 688136 | tf_op jit(solution)/shard_map/ppermute | solution.py:231
  28.9 5.2 %shard_map.110 = (bf16[1024,3584]{1,0:T(8,128)(2,1)S(1)}, bf16[1024,3584]{1,0:T(8,128)(2,1)S(1)}) custom-call(bf16[2048,3584]{1,0:T(8,128)(2,1)} %refs_0_.8, bf16[2048,3584]{1,0:T(8,128)(2,1)} %refs_6_.1, bf16[32,3584]{1,0:T(8,128)(2,1)S(1)} %shard_map.109.refs_2_), custom_call_target="tpu_custom_call" | custom-call | tf_op jit(solution)/shard_map/pallas_call | solution.py:137
  34.1 0.0 copy-start.1
  34.1 0.0 collective-permute-done.8.refs_3_
  34.1 0.0 collective-permute-done.7.refs_1_.refs_4_
  34.1 0.1 shard_map.111.refs_7_
  34.2 0.6 %collective-permute-start.9 = (bf16[32,3584]{1,0:T(8,128)(2,1)S(1)}, bf16[32,3584]{1,0:T(8,128)(2,1)S(1)}, u32[]{:S(2)}, u32[]{:S(2)}) collective-permute-start(bf16[32,3584]{1,0:T(8,128)(2,1)S(1)} %shard_map.111.refs_7_), channel_id=1, source_target_pairs={{0,2},{1,3},{2,0},{3,1},{4,6},{5,7},{6,4},{7,5},{8,10},{9,11},{10,... | collective-permute-start | bytes 688136 | tf_op jit(solution)/shard_map/ppermute | solution.py:231
  34.8 0.2 copy-done.1
  35.0 3.1 %shard_map.112 = (bf16[1024,3584]{1,0:T(8,128)(2,1)S(1)}, bf16[128,2048]{1,0:T(8,128)(2,1)S(1)}, bf16[64,3584]{1,0:T(8,128)(2,1)S(1)}, bf16[32,3584]{1,0:T(8,128)(2,1)S(1)}, bf16[32,3584]{1,0:T(8,128)(2,1)S(1)}) custom-call(bf16[32,2048]{1,0:T(8,128)(2,1)S(1)} %copy-done.1, bf16[32,2048]{1,0:T(8,128)(2,1)S(1)} %collective-permute-done.3.refs_7_.refs_1_, ...), custom_call_target="tpu_custom_call" | custom-call | tf_op jit(solution)/shard_map/pallas_call | solution.py:194
  38.2 0.1 collective-permute-start.10
  38.3 0.0 collective-permute-done.6.refs_4_.refs_2_
  38.3 3.0 %collective-permute-done.9.refs_5_ = bf16[32,3584]{1,0:T(8,128)(2,1)S(1)} collective-permute-done((bf16[32,3584]{1,0:T(8,128)(2,1)S(1)}, bf16[32,3584]{1,0:T(8,128)(2,1)S(1)}, u32[]{:S(2)}, u32[]{:S(2)}) %collective-permute-start.9) | collective-permute-done | bytes 229408 | tf_op jit(solution)/shard_map/ppermute | solution.py:231
  41.3 2.1 %shard_map.113 = (bf16[64,3584]{1,0:T(8,128)(2,1)S(1)}, bf16[32,3584]{1,0:T(8,128)(2,1)S(1)}, bf16[32,3584]{1,0:T(8,128)(2,1)S(1)}) custom-call(bf16[128,2048]{1,0:T(8,128)(2,1)S(1)} %get-tuple-element.44.refs_0_, bf16[1024,3584]{1,0:T(8,128)(2,1)S(1)} %get-tuple-element.45.refs_1_, bf16[1024,3584]{1,0:T(8,128)(2,1)S(1)} %get-tuple-element.46.refs_2_, ...), custom_call_target="tpu_custom_call" | custom-call | tf_op jit(solution)/shard_map/pallas_call | solution.py:194
  43.4 0.1 collective-permute-start.12
  43.5 0.0 collective-permute-done.10.refs_1_
  43.5 0.1 shard_map.114.refs_6_
  43.6 0.6 %collective-permute-start.11 = (bf16[32,3584]{1,0:T(8,128)(2,1)S(1)}, bf16[32,3584]{1,0:T(8,128)(2,1)S(1)}, u32[]{:S(2)}, u32[]{:S(2)}) collective-permute-start(bf16[32,3584]{1,0:T(8,128)(2,1)S(1)} %shard_map.114.refs_6_), channel_id=1, source_target_pairs={{0,2},{1,3},{2,0},{3,1},{4,6},{5,7},{6,4},{7,5},{8,10},{9,11},{10,... | collective-permute-start | bytes 688136 | tf_op jit(solution)/shard_map/ppermute | solution.py:231
  44.2 0.9 %shard_map.115 = (f32[32,3584]{1,0:T(8,128)S(1)}, bf16[32,3584]{1,0:T(8,128)(2,1)}) custom-call(f32[32,128]{1,0:T(8,128)S(1)} %get-tuple-element.28.refs_0_.refs_2_.live, bf16[32,3584]{1,0:T(8,128)(2,1)S(1)} %get-tuple-element.32.refs_0_, bf16[64,3584]{1,0:T(8,128)(2,1)S(1)} %collective-permute-done.5.refs_1_, ...), custom_call_target="tpu_custom_call" | custom-call | tf_op jit(solution)/shard_map/pallas_call | solution.py:262
  45.1 0.2 collective-permute-done.12.refs_1_
  45.3 0.1 shard_map.117
  45.3 1.4 %collective-permute-start.13 = (bf16[32,3584]{1,0:T(8,128)(2,1)S(1)}, bf16[32,3584]{1,0:T(8,128)(2,1)S(1)}, u32[]{:S(2)}, u32[]{:S(2)}) collective-permute-start(bf16[32,3584]{1,0:T(8,128)(2,1)S(1)} %shard_map.117), channel_id=1, source_target_pairs={{0,2},{1,3},{2,0},{3,1},{4,6},{5,7},{6,4},{7,5},{8,10},{9,11},{10,... | collective-permute-start | bytes 688136 | tf_op jit(solution)/shard_map/ppermute | solution.py:231
  46.7 5.3 %collective-permute-done.11.refs_2_ = bf16[32,3584]{1,0:T(8,128)(2,1)S(1)} collective-permute-done((bf16[32,3584]{1,0:T(8,128)(2,1)S(1)}, bf16[32,3584]{1,0:T(8,128)(2,1)S(1)}, u32[]{:S(2)}, u32[]{:S(2)}) %collective-permute-start.11) | collective-permute-done | bytes 229408 | tf_op jit(solution)/shard_map/ppermute | solution.py:231
  52.0 0.1 shard_map.116.gated
  52.2 4.4 %collective-permute-done.13.refs_2_ = bf16[32,3584]{1,0:T(8,128)(2,1)S(1)} collective-permute-done((bf16[32,3584]{1,0:T(8,128)(2,1)S(1)}, bf16[32,3584]{1,0:T(8,128)(2,1)S(1)}, u32[]{:S(2)}, u32[]{:S(2)}) %collective-permute-start.13) | collective-permute-done | bytes 229408 | tf_op jit(solution)/shard_map/ppermute | solution.py:231
  56.5 0.8 %shard_map.118 = bf16[32,3584]{1,0:T(8,128)(2,1)} custom-call(f32[32,3584]{1,0:T(8,128)S(1)} %get-tuple-element.49.refs_2_.act, f32[32,3584]{1,0:T(8,128)S(1)} %shard_map.116.gated, bf16[32,3584]{1,0:T(8,128)(2,1)S(1)} %get-tuple-element.52.refs_0_, bf16[64,3584]{1,0:T(8,128)(2,1)S(1)} %collective-permute-done.12.refs_1_, ...), custom_call_target="tpu_custom_call" | custom-call | tf_op jit(solution)/shard_map/pallas_call | solution.py:294
  (1 shorter events, 0.0 us)
Async XLA Ops:
  0.6 12.3 %collective-permute-start.1 = (bf16[32,2048]{1,0:T(8,128)(2,1)}, bf16[32,2048]{1,0:T(8,128)(2,1)S(1)}, u32[]{:S(2)}, u32[]{:S(2)}) collective-permute-start(bf16[32,2048]{1,0:T(8,128)(2,1)} %refs_0_.7), channel_id=1, source_target_pairs={{0,8},{4,12},{8,0},{12,4},{1,9},{5,13},{9,1},{13,5},{2,10},{6,14},... | collective-permute-start | bytes 393224 | tf_op jit(solution)/shard_map/ppermute | solution.py:47
  4.7 15.3 %collective-permute-start = (bf16[32,2048]{1,0:T(8,128)(2,1)}, bf16[32,2048]{1,0:T(8,128)(2,1)S(1)}, u32[]{:S(2)}, u32[]{:S(2)}) collective-permute-start(bf16[32,2048]{1,0:T(8,128)(2,1)} %refs_0_.7), channel_id=1, source_target_pairs={{0,4},{4,0},{8,12},{12,8},{1,5},{5,1},{9,13},{13,9},{2,6},{6,2},{1... | collective-permute-start | bytes 393224 | tf_op jit(solution)/shard_map/ppermute | solution.py:47
  6.3 13.7 %collective-permute-start.3 = (bf16[32,2048]{1,0:T(8,128)(2,1)}, bf16[32,2048]{1,0:T(8,128)(2,1)S(1)}, u32[]{:S(2)}, u32[]{:S(2)}) collective-permute-start(bf16[32,2048]{1,0:T(8,128)(2,1)} %refs_0_.9), channel_id=1, source_target_pairs={{0,4},{4,0},{8,12},{12,8},{1,5},{5,1},{9,13},{13,9},{2,6},{6,2},{1... | collective-permute-start | bytes 393224 | tf_op jit(solution)/shard_map/ppermute | solution.py:47
  6.8 13.3 %collective-permute-start.4 = (bf16[32,2048]{1,0:T(8,128)(2,1)}, bf16[32,2048]{1,0:T(8,128)(2,1)S(1)}, u32[]{:S(2)}, u32[]{:S(2)}) collective-permute-start(bf16[32,2048]{1,0:T(8,128)(2,1)} %refs_0_.9), channel_id=1, source_target_pairs={{0,8},{4,12},{8,0},{12,4},{1,9},{5,13},{9,1},{13,5},{2,10},{6,14},... | collective-permute-start | bytes 393224 | tf_op jit(solution)/shard_map/ppermute | solution.py:47
  12.9 7.1 %copy-start = (bf16[32,2048]{1,0:T(8,128)(2,1)S(1)}, bf16[32,2048]{1,0:T(8,128)(2,1)}, u32[]{:S(2)}) copy-start(bf16[32,2048]{1,0:T(8,128)(2,1)} %refs_0_.7) | copy-start | bytes 393220
  12.9 7.1 %collective-permute-start.2 = (bf16[32,2048]{1,0:T(8,128)(2,1)S(1)}, bf16[32,2048]{1,0:T(8,128)(2,1)S(1)}, u32[]{:S(2)}, u32[]{:S(2)}) collective-permute-start(bf16[32,2048]{1,0:T(8,128)(2,1)S(1)} %shard_map.105), channel_id=1, source_target_pairs={{0,4},{4,0},{8,12},{12,8},{1,5},{5,1},{9,13},{13,9},{2,6},{6,2},{1... | collective-permute-start | bytes 393224 | tf_op jit(solution)/shard_map/ppermute | solution.py:47
  22.2 5.1 %collective-permute-start.5 = (bf16[64,3584]{1,0:T(8,128)(2,1)S(1)}, bf16[64,3584]{1,0:T(8,128)(2,1)S(1)}, u32[]{:S(2)}, u32[]{:S(2)}) collective-permute-start(bf16[64,3584]{1,0:T(8,128)(2,1)S(1)} %get-tuple-element.33.refs_4_), channel_id=1, source_target_pairs={{0,1},{1,0},{2,3},{3,2},{4,5},{5,4},{6,7},{7,6},{8,9},{9,8},{10,11... | collective-permute-start | bytes 1376264 | tf_op jit(solution)/shard_map/ppermute | solution.py:231
  25.4 8.7 %collective-permute-start.7 = (bf16[64,3584]{1,0:T(8,128)(2,1)S(1)}, bf16[64,3584]{1,0:T(8,128)(2,1)S(1)}, u32[]{:S(2)}, u32[]{:S(2)}) collective-permute-start(bf16[64,3584]{1,0:T(8,128)(2,1)S(1)} %get-tuple-element.37.refs_2_), channel_id=1, source_target_pairs={{0,1},{1,0},{2,3},{3,2},{4,5},{5,4},{6,7},{7,6},{8,9},{9,8},{10,11... | collective-permute-start | bytes 1376264 | tf_op jit(solution)/shard_map/ppermute | solution.py:231
  26.0 8.2 %collective-permute-start.8 = (bf16[32,2048]{1,0:T(8,128)(2,1)S(1)}, bf16[32,2048]{1,0:T(8,128)(2,1)S(1)}, u32[]{:S(2)}, u32[]{:S(2)}) collective-permute-start(bf16[32,2048]{1,0:T(8,128)(2,1)S(1)} %collective-permute-done.4.refs_8_.refs_2_), channel_id=1, source_target_pairs={{0,4},{4,0},{8,12},{12,8},{1,5},{5,1},{9,13},{13,9},{2,6},{6,2},{1... | collective-permute-start | bytes 393224 | tf_op jit(solution)/shard_map/ppermute | solution.py:47
  27.4 10.9 %collective-permute-start.6 = (bf16[32,3584]{1,0:T(8,128)(2,1)S(1)}, bf16[32,3584]{1,0:T(8,128)(2,1)S(1)}, u32[]{:S(2)}, u32[]{:S(2)}) collective-permute-start(bf16[32,3584]{1,0:T(8,128)(2,1)S(1)} %shard_map.109.refs_2_), channel_id=1, source_target_pairs={{0,2},{1,3},{2,0},{3,1},{4,6},{5,7},{6,4},{7,5},{8,10},{9,11},{10,... | collective-permute-start | bytes 688136 | tf_op jit(solution)/shard_map/ppermute | solution.py:231
  34.1 0.9 %copy-start.1 = (bf16[32,2048]{1,0:T(8,128)(2,1)S(1)}, bf16[32,2048]{1,0:T(8,128)(2,1)}, u32[]{:S(2)}) copy-start(bf16[32,2048]{1,0:T(8,128)(2,1)} %refs_0_.9) | copy-start | bytes 393220
  34.2 7.1 %collective-permute-start.9 = (bf16[32,3584]{1,0:T(8,128)(2,1)S(1)}, bf16[32,3584]{1,0:T(8,128)(2,1)S(1)}, u32[]{:S(2)}, u32[]{:S(2)}) collective-permute-start(bf16[32,3584]{1,0:T(8,128)(2,1)S(1)} %shard_map.111.refs_7_), channel_id=1, source_target_pairs={{0,2},{1,3},{2,0},{3,1},{4,6},{5,7},{6,4},{7,5},{8,10},{9,11},{10,... | collective-permute-start | bytes 688136 | tf_op jit(solution)/shard_map/ppermute | solution.py:231
  38.2 5.3 %collective-permute-start.10 = (bf16[64,3584]{1,0:T(8,128)(2,1)S(1)}, bf16[64,3584]{1,0:T(8,128)(2,1)S(1)}, u32[]{:S(2)}, u32[]{:S(2)}) collective-permute-start(bf16[64,3584]{1,0:T(8,128)(2,1)S(1)} %get-tuple-element.43.refs_3_), channel_id=1, source_target_pairs={{0,1},{1,0},{2,3},{3,2},{4,5},{5,4},{6,7},{7,6},{8,9},{9,8},{10,11... | collective-permute-start | bytes 1376264 | tf_op jit(solution)/shard_map/ppermute | solution.py:231
  43.4 1.9 %collective-permute-start.12 = (bf16[64,3584]{1,0:T(8,128)(2,1)S(1)}, bf16[64,3584]{1,0:T(8,128)(2,1)S(1)}, u32[]{:S(2)}, u32[]{:S(2)}) collective-permute-start(bf16[64,3584]{1,0:T(8,128)(2,1)S(1)} %get-tuple-element.47.refs_2_), channel_id=1, source_target_pairs={{0,1},{1,0},{2,3},{3,2},{4,5},{5,4},{6,7},{7,6},{8,9},{9,8},{10,11... | collective-permute-start | bytes 1376264 | tf_op jit(solution)/shard_map/ppermute | solution.py:231
  43.6 8.5 %collective-permute-start.11 = (bf16[32,3584]{1,0:T(8,128)(2,1)S(1)}, bf16[32,3584]{1,0:T(8,128)(2,1)S(1)}, u32[]{:S(2)}, u32[]{:S(2)}) collective-permute-start(bf16[32,3584]{1,0:T(8,128)(2,1)S(1)} %shard_map.114.refs_6_), channel_id=1, source_target_pairs={{0,2},{1,3},{2,0},{3,1},{4,6},{5,7},{6,4},{7,5},{8,10},{9,11},{10,... | collective-permute-start | bytes 688136 | tf_op jit(solution)/shard_map/ppermute | solution.py:231
  45.3 11.2 %collective-permute-start.13 = (bf16[32,3584]{1,0:T(8,128)(2,1)S(1)}, bf16[32,3584]{1,0:T(8,128)(2,1)S(1)}, u32[]{:S(2)}, u32[]{:S(2)}) collective-permute-start(bf16[32,3584]{1,0:T(8,128)(2,1)S(1)} %shard_map.117), channel_id=1, source_target_pairs={{0,2},{1,3},{2,0},{3,1},{4,6},{5,7},{6,4},{7,5},{8,10},{9,11},{10,... | collective-permute-start | bytes 688136 | tf_op jit(solution)/shard_map/ppermute | solution.py:231

commit v4 on v3

v4 whole, which is shorter than its diff:
```python
import functools
import math

import jax
import jax.numpy as jnp
from jax import lax
from jax.experimental import pallas as pl
from jax.experimental.pallas import tpu as pltpu
from jax.sharding import PartitionSpec as P

IN_VMEM = pl.BlockSpec(memory_space=pltpu.VMEM)
IN_SMEM = pl.BlockSpec(memory_space=pltpu.SMEM)
ANYWHERE = pl.BlockSpec(memory_space=pl.ANY)
LANES = 128


def in_hbm(array):
    return pltpu.with_memory_space_constraint(array, pltpu.HBM)


def in_vmem(array):
    return pltpu.with_memory_space_constraint(array, pltpu.VMEM)


def pass_kernel(piece, *refs):
    refs[-1][...] = piece[...]


def passed(piece, after):
    return pl.pallas_call(
        pass_kernel,
        out_shape=jax.ShapeDtypeStruct(piece.shape, piece.dtype),
        in_specs=[IN_VMEM] + [ANYWHERE] * len(after),
        out_specs=IN_VMEM,
        compiler_params=pltpu.CompilerParams(vmem_limit_bytes=1 << 20),
    )(piece, *after)


def gather_pieces(piece, axis, size, after=()):
    pieces = [piece]
    for offset in range(1, size):
        low = offset & -offset
        pairs = [(i, i ^ low) for i in range(size)]
        piece = pieces[offset ^ low]
        if after and offset != low:
            piece = passed(piece, after)
        pieces.append(lax.ppermute(piece, axis, pairs))
    return pieces


def halving_order(size):
    bits = size.bit_length() - 1
    reverse = [sum(((p >> b) & 1) << (bits - 1 - b) for b in range(bits)) for p in range(size)]
    return reverse[::-1]


def place_rows(pieces, rows, narrow):
    me_wide, me_narrow = lax.axis_index("wide"), lax.axis_index("narrow")
    piece_rows = pieces[0].shape[0]
    block_rows = piece_rows * len(pieces) // narrow
    size = math.gcd(piece_rows, block_rows)
    for offset, piece in enumerate(pieces):
        for start in range(0, piece_rows, size):
            row = (me_wide ^ offset) * piece_rows + start
            block = (row // block_rows) ^ me_narrow
            place = sum(
                jnp.where(block == known, position, 0)
                for position, known in enumerate(halving_order(narrow))
            )
            spot = pl.multiple_of(place * block_rows + row % block_rows, size)
            rows[pl.ds(spot, size), :] = piece[start : start + size, :]


def start_loads(sources, spans, dests, sems):
    copies = []
    for i, (source, (start, size)) in enumerate(zip(sources, spans)):
        copies.append(pltpu.make_async_copy(source.at[pl.ds(start, size), :], dests[i], sems.at[i]))
        copies[-1].start()
    return copies


def look_up_kernel(slots, ids, lengths, table, *refs):
    live, weight, entries, picked, sem = refs[-5:]
    lookup = pltpu.make_async_copy(table, entries, sem)
    lookup.start()
    for i in range(lengths.shape[0]):
        slot = lax.broadcasted_iota(jnp.int32, (slots, LANES), 0)
        live[i * slots : (i + 1) * slots, :] = (slot < lengths[i]).astype(jnp.float32)
    lookup.wait()

    def pick(i, carry):
        entry = ids[i]
        lane = lax.broadcasted_iota(jnp.int32, (1, LANES), 1)
        row = entries[pl.ds(entry // LANES, 1), :]
        picked[pl.ds(i, 1), :] = jnp.where(lane == entry % LANES, row, 0.0)
        return carry

    lax.fori_loop(0, ids.shape[0], pick, 0)
    weight[...] = jnp.broadcast_to(jnp.sum(picked[...], axis=1, keepdims=True), weight.shape)


def look_up(ids, lengths, table, after):
    table = table.reshape(-1, LANES)
    flag = jax.ShapeDtypeStruct((ids.shape[0], LANES), jnp.float32)
    return pl.pallas_call(
        functools.partial(look_up_kernel, ids.shape[0] // lengths.shape[0]),
        out_shape=[flag, flag],
        in_specs=[IN_SMEM, IN_SMEM] + [ANYWHERE] * (1 + len(after)),
        out_specs=[IN_VMEM, IN_VMEM],
        scratch_shapes=[
            pltpu.VMEM(table.shape, table.dtype),
            pltpu.VMEM(flag.shape, flag.dtype),
            pltpu.SemaphoreType.DMA,
        ],
        compiler_params=pltpu.CompilerParams(vmem_limit_bytes=3 << 20),
    )(*map(in_hbm, (ids, lengths, table)), *after)


def load_kernel(spans, after, *refs):
    dests = refs[len(spans) + after : -1]
    for copy in start_loads(refs[: len(spans)], spans, dests, refs[-1]):
        copy.wait()


def halves(matrix):
    half = matrix.shape[0] // 2
    return [(matrix, (0, half)), (matrix, (half, half))]


def load(loads, after):
    return pl.pallas_call(
        functools.partial(load_kernel, [span for _, span in loads], len(after)),
        out_shape=[pltpu.VMEM((size, m.shape[1]), m.dtype) for m, (_, size) in loads],
        in_specs=[ANYWHERE] * (len(loads) + len(after)),
        out_specs=[IN_VMEM] * len(loads),
        scratch_shapes=[pltpu.SemaphoreType.DMA((len(loads),))],
        compiler_params=pltpu.CompilerParams(vmem_limit_bytes=1 << 20),
    )(*(in_hbm(m) for m, _ in loads), *after)


def tile_of(cols):
    for tile in (512, 256, 128):
        if cols % tile == 0:
            return tile
    return cols


def column_tiles(width):
    tile = tile_of(width)
    return [slice(start, start + tile) for start in range(0, width, tile)]


def product_kernel(pieces, groups, spans, after, narrow, *refs):
    tokens, refs = refs[:pieces], refs[pieces:]
    matrices = []
    for count in groups:
        matrices.append(refs[:count])
        refs = refs[count:]
    sources, refs = refs[: len(spans)], refs[len(spans) + after :]
    dests, outs, sems = refs[: len(spans)], refs[len(spans) : -1], refs[-1]
    copies = start_loads(sources, spans, dests, sems)
    if pieces > 1:
        place_rows(tokens, outs[0], narrow)
        tokens, outs = outs[:1], outs[1:]
    first = 0
    for group in matrices:
        width = group[0].shape[1]
        for cols in column_tiles(width):
            total, depth = None, 0
            for matrix in group:
                rows = tokens[0][:, depth : depth + matrix.shape[0]]
                term = jnp.dot(rows, matrix[:, cols], preferred_element_type=jnp.float32)
                total = term if total is None else total + term
                depth += matrix.shape[0]
            row = 0
            for out in outs:
                out[:, first + cols.start : first + cols.stop] = total[row : row + out.shape[0]].astype(out.dtype)
                row += out.shape[0]
        first += width
    for copy in copies:
        copy.wait()


def part_sizes(total, narrow):
    sizes, left = [], total // 2
    while left > total // narrow:
        left //= 2
        sizes.append(left)
    return sizes + [left]


def product(tokens, groups, narrow, after=(), loads=()):
    placing = len(tokens) > 1
    total = sum(t.shape[0] for t in tokens)
    depth, width = tokens[0].shape[1], sum(group[0].shape[1] for group in groups)
    matrices = [in_vmem(part) for group in groups for part in group]
    sizes = part_sizes(total, narrow)
    found = pl.pallas_call(
        functools.partial(
            product_kernel,
            len(tokens),
            [len(group) for group in groups],
            [span for _, span in loads],
            len(after),
            narrow,
        ),
        out_shape=[pltpu.VMEM((size, m.shape[1]), m.dtype) for m, (_, size) in loads]
        + [jax.ShapeDtypeStruct((total, depth), tokens[0].dtype)] * placing
        + [jax.ShapeDtypeStruct((size, width), jnp.bfloat16) for size in sizes * 2],
        in_specs=[IN_VMEM] * (len(tokens) + len(matrices)) + [ANYWHERE] * (len(loads) + len(after)),
        out_specs=[IN_VMEM] * (len(loads) + placing + 2 * len(sizes)),
        scratch_shapes=[pltpu.SemaphoreType.DMA((max(1, len(loads)),))],
        compiler_params=pltpu.CompilerParams(vmem_limit_bytes=6 << 20),
    )(*tokens, *matrices, *(in_hbm(m) for m, _ in loads), *after)
    loaded, found = found[: len(loads)], found[len(loads) :]
    rows, found = (found[:1], found[1:]) if placing else (tokens, found)
    return loaded, rows, found[: len(sizes)], found[len(sizes) :]


def exchange(array, step, size):
    return lax.ppermute(array, "narrow", [(i, i ^ (1 << step)) for i in range(size)])


def addends(parts, came, k):
    found = [(parts[k], 0)]
    for array, first, behind in came:
        if first <= k < behind:
            found.append((array, sum(part.shape[0] for part in parts[first:k])))
    return [array for array, _ in found], tuple(start for _, start in found)


def added(refs, starts, count, cols):
    return sum(
        ref[start : start + count, cols].astype(jnp.float32) for ref, start in zip(refs, starts)
    )


def next_kernel(starts, *refs):
    out = refs[-1]
    for cols in column_tiles(out.shape[1]):
        out[:, cols] = added(refs, starts, out.shape[0], cols).astype(out.dtype)


def finish(sends, keeps, narrow, after):
    came = [(exchange(send, 0, narrow), k, k + 1) for k, send in enumerate(sends)]
    sent = sends[0]
    for k in range(len(keeps) - 1):
        arrays, starts = addends(keeps, came, k)
        sent = pl.pallas_call(
            functools.partial(next_kernel, starts),
            out_shape=jax.ShapeDtypeStruct(keeps[k].shape, jnp.bfloat16),
            in_specs=[IN_VMEM] * len(arrays) + [ANYWHERE] * len(after),
            out_specs=IN_VMEM,
            compiler_params=pltpu.CompilerParams(vmem_limit_bytes=4 << 20),
        )(*arrays, *after)
        came.append((exchange(sent, k + 1, narrow), k + 1, len(keeps)))
    return sent, addends(keeps, came, len(keeps) - 1)


def own_sum(refs, starts, count, first, cols):
    return added(refs, starts, count, slice(first + cols.start, first + cols.stop))


def target_kernel(starts, live, *refs):
    terms, act, out = refs[: len(starts)], refs[-2], refs[-1]
    count, width = out.shape
    for cols in column_tiles(width):
        gate = own_sum(terms, starts, count, 0, cols)
        upper = own_sum(terms, starts, count, width, cols)
        value = live[:, :1] * (jax.nn.silu(gate) * upper)
        act[:, cols] = value
        out[:, cols] = value.astype(out.dtype)


def target_end(live, own):
    arrays, starts = own
    shape = (live.shape[0], arrays[0].shape[1] // 2)
    return pl.pallas_call(
        functools.partial(target_kernel, starts),
        out_shape=[jax.ShapeDtypeStruct(shape, jnp.float32), jax.ShapeDtypeStruct(shape, jnp.bfloat16)],
        in_specs=[IN_VMEM] * (1 + len(arrays)),
        out_specs=[IN_VMEM] * 2,
        compiler_params=pltpu.CompilerParams(vmem_limit_bytes=6 << 20),
    )(live, *arrays)


def source_kernel(starts, live, weight, *refs):
    terms, out = refs[:-1], refs[-1]
    for cols in column_tiles(out.shape[1]):
        gate = own_sum(terms, starts, out.shape[0], 0, cols)
        out[:, cols] = (live[:, :1] * weight[:, :1]) * jax.nn.silu(gate)


def source_middle(live, weight, own):
    arrays, starts = own
    return pl.pallas_call(
        functools.partial(source_kernel, starts),
        out_shape=jax.ShapeDtypeStruct((live.shape[0], arrays[0].shape[1]), jnp.float32),
        in_specs=[IN_VMEM] * (2 + len(arrays)),
        out_specs=IN_VMEM,
        compiler_params=pltpu.CompilerParams(vmem_limit_bytes=6 << 20),
    )(live, weight, *arrays)


def ratio_kernel(starts, act, gated, *refs):
    terms, out = refs[:-1], refs[-1]
    for cols in column_tiles(out.shape[1]):
        upper = own_sum(terms, starts, out.shape[0], 0, cols)
        out[:, cols] = (act[:, cols] - gated[:, cols] * upper).astype(out.dtype)


def ratio_end(act, gated, own):
    arrays, starts = own
    return pl.pallas_call(
        functools.partial(ratio_kernel, starts),
        out_shape=jax.ShapeDtypeStruct(act.shape, jnp.bfloat16),
        in_specs=[IN_VMEM] * (2 + len(arrays)),
        out_specs=IN_VMEM,
        compiler_params=pltpu.CompilerParams(vmem_limit_bytes=6 << 20),
    )(act, gated, *arrays)


def local(mesh_shape, target_states, source_states, target_gate, target_up, source_gate, source_up, token_ids, lengths, ratio_weight):
    wide, narrow = mesh_shape["wide"], mesh_shape["narrow"]
    gate_top, gate_bottom = halves(source_gate)

    target_gate = load(halves(target_gate), ())
    target_pieces = gather_pieces(target_states, "wide", wide, (target_gate[0],))
    source_pieces = gather_pieces(source_states, "wide", wide)
    target_up = load(halves(target_up), (target_gate[0], target_pieces[wide // 2]))

    after = (target_up[0], source_pieces[1], source_pieces[wide // 2])
    _, _, sends, keeps = product(target_pieces, (target_gate, target_up), narrow, after)
    (gate_top,) = load([gate_top], (sends[0],))
    sent, target = finish(sends, keeps, narrow, (gate_top, source_pieces[-1]))
    (gate_bottom,) = load([gate_bottom], (sent,))

    source_up, rows, gate_sends, gate_keeps = product(
        source_pieces, ((gate_top, gate_bottom),), narrow, (sent,), halves(source_up)
    )
    _, _, sends, keeps = product(rows, (source_up,), narrow, (gate_sends[0],))
    sent, source_g = finish(gate_sends, gate_keeps, narrow, (sends[0], target[0][-1]))
    live, weight = look_up(token_ids, lengths, ratio_weight, (sent,))
    act, target_out = target_end(live, target)
    _, source_u = finish(sends, keeps, narrow, (act,))
    gated = source_middle(live, weight, source_g)
    ratio_out = ratio_end(act, gated, source_u)
    return (target_out, ratio_out)


def solution(mesh):
    placed = (
        P(("groups", "wide"), "narrow"),
        P(("groups", "wide"), "narrow"),
        P("narrow", "wide"),
        P("narrow", "wide"),
        P("narrow", "wide"),
        P("narrow", "wide"),
        P(("groups", "narrow")),
        P(("groups", "narrow")),
        P(),
    )
    mesh_shape = dict(mesh.shape)

    def body(*args):
        return local(mesh_shape, *args)

    return jax.shard_map(
        body,
        mesh=mesh,
        in_specs=placed,
        out_specs=(P(("groups", "narrow"), "wide"), P(("groups", "narrow"), "wide")),
        check_vma=False,
    )
```

time: 57.5 us -> 59.3 us (1.031)
  Pallas kernels: 29 us -> 33.1 us
  waiting for transfers between devices: 12.9 us -> 11.4 us
  starting transfers between devices: 14.3 us -> 13.7 us
    pallas_call x2 -> x4, Pallas kernels: 10.4 us -> 16.6 us  [load(): pl.pallas_call(functools.partial(load_kernel, [span for _, span in loads]...]
    ppermute x8 -> x9, waiting for transfers between devices: 12.9 us -> 7.47 us  [exchange(): lax.ppermute(array, 'narrow', [(i, i ^ 1 << step) for i in range(size)])]
    ppermute x6, waiting for transfers between devices: 0.02 us -> 3.96 us  [gather_pieces(): pieces.append(lax.ppermute(piece, axis, pairs))]
    pallas_call x12 -> x10, Pallas kernels: 18.6 us -> 16.5 us  [the longest x3 12.2 us: product(): pl.pallas_call(functools.partial(product_kernel, len(tokens), [len(group)...]
    ppermute x6, starting transfers between devices: 9.43 us -> 8.36 us  [gather_pieces(): pieces.append(lax.ppermute(piece, axis, pairs))]
    ppermute x8 -> x9, starting transfers between devices: 4.89 us -> 5.33 us  [exchange(): lax.ppermute(array, 'narrow', [(i, i ^ 1 << step) for i in range(size)])]
  transfers between devices with their start and end apart: 14 -> 15, of which waited for: 4 -> 4; matrix products, arithmetic and copies ran while one was open for 0% -> 0% of each run, Pallas kernels for 45% -> 47%
where the time goes in v4:
time: 59.3 us; the launch traced here: 59 us
  Pallas kernels  33.1 us (56%)
  starting transfers between devices  13.7 us (23%)
  waiting for transfers between devices  11.4 us (19%)
  between operations  0.8 us (1%)
    pallas_call x4, Pallas kernels, load(): pl.pallas_call(functools.partial(load_kernel, [span for _, span in loads]...  16.6 us
    pallas_call x3, Pallas kernels, product(): pl.pallas_call(functools.partial(product_kernel, len(tokens), [len(group)...  12.2 us
    ppermute x6, starting transfers between devices, gather_pieces(): pieces.append(lax.ppermute(piece, axis, pairs))  8.36 us
    ppermute x9, waiting for transfers between devices, exchange(): lax.ppermute(array, 'narrow', [(i, i ^ 1 << step) for i in range(size)])  7.47 us
    ppermute x9, starting transfers between devices, exchange(): lax.ppermute(array, 'narrow', [(i, i ^ 1 << step) for i in range(size)])  5.33 us
    ppermute x6, waiting for transfers between devices, gather_pieces(): pieces.append(lax.ppermute(piece, axis, pairs))  3.96 us
    pallas_call x1, Pallas kernels, look_up(): pl.pallas_call(functools.partial(look_up_kernel, ids.shape[0] // lengths....  2.16 us
  transfers between devices with their start and end apart: 15, of which 4 were waited for; matrix products, arithmetic and copies ran while one was open for 0% of the time, Pallas kernels for 47%

profile of v4, /device:TPU:0, one launch (start us, length us, event | category | flops | bytes accessed | tf_op | source)
XLA Modules:
  0.0 59.0 jit_solution(15038399541965880580)
XLA Ops:
  0.6 4.1 %collective-permute-start.4 = (bf16[32,2048]{1,0:T(8,128)(2,1)}, bf16[32,2048]{1,0:T(8,128)(2,1)S(1)}, u32[]{:S(2)}, u32[]{:S(2)}) collective-permute-start(bf16[32,2048]{1,0:T(8,128)(2,1)} %refs_0_.8), channel_id=1, source_target_pairs={{0,8},{4,12},{8,0},{12,4},{1,9},{5,13},{9,1},{13,5},{2,10},{6,14},... | collective-permute-start | bytes 393224 | tf_op jit(solution)/shard_map/ppermute | solution.py:47
  4.7 0.1 collective-permute-start.1
  4.8 1.8 %collective-permute-start = (bf16[32,2048]{1,0:T(8,128)(2,1)}, bf16[32,2048]{1,0:T(8,128)(2,1)S(1)}, u32[]{:S(2)}, u32[]{:S(2)}) collective-permute-start(bf16[32,2048]{1,0:T(8,128)(2,1)} %refs_0_.11), channel_id=1, source_target_pairs={{0,4},{4,0},{8,12},{12,8},{1,5},{5,1},{9,13},{13,9},{2,6},{6,2},{1... | collective-permute-start | bytes 393224 | tf_op jit(solution)/shard_map/ppermute | solution.py:47
  6.6 0.2 collective-permute-start.3
  6.8 5.2 %shard_map.104 = (bf16[1024,3584]{1,0:T(8,128)(2,1)S(1)}, bf16[1024,3584]{1,0:T(8,128)(2,1)S(1)}) custom-call(bf16[2048,3584]{1,0:T(8,128)(2,1)} %refs_1_.2, bf16[2048,3584]{1,0:T(8,128)(2,1)} %refs_1_.2), custom_call_target="tpu_custom_call" | custom-call | tf_op jit(solution)/shard_map/pallas_call | solution.py:131
  12.0 3.0 %collective-permute-done.4.piece.refs_3_.refs_2_ = bf16[32,2048]{1,0:T(8,128)(2,1)S(1)} collective-permute-done((bf16[32,2048]{1,0:T(8,128)(2,1)}, bf16[32,2048]{1,0:T(8,128)(2,1)S(1)}, u32[]{:S(2)}, u32[]{:S(2)}) %collective-permute-start.4) | collective-permute-done | bytes 131104 | tf_op jit(solution)/shard_map/ppermute | solution.py:47
  15.0 0.0 copy-start
  15.0 0.1 collective-permute-start.5
  15.1 5.2 %shard_map.106 = (bf16[1024,3584]{1,0:T(8,128)(2,1)S(1)}, bf16[1024,3584]{1,0:T(8,128)(2,1)S(1)}) custom-call(bf16[2048,3584]{1,0:T(8,128)(2,1)} %refs_1_.3, bf16[2048,3584]{1,0:T(8,128)(2,1)} %refs_1_.3, bf16[1024,3584]{1,0:T(8,128)(2,1)S(1)} %get-tuple-element.25.refs_0_.refs_2_.refs_4_, bf16[32,2048]{1,0:T(8,128)(2,1)S(1)} %collective-permute-done.4.piece.refs_3_.refs_2_), custom_call_target="tpu_custom_call" | custom-call | tf_op jit(solution)/shard_map/pallas_call | solution.py:131
  20.3 0.0 collective-permute-done.1.refs_10_.refs_2_
  20.3 0.0 collective-permute-done.refs_9_.refs_1_
  20.3 0.0 collective-permute-done.3.refs_1_
  20.3 0.0 collective-permute-done.5.refs_3_
  20.3 0.0 copy-done
  20.4 4.7 %shard_map.107 = (bf16[128,2048]{1,0:T(8,128)(2,1)}, bf16[32,7168]{1,0:T(8,128)(2,1)S(1)}, bf16[32,7168]{1,0:T(8,128)(2,1)S(1)}, bf16[32,7168]{1,0:T(8,128)(2,1)S(1)}, bf16[32,7168]{1,0:T(8,128)(2,1)S(1)}) custom-call(bf16[32,2048]{1,0:T(8,128)(2,1)S(1)} %copy-done, bf16[32,2048]{1,0:T(8,128)(2,1)S(1)} %collective-permute-done.3.refs_1_, ...), custom_call_target="tpu_custom_call" | custom-call | tf_op jit(solution)/shard_map/pallas_call | solution.py:198
  25.0 0.1 collective-permute-start.6
  25.1 2.1 %collective-permute-start.2 = (bf16[32,2048]{1,0:T(8,128)(2,1)S(1)}, bf16[32,2048]{1,0:T(8,128)(2,1)S(1)}, u32[]{:S(2)}, u32[]{:S(2)}) collective-permute-start(bf16[32,2048]{1,0:T(8,128)(2,1)S(1)} %collective-permute-done.1.refs_10_.refs_2_), channel_id=1, source_target_pairs={{0,4},{4,0},{8,12},{12,8},{1,5},{5,1},{9,13},{13,9},{2,6},{6,2},{1... | collective-permute-start | bytes 393224 | tf_op jit(solution)/shard_map/ppermute | solution.py:47
  27.2 3.1 %shard_map.108.refs_2_.refs_4_ = bf16[1024,3584]{1,0:T(8,128)(2,1)S(1)} custom-call(bf16[2048,3584]{1,0:T(8,128)(2,1)} %refs_0_.10, bf16[32,7168]{1,0:T(8,128)(2,1)S(1)} %get-tuple-element.29.refs_1_), custom_call_target="tpu_custom_call" | custom-call | tf_op jit(solution)/shard_map/pallas_call | solution.py:131
  30.3 1.0 %collective-permute-done.2.refs_3_ = bf16[32,2048]{1,0:T(8,128)(2,1)S(1)} collective-permute-done((bf16[32,2048]{1,0:T(8,128)(2,1)S(1)}, bf16[32,2048]{1,0:T(8,128)(2,1)S(1)}, u32[]{:S(2)}, u32[]{:S(2)}) %collective-permute-start.2) | collective-permute-done | bytes 131104 | tf_op jit(solution)/shard_map/ppermute | solution.py:47
  31.2 0.0 collective-permute-done.6.refs_1_
  31.2 0.1 shard_map.109.refs_1_.refs_8_
  31.4 1.9 %collective-permute-start.8 = (bf16[32,7168]{1,0:T(8,128)(2,1)S(1)}, bf16[32,7168]{1,0:T(8,128)(2,1)S(1)}, u32[]{:S(2)}, u32[]{:S(2)}) collective-permute-start(bf16[32,7168]{1,0:T(8,128)(2,1)S(1)} %shard_map.109.refs_1_.refs_8_), channel_id=1, source_target_pairs={{0,2},{1,3},{2,0},{3,1},{4,6},{5,7},{6,4},{7,5},{8,10},{9,11},{10,... | collective-permute-start | bytes 1376264 | tf_op jit(solution)/shard_map/ppermute | solution.py:221
  33.3 0.0 copy-start.1
  33.3 0.0 collective-permute-start.9
  33.3 3.1 %shard_map.110.refs_5_ = bf16[1024,3584]{1,0:T(8,128)(2,1)S(1)} custom-call(bf16[2048,3584]{1,0:T(8,128)(2,1)} %refs_0_.10, bf16[32,7168]{1,0:T(8,128)(2,1)S(1)} %shard_map.109.refs_1_.refs_8_), custom_call_target="tpu_custom_call" | custom-call | tf_op jit(solution)/shard_map/pallas_call | solution.py:131
  36.4 0.0 copy-done.1
  36.4 5.5 %shard_map.111 = (bf16[1024,3584]{1,0:T(8,128)(2,1)S(1)}, bf16[1024,3584]{1,0:T(8,128)(2,1)S(1)}, bf16[128,2048]{1,0:T(8,128)(2,1)S(1)}, bf16[32,3584]{1,0:T(8,1...) custom-call(bf16[32,2048]{1,0:T(8,128)(2,1)S(1)} %copy-done.1, ...), custom_call_target="tpu_custom_call" | custom-call | tf_op jit(solution)/shard_map/pallas_call | solution.py:198
  41.9 0.5 collective-permute-start.7
  42.5 2.1 %shard_map.112 = (bf16[32,3584]{1,0:T(8,128)(2,1)S(1)}, bf16[32,3584]{1,0:T(8,128)(2,1)S(1)}, bf16[32,3584]{1,0:T(8,128)(2,1)S(1)}, bf16[32,3584]{1,0:T(8,128)(2,1)S(1)}) custom-call(bf16[128,2048]{1,0:T(8,128)(2,1)S(1)} %get-tuple-element.33.refs_0_, bf16[1024,3584]{1,0:T(8,128)(2,1)S(1)} %get-tuple-element.34.refs_1_, ...), custom_call_target="tpu_custom_call" | custom-call | tf_op jit(solution)/shard_map/pallas_call | solution.py:198
  44.6 0.1 collective-permute-start.13
  44.7 0.5 collective-permute-start.10
  45.1 0.0 collective-permute-done.7.refs_1_
  45.1 0.1 collective-permute-start.12
  45.2 0.0 collective-permute-done.8.refs_3_.refs_2_
  45.2 0.1 shard_map.113.refs_0_
  45.3 0.4 collective-permute-start.11
  45.7 2.2 %shard_map.114 = (f32[32,128]{1,0:T(8,128)S(1)}, f32[32,128]{1,0:T(8,128)S(1)}) custom-call(s32[32]{0:T(128)} %ids.1, s32[2]{0:T(128)} %lengths.1, f32[1002,128]{1,0:T(8,128)} %bitcast.1, bf16[32,3584]{1,0:T(8,128)(2,1)S(1)} %shard_map.113.refs_0_), custom_call_target="tpu_custom_call" | custom-call | tf_op jit(solution)/shard_map/pallas_call | solution.py:105
  47.8 0.0 collective-permute-done.9.refs_1_
  47.8 0.9 %shard_map.115 = (f32[32,3584]{1,0:T(8,128)S(1)}, bf16[32,3584]{1,0:T(8,128)(2,1)}) custom-call(f32[32,128]{1,0:T(8,128)S(1)} %get-tuple-element.37.live, bf16[32,7168]{1,0:T(8,128)(2,1)S(1)} %get-tuple-element.38.refs_0_, bf16[32,7168]{1,0:T(8,128)(2,1)S(1)} %collective-permute-done.9.refs_1_, bf16[32,7168]{1,0:T(8,128)(2,1)S(1)} %collective-permute-done.8.refs_3_.refs_2_), custom_call_target="tpu_custom_call" | custom-call | tf_op jit(solution)/shard_map/pallas_call | solution.py:278
  48.8 0.0 collective-permute-done.13.refs_1_
  48.8 0.1 shard_map.117
  48.8 1.8 %collective-permute-start.14 = (bf16[32,3584]{1,0:T(8,128)(2,1)S(1)}, bf16[32,3584]{1,0:T(8,128)(2,1)S(1)}, u32[]{:S(2)}, u32[]{:S(2)}) collective-permute-start(bf16[32,3584]{1,0:T(8,128)(2,1)S(1)} %shard_map.117), channel_id=1, source_target_pairs={{0,2},{1,3},{2,0},{3,1},{4,6},{5,7},{6,4},{7,5},{8,10},{9,11},{10,... | collective-permute-start | bytes 688136 | tf_op jit(solution)/shard_map/ppermute | solution.py:221
  50.6 0.0 collective-permute-done.10.refs_1_
  50.6 3.1 %collective-permute-done.11.refs_2_ = bf16[32,3584]{1,0:T(8,128)(2,1)S(1)} collective-permute-done((bf16[32,3584]{1,0:T(8,128)(2,1)S(1)}, bf16[32,3584]{1,0:T(8,128)(2,1)S(1)}, u32[]{:S(2)}, u32[]{:S(2)}) %collective-permute-start.11) | collective-permute-done | bytes 229408 | tf_op jit(solution)/shard_map/ppermute | solution.py:221
  53.7 0.1 shard_map.116.gated
  53.9 0.0 collective-permute-done.12.refs_1_
  53.9 4.3 %collective-permute-done.14.refs_2_ = bf16[32,3584]{1,0:T(8,128)(2,1)S(1)} collective-permute-done((bf16[32,3584]{1,0:T(8,128)(2,1)S(1)}, bf16[32,3584]{1,0:T(8,128)(2,1)S(1)}, u32[]{:S(2)}, u32[]{:S(2)}) %collective-permute-start.14) | collective-permute-done | bytes 229408 | tf_op jit(solution)/shard_map/ppermute | solution.py:221
  58.2 0.8 %shard_map.118 = bf16[32,3584]{1,0:T(8,128)(2,1)} custom-call(f32[32,3584]{1,0:T(8,128)S(1)} %get-tuple-element.41.refs_2_.act, f32[32,3584]{1,0:T(8,128)S(1)} %shard_map.116.gated, bf16[32,3584]{1,0:T(8,128)(2,1)S(1)} %get-tuple-element.45.refs_0_, bf16[32,3584]{1,0:T(8,128)(2,1)S(1)} %collective-permute-done.12.refs_1_, ...), custom_call_target="tpu_custom_call" | custom-call | tf_op jit(solution)/shard_map/pallas_call | solution.py:314
  (1 shorter events, 0.0 us)
Async XLA Ops:
  0.6 14.4 %collective-permute-start.4 = (bf16[32,2048]{1,0:T(8,128)(2,1)}, bf16[32,2048]{1,0:T(8,128)(2,1)S(1)}, u32[]{:S(2)}, u32[]{:S(2)}) collective-permute-start(bf16[32,2048]{1,0:T(8,128)(2,1)} %refs_0_.8), channel_id=1, source_target_pairs={{0,8},{4,12},{8,0},{12,4},{1,9},{5,13},{9,1},{13,5},{2,10},{6,14},... | collective-permute-start | bytes 393224 | tf_op jit(solution)/shard_map/ppermute | solution.py:47
  4.7 15.6 %collective-permute-start.1 = (bf16[32,2048]{1,0:T(8,128)(2,1)}, bf16[32,2048]{1,0:T(8,128)(2,1)S(1)}, u32[]{:S(2)}, u32[]{:S(2)}) collective-permute-start(bf16[32,2048]{1,0:T(8,128)(2,1)} %refs_0_.11), channel_id=1, source_target_pairs={{0,8},{4,12},{8,0},{12,4},{1,9},{5,13},{9,1},{13,5},{2,10},{6,14},... | collective-permute-start | bytes 393224 | tf_op jit(solution)/shard_map/ppermute | solution.py:47
  4.8 15.5 %collective-permute-start = (bf16[32,2048]{1,0:T(8,128)(2,1)}, bf16[32,2048]{1,0:T(8,128)(2,1)S(1)}, u32[]{:S(2)}, u32[]{:S(2)}) collective-permute-start(bf16[32,2048]{1,0:T(8,128)(2,1)} %refs_0_.11), channel_id=1, source_target_pairs={{0,4},{4,0},{8,12},{12,8},{1,5},{5,1},{9,13},{13,9},{2,6},{6,2},{1... | collective-permute-start | bytes 393224 | tf_op jit(solution)/shard_map/ppermute | solution.py:47
  6.6 13.7 %collective-permute-start.3 = (bf16[32,2048]{1,0:T(8,128)(2,1)}, bf16[32,2048]{1,0:T(8,128)(2,1)S(1)}, u32[]{:S(2)}, u32[]{:S(2)}) collective-permute-start(bf16[32,2048]{1,0:T(8,128)(2,1)} %refs_0_.8), channel_id=1, source_target_pairs={{0,4},{4,0},{8,12},{12,8},{1,5},{5,1},{9,13},{13,9},{2,6},{6,2},{1... | collective-permute-start | bytes 393224 | tf_op jit(solution)/shard_map/ppermute | solution.py:47
  15.0 5.3 %copy-start = (bf16[32,2048]{1,0:T(8,128)(2,1)S(1)}, bf16[32,2048]{1,0:T(8,128)(2,1)}, u32[]{:S(2)}) copy-start(bf16[32,2048]{1,0:T(8,128)(2,1)} %refs_0_.8) | copy-start | bytes 393220
  15.0 5.3 %collective-permute-start.5 = (bf16[32,2048]{1,0:T(8,128)(2,1)S(1)}, bf16[32,2048]{1,0:T(8,128)(2,1)S(1)}, u32[]{:S(2)}, u32[]{:S(2)}) collective-permute-start(bf16[32,2048]{1,0:T(8,128)(2,1)S(1)} %shard_map.105), channel_id=1, source_target_pairs={{0,4},{4,0},{8,12},{12,8},{1,5},{5,1},{9,13},{13,9},{2,6},{6,2},{1... | collective-permute-start | bytes 393224 | tf_op jit(solution)/shard_map/ppermute | solution.py:47
  25.0 6.2 %collective-permute-start.6 = (bf16[32,7168]{1,0:T(8,128)(2,1)S(1)}, bf16[32,7168]{1,0:T(8,128)(2,1)S(1)}, u32[]{:S(2)}, u32[]{:S(2)}) collective-permute-start(bf16[32,7168]{1,0:T(8,128)(2,1)S(1)} %get-tuple-element.29.refs_1_), channel_id=1, source_target_pairs={{0,1},{1,0},{2,3},{3,2},{4,5},{5,4},{6,7},{7,6},{8,9},{9,8},{10,11... | collective-permute-start | bytes 1376264 | tf_op jit(solution)/shard_map/ppermute | solution.py:221
  25.1 6.1 %collective-permute-start.2 = (bf16[32,2048]{1,0:T(8,128)(2,1)S(1)}, bf16[32,2048]{1,0:T(8,128)(2,1)S(1)}, u32[]{:S(2)}, u32[]{:S(2)}) collective-permute-start(bf16[32,2048]{1,0:T(8,128)(2,1)S(1)} %collective-permute-done.1.refs_10_.refs_2_), channel_id=1, source_target_pairs={{0,4},{4,0},{8,12},{12,8},{1,5},{5,1},{9,13},{13,9},{2,6},{6,2},{1... | collective-permute-start | bytes 393224 | tf_op jit(solution)/shard_map/ppermute | solution.py:47
  31.4 13.9 %collective-permute-start.8 = (bf16[32,7168]{1,0:T(8,128)(2,1)S(1)}, bf16[32,7168]{1,0:T(8,128)(2,1)S(1)}, u32[]{:S(2)}, u32[]{:S(2)}) collective-permute-start(bf16[32,7168]{1,0:T(8,128)(2,1)S(1)} %shard_map.109.refs_1_.refs_8_), channel_id=1, source_target_pairs={{0,2},{1,3},{2,0},{3,1},{4,6},{5,7},{6,4},{7,5},{8,10},{9,11},{10,... | collective-permute-start | bytes 1376264 | tf_op jit(solution)/shard_map/ppermute | solution.py:221
  33.3 3.1 %copy-start.1 = (bf16[32,2048]{1,0:T(8,128)(2,1)S(1)}, bf16[32,2048]{1,0:T(8,128)(2,1)}, u32[]{:S(2)}) copy-start(bf16[32,2048]{1,0:T(8,128)(2,1)} %refs_0_.11) | copy-start | bytes 393220
  33.3 14.5 %collective-permute-start.9 = (bf16[32,7168]{1,0:T(8,128)(2,1)S(1)}, bf16[32,7168]{1,0:T(8,128)(2,1)S(1)}, u32[]{:S(2)}, u32[]{:S(2)}) collective-permute-start(bf16[32,7168]{1,0:T(8,128)(2,1)S(1)} %get-tuple-element.39), channel_id=1, source_target_pairs={{0,1},{1,0},{2,3},{3,2},{4,5},{5,4},{6,7},{7,6},{8,9},{9,8},{10,11... | collective-permute-start | bytes 1376264 | tf_op jit(solution)/shard_map/ppermute | solution.py:221
  41.9 3.2 %collective-permute-start.7 = (bf16[32,3584]{1,0:T(8,128)(2,1)S(1)}, bf16[32,3584]{1,0:T(8,128)(2,1)S(1)}, u32[]{:S(2)}, u32[]{:S(2)}) collective-permute-start(bf16[32,3584]{1,0:T(8,128)(2,1)S(1)} %get-tuple-element.32.refs_3_), channel_id=1, source_target_pairs={{0,1},{1,0},{2,3},{3,2},{4,5},{5,4},{6,7},{7,6},{8,9},{9,8},{10,11... | collective-permute-start | bytes 688136 | tf_op jit(solution)/shard_map/ppermute | solution.py:221
  44.6 4.2 %collective-permute-start.13 = (bf16[32,3584]{1,0:T(8,128)(2,1)S(1)}, bf16[32,3584]{1,0:T(8,128)(2,1)S(1)}, u32[]{:S(2)}, u32[]{:S(2)}) collective-permute-start(bf16[32,3584]{1,0:T(8,128)(2,1)S(1)} %get-tuple-element.36.refs_2_), channel_id=1, source_target_pairs={{0,1},{1,0},{2,3},{3,2},{4,5},{5,4},{6,7},{7,6},{8,9},{9,8},{10,11... | collective-permute-start | bytes 688136 | tf_op jit(solution)/shard_map/ppermute | solution.py:221
  44.7 5.9 %collective-permute-start.10 = (bf16[32,3584]{1,0:T(8,128)(2,1)S(1)}, bf16[32,3584]{1,0:T(8,128)(2,1)S(1)}, u32[]{:S(2)}, u32[]{:S(2)}) collective-permute-start(bf16[32,3584]{1,0:T(8,128)(2,1)S(1)} %get-tuple-element.44), channel_id=1, source_target_pairs={{0,1},{1,0},{2,3},{3,2},{4,5},{5,4},{6,7},{7,6},{8,9},{9,8},{10,11... | collective-permute-start | bytes 688136 | tf_op jit(solution)/shard_map/ppermute | solution.py:221
  45.1 8.8 %collective-permute-start.12 = (bf16[32,3584]{1,0:T(8,128)(2,1)S(1)}, bf16[32,3584]{1,0:T(8,128)(2,1)S(1)}, u32[]{:S(2)}, u32[]{:S(2)}) collective-permute-start(bf16[32,3584]{1,0:T(8,128)(2,1)S(1)} %get-tuple-element.46), channel_id=1, source_target_pairs={{0,1},{1,0},{2,3},{3,2},{4,5},{5,4},{6,7},{7,6},{8,9},{9,8},{10,11... | collective-permute-start | bytes 688136 | tf_op jit(solution)/shard_map/ppermute | solution.py:221
  45.3 8.5 %collective-permute-start.11 = (bf16[32,3584]{1,0:T(8,128)(2,1)S(1)}, bf16[32,3584]{1,0:T(8,128)(2,1)S(1)}, u32[]{:S(2)}, u32[]{:S(2)}) collective-permute-start(bf16[32,3584]{1,0:T(8,128)(2,1)S(1)} %shard_map.113.refs_0_), channel_id=1, source_target_pairs={{0,2},{1,3},{2,0},{3,1},{4,6},{5,7},{6,4},{7,5},{8,10},{9,11},{10,... | collective-permute-start | bytes 688136 | tf_op jit(solution)/shard_map/ppermute | solution.py:221
  48.8 9.4 %collective-permute-start.14 = (bf16[32,3584]{1,0:T(8,128)(2,1)S(1)}, bf16[32,3584]{1,0:T(8,128)(2,1)S(1)}, u32[]{:S(2)}, u32[]{:S(2)}) collective-permute-start(bf16[32,3584]{1,0:T(8,128)(2,1)S(1)} %shard_map.117), channel_id=1, source_target_pairs={{0,2},{1,3},{2,0},{3,1},{4,6},{5,7},{6,4},{7,5},{8,10},{9,11},{10,... | collective-permute-start | bytes 688136 | tf_op jit(solution)/shard_map/ppermute | solution.py:221

commit v5 on v4

--- a/solution.py
+++ b/solution.py
@@ -150,7 +150,11 @@
     return [slice(start, start + tile) for start in range(0, width, tile)]
 
 
-def product_kernel(pieces, groups, spans, after, narrow, *refs):
+def shifted(cols, first):
+    return slice(first + cols.start, first + cols.stop)
+
+
+def product_kernel(pieces, groups, chunk, spans, after, narrow, *refs):
     tokens, refs = refs[:pieces], refs[pieces:]
     matrices = []
     for count in groups:
@@ -162,21 +166,20 @@
     if pieces > 1:
         place_rows(tokens, outs[0], narrow)
         tokens, outs = outs[:1], outs[1:]
-    first = 0
-    for group in matrices:
-        width = group[0].shape[1]
+    begin, width = chunk
+    for place, group in enumerate(matrices):
         for cols in column_tiles(width):
             total, depth = None, 0
             for matrix in group:
                 rows = tokens[0][:, depth : depth + matrix.shape[0]]
-                term = jnp.dot(rows, matrix[:, cols], preferred_element_type=jnp.float32)
+                part = matrix[:, begin + cols.start : begin + cols.stop]
+                term = jnp.dot(rows, part, preferred_element_type=jnp.float32)
                 total = term if total is None else total + term
                 depth += matrix.shape[0]
-            row = 0
+            cols, row = shifted(cols, place * width), 0
             for out in outs:
-                out[:, first + cols.start : first + cols.stop] = total[row : row + out.shape[0]].astype(out.dtype)
+                out[:, cols] = total[row : row + out.shape[0]].astype(out.dtype)
                 row += out.shape[0]
-        first += width
     for copy in copies:
         copy.wait()
 
@@ -189,10 +192,10 @@
     return sizes + [left]
 
 
-def product(tokens, groups, narrow, after=(), loads=()):
+def product(tokens, groups, chunk, narrow, after=(), loads=()):
     placing = len(tokens) > 1
     total = sum(t.shape[0] for t in tokens)
-    depth, width = tokens[0].shape[1], sum(group[0].shape[1] for group in groups)
+    depth, width = tokens[0].shape[1], chunk[1] * len(groups)
     matrices = [in_vmem(part) for group in groups for part in group]
     sizes = part_sizes(total, narrow)
     found = pl.pallas_call(
@@ -200,6 +203,7 @@
             product_kernel,
             len(tokens),
             [len(group) for group in groups],
+            chunk,
             [span for _, span in loads],
             len(after),
             narrow,
@@ -257,26 +261,23 @@
     return sent, addends(keeps, came, len(keeps) - 1)
 
 
-def own_sum(refs, starts, count, first, cols):
-    return added(refs, starts, count, slice(first + cols.start, first + cols.stop))
-
-
-def target_kernel(starts, live, *refs):
-    terms, act, out = refs[: len(starts)], refs[-2], refs[-1]
-    count, width = out.shape
-    for cols in column_tiles(width):
-        gate = own_sum(terms, starts, count, 0, cols)
-        upper = own_sum(terms, starts, count, width, cols)
-        value = live[:, :1] * (jax.nn.silu(gate) * upper)
-        act[:, cols] = value
-        out[:, cols] = value.astype(out.dtype)
-
-
-def target_end(live, own):
-    arrays, starts = own
-    shape = (live.shape[0], arrays[0].shape[1] // 2)
-    return pl.pallas_call(
-        functools.partial(target_kernel, starts),
+def target_kernel(chunks, starts, live, *refs):
+    act, out = refs[-2:]
+    for (first, width), offsets in zip(chunks, starts):
+        terms, refs = refs[: len(offsets)], refs[len(offsets) :]
+        for cols in column_tiles(width):
+            gate = added(terms, offsets, out.shape[0], cols)
+            upper = added(terms, offsets, out.shape[0], shifted(cols, width))
+            value = live[:, :1] * (jax.nn.silu(gate) * upper)
+            act[:, shifted(cols, first)] = value
+            out[:, shifted(cols, first)] = value.astype(out.dtype)
+
+
+def target_end(live, chunks, owns):
+    arrays = [array for own in owns for array in own[0]]
+    shape = (live.shape[0], sum(width for _, width in chunks))
+    return pl.pallas_call(
+        functools.partial(target_kernel, chunks, [own[1] for own in owns]),
         out_shape=[jax.ShapeDtypeStruct(shape, jnp.float32), jax.ShapeDtypeStruct(shape, jnp.bfloat16)],
         in_specs=[IN_VMEM] * (1 + len(arrays)),
         out_specs=[IN_VMEM] * 2,
@@ -287,7 +288,7 @@
 def source_kernel(starts, live, weight, *refs):
     terms, out = refs[:-1], refs[-1]
     for cols in column_tiles(out.shape[1]):
-        gate = own_sum(terms, starts, out.shape[0], 0, cols)
+        gate = added(terms, starts, out.shape[0], cols)
         out[:, cols] = (live[:, :1] * weight[:, :1]) * jax.nn.silu(gate)
 
 
@@ -305,7 +306,7 @@
 def ratio_kernel(starts, act, gated, *refs):
     terms, out = refs[:-1], refs[-1]
     for cols in column_tiles(out.shape[1]):
-        upper = own_sum(terms, starts, out.shape[0], 0, cols)
+        upper = added(terms, starts, out.shape[0], cols)
         out[:, cols] = (act[:, cols] - gated[:, cols] * upper).astype(out.dtype)
 
 
@@ -320,28 +321,50 @@
     )(act, gated, *arrays)
 
 
+def column_chunks(width):
+    tile = tile_of(width)
+    first = width // tile // 2 * tile
+    return [(0, first), (first, width - first)] if first else [(0, width)]
+
+
 def local(mesh_shape, target_states, source_states, target_gate, target_up, source_gate, source_up, token_ids, lengths, ratio_weight):
     wide, narrow = mesh_shape["wide"], mesh_shape["narrow"]
+    width = target_gate.shape[1]
     gate_top, gate_bottom = halves(source_gate)
-
+    up_top, up_bottom = halves(source_up)
     target_gate = load(halves(target_gate), ())
-    target_pieces = gather_pieces(target_states, "wide", wide, (target_gate[0],))
-    source_pieces = gather_pieces(source_states, "wide", wide)
-    target_up = load(halves(target_up), (target_gate[0], target_pieces[wide // 2]))
-
-    after = (target_up[0], source_pieces[1], source_pieces[wide // 2])
-    _, _, sends, keeps = product(target_pieces, (target_gate, target_up), narrow, after)
-    (gate_top,) = load([gate_top], (sends[0],))
-    sent, target = finish(sends, keeps, narrow, (gate_top, source_pieces[-1]))
-    (gate_bottom,) = load([gate_bottom], (sent,))
-
-    source_up, rows, gate_sends, gate_keeps = product(
-        source_pieces, ((gate_top, gate_bottom),), narrow, (sent,), halves(source_up)
+    live, weight = look_up(token_ids, lengths, ratio_weight, (target_gate[0],))
+    first = (live,)
+    target_pieces = gather_pieces(target_states, "wide", wide, first)
+    source_pieces = gather_pieces(source_states, "wide", wide, first)
+    after = (*first, target_pieces[wide // 2], source_pieces[wide // 2])
+    target_up = load(halves(target_up), after)
+
+    groups = (target_gate, target_up)
+    tokens, after = target_pieces, (target_up[0], *source_pieces[1:])
+    chunks, made = column_chunks(width), []
+    for chunk in chunks:
+        loads = [gate_top] if chunk is chunks[-1] else []
+        loaded, tokens, sends, keeps = product(tokens, groups, chunk, narrow, after, loads)
+        made.append((sends, keeps))
+        after = (sends[0],)
+    (gate_top,) = loaded
+    owns = []
+    for sends, keeps in made:
+        sent, own = finish(sends, keeps, narrow, after)
+        if not owns:
+            gate_bottom, up_top = load([gate_bottom, up_top], (sent,))
+        owns.append(own)
+        after = (up_top, own[0][-1])
+
+    groups, after = ((gate_top, gate_bottom),), (sent, gate_bottom)
+    (up_bottom,), rows, gate_sends, gate_keeps = product(
+        source_pieces, groups, (0, width), narrow, after, [up_bottom]
     )
-    _, _, sends, keeps = product(rows, (source_up,), narrow, (gate_sends[0],))
-    sent, source_g = finish(gate_sends, gate_keeps, narrow, (sends[0], target[0][-1]))
-    live, weight = look_up(token_ids, lengths, ratio_weight, (sent,))
-    act, target_out = target_end(live, target)
+    groups, after = ((up_top, up_bottom),), (gate_sends[0],)
+    _, _, sends, keeps = product(rows, groups, (0, width), narrow, after)
+    sent, source_g = finish(gate_sends, gate_keeps, narrow, (sends[0], owns[-1][0][-1]))
+    act, target_out = target_end(live, chunks, owns)
     _, source_u = finish(sends, keeps, narrow, (act,))
     gated = source_middle(live, weight, source_g)
     ratio_out = ratio_end(act, gated, source_u)

time: 59.3 us -> 61.2 us (1.032)
  starting transfers between devices: 13.7 us -> 15.6 us
  Pallas kernels: 33.1 us -> 32 us
  local copies, waits for them, and re-layouts: 0.01 us -> 0.73 us
    ppermute x9 -> x12, waiting for transfers between devices: 7.47 us -> 10.2 us  [exchange(): lax.ppermute(array, 'narrow', [(i, i ^ 1 << step) for i in range(size)])]
    ppermute x6, waiting for transfers between devices: 3.96 us -> 1.64 us  [gather_pieces(): pieces.append(lax.ppermute(piece, axis, pairs))]
    ppermute x9 -> x12, starting transfers between devices: 5.33 us -> 7.43 us  [exchange(): lax.ppermute(array, 'narrow', [(i, i ^ 1 << step) for i in range(size)])]
    pallas_call x4 -> x3, Pallas kernels: 16.6 us -> 15.6 us  [load(): pl.pallas_call(functools.partial(load_kernel, [span for _, span in loads]...]
    unnamed x4 -> x12, local copies, waits for them, and re-layouts: 0.01 us -> 0.73 us
    pallas_call x3 -> x4, Pallas kernels: 12.2 us -> 12.2 us  [product(): pl.pallas_call(functools.partial(product_kernel, len(tokens), [len(group)...]
  transfers between devices with their start and end apart: 15 -> 18, of which waited for: 4 -> 6; matrix products, arithmetic and copies ran while one was open for 0% -> 0% of each run, Pallas kernels for 47% -> 48%
where the time goes in v5:
time: 61.2 us; the launch traced here: 61 us
  Pallas kernels  32 us (52%)
  starting transfers between devices  15.6 us (25%)
  waiting for transfers between devices  11.8 us (19%)
  between operations  0.84 us (1%)
  local copies, waits for them, and re-layouts  0.73 us (1%)
    pallas_call x3, Pallas kernels, load(): pl.pallas_call(functools.partial(load_kernel, [span for _, span in loads]...  15.6 us
    pallas_call x4, Pallas kernels, product(): pl.pallas_call(functools.partial(product_kernel, len(tokens), [len(group)...  12.2 us
    ppermute x12, waiting for transfers between devices, exchange(): lax.ppermute(array, 'narrow', [(i, i ^ 1 << step) for i in range(size)])  10.2 us
    ppermute x6, starting transfers between devices, gather_pieces(): pieces.append(lax.ppermute(piece, axis, pairs))  8.16 us
    ppermute x12, starting transfers between devices, exchange(): lax.ppermute(array, 'narrow', [(i, i ^ 1 << step) for i in range(size)])  7.43 us
    pallas_call x1, Pallas kernels, look_up(): pl.pallas_call(functools.partial(look_up_kernel, ids.shape[0] // lengths....  2.16 us
    ppermute x6, waiting for transfers between devices, gather_pieces(): pieces.append(lax.ppermute(piece, axis, pairs))  1.64 us
  transfers between devices with their start and end apart: 18, of which 6 were waited for; matrix products, arithmetic and copies ran while one was open for 0% of the time, Pallas kernels for 48%

profile of v5, /device:TPU:0, one launch (start us, length us, event | category | flops | bytes accessed | tf_op | source)
XLA Modules:
  0.0 61.0 jit_solution(4572941211844666019)
XLA Ops:
  0.6 4.1 %collective-permute-start.1 = (bf16[32,2048]{1,0:T(8,128)(2,1)}, bf16[32,2048]{1,0:T(8,128)(2,1)S(1)}, u32[]{:S(2)}, u32[]{:S(2)}) collective-permute-start(bf16[32,2048]{1,0:T(8,128)(2,1)} %refs_0_.7), channel_id=1, source_target_pairs={{0,8},{4,12},{8,0},{12,4},{1,9},{5,13},{9,1},{13,5},{2,10},{6,14},... | collective-permute-start | bytes 393224 | tf_op jit(solution)/shard_map/ppermute | solution.py:47
  4.7 0.1 collective-permute-start.3
  4.8 1.8 %collective-permute-start = (bf16[32,2048]{1,0:T(8,128)(2,1)}, bf16[32,2048]{1,0:T(8,128)(2,1)S(1)}, u32[]{:S(2)}, u32[]{:S(2)}) collective-permute-start(bf16[32,2048]{1,0:T(8,128)(2,1)} %refs_0_.7), channel_id=1, source_target_pairs={{0,4},{4,0},{8,12},{12,8},{1,5},{5,1},{9,13},{13,9},{2,6},{6,2},{1... | collective-permute-start | bytes 393224 | tf_op jit(solution)/shard_map/ppermute | solution.py:47
  6.6 0.2 collective-permute-start.4
  6.8 5.2 %shard_map.104 = (bf16[1024,3584]{1,0:T(8,128)(2,1)S(1)}, bf16[1024,3584]{1,0:T(8,128)(2,1)S(1)}) custom-call(bf16[2048,3584]{1,0:T(8,128)(2,1)} %refs_1_.3, bf16[2048,3584]{1,0:T(8,128)(2,1)} %refs_1_.3), custom_call_target="tpu_custom_call" | custom-call | tf_op jit(solution)/shard_map/pallas_call | solution.py:131
  12.0 2.2 %shard_map.105 = (f32[32,128]{1,0:T(8,128)S(1)}, f32[32,128]{1,0:T(8,128)S(1)}) custom-call(s32[32]{0:T(128)} %ids.1, s32[2]{0:T(128)} %lengths.1, f32[1002,128]{1,0:T(8,128)} %bitcast.1, bf16[1024,3584]{1,0:T(8,128)(2,1)S(1)} %get-tuple-element.32.refs_0_.refs_4_.refs_1_), custom_call_target="tpu_custom_call" | custom-call | tf_op jit(solution)/shard_map/pallas_call | solution.py:105
  14.2 0.8 %collective-permute-done.1.piece.refs_3_.refs_2_ = bf16[32,2048]{1,0:T(8,128)(2,1)S(1)} collective-permute-done((bf16[32,2048]{1,0:T(8,128)(2,1)}, bf16[32,2048]{1,0:T(8,128)(2,1)S(1)}, u32[]{:S(2)}, u32[]{:S(2)}) %collective-permute-start.1) | collective-permute-done | bytes 131104 | tf_op jit(solution)/shard_map/ppermute | solution.py:47
  15.0 1.1 %collective-permute-start.2 = (bf16[32,2048]{1,0:T(8,128)(2,1)S(1)}, bf16[32,2048]{1,0:T(8,128)(2,1)S(1)}, u32[]{:S(2)}, u32[]{:S(2)}) collective-permute-start(bf16[32,2048]{1,0:T(8,128)(2,1)S(1)} %shard_map.106), channel_id=1, source_target_pairs={{0,4},{4,0},{8,12},{12,8},{1,5},{5,1},{9,13},{13,9},{2,6},{6,2},{1... | collective-permute-start | bytes 393224 | tf_op jit(solution)/shard_map/ppermute | solution.py:47
  16.1 0.8 %collective-permute-done.3.refs_4_.piece.refs_10_.refs_2_ = bf16[32,2048]{1,0:T(8,128)(2,1)S(1)} collective-permute-done((bf16[32,2048]{1,0:T(8,128)(2,1)}, bf16[32,2048]{1,0:T(8,128)(2,1)S(1)}, u32[]{:S(2)}, u32[]{:S(2)}) %collective-permute-start.3) | collective-permute-done | bytes 131104 | tf_op jit(solution)/shard_map/ppermute | solution.py:47
  17.0 0.0 copy-start.2
  17.0 0.8 %collective-permute-start.5 = (bf16[32,2048]{1,0:T(8,128)(2,1)S(1)}, bf16[32,2048]{1,0:T(8,128)(2,1)S(1)}, u32[]{:S(2)}, u32[]{:S(2)}) collective-permute-start(bf16[32,2048]{1,0:T(8,128)(2,1)S(1)} %shard_map.108), channel_id=1, source_target_pairs={{0,4},{4,0},{8,12},{12,8},{1,5},{5,1},{9,13},{13,9},{2,6},{6,2},{1... | collective-permute-start | bytes 393224 | tf_op jit(solution)/shard_map/ppermute | solution.py:47
  17.8 5.2 %shard_map.107 = (bf16[1024,3584]{1,0:T(8,128)(2,1)S(1)}, bf16[1024,3584]{1,0:T(8,128)(2,1)S(1)}) custom-call(bf16[2048,3584]{1,0:T(8,128)(2,1)} %refs_1_.4, bf16[2048,3584]{1,0:T(8,128)(2,1)} %refs_1_.4, f32[32,128]{1,0:T(8,128)S(1)} %get-tuple-element.33.refs_0_.refs_2_.live, bf16[32,2048]{1,0:T(8,128)(2,1)S(1)} %collective-permute-done.1.piece.refs_3_.refs_2_, ...), custom_call_target="tpu_custom_call" | custom-call | tf_op jit(solution)/shard_map/pallas_call | solution.py:131
  23.0 0.0 collective-permute-done.refs_1_
  23.0 0.0 collective-permute-done.4.refs_9_.refs_1_
  23.0 0.0 collective-permute-done.2.refs_3_
  23.1 0.0 collective-permute-done.5.refs_11_.refs_3_
  23.1 0.0 copy-done.2
  23.1 1.9 %shard_map.109 = (bf16[128,2048]{1,0:T(8,128)(2,1)S(1)}, bf16[32,3072]{1,0:T(8,128)(2,1)S(1)}, bf16[32,3072]{1,0:T(8,128)(2,1)S(1)}, bf16[32,3072]{1,0:T(8,128)(2,1)S(1)}, bf16[32,3072]{1,0:T(8,128)(2,1)S(1)}) custom-call(bf16[32,2048]{1,0:T(8,128)(2,1)S(1)} %copy-done.2, bf16[32,2048]{1,0:T(8,128)(2,1)S(1)} %collective-permute-done.refs_1_, ...), custom_call_target="tpu_custom_call" | custom-call | tf_op jit(solution)/shard_map/pallas_call | solution.py:201
  24.9 0.0 copy-start.4
  24.9 0.1 collective-permute-start.7
  25.0 5.1 %shard_map.110 = (bf16[1024,3584]{1,0:T(8,128)(2,1)S(1)}, bf16[32,4096]{1,0:T(8,128)(2,1)S(1)}, bf16[32,4096]{1,0:T(8,128)(2,1)}, bf16[32,4096]{1,0:T(8,128)(2,1)S(1)}, bf16[32,4096]{1,0:T(8,128)(2,1)S(1)}) custom-call(bf16[128,2048]{1,0:T(8,128)(2,1)S(1)} %get-tuple-element.41.refs_0_, bf16[1024,3584]{1,0:T(8,128)(2,1)S(1)} %get-tuple-element.32.refs_0_.refs_4_.refs_1_, ...), custom_call_target="tpu_custom_call" | custom-call | tf_op jit(solution)/shard_map/pallas_call | solution.py:201
  30.1 0.0 copy-done.4
  30.2 0.0 copy-start
  30.2 0.7 %copy-done = bf16[32,4096]{1,0:T(8,128)(2,1)} copy-done((bf16[32,4096]{1,0:T(8,128)(2,1)}, bf16[32,4096]{1,0:T(8,128)(2,1)S(1)}, u32[]{:S(2)}) %copy-start) | copy-done | bytes 262168
  30.9 0.5 collective-permute-start.10
  31.4 0.0 collective-permute-done.7.refs_1_
  31.4 1.6 %collective-permute-start.8 = (bf16[32,3072]{1,0:T(8,128)(2,1)S(1)}, bf16[32,3072]{1,0:T(8,128)(2,1)S(1)}, u32[]{:S(2)}, u32[]{:S(2)}) collective-permute-start(bf16[32,3072]{1,0:T(8,128)(2,1)S(1)} %shard_map.111.refs_2_), channel_id=1, source_target_pairs={{0,2},{1,3},{2,0},{3,1},{4,6},{5,7},{6,4},{7,5},{8,10},{9,11},{10,... | collective-permute-start | bytes 589832 | tf_op jit(solution)/shard_map/ppermute | solution.py:225
  33.0 5.2 %shard_map.112 = (bf16[1024,3584]{1,0:T(8,128)(2,1)S(1)}, bf16[1024,3584]{1,0:T(8,128)(2,1)S(1)}) custom-call(bf16[2048,3584]{1,0:T(8,128)(2,1)} %refs_0_.8, bf16[2048,3584]{1,0:T(8,128)(2,1)} %refs_6_.1, bf16[32,3072]{1,0:T(8,128)(2,1)S(1)} %shard_map.111.refs_2_), custom_call_target="tpu_custom_call" | custom-call | tf_op jit(solution)/shard_map/pallas_call | solution.py:131
  38.2 0.0 copy-start.3
  38.2 0.0 collective-permute-done.10.refs_1_
  38.2 0.1 collective-permute-done.8.refs_3_.refs_2_
  38.3 0.1 shard_map.113.refs_7_
  38.4 1.6 %collective-permute-start.11 = (bf16[32,4096]{1,0:T(8,128)(2,1)S(1)}, bf16[32,4096]{1,0:T(8,128)(2,1)S(1)}, u32[]{:S(2)}, u32[]{:S(2)}) collective-permute-start(bf16[32,4096]{1,0:T(8,128)(2,1)S(1)} %shard_map.113.refs_7_), channel_id=1, source_target_pairs={{0,2},{1,3},{2,0},{3,1},{4,6},{5,7},{6,4},{7,5},{8,10},{9,11},{10,... | collective-permute-start | bytes 786440 | tf_op jit(solution)/shard_map/ppermute | solution.py:225
  39.9 0.0 collective-permute-start.9
  39.9 0.0 copy-done.3
  39.9 3.1 %shard_map.115 = (bf16[1024,3584]{1,0:T(8,128)(2,1)S(1)}, bf16[128,2048]{1,0:T(8,128)(2,1)S(1)}, bf16[32,3584]{1,0:T(8,128)(2,1)S(1)}, bf16[32,3584]{1,0:T(8,128...) custom-call(bf16[32,2048]{1,0:T(8,128)(2,1)S(1)} %copy-done.3, ...), custom_call_target="tpu_custom_call" | custom-call | tf_op jit(solution)/shard_map/pallas_call | solution.py:201
  43.1 0.6 collective-permute-start.13
  43.7 0.0 copy-start.5
  43.7 0.0 copy-start.1
  43.7 2.1 %shard_map.116 = (bf16[32,3584]{1,0:T(8,128)(2,1)S(1)}, bf16[32,3584]{1,0:T(8,128)(2,1)S(1)}, bf16[32,3584]{1,0:T(8,128)(2,1)S(1)}, bf16[32,3584]{1,0:T(8,128)(2,1)S(1)}) custom-call(bf16[128,2048]{1,0:T(8,128)(2,1)S(1)} %get-tuple-element.56.refs_0_, bf16[1024,3584]{1,0:T(8,128)(2,1)S(1)} %get-tuple-element.46.refs_2_.refs_1_, ...), custom_call_target="tpu_custom_call" | custom-call | tf_op jit(solution)/shard_map/pallas_call | solution.py:201
  45.7 0.1 collective-permute-start.16
  45.9 0.0 copy-done.5
  45.9 0.5 collective-permute-start.6
  46.3 0.0 collective-permute-done.13.refs_1_
  46.3 0.1 collective-permute-start.12
  46.4 0.0 collective-permute-done.11.refs_5_.refs_3_
  46.4 0.4 collective-permute-start.15
  46.8 0.1 shard_map.117
  46.9 0.7 %collective-permute-done.6.refs_1_ = bf16[32,3072]{1,0:T(8,128)(2,1)S(1)} collective-permute-done((bf16[32,3072]{1,0:T(8,128)(2,1)S(1)}, bf16[32,3072]{1,0:T(8,128)(2,1)S(1)}, u32[]{:S(2)}, u32[]{:S(2)}) %collective-permute-start.6) | collective-permute-done | bytes 196640 | tf_op jit(solution)/shard_map/ppermute | solution.py:225
  47.6 0.5 collective-permute-start.14
  48.1 0.0 collective-permute-done.9.refs_4_
  48.1 0.0 copy-done.1
  48.1 0.9 %shard_map.114 = (f32[32,3584]{1,0:T(8,128)S(1)}, bf16[32,3584]{1,0:T(8,128)(2,1)}) custom-call(f32[32,128]{1,0:T(8,128)S(1)} %get-tuple-element.33.refs_0_.refs_2_.live, bf16[32,3072]{1,0:T(8,128)(2,1)S(1)} %get-tuple-element.37.refs_0_, bf16[32,3072]{1,0:T(8,128)(2,1)S(1)} %collective-permute-done.6.refs_1_, ...), custom_call_target="tpu_custom_call" | custom-call | tf_op jit(solution)/shard_map/pallas_call | solution.py:279
  49.1 0.0 collective-permute-done.16.refs_1_
  49.1 0.1 shard_map.119
  49.1 1.6 %collective-permute-start.17 = (bf16[32,3584]{1,0:T(8,128)(2,1)S(1)}, bf16[32,3584]{1,0:T(8,128)(2,1)S(1)}, u32[]{:S(2)}, u32[]{:S(2)}) collective-permute-start(bf16[32,3584]{1,0:T(8,128)(2,1)S(1)} %shard_map.119), channel_id=1, source_target_pairs={{0,2},{1,3},{2,0},{3,1},{4,6},{5,7},{6,4},{7,5},{8,10},{9,11},{10,... | collective-permute-start | bytes 688136 | tf_op jit(solution)/shard_map/ppermute | solution.py:225
  50.7 0.0 collective-permute-done.12.refs_1_
  50.7 5.4 %collective-permute-done.14.refs_2_ = bf16[32,3584]{1,0:T(8,128)(2,1)S(1)} collective-permute-done((bf16[32,3584]{1,0:T(8,128)(2,1)S(1)}, bf16[32,3584]{1,0:T(8,128)(2,1)S(1)}, u32[]{:S(2)}, u32[]{:S(2)}) %collective-permute-start.14) | collective-permute-done | bytes 229408 | tf_op jit(solution)/shard_map/ppermute | solution.py:225
  56.0 0.1 shard_map.118.gated
  56.2 0.0 collective-permute-done.15.refs_1_
  56.2 4.0 %collective-permute-done.17.refs_2_ = bf16[32,3584]{1,0:T(8,128)(2,1)S(1)} collective-permute-done((bf16[32,3584]{1,0:T(8,128)(2,1)S(1)}, bf16[32,3584]{1,0:T(8,128)(2,1)S(1)}, u32[]{:S(2)}, u32[]{:S(2)}) %collective-permute-start.17) | collective-permute-done | bytes 229408 | tf_op jit(solution)/shard_map/ppermute | solution.py:225
  60.2 0.8 %shard_map.120 = bf16[32,3584]{1,0:T(8,128)(2,1)} custom-call(f32[32,3584]{1,0:T(8,128)S(1)} %get-tuple-element.48.refs_2_.act, f32[32,3584]{1,0:T(8,128)S(1)} %shard_map.118.gated, bf16[32,3584]{1,0:T(8,128)(2,1)S(1)} %get-tuple-element.59.refs_0_, bf16[32,3584]{1,0:T(8,128)(2,1)S(1)} %collective-permute-done.15.refs_1_, ...), custom_call_target="tpu_custom_call" | custom-call | tf_op jit(solution)/shard_map/pallas_call | solution.py:315
  (3 shorter events, 0.1 us)
Async XLA Ops:
  0.6 14.4 %collective-permute-start.1 = (bf16[32,2048]{1,0:T(8,128)(2,1)}, bf16[32,2048]{1,0:T(8,128)(2,1)S(1)}, u32[]{:S(2)}, u32[]{:S(2)}) collective-permute-start(bf16[32,2048]{1,0:T(8,128)(2,1)} %refs_0_.7), channel_id=1, source_target_pairs={{0,8},{4,12},{8,0},{12,4},{1,9},{5,13},{9,1},{13,5},{2,10},{6,14},... | collective-permute-start | bytes 393224 | tf_op jit(solution)/shard_map/ppermute | solution.py:47
  4.7 12.2 %collective-permute-start.3 = (bf16[32,2048]{1,0:T(8,128)(2,1)}, bf16[32,2048]{1,0:T(8,128)(2,1)S(1)}, u32[]{:S(2)}, u32[]{:S(2)}) collective-permute-start(bf16[32,2048]{1,0:T(8,128)(2,1)} %refs_0_.9), channel_id=1, source_target_pairs={{0,8},{4,12},{8,0},{12,4},{1,9},{5,13},{9,1},{13,5},{2,10},{6,14},... | collective-permute-start | bytes 393224 | tf_op jit(solution)/shard_map/ppermute | solution.py:47
  4.8 18.2 %collective-permute-start = (bf16[32,2048]{1,0:T(8,128)(2,1)}, bf16[32,2048]{1,0:T(8,128)(2,1)S(1)}, u32[]{:S(2)}, u32[]{:S(2)}) collective-permute-start(bf16[32,2048]{1,0:T(8,128)(2,1)} %refs_0_.7), channel_id=1, source_target_pairs={{0,4},{4,0},{8,12},{12,8},{1,5},{5,1},{9,13},{13,9},{2,6},{6,2},{1... | collective-permute-start | bytes 393224 | tf_op jit(solution)/shard_map/ppermute | solution.py:47
  6.6 16.4 %collective-permute-start.4 = (bf16[32,2048]{1,0:T(8,128)(2,1)}, bf16[32,2048]{1,0:T(8,128)(2,1)S(1)}, u32[]{:S(2)}, u32[]{:S(2)}) collective-permute-start(bf16[32,2048]{1,0:T(8,128)(2,1)} %refs_0_.9), channel_id=1, source_target_pairs={{0,4},{4,0},{8,12},{12,8},{1,5},{5,1},{9,13},{13,9},{2,6},{6,2},{1... | collective-permute-start | bytes 393224 | tf_op jit(solution)/shard_map/ppermute | solution.py:47
  15.0 8.0 %collective-permute-start.2 = (bf16[32,2048]{1,0:T(8,128)(2,1)S(1)}, bf16[32,2048]{1,0:T(8,128)(2,1)S(1)}, u32[]{:S(2)}, u32[]{:S(2)}) collective-permute-start(bf16[32,2048]{1,0:T(8,128)(2,1)S(1)} %shard_map.106), channel_id=1, source_target_pairs={{0,4},{4,0},{8,12},{12,8},{1,5},{5,1},{9,13},{13,9},{2,6},{6,2},{1... | collective-permute-start | bytes 393224 | tf_op jit(solution)/shard_map/ppermute | solution.py:47
  17.0 6.1 %copy-start.2 = (bf16[32,2048]{1,0:T(8,128)(2,1)S(1)}, bf16[32,2048]{1,0:T(8,128)(2,1)}, u32[]{:S(2)}) copy-start(bf16[32,2048]{1,0:T(8,128)(2,1)} %refs_0_.7) | copy-start | bytes 393220
  17.0 6.1 %collective-permute-start.5 = (bf16[32,2048]{1,0:T(8,128)(2,1)S(1)}, bf16[32,2048]{1,0:T(8,128)(2,1)S(1)}, u32[]{:S(2)}, u32[]{:S(2)}) collective-permute-start(bf16[32,2048]{1,0:T(8,128)(2,1)S(1)} %shard_map.108), channel_id=1, source_target_pairs={{0,4},{4,0},{8,12},{12,8},{1,5},{5,1},{9,13},{13,9},{2,6},{6,2},{1... | collective-permute-start | bytes 393224 | tf_op jit(solution)/shard_map/ppermute | solution.py:47
  24.9 5.2 %copy-start.4 = (bf16[32,3072]{1,0:T(8,128)(2,1)}, bf16[32,3072]{1,0:T(8,128)(2,1)S(1)}, u32[]{:S(2)}) copy-start(bf16[32,3072]{1,0:T(8,128)(2,1)S(1)} %get-tuple-element.38) | copy-start | bytes 589828
  24.9 6.4 %collective-permute-start.7 = (bf16[32,3072]{1,0:T(8,128)(2,1)S(1)}, bf16[32,3072]{1,0:T(8,128)(2,1)S(1)}, u32[]{:S(2)}, u32[]{:S(2)}) collective-permute-start(bf16[32,3072]{1,0:T(8,128)(2,1)S(1)} %get-tuple-element.40.refs_6_), channel_id=1, source_target_pairs={{0,1},{1,0},{2,3},{3,2},{4,5},{5,4},{6,7},{7,6},{8,9},{9,8},{10,11... | collective-permute-start | bytes 589832 | tf_op jit(solution)/shard_map/ppermute | solution.py:225
  30.2 0.7 %copy-start = (bf16[32,4096]{1,0:T(8,128)(2,1)}, bf16[32,4096]{1,0:T(8,128)(2,1)S(1)}, u32[]{:S(2)}) copy-start(bf16[32,4096]{1,0:T(8,128)(2,1)S(1)} %get-tuple-element.43.refs_3_) | copy-start | bytes 786436
  30.9 7.3 %collective-permute-start.10 = (bf16[32,4096]{1,0:T(8,128)(2,1)S(1)}, bf16[32,4096]{1,0:T(8,128)(2,1)S(1)}, u32[]{:S(2)}, u32[]{:S(2)}) collective-permute-start(bf16[32,4096]{1,0:T(8,128)(2,1)S(1)} %get-tuple-element.42.refs_2_), channel_id=1, source_target_pairs={{0,1},{1,0},{2,3},{3,2},{4,5},{5,4},{6,7},{7,6},{8,9},{9,8},{10,11... | collective-permute-start | bytes 786440 | tf_op jit(solution)/shard_map/ppermute | solution.py:225
  31.4 6.9 %collective-permute-start.8 = (bf16[32,3072]{1,0:T(8,128)(2,1)S(1)}, bf16[32,3072]{1,0:T(8,128)(2,1)S(1)}, u32[]{:S(2)}, u32[]{:S(2)}) collective-permute-start(bf16[32,3072]{1,0:T(8,128)(2,1)S(1)} %shard_map.111.refs_2_), channel_id=1, source_target_pairs={{0,2},{1,3},{2,0},{3,1},{4,6},{5,7},{6,4},{7,5},{8,10},{9,11},{10,... | collective-permute-start | bytes 589832 | tf_op jit(solution)/shard_map/ppermute | solution.py:225
  38.2 1.8 %copy-start.3 = (bf16[32,2048]{1,0:T(8,128)(2,1)S(1)}, bf16[32,2048]{1,0:T(8,128)(2,1)}, u32[]{:S(2)}) copy-start(bf16[32,2048]{1,0:T(8,128)(2,1)} %refs_0_.9) | copy-start | bytes 393220
  38.4 8.1 %collective-permute-start.11 = (bf16[32,4096]{1,0:T(8,128)(2,1)S(1)}, bf16[32,4096]{1,0:T(8,128)(2,1)S(1)}, u32[]{:S(2)}, u32[]{:S(2)}) collective-permute-start(bf16[32,4096]{1,0:T(8,128)(2,1)S(1)} %shard_map.113.refs_7_), channel_id=1, source_target_pairs={{0,2},{1,3},{2,0},{3,1},{4,6},{5,7},{6,4},{7,5},{8,10},{9,11},{10,... | collective-permute-start | bytes 786440 | tf_op jit(solution)/shard_map/ppermute | solution.py:225
  39.9 8.2 %collective-permute-start.9 = (bf16[32,4096]{1,0:T(8,128)(2,1)}, bf16[32,4096]{1,0:T(8,128)(2,1)S(1)}, u32[]{:S(2)}, u32[]{:S(2)}) collective-permute-start(bf16[32,4096]{1,0:T(8,128)(2,1)} %get-tuple-element.44), channel_id=1, source_target_pairs={{0,1},{1,0},{2,3},{3,2},{4,5},{5,4},{6,7},{7,6},{8,9},{9,8},{10,11... | collective-permute-start | bytes 786440 | tf_op jit(solution)/shard_map/ppermute | solution.py:225
  43.1 3.2 %collective-permute-start.13 = (bf16[32,3584]{1,0:T(8,128)(2,1)S(1)}, bf16[32,3584]{1,0:T(8,128)(2,1)S(1)}, u32[]{:S(2)}, u32[]{:S(2)}) collective-permute-start(bf16[32,3584]{1,0:T(8,128)(2,1)S(1)} %get-tuple-element.55.refs_3_), channel_id=1, source_target_pairs={{0,1},{1,0},{2,3},{3,2},{4,5},{5,4},{6,7},{7,6},{8,9},{9,8},{10,11... | collective-permute-start | bytes 688136 | tf_op jit(solution)/shard_map/ppermute | solution.py:225
  43.7 2.2 %copy-start.5 = (bf16[32,3072]{1,0:T(8,128)(2,1)S(1)}, bf16[32,3072]{1,0:T(8,128)(2,1)}, u32[]{:S(2)}) copy-start(bf16[32,3072]{1,0:T(8,128)(2,1)} %copy-done.4) | copy-start | bytes 589828
  43.7 4.5 %copy-start.1 = (bf16[32,4096]{1,0:T(8,128)(2,1)S(1)}, bf16[32,4096]{1,0:T(8,128)(2,1)}, u32[]{:S(2)}) copy-start(bf16[32,4096]{1,0:T(8,128)(2,1)} %copy-done) | copy-start | bytes 786436
  45.7 3.3 %collective-permute-start.16 = (bf16[32,3584]{1,0:T(8,128)(2,1)S(1)}, bf16[32,3584]{1,0:T(8,128)(2,1)S(1)}, u32[]{:S(2)}, u32[]{:S(2)}) collective-permute-start(bf16[32,3584]{1,0:T(8,128)(2,1)S(1)} %get-tuple-element.58.refs_2_), channel_id=1, source_target_pairs={{0,1},{1,0},{2,3},{3,2},{4,5},{5,4},{6,7},{7,6},{8,9},{9,8},{10,11... | collective-permute-start | bytes 688136 | tf_op jit(solution)/shard_map/ppermute | solution.py:225
  45.9 1.7 %collective-permute-start.6 = (bf16[32,3072]{1,0:T(8,128)(2,1)S(1)}, bf16[32,3072]{1,0:T(8,128)(2,1)S(1)}, u32[]{:S(2)}, u32[]{:S(2)}) collective-permute-start(bf16[32,3072]{1,0:T(8,128)(2,1)S(1)} %copy-done.5), channel_id=1, source_target_pairs={{0,1},{1,0},{2,3},{3,2},{4,5},{5,4},{6,7},{7,6},{8,9},{9,8},{10,11... | collective-permute-start | bytes 589832 | tf_op jit(solution)/shard_map/ppermute | solution.py:225
  46.3 4.3 %collective-permute-start.12 = (bf16[32,3584]{1,0:T(8,128)(2,1)S(1)}, bf16[32,3584]{1,0:T(8,128)(2,1)S(1)}, u32[]{:S(2)}, u32[]{:S(2)}) collective-permute-start(bf16[32,3584]{1,0:T(8,128)(2,1)S(1)} %get-tuple-element.53), channel_id=1, source_target_pairs={{0,1},{1,0},{2,3},{3,2},{4,5},{5,4},{6,7},{7,6},{8,9},{9,8},{10,11... | collective-permute-start | bytes 688136 | tf_op jit(solution)/shard_map/ppermute | solution.py:225
  46.4 9.8 %collective-permute-start.15 = (bf16[32,3584]{1,0:T(8,128)(2,1)S(1)}, bf16[32,3584]{1,0:T(8,128)(2,1)S(1)}, u32[]{:S(2)}, u32[]{:S(2)}) collective-permute-start(bf16[32,3584]{1,0:T(8,128)(2,1)S(1)} %get-tuple-element.60), channel_id=1, source_target_pairs={{0,1},{1,0},{2,3},{3,2},{4,5},{5,4},{6,7},{7,6},{8,9},{9,8},{10,11... | collective-permute-start | bytes 688136 | tf_op jit(solution)/shard_map/ppermute | solution.py:225
  47.6 8.4 %collective-permute-start.14 = (bf16[32,3584]{1,0:T(8,128)(2,1)S(1)}, bf16[32,3584]{1,0:T(8,128)(2,1)S(1)}, u32[]{:S(2)}, u32[]{:S(2)}) collective-permute-start(bf16[32,3584]{1,0:T(8,128)(2,1)S(1)} %shard_map.117), channel_id=1, source_target_pairs={{0,2},{1,3},{2,0},{3,1},{4,6},{5,7},{6,4},{7,5},{8,10},{9,11},{10,... | collective-permute-start | bytes 688136 | tf_op jit(solution)/shard_map/ppermute | solution.py:225
  49.1 11.1 %collective-permute-start.17 = (bf16[32,3584]{1,0:T(8,128)(2,1)S(1)}, bf16[32,3584]{1,0:T(8,128)(2,1)S(1)}, u32[]{:S(2)}, u32[]{:S(2)}) collective-permute-start(bf16[32,3584]{1,0:T(8,128)(2,1)S(1)} %shard_map.119), channel_id=1, source_target_pairs={{0,2},{1,3},{2,0},{3,1},{4,6},{5,7},{6,4},{7,5},{8,10},{9,11},{10,... | collective-permute-start | bytes 688136 | tf_op jit(solution)/shard_map/ppermute | solution.py:225

commit v6 on v4

v6 whole, which is shorter than its diff:
```python
import functools
import math

import jax
import jax.numpy as jnp
from jax import lax
from jax.experimental import pallas as pl
from jax.experimental.pallas import tpu as pltpu
from jax.sharding import PartitionSpec as P

IN_VMEM = pl.BlockSpec(memory_space=pltpu.VMEM)
IN_SMEM = pl.BlockSpec(memory_space=pltpu.SMEM)
ANYWHERE = pl.BlockSpec(memory_space=pl.ANY)
LANES = 128


def in_hbm(array):
    return pltpu.with_memory_space_constraint(array, pltpu.HBM)


def in_vmem(array):
    return pltpu.with_memory_space_constraint(array, pltpu.VMEM)


def gather_pieces(piece, axis, size, relayed):
    pieces = [piece]
    for offset in range(1, size):
        low = offset & -offset if relayed else offset
        pairs = [(i, i ^ low) for i in range(size)]
        pieces.append(lax.ppermute(pieces[offset ^ low], axis, pairs))
    return pieces


def halving_order(size):
    bits = size.bit_length() - 1
    reverse = [sum(((p >> b) & 1) << (bits - 1 - b) for b in range(bits)) for p in range(size)]
    return reverse[::-1]


def place_rows(pieces, rows, narrow):
    me_wide, me_narrow = lax.axis_index("wide"), lax.axis_index("narrow")
    piece_rows = pieces[0].shape[0]
    block_rows = piece_rows * len(pieces) // narrow
    size = math.gcd(piece_rows, block_rows)
    for offset, piece in enumerate(pieces):
        for start in range(0, piece_rows, size):
            row = (me_wide ^ offset) * piece_rows + start
            block = (row // block_rows) ^ me_narrow
            place = sum(
                jnp.where(block == known, position, 0)
                for position, known in enumerate(halving_order(narrow))
            )
            spot = pl.multiple_of(place * block_rows + row % block_rows, size)
            rows[pl.ds(spot, size), :] = piece[start : start + size, :]


def start_loads(sources, spans, dests, sems):
    copies = []
    for i, (source, (start, size)) in enumerate(zip(sources, spans)):
        copies.append(pltpu.make_async_copy(source.at[pl.ds(start, size), :], dests[i], sems.at[i]))
        copies[-1].start()
    return copies


def look_up_kernel(slots, ids, lengths, table, *refs):
    live, weight, entries, picked, sem = refs[-5:]
    lookup = pltpu.make_async_copy(table, entries, sem)
    lookup.start()
    for i in range(lengths.shape[0]):
        slot = lax.broadcasted_iota(jnp.int32, (slots, LANES), 0)
        live[i * slots : (i + 1) * slots, :] = (slot < lengths[i]).astype(jnp.float32)
    lookup.wait()

    def pick(i, carry):
        entry = ids[i]
        lane = lax.broadcasted_iota(jnp.int32, (1, LANES), 1)
        row = entries[pl.ds(entry // LANES, 1), :]
        picked[pl.ds(i, 1), :] = jnp.where(lane == entry % LANES, row, 0.0)
        return carry

    lax.fori_loop(0, ids.shape[0], pick, 0)
    weight[...] = jnp.broadcast_to(jnp.sum(picked[...], axis=1, keepdims=True), weight.shape)


def look_up(ids, lengths, table, after):
    table = table.reshape(-1, LANES)
    flag = jax.ShapeDtypeStruct((ids.shape[0], LANES), jnp.float32)
    return pl.pallas_call(
        functools.partial(look_up_kernel, ids.shape[0] // lengths.shape[0]),
        out_shape=[flag, flag],
        in_specs=[IN_SMEM, IN_SMEM] + [ANYWHERE] * (1 + len(after)),
        out_specs=[IN_VMEM, IN_VMEM],
        scratch_shapes=[
            pltpu.VMEM(table.shape, table.dtype),
            pltpu.VMEM(flag.shape, flag.dtype),
            pltpu.SemaphoreType.DMA,
        ],
        compiler_params=pltpu.CompilerParams(vmem_limit_bytes=3 << 20),
    )(*map(in_hbm, (ids, lengths, table)), *after)


def load_kernel(spans, after, *refs):
    dests = refs[len(spans) + after : -1]
    for copy in start_loads(refs[: len(spans)], spans, dests, refs[-1]):
        copy.wait()


def halves(matrix):
    half = matrix.shape[0] // 2
    return [(matrix, (0, half)), (matrix, (half, half))]


def load(loads, after):
    return pl.pallas_call(
        functools.partial(load_kernel, [span for _, span in loads], len(after)),
        out_shape=[pltpu.VMEM((size, m.shape[1]), m.dtype) for m, (_, size) in loads],
        in_specs=[ANYWHERE] * (len(loads) + len(after)),
        out_specs=[IN_VMEM] * len(loads),
        scratch_shapes=[pltpu.SemaphoreType.DMA((len(loads),))],
        compiler_params=pltpu.CompilerParams(vmem_limit_bytes=1 << 20),
    )(*(in_hbm(m) for m, _ in loads), *after)


def tile_of(cols):
    for tile in (512, 256, 128):
        if cols % tile == 0:
            return tile
    return cols


def column_tiles(width):
    tile = tile_of(width)
    return [slice(start, start + tile) for start in range(0, width, tile)]


def column_chunks(width):
    tile = tile_of(width)
    first = width // tile // 2 * tile
    return [(0, first), (first, width - first)] if first else [(0, width)]


def product_kernel(pieces, parts, spans, after, narrow, blocks, *refs):
    tokens, matrices = refs[:pieces], refs[pieces : pieces + parts]
    refs = refs[pieces + parts :]
    sources, refs = refs[: len(spans)], refs[len(spans) + after :]
    dests, outs, sems = refs[: len(spans)], refs[len(spans) : -1], refs[-1]
    copies = start_loads(sources, spans, dests, sems)
    if pieces > 1:
        place_rows(tokens, outs[0], narrow)
        tokens, outs = outs[:1], outs[1:]
    for cols in column_tiles(matrices[0].shape[1]):
        total, depth = None, 0
        for matrix in matrices:
            rows = tokens[0][:, depth : depth + matrix.shape[0]]
            term = jnp.dot(rows, matrix[:, cols], preferred_element_type=jnp.float32)
            total = term if total is None else total + term
            depth += matrix.shape[0]
        for out, (row, col) in zip(outs, blocks):
            if col <= cols.start and cols.stop <= col + out.shape[1]:
                value = total[row : row + out.shape[0]].astype(out.dtype)
                out[:, cols.start - col : cols.stop - col] = value
    for copy in copies:
        copy.wait()


def part_sizes(total, narrow):
    sizes, left = [], total // 2
    while left > total // narrow:
        left //= 2
        sizes.append(left)
    return sizes + [left]


def product(tokens, matrices, narrow, after=(), loads=()):
    placing = len(tokens) > 1
    total = sum(t.shape[0] for t in tokens)
    depth, width = tokens[0].shape[1], matrices[0].shape[1]
    sizes = part_sizes(total, narrow)
    sent = []
    for k in range(len(sizes)):
        sent += [(k, *chunk) for chunk in (column_chunks(width) if k + 1 < len(sizes) else [(0, width)])]
    blocks = [(sum(sizes[:k]), first) for k, first, _ in sent]
    blocks += [(total // 2 + sum(sizes[:k]), 0) for k in range(len(sizes))]
    shapes = [(sizes[k], count) for k, _, count in sent] + [(size, width) for size in sizes]
    found = pl.pallas_call(
        functools.partial(
            product_kernel, len(tokens), len(matrices), [span for _, span in loads], len(after), narrow, blocks
        ),
        out_shape=[pltpu.VMEM((size, m.shape[1]), m.dtype) for m, (_, size) in loads]
        + [jax.ShapeDtypeStruct((total, depth), tokens[0].dtype)] * placing
        + [jax.ShapeDtypeStruct(shape, jnp.bfloat16) for shape in shapes],
        in_specs=[IN_VMEM] * (len(tokens) + len(matrices)) + [ANYWHERE] * (len(loads) + len(after)),
        out_specs=[IN_VMEM] * (len(loads) + placing + len(shapes)),
        scratch_shapes=[pltpu.SemaphoreType.DMA((max(1, len(loads)),))],
        compiler_params=pltpu.CompilerParams(vmem_limit_bytes=4 << 20),
    )(*tokens, *map(in_vmem, matrices), *(in_hbm(m) for m, _ in loads), *after)
    loaded, found = found[: len(loads)], found[len(loads) :]
    rows, found = (found[:1], found[1:]) if placing else (tokens, found)
    sends = [(array, k, first) for array, (k, first, _) in zip(found, sent)]
    return loaded, rows, sends, found[len(sent) :]


def exchange(array, step, size):
    return lax.ppermute(array, "narrow", [(i, i ^ (1 << step)) for i in range(size)])


def addends(parts, came, k):
    found = [(parts[k], (0, 0))]
    for array, first, behind, col in came:
        if first <= k < behind:
            found.append((array, (sum(part.shape[0] for part in parts[first:k]), col)))
    return [array for array, _ in found], tuple(place for _, place in found)


def added(refs, places, count, cols):
    total = None
    for ref, (row, col) in zip(refs, places):
        if col <= cols.start and cols.stop <= col + ref.shape[1]:
            term = ref[row : row + count, cols.start - col : cols.stop - col].astype(jnp.float32)
            total = term if total is None else total + term
    return total


def next_kernel(places, *refs):
    out = refs[-1]
    for cols in column_tiles(out.shape[1]):
        out[:, cols] = added(refs, places, out.shape[0], cols).astype(out.dtype)


def finish(sends, keeps, narrow, after):
    came = [(exchange(array, 0, narrow), k, k + 1, col) for array, k, col in sends]
    sent = sends[0][0]
    for k in range(len(keeps) - 1):
        arrays, places = addends(keeps, came, k)
        sent = pl.pallas_call(
            functools.partial(next_kernel, places),
            out_shape=jax.ShapeDtypeStruct(keeps[k].shape, jnp.bfloat16),
            in_specs=[IN_VMEM] * len(arrays) + [ANYWHERE] * len(after),
            out_specs=IN_VMEM,
            compiler_params=pltpu.CompilerParams(vmem_limit_bytes=2 << 20),
        )(*arrays, *after)
        came.append((exchange(sent, k + 1, narrow), k + 1, len(keeps), 0))
    return sent, addends(keeps, came, len(keeps) - 1)


def target_kernel(starts, live, *refs):
    act, out = refs[-2:]
    count = len(starts[0])
    for cols in column_tiles(out.shape[1]):
        gate = added(refs[:count], starts[0], out.shape[0], cols)
        upper = added(refs[count:], starts[1], out.shape[0], cols)
        value = live[:, :1] * (jax.nn.silu(gate) * upper)
        act[:, cols] = value
        out[:, cols] = value.astype(out.dtype)


def target_end(live, gate, upper):
    arrays = gate[0] + upper[0]
    shape = gate[0][0].shape
    return pl.pallas_call(
        functools.partial(target_kernel, (gate[1], upper[1])),
        out_shape=[jax.ShapeDtypeStruct(shape, jnp.float32), jax.ShapeDtypeStruct(shape, jnp.bfloat16)],
        in_specs=[IN_VMEM] * (1 + len(arrays)),
        out_specs=[IN_VMEM] * 2,
        compiler_params=pltpu.CompilerParams(vmem_limit_bytes=4 << 20),
    )(live, *arrays)


def source_kernel(starts, live, weight, *refs):
    terms, out = refs[:-1], refs[-1]
    for cols in column_tiles(out.shape[1]):
        gate = added(terms, starts, out.shape[0], cols)
        out[:, cols] = (live[:, :1] * weight[:, :1]) * jax.nn.silu(gate)


def source_middle(live, weight, own):
    arrays, starts = own
    return pl.pallas_call(
        functools.partial(source_kernel, starts),
        out_shape=jax.ShapeDtypeStruct((live.shape[0], arrays[0].shape[1]), jnp.float32),
        in_specs=[IN_VMEM] * (2 + len(arrays)),
        out_specs=IN_VMEM,
        compiler_params=pltpu.CompilerParams(vmem_limit_bytes=4 << 20),
    )(live, weight, *arrays)


def ratio_kernel(starts, act, gated, *refs):
    terms, out = refs[:-1], refs[-1]
    for cols in column_tiles(out.shape[1]):
        upper = added(terms, starts, out.shape[0], cols)
        out[:, cols] = (act[:, cols] - gated[:, cols] * upper).astype(out.dtype)


def ratio_end(act, gated, own):
    arrays, starts = own
    return pl.pallas_call(
        functools.partial(ratio_kernel, starts),
        out_shape=jax.ShapeDtypeStruct(act.shape, jnp.bfloat16),
        in_specs=[IN_VMEM] * (2 + len(arrays)),
        out_specs=IN_VMEM,
        compiler_params=pltpu.CompilerParams(vmem_limit_bytes=4 << 20),
    )(act, gated, *arrays)


def local(mesh_shape, target_states, source_states, target_gate, target_up, source_gate, source_up, token_ids, lengths, ratio_weight):
    wide, narrow = mesh_shape["wide"], mesh_shape["narrow"]
    gate_top, gate_bottom = halves(source_gate)
    up_top, up_bottom = halves(source_up)

    target_pieces = gather_pieces(target_states, "wide", wide, False)
    source_pieces = gather_pieces(source_states, "wide", wide, True)
    target_gate = load(halves(target_gate), ())
    target_up = load(halves(target_up), (target_gate[0],))

    after = (target_up[0], source_pieces[1])
    _, rows, sends, keeps = product(target_pieces, target_gate, narrow, after)
    after = (sends[0][0],)
    (gate_top,), _, up_sends, up_keeps = product(rows, target_up, narrow, after, [gate_top])
    sent, target_g = finish(sends, keeps, narrow, (up_sends[0][0],))
    gate_bottom, up_top = load([gate_bottom, up_top], (sent,))
    sent, target_u = finish(up_sends, up_keeps, narrow, (up_top,))

    (up_bottom,), rows, sends, keeps = product(
        source_pieces, (gate_top, gate_bottom), narrow, (sent,), [up_bottom]
    )
    after = (sends[0][0], target_g[0][-1])
    _, _, up_sends, up_keeps = product(rows, (up_top, up_bottom), narrow, after)
    after = (up_sends[0][0], target_u[0][-1])
    sent, source_g = finish(sends, keeps, narrow, after)
    sent, source_u = finish(up_sends, up_keeps, narrow, (sent,))
    live, weight = look_up(token_ids, lengths, ratio_weight, (sent,))
    act, target_out = target_end(live, target_g, target_u)
    gated = source_middle(live, weight, source_g)
    ratio_out = ratio_end(act, gated, source_u)
    return (target_out, ratio_out)


def solution(mesh):
    placed = (
        P(("groups", "wide"), "narrow"),
        P(("groups", "wide"), "narrow"),
        P("narrow", "wide"),
        P("narrow", "wide"),
        P("narrow", "wide"),
        P("narrow", "wide"),
        P(("groups", "narrow")),
        P(("groups", "narrow")),
        P(),
    )
    mesh_shape = dict(mesh.shape)

    def body(*args):
        return local(mesh_shape, *args)

    return jax.shard_map(
        body,
        mesh=mesh,
        in_specs=placed,
        out_specs=(P(("groups", "narrow"), "wide"), P(("groups", "narrow"), "wide")),
        check_vma=False,
    )
```

time: 59.3 us -> 60.4 us (1.019)
  starting transfers between devices: 13.7 us -> 16.8 us
  waiting for transfers between devices: 11.4 us -> 9.27 us
    ppermute x6, waiting for transfers between devices: 3.96 us -> 1.42 us  [gather_pieces(): pieces.append(lax.ppermute(pieces[offset ^ low], axis, pairs))]
    ppermute x9 -> x16, starting transfers between devices: 5.33 us -> 7.6 us  [exchange(): lax.ppermute(array, 'narrow', [(i, i ^ 1 << step) for i in range(size)])]
    pallas_call x8 -> x9, Pallas kernels: 13.4 us -> 14.5 us  [the longest x4 13.3 us: product(): pl.pallas_call(functools.partial(product_kernel, len(tokens), len(matrice...]
    pallas_call x4 -> x3, Pallas kernels: 16.6 us -> 15.6 us  [load(): pl.pallas_call(functools.partial(load_kernel, [span for _, span in loads]...]
    ppermute x6, starting transfers between devices: 8.36 us -> 9.23 us  [gather_pieces(): pieces.append(lax.ppermute(pieces[offset ^ low], axis, pairs))]
    ppermute x9 -> x16, waiting for transfers between devices: 7.47 us -> 7.85 us  [exchange(): lax.ppermute(array, 'narrow', [(i, i ^ 1 << step) for i in range(size)])]
  transfers between devices with their start and end apart: 15 -> 22, of which waited for: 4 -> 4; matrix products, arithmetic and copies ran while one was open for 0% -> 0% of each run, Pallas kernels for 47% -> 50%
where the time goes in v6:
time: 60.4 us; the launch traced here: 60.1 us
  Pallas kernels  33.2 us (55%)
  starting transfers between devices  16.8 us (28%)
  waiting for transfers between devices  9.27 us (15%)
  between operations  0.84 us (1%)
    pallas_call x3, Pallas kernels, load(): pl.pallas_call(functools.partial(load_kernel, [span for _, span in loads]...  15.6 us
    pallas_call x4, Pallas kernels, product(): pl.pallas_call(functools.partial(product_kernel, len(tokens), len(matrice...  13.3 us
    ppermute x6, starting transfers between devices, gather_pieces(): pieces.append(lax.ppermute(pieces[offset ^ low], axis, pairs))  9.23 us
    ppermute x16, waiting for transfers between devices, exchange(): lax.ppermute(array, 'narrow', [(i, i ^ 1 << step) for i in range(size)])  7.85 us
    ppermute x16, starting transfers between devices, exchange(): lax.ppermute(array, 'narrow', [(i, i ^ 1 << step) for i in range(size)])  7.6 us
    pallas_call x1, Pallas kernels, look_up(): pl.pallas_call(functools.partial(look_up_kernel, ids.shape[0] // lengths....  2.16 us
    ppermute x6, waiting for transfers between devices, gather_pieces(): pieces.append(lax.ppermute(pieces[offset ^ low], axis, pairs))  1.42 us
  transfers between devices with their start and end apart: 22, of which 4 were waited for; matrix products, arithmetic and copies ran while one was open for 0% of the time, Pallas kernels for 50%

profile of v6, /device:TPU:0, one launch (start us, length us, event | category | flops | bytes accessed | tf_op | source)
XLA Modules:
  0.0 60.1 jit_solution(2512275603426583339)
XLA Ops:
  0.6 3.1 %collective-permute-start = (bf16[32,2048]{1,0:T(8,128)(2,1)}, bf16[32,2048]{1,0:T(8,128)(2,1)S(1)}, u32[]{:S(2)}, u32[]{:S(2)}) collective-permute-start(bf16[32,2048]{1,0:T(8,128)(2,1)} %refs_0_.9), channel_id=1, source_target_pairs={{0,4},{4,0},{8,12},{12,8},{1,5},{5,1},{9,13},{13,9},{2,6},{6,2},{1... | collective-permute-start | bytes 393224 | tf_op jit(solution)/shard_map/ppermute | solution.py:30
  3.7 2.6 %collective-permute-start.4 = (bf16[32,2048]{1,0:T(8,128)(2,1)}, bf16[32,2048]{1,0:T(8,128)(2,1)S(1)}, u32[]{:S(2)}, u32[]{:S(2)}) collective-permute-start(bf16[32,2048]{1,0:T(8,128)(2,1)} %refs_0_.7), channel_id=1, source_target_pairs={{0,8},{4,12},{8,0},{12,4},{1,9},{5,13},{9,1},{13,5},{2,10},{6,14},... | collective-permute-start | bytes 393224 | tf_op jit(solution)/shard_map/ppermute | solution.py:30
  6.3 0.4 collective-permute-start.3
  6.8 1.3 %collective-permute-start.5 = (bf16[32,2048]{1,0:T(8,128)(2,1)}, bf16[32,2048]{1,0:T(8,128)(2,1)S(1)}, u32[]{:S(2)}, u32[]{:S(2)}) collective-permute-start(bf16[32,2048]{1,0:T(8,128)(2,1)} %refs_0_.7), channel_id=1, source_target_pairs={{0,12},{4,8},{8,4},{12,0},{1,13},{5,9},{9,5},{13,1},{2,14},{6,10},... | collective-permute-start | bytes 393224 | tf_op jit(solution)/shard_map/ppermute | solution.py:30
  8.1 5.2 %shard_map.104 = (bf16[1024,3584]{1,0:T(8,128)(2,1)S(1)}, bf16[1024,3584]{1,0:T(8,128)(2,1)S(1)}) custom-call(bf16[2048,3584]{1,0:T(8,128)(2,1)} %refs_1_.3, bf16[2048,3584]{1,0:T(8,128)(2,1)} %refs_1_.3), custom_call_target="tpu_custom_call" | custom-call | tf_op jit(solution)/shard_map/pallas_call | solution.py:114
  13.3 0.0 copy-start
  13.3 5.2 %shard_map.105 = (bf16[1024,3584]{1,0:T(8,128)(2,1)S(1)}, bf16[1024,3584]{1,0:T(8,128)(2,1)S(1)}) custom-call(bf16[2048,3584]{1,0:T(8,128)(2,1)} %refs_1_.4, bf16[2048,3584]{1,0:T(8,128)(2,1)} %refs_1_.4, bf16[1024,3584]{1,0:T(8,128)(2,1)S(1)} %get-tuple-element.36.refs_2_.refs_4_), custom_call_target="tpu_custom_call" | custom-call | tf_op jit(solution)/shard_map/pallas_call | solution.py:114
  18.6 0.0 collective-permute-done.refs_7_.refs_1_
  18.6 0.0 collective-permute-done.4.refs_2_
  18.6 0.0 collective-permute-done.3.refs_1_
  18.6 0.0 collective-permute-done.5.refs_3_
  18.6 0.0 copy-done
  18.6 0.0 copy-start.1
  18.6 2.1 %shard_map.106 = (bf16[128,2048]{1,0:T(8,128)(2,1)S(1)}, bf16[32,1536]{1,0:T(8,128)(2,1)S(1)}, bf16[32,2048]{1,0:T(8,128)(2,1)S(1)}, bf16[32,3584]{1,0:T(8,128)(...) custom-call(bf16[32,2048]{1,0:T(8,128)(2,1)S(1)} %copy-done, ...), custom_call_target="tpu_custom_call" | custom-call | tf_op jit(solution)/shard_map/pallas_call | solution.py:185
  20.7 0.1 collective-permute-start.7
  20.8 0.0 copy-done.1
  20.8 1.8 %collective-permute-start.1 = (bf16[32,2048]{1,0:T(8,128)(2,1)S(1)}, bf16[32,2048]{1,0:T(8,128)(2,1)S(1)}, u32[]{:S(2)}, u32[]{:S(2)}) collective-permute-start(bf16[32,2048]{1,0:T(8,128)(2,1)S(1)} %copy-done.1), channel_id=1, source_target_pairs={{0,8},{4,12},{8,0},{12,4},{1,9},{5,13},{9,1},{13,5},{2,10},{6,14},... | collective-permute-start | bytes 393224 | tf_op jit(solution)/shard_map/ppermute | solution.py:30
  22.6 0.2 collective-permute-start.6
  22.7 4.1 %shard_map.107 = (bf16[1024,3584]{1,0:T(8,128)(2,1)S(1)}, bf16[32,1536]{1,0:T(8,128)(2,1)S(1)}, bf16[32,2048]{1,0:T(8,128)(2,1)S(1)}, bf16[32,3584]{1,0:T(8,128)...) custom-call(bf16[128,2048]{1,0:T(8,128)(2,1)S(1)} %get-tuple-element.39.refs_0_, ...), custom_call_target="tpu_custom_call" | custom-call | tf_op jit(solution)/shard_map/pallas_call | solution.py:185
  26.8 0.4 collective-permute-start.9
  27.2 0.0 collective-permute-done.6.refs_1_
  27.2 0.0 collective-permute-done.7.refs_2_
  27.2 0.1 shard_map.108.refs_2_
  27.3 1.6 %collective-permute-start.10 = (bf16[32,3584]{1,0:T(8,128)(2,1)S(1)}, bf16[32,3584]{1,0:T(8,128)(2,1)S(1)}, u32[]{:S(2)}, u32[]{:S(2)}) collective-permute-start(bf16[32,3584]{1,0:T(8,128)(2,1)S(1)} %shard_map.108.refs_2_), channel_id=1, source_target_pairs={{0,2},{1,3},{2,0},{3,1},{4,6},{5,7},{6,4},{7,5},{8,10},{9,11},{10,... | collective-permute-start | bytes 688136 | tf_op jit(solution)/shard_map/ppermute | solution.py:204
  28.9 0.0 collective-permute-start.8
  28.9 1.4 %collective-permute-done.1.refs_2_ = bf16[32,2048]{1,0:T(8,128)(2,1)S(1)} collective-permute-done((bf16[32,2048]{1,0:T(8,128)(2,1)S(1)}, bf16[32,2048]{1,0:T(8,128)(2,1)S(1)}, u32[]{:S(2)}, u32[]{:S(2)}) %collective-permute-start.1) | collective-permute-done | bytes 131104 | tf_op jit(solution)/shard_map/ppermute | solution.py:30
  30.3 0.0 collective-permute-start.2
  30.3 5.2 %shard_map.109 = (bf16[1024,3584]{1,0:T(8,128)(2,1)S(1)}, bf16[1024,3584]{1,0:T(8,128)(2,1)S(1)}) custom-call(bf16[2048,3584]{1,0:T(8,128)(2,1)} %refs_0_.8, bf16[2048,3584]{1,0:T(8,128)(2,1)} %refs_6_.1, bf16[32,3584]{1,0:T(8,128)(2,1)S(1)} %shard_map.108.refs_2_), custom_call_target="tpu_custom_call" | custom-call | tf_op jit(solution)/shard_map/pallas_call | solution.py:114
  35.5 0.0 collective-permute-done.8.refs_1_
  35.5 0.0 collective-permute-done.9.refs_2_
  35.5 0.1 shard_map.110.refs_7_
  35.6 1.6 %collective-permute-start.15 = (bf16[32,3584]{1,0:T(8,128)(2,1)S(1)}, bf16[32,3584]{1,0:T(8,128)(2,1)S(1)}, u32[]{:S(2)}, u32[]{:S(2)}) collective-permute-start(bf16[32,3584]{1,0:T(8,128)(2,1)S(1)} %shard_map.110.refs_7_), channel_id=1, source_target_pairs={{0,2},{1,3},{2,0},{3,1},{4,6},{5,7},{6,4},{7,5},{8,10},{9,11},{10,... | collective-permute-start | bytes 688136 | tf_op jit(solution)/shard_map/ppermute | solution.py:204
  37.1 0.0 collective-permute-start.17
  37.1 0.0 collective-permute-done.2.refs_3_
  37.1 5.0 %shard_map.111 = (bf16[1024,3584]{1,0:T(8,128)(2,1)S(1)}, bf16[128,2048]{1,0:T(8,128)(2,1)S(1)}, bf16[32,1536]{1,0:T(8,128)(2,1)S(1)}, bf16[32,2048]{1,0:T(8,128...) custom-call(bf16[32,2048]{1,0:T(8,128)(2,1)S(1)} %copy-done.1, ...), custom_call_target="tpu_custom_call" | custom-call | tf_op jit(solution)/shard_map/pallas_call | solution.py:185
  42.2 0.6 collective-permute-start.13
  42.7 0.1 collective-permute-start.14
  42.8 0.0 collective-permute-done.10.refs_4_.refs_2_
  42.8 2.1 %shard_map.112 = (bf16[32,1536]{1,0:T(8,128)(2,1)S(1)}, bf16[32,2048]{1,0:T(8,128)(2,1)S(1)}, bf16[32,3584]{1,0:T(8,128)(2,1)S(1)}, bf16[32,3584]{1,0:T(8,128)(2,1)S(1)}, bf16[32,3584]{1,0:T(8,128)(2,1)S(1)}) custom-call(bf16[128,2048]{1,0:T(8,128)(2,1)S(1)} %get-tuple-element.50.refs_0_, bf16[1024,3584]{1,0:T(8,128)(2,1)S(1)} %get-tuple-element.49.refs_3_.refs_1_, ...), custom_call_target="tpu_custom_call" | custom-call | tf_op jit(solution)/shard_map/pallas_call | solution.py:185
  44.9 0.5 collective-permute-start.12
  45.4 0.0 collective-permute-done.13.refs_1_
  45.4 0.1 collective-permute-start.11
  45.5 0.0 collective-permute-done.14.refs_2_
  45.5 0.4 collective-permute-start.16
  45.9 0.0 collective-permute-done.15.refs_4_.refs_5_
  45.9 0.1 collective-permute-start.18
  46.0 0.1 shard_map.113.refs_3_
  46.1 0.6 %collective-permute-done.11.refs_1_ = bf16[32,1536]{1,0:T(8,128)(2,1)S(1)} collective-permute-done((bf16[32,1536]{1,0:T(8,128)(2,1)S(1)}, bf16[32,1536]{1,0:T(8,128)(2,1)S(1)}, u32[]{:S(2)}, u32[]{:S(2)}) %collective-permute-start.11) | collective-permute-done | bytes 98336 | tf_op jit(solution)/shard_map/ppermute | solution.py:204
  46.7 0.5 collective-permute-start.19
  47.2 0.0 collective-permute-done.12.refs_2_
  47.2 0.0 collective-permute-start.20
  47.2 0.1 shard_map.114.refs_0_
  47.3 0.0 collective-permute-done.17.refs_4_
  47.3 1.6 %collective-permute-start.21 = (bf16[32,3584]{1,0:T(8,128)(2,1)S(1)}, bf16[32,3584]{1,0:T(8,128)(2,1)S(1)}, u32[]{:S(2)}, u32[]{:S(2)}) collective-permute-start(bf16[32,3584]{1,0:T(8,128)(2,1)S(1)} %shard_map.114.refs_0_), channel_id=1, source_target_pairs={{0,2},{1,3},{2,0},{3,1},{4,6},{5,7},{6,4},{7,5},{8,10},{9,11},{10,... | collective-permute-start | bytes 688136 | tf_op jit(solution)/shard_map/ppermute | solution.py:204
  48.9 2.2 %shard_map.115 = (f32[32,128]{1,0:T(8,128)S(1)}, f32[32,128]{1,0:T(8,128)S(1)}) custom-call(s32[32]{0:T(128)} %ids.1, s32[2]{0:T(128)} %lengths.1, f32[1002,128]{1,0:T(8,128)} %bitcast.1, bf16[32,3584]{1,0:T(8,128)(2,1)S(1)} %shard_map.114.refs_0_), custom_call_target="tpu_custom_call" | custom-call | tf_op jit(solution)/shard_map/pallas_call | solution.py:88
  51.0 0.0 collective-permute-done.16.refs_1_
  51.0 0.9 %shard_map.116 = (f32[32,3584]{1,0:T(8,128)S(1)}, bf16[32,3584]{1,0:T(8,128)(2,1)}) custom-call(f32[32,128]{1,0:T(8,128)S(1)} %get-tuple-element.58.live, bf16[32,3584]{1,0:T(8,128)(2,1)S(1)} %get-tuple-element.59.refs_0_, bf16[32,3584]{1,0:T(8,128)(2,1)S(1)} %collective-permute-done.16.refs_1_, ...), custom_call_target="tpu_custom_call" | custom-call | tf_op jit(solution)/shard_map/pallas_call | solution.py:260
  52.0 0.0 collective-permute-done.18.refs_1_
  52.0 3.2 %collective-permute-done.19.refs_2_ = bf16[32,3584]{1,0:T(8,128)(2,1)S(1)} collective-permute-done((bf16[32,3584]{1,0:T(8,128)(2,1)S(1)}, bf16[32,3584]{1,0:T(8,128)(2,1)S(1)}, u32[]{:S(2)}, u32[]{:S(2)}) %collective-permute-start.19) | collective-permute-done | bytes 229408 | tf_op jit(solution)/shard_map/ppermute | solution.py:204
  55.1 0.1 shard_map.117.gated
  55.3 0.0 collective-permute-done.20.refs_1_
  55.3 4.0 %collective-permute-done.21.refs_2_ = bf16[32,3584]{1,0:T(8,128)(2,1)S(1)} collective-permute-done((bf16[32,3584]{1,0:T(8,128)(2,1)S(1)}, bf16[32,3584]{1,0:T(8,128)(2,1)S(1)}, u32[]{:S(2)}, u32[]{:S(2)}) %collective-permute-start.21) | collective-permute-done | bytes 229408 | tf_op jit(solution)/shard_map/ppermute | solution.py:204
  59.3 0.8 %shard_map.118 = bf16[32,3584]{1,0:T(8,128)(2,1)} custom-call(f32[32,3584]{1,0:T(8,128)S(1)} %get-tuple-element.64.act, f32[32,3584]{1,0:T(8,128)S(1)} %shard_map.117.gated, bf16[32,3584]{1,0:T(8,128)(2,1)S(1)} %get-tuple-element.68.refs_0_, bf16[32,3584]{1,0:T(8,128)(2,1)S(1)} %collective-permute-done.20.refs_1_, ...), custom_call_target="tpu_custom_call" | custom-call | tf_op jit(solution)/shard_map/pallas_call | solution.py:296
Async XLA Ops:
  0.6 17.9 %collective-permute-start = (bf16[32,2048]{1,0:T(8,128)(2,1)}, bf16[32,2048]{1,0:T(8,128)(2,1)S(1)}, u32[]{:S(2)}, u32[]{:S(2)}) collective-permute-start(bf16[32,2048]{1,0:T(8,128)(2,1)} %refs_0_.9), channel_id=1, source_target_pairs={{0,4},{4,0},{8,12},{12,8},{1,5},{5,1},{9,13},{13,9},{2,6},{6,2},{1... | collective-permute-start | bytes 393224 | tf_op jit(solution)/shard_map/ppermute | solution.py:30
  3.7 14.8 %collective-permute-start.4 = (bf16[32,2048]{1,0:T(8,128)(2,1)}, bf16[32,2048]{1,0:T(8,128)(2,1)S(1)}, u32[]{:S(2)}, u32[]{:S(2)}) collective-permute-start(bf16[32,2048]{1,0:T(8,128)(2,1)} %refs_0_.7), channel_id=1, source_target_pairs={{0,8},{4,12},{8,0},{12,4},{1,9},{5,13},{9,1},{13,5},{2,10},{6,14},... | collective-permute-start | bytes 393224 | tf_op jit(solution)/shard_map/ppermute | solution.py:30
  6.3 12.3 %collective-permute-start.3 = (bf16[32,2048]{1,0:T(8,128)(2,1)}, bf16[32,2048]{1,0:T(8,128)(2,1)S(1)}, u32[]{:S(2)}, u32[]{:S(2)}) collective-permute-start(bf16[32,2048]{1,0:T(8,128)(2,1)} %refs_0_.7), channel_id=1, source_target_pairs={{0,4},{4,0},{8,12},{12,8},{1,5},{5,1},{9,13},{13,9},{2,6},{6,2},{1... | collective-permute-start | bytes 393224 | tf_op jit(solution)/shard_map/ppermute | solution.py:30
  6.8 11.8 %collective-permute-start.5 = (bf16[32,2048]{1,0:T(8,128)(2,1)}, bf16[32,2048]{1,0:T(8,128)(2,1)S(1)}, u32[]{:S(2)}, u32[]{:S(2)}) collective-permute-start(bf16[32,2048]{1,0:T(8,128)(2,1)} %refs_0_.7), channel_id=1, source_target_pairs={{0,12},{4,8},{8,4},{12,0},{1,13},{5,9},{9,5},{13,1},{2,14},{6,10},... | collective-permute-start | bytes 393224 | tf_op jit(solution)/shard_map/ppermute | solution.py:30
  13.3 5.3 %copy-start = (bf16[32,2048]{1,0:T(8,128)(2,1)S(1)}, bf16[32,2048]{1,0:T(8,128)(2,1)}, u32[]{:S(2)}) copy-start(bf16[32,2048]{1,0:T(8,128)(2,1)} %refs_0_.7) | copy-start | bytes 393220
  18.6 2.2 %copy-start.1 = (bf16[32,2048]{1,0:T(8,128)(2,1)S(1)}, bf16[32,2048]{1,0:T(8,128)(2,1)}, u32[]{:S(2)}) copy-start(bf16[32,2048]{1,0:T(8,128)(2,1)} %refs_0_.9) | copy-start | bytes 393220
  20.7 6.5 %collective-permute-start.7 = (bf16[32,2048]{1,0:T(8,128)(2,1)S(1)}, bf16[32,2048]{1,0:T(8,128)(2,1)S(1)}, u32[]{:S(2)}, u32[]{:S(2)}) collective-permute-start(bf16[32,2048]{1,0:T(8,128)(2,1)S(1)} %get-tuple-element.44), channel_id=1, source_target_pairs={{0,1},{1,0},{2,3},{3,2},{4,5},{5,4},{6,7},{7,6},{8,9},{9,8},{10,11... | collective-permute-start | bytes 393224 | tf_op jit(solution)/shard_map/ppermute | solution.py:204
  20.8 9.4 %collective-permute-start.1 = (bf16[32,2048]{1,0:T(8,128)(2,1)S(1)}, bf16[32,2048]{1,0:T(8,128)(2,1)S(1)}, u32[]{:S(2)}, u32[]{:S(2)}) collective-permute-start(bf16[32,2048]{1,0:T(8,128)(2,1)S(1)} %copy-done.1), channel_id=1, source_target_pairs={{0,8},{4,12},{8,0},{12,4},{1,9},{5,13},{9,1},{13,5},{2,10},{6,14},... | collective-permute-start | bytes 393224 | tf_op jit(solution)/shard_map/ppermute | solution.py:30
  22.6 4.6 %collective-permute-start.6 = (bf16[32,1536]{1,0:T(8,128)(2,1)S(1)}, bf16[32,1536]{1,0:T(8,128)(2,1)S(1)}, u32[]{:S(2)}, u32[]{:S(2)}) collective-permute-start(bf16[32,1536]{1,0:T(8,128)(2,1)S(1)} %get-tuple-element.41.refs_4_), channel_id=1, source_target_pairs={{0,1},{1,0},{2,3},{3,2},{4,5},{5,4},{6,7},{7,6},{8,9},{9,8},{10,11... | collective-permute-start | bytes 294920 | tf_op jit(solution)/shard_map/ppermute | solution.py:204
  26.8 8.7 %collective-permute-start.9 = (bf16[32,2048]{1,0:T(8,128)(2,1)S(1)}, bf16[32,2048]{1,0:T(8,128)(2,1)S(1)}, u32[]{:S(2)}, u32[]{:S(2)}) collective-permute-start(bf16[32,2048]{1,0:T(8,128)(2,1)S(1)} %get-tuple-element.48), channel_id=1, source_target_pairs={{0,1},{1,0},{2,3},{3,2},{4,5},{5,4},{6,7},{7,6},{8,9},{9,8},{10,11... | collective-permute-start | bytes 393224 | tf_op jit(solution)/shard_map/ppermute | solution.py:204
  27.3 15.5 %collective-permute-start.10 = (bf16[32,3584]{1,0:T(8,128)(2,1)S(1)}, bf16[32,3584]{1,0:T(8,128)(2,1)S(1)}, u32[]{:S(2)}, u32[]{:S(2)}) collective-permute-start(bf16[32,3584]{1,0:T(8,128)(2,1)S(1)} %shard_map.108.refs_2_), channel_id=1, source_target_pairs={{0,2},{1,3},{2,0},{3,1},{4,6},{5,7},{6,4},{7,5},{8,10},{9,11},{10,... | collective-permute-start | bytes 688136 | tf_op jit(solution)/shard_map/ppermute | solution.py:204
  28.9 6.6 %collective-permute-start.8 = (bf16[32,1536]{1,0:T(8,128)(2,1)S(1)}, bf16[32,1536]{1,0:T(8,128)(2,1)S(1)}, u32[]{:S(2)}, u32[]{:S(2)}) collective-permute-start(bf16[32,1536]{1,0:T(8,128)(2,1)S(1)} %get-tuple-element.45.refs_3_), channel_id=1, source_target_pairs={{0,1},{1,0},{2,3},{3,2},{4,5},{5,4},{6,7},{7,6},{8,9},{9,8},{10,11... | collective-permute-start | bytes 294920 | tf_op jit(solution)/shard_map/ppermute | solution.py:204
  30.3 6.8 %collective-permute-start.2 = (bf16[32,2048]{1,0:T(8,128)(2,1)S(1)}, bf16[32,2048]{1,0:T(8,128)(2,1)S(1)}, u32[]{:S(2)}, u32[]{:S(2)}) collective-permute-start(bf16[32,2048]{1,0:T(8,128)(2,1)S(1)} %collective-permute-done.1.refs_2_), channel_id=1, source_target_pairs={{0,4},{4,0},{8,12},{12,8},{1,5},{5,1},{9,13},{13,9},{2,6},{6,2},{1... | collective-permute-start | bytes 393224 | tf_op jit(solution)/shard_map/ppermute | solution.py:30
  35.6 10.4 %collective-permute-start.15 = (bf16[32,3584]{1,0:T(8,128)(2,1)S(1)}, bf16[32,3584]{1,0:T(8,128)(2,1)S(1)}, u32[]{:S(2)}, u32[]{:S(2)}) collective-permute-start(bf16[32,3584]{1,0:T(8,128)(2,1)S(1)} %shard_map.110.refs_7_), channel_id=1, source_target_pairs={{0,2},{1,3},{2,0},{3,1},{4,6},{5,7},{6,4},{7,5},{8,10},{9,11},{10,... | collective-permute-start | bytes 688136 | tf_op jit(solution)/shard_map/ppermute | solution.py:204
  37.1 10.2 %collective-permute-start.17 = (bf16[32,3584]{1,0:T(8,128)(2,1)S(1)}, bf16[32,3584]{1,0:T(8,128)(2,1)S(1)}, u32[]{:S(2)}, u32[]{:S(2)}) collective-permute-start(bf16[32,3584]{1,0:T(8,128)(2,1)S(1)} %get-tuple-element.62), channel_id=1, source_target_pairs={{0,1},{1,0},{2,3},{3,2},{4,5},{5,4},{6,7},{7,6},{8,9},{9,8},{10,11... | collective-permute-start | bytes 688136 | tf_op jit(solution)/shard_map/ppermute | solution.py:204
  42.2 3.2 %collective-permute-start.13 = (bf16[32,1536]{1,0:T(8,128)(2,1)S(1)}, bf16[32,1536]{1,0:T(8,128)(2,1)S(1)}, u32[]{:S(2)}, u32[]{:S(2)}) collective-permute-start(bf16[32,1536]{1,0:T(8,128)(2,1)S(1)} %get-tuple-element.52.refs_3_), channel_id=1, source_target_pairs={{0,1},{1,0},{2,3},{3,2},{4,5},{5,4},{6,7},{7,6},{8,9},{9,8},{10,11... | collective-permute-start | bytes 294920 | tf_op jit(solution)/shard_map/ppermute | solution.py:204
  42.7 2.8 %collective-permute-start.14 = (bf16[32,2048]{1,0:T(8,128)(2,1)S(1)}, bf16[32,2048]{1,0:T(8,128)(2,1)S(1)}, u32[]{:S(2)}, u32[]{:S(2)}) collective-permute-start(bf16[32,2048]{1,0:T(8,128)(2,1)S(1)} %get-tuple-element.57), channel_id=1, source_target_pairs={{0,1},{1,0},{2,3},{3,2},{4,5},{5,4},{6,7},{7,6},{8,9},{9,8},{10,11... | collective-permute-start | bytes 393224 | tf_op jit(solution)/shard_map/ppermute | solution.py:204
  44.9 2.3 %collective-permute-start.12 = (bf16[32,2048]{1,0:T(8,128)(2,1)S(1)}, bf16[32,2048]{1,0:T(8,128)(2,1)S(1)}, u32[]{:S(2)}, u32[]{:S(2)}) collective-permute-start(bf16[32,2048]{1,0:T(8,128)(2,1)S(1)} %get-tuple-element.55), channel_id=1, source_target_pairs={{0,1},{1,0},{2,3},{3,2},{4,5},{5,4},{6,7},{7,6},{8,9},{9,8},{10,11... | collective-permute-start | bytes 393224 | tf_op jit(solution)/shard_map/ppermute | solution.py:204
  45.4 1.3 %collective-permute-start.11 = (bf16[32,1536]{1,0:T(8,128)(2,1)S(1)}, bf16[32,1536]{1,0:T(8,128)(2,1)S(1)}, u32[]{:S(2)}, u32[]{:S(2)}) collective-permute-start(bf16[32,1536]{1,0:T(8,128)(2,1)S(1)} %get-tuple-element.54.refs_3_), channel_id=1, source_target_pairs={{0,1},{1,0},{2,3},{3,2},{4,5},{5,4},{6,7},{7,6},{8,9},{9,8},{10,11... | collective-permute-start | bytes 294920 | tf_op jit(solution)/shard_map/ppermute | solution.py:204
  45.5 5.5 %collective-permute-start.16 = (bf16[32,3584]{1,0:T(8,128)(2,1)S(1)}, bf16[32,3584]{1,0:T(8,128)(2,1)S(1)}, u32[]{:S(2)}, u32[]{:S(2)}) collective-permute-start(bf16[32,3584]{1,0:T(8,128)(2,1)S(1)} %get-tuple-element.60), channel_id=1, source_target_pairs={{0,1},{1,0},{2,3},{3,2},{4,5},{5,4},{6,7},{7,6},{8,9},{9,8},{10,11... | collective-permute-start | bytes 688136 | tf_op jit(solution)/shard_map/ppermute | solution.py:204
  45.9 6.1 %collective-permute-start.18 = (bf16[32,3584]{1,0:T(8,128)(2,1)S(1)}, bf16[32,3584]{1,0:T(8,128)(2,1)S(1)}, u32[]{:S(2)}, u32[]{:S(2)}) collective-permute-start(bf16[32,3584]{1,0:T(8,128)(2,1)S(1)} %get-tuple-element.67), channel_id=1, source_target_pairs={{0,1},{1,0},{2,3},{3,2},{4,5},{5,4},{6,7},{7,6},{8,9},{9,8},{10,11... | collective-permute-start | bytes 688136 | tf_op jit(solution)/shard_map/ppermute | solution.py:204
  46.7 8.4 %collective-permute-start.19 = (bf16[32,3584]{1,0:T(8,128)(2,1)S(1)}, bf16[32,3584]{1,0:T(8,128)(2,1)S(1)}, u32[]{:S(2)}, u32[]{:S(2)}) collective-permute-start(bf16[32,3584]{1,0:T(8,128)(2,1)S(1)} %shard_map.113.refs_3_), channel_id=1, source_target_pairs={{0,2},{1,3},{2,0},{3,1},{4,6},{5,7},{6,4},{7,5},{8,10},{9,11},{10,... | collective-permute-start | bytes 688136 | tf_op jit(solution)/shard_map/ppermute | solution.py:204
  47.2 8.1 %collective-permute-start.20 = (bf16[32,3584]{1,0:T(8,128)(2,1)S(1)}, bf16[32,3584]{1,0:T(8,128)(2,1)S(1)}, u32[]{:S(2)}, u32[]{:S(2)}) collective-permute-start(bf16[32,3584]{1,0:T(8,128)(2,1)S(1)} %get-tuple-element.69), channel_id=1, source_target_pairs={{0,1},{1,0},{2,3},{3,2},{4,5},{5,4},{6,7},{7,6},{8,9},{9,8},{10,11... | collective-permute-start | bytes 688136 | tf_op jit(solution)/shard_map/ppermute | solution.py:204
  47.3 12.0 %collective-permute-start.21 = (bf16[32,3584]{1,0:T(8,128)(2,1)S(1)}, bf16[32,3584]{1,0:T(8,128)(2,1)S(1)}, u32[]{:S(2)}, u32[]{:S(2)}) collective-permute-start(bf16[32,3584]{1,0:T(8,128)(2,1)S(1)} %shard_map.114.refs_0_), channel_id=1, source_target_pairs={{0,2},{1,3},{2,0},{3,1},{4,6},{5,7},{6,4},{7,5},{8,10},{9,11},{10,... | collective-permute-start | bytes 688136 | tf_op jit(solution)/shard_map/ppermute | solution.py:204

commit v7 on v6

--- a/solution.py
+++ b/solution.py
@@ -12,6 +12,7 @@
 IN_SMEM = pl.BlockSpec(memory_space=pltpu.SMEM)
 ANYWHERE = pl.BlockSpec(memory_space=pl.ANY)
 LANES = 128
+IN_FLIGHT = 4
 
 
 def in_hbm(array):
@@ -22,12 +23,29 @@
     return pltpu.with_memory_space_constraint(array, pltpu.VMEM)
 
 
-def gather_pieces(piece, axis, size, relayed):
+def pass_kernel(piece, *refs):
+    refs[-1][...] = piece[...]
+
+
+def passed(piece, after):
+    return pl.pallas_call(
+        pass_kernel,
+        out_shape=jax.ShapeDtypeStruct(piece.shape, piece.dtype),
+        in_specs=[IN_VMEM] + [ANYWHERE] * len(after),
+        out_specs=IN_VMEM,
+        compiler_params=pltpu.CompilerParams(vmem_limit_bytes=1 << 20),
+    )(piece, *after)
+
+
+def gather_pieces(piece, axis, size, after=()):
     pieces = [piece]
     for offset in range(1, size):
-        low = offset & -offset if relayed else offset
+        low = offset & -offset
         pairs = [(i, i ^ low) for i in range(size)]
-        pieces.append(lax.ppermute(pieces[offset ^ low], axis, pairs))
+        piece = pieces[offset ^ low]
+        if after and offset != low:
+            piece = passed(piece, after)
+        pieces.append(lax.ppermute(piece, axis, pairs))
     return pieces
 
 
@@ -54,14 +72,6 @@
             rows[pl.ds(spot, size), :] = piece[start : start + size, :]
 
 
-def start_loads(sources, spans, dests, sems):
-    copies = []
-    for i, (source, (start, size)) in enumerate(zip(sources, spans)):
-        copies.append(pltpu.make_async_copy(source.at[pl.ds(start, size), :], dests[i], sems.at[i]))
-        copies[-1].start()
-    return copies
-
-
 def look_up_kernel(slots, ids, lengths, table, *refs):
     live, weight, entries, picked, sem = refs[-5:]
     lookup = pltpu.make_async_copy(table, entries, sem)
@@ -99,26 +109,22 @@
     )(*map(in_hbm, (ids, lengths, table)), *after)
 
 
-def load_kernel(spans, after, *refs):
-    dests = refs[len(spans) + after : -1]
-    for copy in start_loads(refs[: len(spans)], spans, dests, refs[-1]):
-        copy.wait()
-
-
-def halves(matrix):
-    half = matrix.shape[0] // 2
-    return [(matrix, (0, half)), (matrix, (half, half))]
-
-
-def load(loads, after):
-    return pl.pallas_call(
-        functools.partial(load_kernel, [span for _, span in loads], len(after)),
-        out_shape=[pltpu.VMEM((size, m.shape[1]), m.dtype) for m, (_, size) in loads],
-        in_specs=[ANYWHERE] * (len(loads) + len(after)),
-        out_specs=[IN_VMEM] * len(loads),
-        scratch_shapes=[pltpu.SemaphoreType.DMA((len(loads),))],
+def load_kernel(matrix, *refs):
+    dest, sem = refs[-2:]
+    copy = pltpu.make_async_copy(matrix, dest, sem)
+    copy.start()
+    copy.wait()
+
+
+def load(matrix, after=()):
+    return pl.pallas_call(
+        load_kernel,
+        out_shape=pltpu.VMEM(matrix.shape, matrix.dtype),
+        in_specs=[ANYWHERE] * (1 + len(after)),
+        out_specs=IN_VMEM,
+        scratch_shapes=[pltpu.SemaphoreType.DMA],
         compiler_params=pltpu.CompilerParams(vmem_limit_bytes=1 << 20),
-    )(*(in_hbm(m) for m, _ in loads), *after)
+    )(in_hbm(matrix), *after)
 
 
 def tile_of(cols):
@@ -139,28 +145,30 @@
     return [(0, first), (first, width - first)] if first else [(0, width)]
 
 
-def product_kernel(pieces, parts, spans, after, narrow, blocks, *refs):
-    tokens, matrices = refs[:pieces], refs[pieces : pieces + parts]
-    refs = refs[pieces + parts :]
-    sources, refs = refs[: len(spans)], refs[len(spans) + after :]
-    dests, outs, sems = refs[: len(spans)], refs[len(spans) : -1], refs[-1]
-    copies = start_loads(sources, spans, dests, sems)
+def product_kernel(pieces, after, narrow, blocks, *refs):
+    tokens, matrix, refs = refs[:pieces], refs[pieces], refs[pieces + 1 + after :]
+    tiles, copies = column_tiles(matrix.shape[1]), []
+    if len(blocks) < len(refs) - (pieces > 1):
+        here, sems = refs[-2:]
+        refs = refs[:-2]
+        for i, cols in enumerate(tiles):
+            copies.append(pltpu.make_async_copy(matrix.at[:, cols], here.at[:, cols], sems.at[i]))
+        matrix = here
+    for copy in copies[:IN_FLIGHT]:
+        copy.start()
     if pieces > 1:
-        place_rows(tokens, outs[0], narrow)
-        tokens, outs = outs[:1], outs[1:]
-    for cols in column_tiles(matrices[0].shape[1]):
-        total, depth = None, 0
-        for matrix in matrices:
-            rows = tokens[0][:, depth : depth + matrix.shape[0]]
-            term = jnp.dot(rows, matrix[:, cols], preferred_element_type=jnp.float32)
-            total = term if total is None else total + term
-            depth += matrix.shape[0]
-        for out, (row, col) in zip(outs, blocks):
+        place_rows(tokens, refs[0], narrow)
+        tokens, refs = refs[:1], refs[1:]
+    for i, cols in enumerate(tiles):
+        if copies:
+            copies[i].wait()
+        if i + IN_FLIGHT < len(copies):
+            copies[i + IN_FLIGHT].start()
+        total = jnp.dot(tokens[0][...], matrix[:, cols], preferred_element_type=jnp.float32)
+        for out, (row, col) in zip(refs, blocks):
             if col <= cols.start and cols.stop <= col + out.shape[1]:
                 value = total[row : row + out.shape[0]].astype(out.dtype)
                 out[:, cols.start - col : cols.stop - col] = value
-    for copy in copies:
-        copy.wait()
 
 
 def part_sizes(total, narrow):
@@ -171,10 +179,10 @@
     return sizes + [left]
 
 
-def product(tokens, matrices, narrow, after=(), loads=()):
+def product(tokens, matrix, held, narrow, after):
     placing = len(tokens) > 1
     total = sum(t.shape[0] for t in tokens)
-    depth, width = tokens[0].shape[1], matrices[0].shape[1]
+    depth, width = matrix.shape
     sizes = part_sizes(total, narrow)
     sent = []
     for k in range(len(sizes)):
@@ -182,22 +190,23 @@
     blocks = [(sum(sizes[:k]), first) for k, first, _ in sent]
     blocks += [(total // 2 + sum(sizes[:k]), 0) for k in range(len(sizes))]
     shapes = [(sizes[k], count) for k, _, count in sent] + [(size, width) for size in sizes]
+    stream = [
+        pltpu.VMEM(matrix.shape, matrix.dtype),
+        pltpu.SemaphoreType.DMA((len(column_tiles(width)),)),
+    ]
+    room = 4 + (0 if held else 1 + matrix.size * matrix.dtype.itemsize >> 20)
     found = pl.pallas_call(
-        functools.partial(
-            product_kernel, len(tokens), len(matrices), [span for _, span in loads], len(after), narrow, blocks
-        ),
-        out_shape=[pltpu.VMEM((size, m.shape[1]), m.dtype) for m, (_, size) in loads]
-        + [jax.ShapeDtypeStruct((total, depth), tokens[0].dtype)] * placing
+        functools.partial(product_kernel, len(tokens), len(after), narrow, blocks),
+        out_shape=[jax.ShapeDtypeStruct((total, depth), tokens[0].dtype)] * placing
         + [jax.ShapeDtypeStruct(shape, jnp.bfloat16) for shape in shapes],
-        in_specs=[IN_VMEM] * (len(tokens) + len(matrices)) + [ANYWHERE] * (len(loads) + len(after)),
-        out_specs=[IN_VMEM] * (len(loads) + placing + len(shapes)),
-        scratch_shapes=[pltpu.SemaphoreType.DMA((max(1, len(loads)),))],
-        compiler_params=pltpu.CompilerParams(vmem_limit_bytes=4 << 20),
-    )(*tokens, *map(in_vmem, matrices), *(in_hbm(m) for m, _ in loads), *after)
-    loaded, found = found[: len(loads)], found[len(loads) :]
+        in_specs=[IN_VMEM] * len(tokens) + [IN_VMEM if held else ANYWHERE] + [ANYWHERE] * len(after),
+        out_specs=[IN_VMEM] * (placing + len(shapes)),
+        scratch_shapes=[] if held else stream,
+        compiler_params=pltpu.CompilerParams(vmem_limit_bytes=room << 20),
+    )(*tokens, (in_vmem if held else in_hbm)(matrix), *after)
     rows, found = (found[:1], found[1:]) if placing else (tokens, found)
     sends = [(array, k, first) for array, (k, first, _) in zip(found, sent)]
-    return loaded, rows, sends, found[len(sent) :]
+    return rows, sends, found[len(sent) :]
 
 
 def exchange(array, step, size):
@@ -304,27 +313,20 @@
 
 def local(mesh_shape, target_states, source_states, target_gate, target_up, source_gate, source_up, token_ids, lengths, ratio_weight):
     wide, narrow = mesh_shape["wide"], mesh_shape["narrow"]
-    gate_top, gate_bottom = halves(source_gate)
-    up_top, up_bottom = halves(source_up)
-
-    target_pieces = gather_pieces(target_states, "wide", wide, False)
-    source_pieces = gather_pieces(source_states, "wide", wide, True)
-    target_gate = load(halves(target_gate), ())
-    target_up = load(halves(target_up), (target_gate[0],))
-
-    after = (target_up[0], source_pieces[1])
-    _, rows, sends, keeps = product(target_pieces, target_gate, narrow, after)
-    after = (sends[0][0],)
-    (gate_top,), _, up_sends, up_keeps = product(rows, target_up, narrow, after, [gate_top])
-    sent, target_g = finish(sends, keeps, narrow, (up_sends[0][0],))
-    gate_bottom, up_top = load([gate_bottom, up_top], (sent,))
-    sent, target_u = finish(up_sends, up_keeps, narrow, (up_top,))
-
-    (up_bottom,), rows, sends, keeps = product(
-        source_pieces, (gate_top, gate_bottom), narrow, (sent,), [up_bottom]
-    )
+    target_gate = load(target_gate)
+    target_pieces = gather_pieces(target_states, "wide", wide, (target_gate,))
+    source_pieces = gather_pieces(source_states, "wide", wide)
+    target_up = load(target_up, (target_gate, target_pieces[wide // 2]))
+
+    after = (target_up, source_pieces[1], source_pieces[wide // 2])
+    rows, sends, keeps = product(target_pieces, target_gate, True, narrow, after)
+    _, up_sends, up_keeps = product(rows, target_up, True, narrow, (sends[0][0],))
+    sent, target_g = finish(sends, keeps, narrow, (up_sends[0][0], source_pieces[-1]))
+    sent, target_u = finish(up_sends, up_keeps, narrow, (sent,))
+
+    rows, sends, keeps = product(source_pieces, source_gate, False, narrow, (sent,))
     after = (sends[0][0], target_g[0][-1])
-    _, _, up_sends, up_keeps = product(rows, (up_top, up_bottom), narrow, after)
+    _, up_sends, up_keeps = product(rows, source_up, False, narrow, after)
     after = (up_sends[0][0], target_u[0][-1])
     sent, source_g = finish(sends, keeps, narrow, after)
     sent, source_u = finish(up_sends, up_keeps, narrow, (sent,))

time: 60.4 us -> 59.2 us (0.980)
  waiting for transfers between devices: 9.27 us -> 12 us
  Pallas kernels: 33.2 us -> 30.9 us
  starting transfers between devices: 16.8 us -> 15.2 us
    pallas_call x7, Pallas kernels: 28.9 us -> 26.6 us  [the longest x4 16.3 us: product(): pl.pallas_call(functools.partial(product_kernel, len(tokens), len(after),...]
    ppermute x6, waiting for transfers between devices: 1.42 us -> 2.97 us  [gather_pieces(): pieces.append(lax.ppermute(piece, axis, pairs))]
    ppermute x16, waiting for transfers between devices: 7.85 us -> 9.07 us  [exchange(): lax.ppermute(array, 'narrow', [(i, i ^ 1 << step) for i in range(size)])]
    ppermute x6, starting transfers between devices: 9.23 us -> 8.36 us  [gather_pieces(): pieces.append(lax.ppermute(piece, axis, pairs))]
    ppermute x16, starting transfers between devices: 7.6 us -> 6.87 us  [exchange(): lax.ppermute(array, 'narrow', [(i, i ^ 1 << step) for i in range(size)])]
  transfers between devices with their start and end apart: 22 -> 22, of which waited for: 4 -> 5; matrix products, arithmetic and copies ran while one was open for 0% -> 0% of each run, Pallas kernels for 50% -> 51%
where the time goes in v7:
time: 59.2 us; the launch traced here: 59 us
  Pallas kernels  30.9 us (52%)
  starting transfers between devices  15.2 us (26%)
  waiting for transfers between devices  12 us (20%)
  between operations  0.8 us (1%)
    pallas_call x4, Pallas kernels, product(): pl.pallas_call(functools.partial(product_kernel, len(tokens), len(after),...  16.3 us
    pallas_call x2, Pallas kernels, load(): pl.pallas_call(load_kernel, out_shape=pltpu.VMEM(matrix.shape, matrix.dty...  10.4 us
    ppermute x16, waiting for transfers between devices, exchange(): lax.ppermute(array, 'narrow', [(i, i ^ 1 << step) for i in range(size)])  9.07 us
    ppermute x6, starting transfers between devices, gather_pieces(): pieces.append(lax.ppermute(piece, axis, pairs))  8.36 us
    ppermute x16, starting transfers between devices, exchange(): lax.ppermute(array, 'narrow', [(i, i ^ 1 << step) for i in range(size)])  6.87 us
    ppermute x6, waiting for transfers between devices, gather_pieces(): pieces.append(lax.ppermute(piece, axis, pairs))  2.97 us
    pallas_call x1, Pallas kernels, look_up(): pl.pallas_call(functools.partial(look_up_kernel, ids.shape[0] // lengths....  2.16 us
  transfers between devices with their start and end apart: 22, of which 5 were waited for; matrix products, arithmetic and copies ran while one was open for 0% of the time, Pallas kernels for 51%

profile of v7, /device:TPU:0, one launch (start us, length us, event | category | flops | bytes accessed | tf_op | source)
XLA Modules:
  0.0 59.0 jit_solution(1385299620693277843)
XLA Ops:
  0.6 4.1 %collective-permute-start.4 = (bf16[32,2048]{1,0:T(8,128)(2,1)}, bf16[32,2048]{1,0:T(8,128)(2,1)S(1)}, u32[]{:S(2)}, u32[]{:S(2)}) collective-permute-start(bf16[32,2048]{1,0:T(8,128)(2,1)} %refs_0_.2), channel_id=1, source_target_pairs={{0,8},{4,12},{8,0},{12,4},{1,9},{5,13},{9,1},{13,5},{2,10},{6,14},... | collective-permute-start | bytes 393224 | tf_op jit(solution)/shard_map/ppermute | solution.py:48
  4.7 0.1 collective-permute-start.1
  4.8 1.8 %collective-permute-start = (bf16[32,2048]{1,0:T(8,128)(2,1)}, bf16[32,2048]{1,0:T(8,128)(2,1)S(1)}, u32[]{:S(2)}, u32[]{:S(2)}) collective-permute-start(bf16[32,2048]{1,0:T(8,128)(2,1)} %refs_0_.3), channel_id=1, source_target_pairs={{0,4},{4,0},{8,12},{12,8},{1,5},{5,1},{9,13},{13,9},{2,6},{6,2},{1... | collective-permute-start | bytes 393224 | tf_op jit(solution)/shard_map/ppermute | solution.py:48
  6.6 0.2 collective-permute-start.3
  6.8 5.2 %shard_map.104.refs_0_.refs_4_ = bf16[2048,3584]{1,0:T(8,128)(2,1)S(1)} custom-call(bf16[2048,3584]{1,0:T(8,128)(2,1)} %matrix.2), custom_call_target="tpu_custom_call" | custom-call | tf_op jit(solution)/shard_map/pallas_call | solution.py:120
  12.0 3.0 %collective-permute-done.4.piece.refs_1_.refs_2_ = bf16[32,2048]{1,0:T(8,128)(2,1)S(1)} collective-permute-done((bf16[32,2048]{1,0:T(8,128)(2,1)}, bf16[32,2048]{1,0:T(8,128)(2,1)S(1)}, u32[]{:S(2)}, u32[]{:S(2)}) %collective-permute-start.4) | collective-permute-done | bytes 131104 | tf_op jit(solution)/shard_map/ppermute | solution.py:48
  15.0 0.0 copy-start
  15.0 0.1 collective-permute-start.5
  15.1 5.2 %shard_map.106.refs_5_.refs_1_ = bf16[2048,3584]{1,0:T(8,128)(2,1)S(1)} custom-call(bf16[2048,3584]{1,0:T(8,128)(2,1)} %matrix.3, bf16[2048,3584]{1,0:T(8,128)(2,1)S(1)} %shard_map.104.refs_0_.refs_4_, bf16[32,2048]{1,0:T(8,128)(2,1)S(1)} %collective-permute-done.4.piece.refs_1_.refs_2_), custom_call_target="tpu_custom_call" | custom-call | tf_op jit(solution)/shard_map/pallas_call | solution.py:120
  20.3 0.0 collective-permute-done.1.refs_7_.refs_2_
  20.3 2.1 %collective-permute-start.2 = (bf16[32,2048]{1,0:T(8,128)(2,1)S(1)}, bf16[32,2048]{1,0:T(8,128)(2,1)S(1)}, u32[]{:S(2)}, u32[]{:S(2)}) collective-permute-start(bf16[32,2048]{1,0:T(8,128)(2,1)S(1)} %collective-permute-done.1.refs_7_.refs_2_), channel_id=1, source_target_pairs={{0,4},{4,0},{8,12},{12,8},{1,5},{5,1},{9,13},{13,9},{2,6},{6,2},{1... | collective-permute-start | bytes 393224 | tf_op jit(solution)/shard_map/ppermute | solution.py:48
  22.4 0.0 collective-permute-done.refs_6_.refs_1_
  22.4 0.0 collective-permute-done.3.refs_1_
  22.4 0.0 collective-permute-done.5.refs_3_
  22.4 0.0 copy-done
  22.4 2.1 %shard_map.107 = (bf16[128,2048]{1,0:T(8,128)(2,1)S(1)}, bf16[32,1536]{1,0:T(8,128)(2,1)S(1)}, bf16[32,2048]{1,0:T(8,128)(2,1)S(1)}, bf16[32,3584]{1,0:T(8,128)(...) custom-call(bf16[32,2048]{1,0:T(8,128)(2,1)S(1)} %copy-done, ...), custom_call_target="tpu_custom_call" | custom-call | tf_op jit(solution)/shard_map/pallas_call | solution.py:198
  24.5 0.0 copy-start.1
  24.5 0.1 collective-permute-start.9
  24.6 0.5 collective-permute-start.8
  25.1 2.1 %shard_map.108 = (bf16[32,1536]{1,0:T(8,128)(2,1)S(1)}, bf16[32,2048]{1,0:T(8,128)(2,1)S(1)}, bf16[32,3584]{1,0:T(8,128)(2,1)S(1)}, bf16[32,3584]{1,0:T(8,128)(2,1)S(1)}, bf16[32,3584]{1,0:T(8,128)(2,1)S(1)}) custom-call(bf16[128,2048]{1,0:T(8,128)(2,1)S(1)} %get-tuple-element.28.refs_0_, bf16[2048,3584]{1,0:T(8,128)(2,1)S(1)} %shard_map.106.refs_5_.refs_1_, ...), custom_call_target="tpu_custom_call" | custom-call | tf_op jit(solution)/shard_map/pallas_call | solution.py:198
  27.2 0.1 collective-permute-start.7
  27.3 0.0 collective-permute-done.2.refs_4_.refs_3_
  27.3 0.0 collective-permute-done.8.refs_1_
  27.3 0.0 collective-permute-done.9.refs_2_
  27.3 0.1 shard_map.109.refs_3_
  27.4 1.9 %collective-permute-start.10 = (bf16[32,3584]{1,0:T(8,128)(2,1)S(1)}, bf16[32,3584]{1,0:T(8,128)(2,1)S(1)}, u32[]{:S(2)}, u32[]{:S(2)}) collective-permute-start(bf16[32,3584]{1,0:T(8,128)(2,1)S(1)} %shard_map.109.refs_3_), channel_id=1, source_target_pairs={{0,2},{1,3},{2,0},{3,1},{4,6},{5,7},{6,4},{7,5},{8,10},{9,11},{10,... | collective-permute-start | bytes 688136 | tf_op jit(solution)/shard_map/ppermute | solution.py:213
  29.3 0.2 collective-permute-start.6
  29.5 1.1 %collective-permute-done.6.refs_1_ = bf16[32,1536]{1,0:T(8,128)(2,1)S(1)} collective-permute-done((bf16[32,1536]{1,0:T(8,128)(2,1)S(1)}, bf16[32,1536]{1,0:T(8,128)(2,1)S(1)}, u32[]{:S(2)}, u32[]{:S(2)}) %collective-permute-start.6) | collective-permute-done | bytes 98336 | tf_op jit(solution)/shard_map/ppermute | solution.py:213
  30.6 0.0 collective-permute-done.7.refs_2_
  30.6 0.1 shard_map.110.refs_5_
  30.7 0.3 collective-permute-start.15
  30.9 0.1 collective-permute-start.17
  31.0 0.0 copy-done.1
  31.0 6.0 %shard_map.111 = (bf16[128,2048]{1,0:T(8,128)(2,1)S(1)}, bf16[32,1536]{1,0:T(8,128)(2,1)S(1)}, bf16[32,2048]{1,0:T(8,128)(2,1)S(1)}, bf16[32,3584]{1,0:T(8,128)(...) custom-call(bf16[32,2048]{1,0:T(8,128)(2,1)S(1)} %copy-done.1, ...), custom_call_target="tpu_custom_call" | custom-call | tf_op jit(solution)/shard_map/pallas_call | solution.py:198
  37.0 0.5 collective-permute-start.13
  37.5 0.1 collective-permute-start.14
  37.6 0.0 collective-permute-done.10.refs_3_.refs_2_
  37.6 6.0 %shard_map.112 = (bf16[32,1536]{1,0:T(8,128)(2,1)S(1)}, bf16[32,2048]{1,0:T(8,128)(2,1)S(1)}, bf16[32,3584]{1,0:T(8,128)(2,1)S(1)}, bf16[32,3584]{1,0:T(8,128)(2,1)S(1)}, bf16[32,3584]{1,0:T(8,128)(2,1)S(1)}) custom-call(bf16[128,2048]{1,0:T(8,128)(2,1)S(1)} %get-tuple-element.35.refs_0_, bf16[2048,3584]{1,0:T(8,128)(2,1)} %refs_1_.1, ...), custom_call_target="tpu_custom_call" | custom-call | tf_op jit(solution)/shard_map/pallas_call | solution.py:198
  43.7 0.5 collective-permute-start.12
  44.2 0.0 collective-permute-done.13.refs_1_
  44.2 0.1 collective-permute-start.11
  44.2 0.0 collective-permute-done.14.refs_2_
  44.3 0.4 collective-permute-start.16
  44.7 0.0 collective-permute-done.15.refs_4_.refs_5_
  44.7 0.1 collective-permute-start.18
  44.8 0.1 shard_map.113.refs_3_
  44.8 0.6 %collective-permute-done.11.refs_1_ = bf16[32,1536]{1,0:T(8,128)(2,1)S(1)} collective-permute-done((bf16[32,1536]{1,0:T(8,128)(2,1)S(1)}, bf16[32,1536]{1,0:T(8,128)(2,1)S(1)}, u32[]{:S(2)}, u32[]{:S(2)}) %collective-permute-start.11) | collective-permute-done | bytes 98336 | tf_op jit(solution)/shard_map/ppermute | solution.py:213
  45.5 1.8 %collective-permute-start.19 = (bf16[32,3584]{1,0:T(8,128)(2,1)S(1)}, bf16[32,3584]{1,0:T(8,128)(2,1)S(1)}, u32[]{:S(2)}, u32[]{:S(2)}) collective-permute-start(bf16[32,3584]{1,0:T(8,128)(2,1)S(1)} %shard_map.113.refs_3_), channel_id=1, source_target_pairs={{0,2},{1,3},{2,0},{3,1},{4,6},{5,7},{6,4},{7,5},{8,10},{9,11},{10,... | collective-permute-start | bytes 688136 | tf_op jit(solution)/shard_map/ppermute | solution.py:213
  47.3 0.0 collective-permute-done.12.refs_2_
  47.3 0.0 collective-permute-start.20
  47.3 0.1 shard_map.114.refs_0_
  47.4 0.0 collective-permute-done.17.refs_4_
  47.4 0.3 collective-permute-start.21
  47.6 2.2 %shard_map.115 = (f32[32,128]{1,0:T(8,128)S(1)}, f32[32,128]{1,0:T(8,128)S(1)}) custom-call(s32[32]{0:T(128)} %ids.1, s32[2]{0:T(128)} %lengths.1, f32[1002,128]{1,0:T(8,128)} %bitcast.1, bf16[32,3584]{1,0:T(8,128)(2,1)S(1)} %shard_map.114.refs_0_), custom_call_target="tpu_custom_call" | custom-call | tf_op jit(solution)/shard_map/pallas_call | solution.py:98
  49.8 0.0 collective-permute-done.16.refs_1_
  49.8 0.9 %shard_map.116 = (f32[32,3584]{1,0:T(8,128)S(1)}, bf16[32,3584]{1,0:T(8,128)(2,1)}) custom-call(f32[32,128]{1,0:T(8,128)S(1)} %get-tuple-element.42.live, bf16[32,3584]{1,0:T(8,128)(2,1)S(1)} %get-tuple-element.43.refs_0_, bf16[32,3584]{1,0:T(8,128)(2,1)S(1)} %collective-permute-done.16.refs_1_, ...), custom_call_target="tpu_custom_call" | custom-call | tf_op jit(solution)/shard_map/pallas_call | solution.py:269
  50.7 0.0 collective-permute-done.18.refs_1_
  50.7 3.2 %collective-permute-done.19.refs_2_ = bf16[32,3584]{1,0:T(8,128)(2,1)S(1)} collective-permute-done((bf16[32,3584]{1,0:T(8,128)(2,1)S(1)}, bf16[32,3584]{1,0:T(8,128)(2,1)S(1)}, u32[]{:S(2)}, u32[]{:S(2)}) %collective-permute-start.19) | collective-permute-done | bytes 229408 | tf_op jit(solution)/shard_map/ppermute | solution.py:213
  53.9 0.1 shard_map.117.gated
  54.0 0.0 collective-permute-done.20.refs_1_
  54.1 4.1 %collective-permute-done.21.refs_2_ = bf16[32,3584]{1,0:T(8,128)(2,1)S(1)} collective-permute-done((bf16[32,3584]{1,0:T(8,128)(2,1)S(1)}, bf16[32,3584]{1,0:T(8,128)(2,1)S(1)}, u32[]{:S(2)}, u32[]{:S(2)}) %collective-permute-start.21) | collective-permute-done | bytes 229408 | tf_op jit(solution)/shard_map/ppermute | solution.py:213
  58.2 0.8 %shard_map.118 = bf16[32,3584]{1,0:T(8,128)(2,1)} custom-call(f32[32,3584]{1,0:T(8,128)S(1)} %get-tuple-element.48.act, f32[32,3584]{1,0:T(8,128)S(1)} %shard_map.117.gated, bf16[32,3584]{1,0:T(8,128)(2,1)S(1)} %get-tuple-element.52.refs_0_, bf16[32,3584]{1,0:T(8,128)(2,1)S(1)} %collective-permute-done.20.refs_1_, ...), custom_call_target="tpu_custom_call" | custom-call | tf_op jit(solution)/shard_map/pallas_call | solution.py:305
  (1 shorter events, 0.0 us)
Async XLA Ops:
  0.6 14.4 %collective-permute-start.4 = (bf16[32,2048]{1,0:T(8,128)(2,1)}, bf16[32,2048]{1,0:T(8,128)(2,1)S(1)}, u32[]{:S(2)}, u32[]{:S(2)}) collective-permute-start(bf16[32,2048]{1,0:T(8,128)(2,1)} %refs_0_.2), channel_id=1, source_target_pairs={{0,8},{4,12},{8,0},{12,4},{1,9},{5,13},{9,1},{13,5},{2,10},{6,14},... | collective-permute-start | bytes 393224 | tf_op jit(solution)/shard_map/ppermute | solution.py:48
  4.7 15.6 %collective-permute-start.1 = (bf16[32,2048]{1,0:T(8,128)(2,1)}, bf16[32,2048]{1,0:T(8,128)(2,1)S(1)}, u32[]{:S(2)}, u32[]{:S(2)}) collective-permute-start(bf16[32,2048]{1,0:T(8,128)(2,1)} %refs_0_.3), channel_id=1, source_target_pairs={{0,8},{4,12},{8,0},{12,4},{1,9},{5,13},{9,1},{13,5},{2,10},{6,14},... | collective-permute-start | bytes 393224 | tf_op jit(solution)/shard_map/ppermute | solution.py:48
  4.8 17.6 %collective-permute-start = (bf16[32,2048]{1,0:T(8,128)(2,1)}, bf16[32,2048]{1,0:T(8,128)(2,1)S(1)}, u32[]{:S(2)}, u32[]{:S(2)}) collective-permute-start(bf16[32,2048]{1,0:T(8,128)(2,1)} %refs_0_.3), channel_id=1, source_target_pairs={{0,4},{4,0},{8,12},{12,8},{1,5},{5,1},{9,13},{13,9},{2,6},{6,2},{1... | collective-permute-start | bytes 393224 | tf_op jit(solution)/shard_map/ppermute | solution.py:48
  6.6 15.7 %collective-permute-start.3 = (bf16[32,2048]{1,0:T(8,128)(2,1)}, bf16[32,2048]{1,0:T(8,128)(2,1)S(1)}, u32[]{:S(2)}, u32[]{:S(2)}) collective-permute-start(bf16[32,2048]{1,0:T(8,128)(2,1)} %refs_0_.2), channel_id=1, source_target_pairs={{0,4},{4,0},{8,12},{12,8},{1,5},{5,1},{9,13},{13,9},{2,6},{6,2},{1... | collective-permute-start | bytes 393224 | tf_op jit(solution)/shard_map/ppermute | solution.py:48
  15.0 7.4 %copy-start = (bf16[32,2048]{1,0:T(8,128)(2,1)S(1)}, bf16[32,2048]{1,0:T(8,128)(2,1)}, u32[]{:S(2)}) copy-start(bf16[32,2048]{1,0:T(8,128)(2,1)} %refs_0_.2) | copy-start | bytes 393220
  15.0 7.4 %collective-permute-start.5 = (bf16[32,2048]{1,0:T(8,128)(2,1)S(1)}, bf16[32,2048]{1,0:T(8,128)(2,1)S(1)}, u32[]{:S(2)}, u32[]{:S(2)}) collective-permute-start(bf16[32,2048]{1,0:T(8,128)(2,1)S(1)} %shard_map.105), channel_id=1, source_target_pairs={{0,4},{4,0},{8,12},{12,8},{1,5},{5,1},{9,13},{13,9},{2,6},{6,2},{1... | collective-permute-start | bytes 393224 | tf_op jit(solution)/shard_map/ppermute | solution.py:48
  20.3 7.0 %collective-permute-start.2 = (bf16[32,2048]{1,0:T(8,128)(2,1)S(1)}, bf16[32,2048]{1,0:T(8,128)(2,1)S(1)}, u32[]{:S(2)}, u32[]{:S(2)}) collective-permute-start(bf16[32,2048]{1,0:T(8,128)(2,1)S(1)} %collective-permute-done.1.refs_7_.refs_2_), channel_id=1, source_target_pairs={{0,4},{4,0},{8,12},{12,8},{1,5},{5,1},{9,13},{13,9},{2,6},{6,2},{1... | collective-permute-start | bytes 393224 | tf_op jit(solution)/shard_map/ppermute | solution.py:48
  24.5 6.5 %copy-start.1 = (bf16[32,2048]{1,0:T(8,128)(2,1)S(1)}, bf16[32,2048]{1,0:T(8,128)(2,1)}, u32[]{:S(2)}) copy-start(bf16[32,2048]{1,0:T(8,128)(2,1)} %refs_0_.3) | copy-start | bytes 393220
  24.5 2.8 %collective-permute-start.9 = (bf16[32,2048]{1,0:T(8,128)(2,1)S(1)}, bf16[32,2048]{1,0:T(8,128)(2,1)S(1)}, u32[]{:S(2)}, u32[]{:S(2)}) collective-permute-start(bf16[32,2048]{1,0:T(8,128)(2,1)S(1)} %get-tuple-element.34), channel_id=1, source_target_pairs={{0,1},{1,0},{2,3},{3,2},{4,5},{5,4},{6,7},{7,6},{8,9},{9,8},{10,11... | collective-permute-start | bytes 393224 | tf_op jit(solution)/shard_map/ppermute | solution.py:213
  24.6 2.7 %collective-permute-start.8 = (bf16[32,1536]{1,0:T(8,128)(2,1)S(1)}, bf16[32,1536]{1,0:T(8,128)(2,1)S(1)}, u32[]{:S(2)}, u32[]{:S(2)}) collective-permute-start(bf16[32,1536]{1,0:T(8,128)(2,1)S(1)} %get-tuple-element.29.refs_2_), channel_id=1, source_target_pairs={{0,1},{1,0},{2,3},{3,2},{4,5},{5,4},{6,7},{7,6},{8,9},{9,8},{10,11... | collective-permute-start | bytes 294920 | tf_op jit(solution)/shard_map/ppermute | solution.py:213
  27.2 3.4 %collective-permute-start.7 = (bf16[32,2048]{1,0:T(8,128)(2,1)S(1)}, bf16[32,2048]{1,0:T(8,128)(2,1)S(1)}, u32[]{:S(2)}, u32[]{:S(2)}) collective-permute-start(bf16[32,2048]{1,0:T(8,128)(2,1)S(1)} %get-tuple-element.32), channel_id=1, source_target_pairs={{0,1},{1,0},{2,3},{3,2},{4,5},{5,4},{6,7},{7,6},{8,9},{9,8},{10,11... | collective-permute-start | bytes 393224 | tf_op jit(solution)/shard_map/ppermute | solution.py:213
  27.4 10.2 %collective-permute-start.10 = (bf16[32,3584]{1,0:T(8,128)(2,1)S(1)}, bf16[32,3584]{1,0:T(8,128)(2,1)S(1)}, u32[]{:S(2)}, u32[]{:S(2)}) collective-permute-start(bf16[32,3584]{1,0:T(8,128)(2,1)S(1)} %shard_map.109.refs_3_), channel_id=1, source_target_pairs={{0,2},{1,3},{2,0},{3,1},{4,6},{5,7},{6,4},{7,5},{8,10},{9,11},{10,... | collective-permute-start | bytes 688136 | tf_op jit(solution)/shard_map/ppermute | solution.py:213
  29.3 1.3 %collective-permute-start.6 = (bf16[32,1536]{1,0:T(8,128)(2,1)S(1)}, bf16[32,1536]{1,0:T(8,128)(2,1)S(1)}, u32[]{:S(2)}, u32[]{:S(2)}) collective-permute-start(bf16[32,1536]{1,0:T(8,128)(2,1)S(1)} %get-tuple-element.31.refs_3_), channel_id=1, source_target_pairs={{0,1},{1,0},{2,3},{3,2},{4,5},{5,4},{6,7},{7,6},{8,9},{9,8},{10,11... | collective-permute-start | bytes 294920 | tf_op jit(solution)/shard_map/ppermute | solution.py:213
  30.7 14.0 %collective-permute-start.15 = (bf16[32,3584]{1,0:T(8,128)(2,1)S(1)}, bf16[32,3584]{1,0:T(8,128)(2,1)S(1)}, u32[]{:S(2)}, u32[]{:S(2)}) collective-permute-start(bf16[32,3584]{1,0:T(8,128)(2,1)S(1)} %shard_map.110.refs_5_), channel_id=1, source_target_pairs={{0,2},{1,3},{2,0},{3,1},{4,6},{5,7},{6,4},{7,5},{8,10},{9,11},{10,... | collective-permute-start | bytes 688136 | tf_op jit(solution)/shard_map/ppermute | solution.py:213
  30.9 16.5 %collective-permute-start.17 = (bf16[32,3584]{1,0:T(8,128)(2,1)S(1)}, bf16[32,3584]{1,0:T(8,128)(2,1)S(1)}, u32[]{:S(2)}, u32[]{:S(2)}) collective-permute-start(bf16[32,3584]{1,0:T(8,128)(2,1)S(1)} %get-tuple-element.46), channel_id=1, source_target_pairs={{0,1},{1,0},{2,3},{3,2},{4,5},{5,4},{6,7},{7,6},{8,9},{9,8},{10,11... | collective-permute-start | bytes 688136 | tf_op jit(solution)/shard_map/ppermute | solution.py:213
  37.0 7.1 %collective-permute-start.13 = (bf16[32,1536]{1,0:T(8,128)(2,1)S(1)}, bf16[32,1536]{1,0:T(8,128)(2,1)S(1)}, u32[]{:S(2)}, u32[]{:S(2)}) collective-permute-start(bf16[32,1536]{1,0:T(8,128)(2,1)S(1)} %get-tuple-element.36.refs_2_), channel_id=1, source_target_pairs={{0,1},{1,0},{2,3},{3,2},{4,5},{5,4},{6,7},{7,6},{8,9},{9,8},{10,11... | collective-permute-start | bytes 294920 | tf_op jit(solution)/shard_map/ppermute | solution.py:213
  37.5 6.7 %collective-permute-start.14 = (bf16[32,2048]{1,0:T(8,128)(2,1)S(1)}, bf16[32,2048]{1,0:T(8,128)(2,1)S(1)}, u32[]{:S(2)}, u32[]{:S(2)}) collective-permute-start(bf16[32,2048]{1,0:T(8,128)(2,1)S(1)} %get-tuple-element.41), channel_id=1, source_target_pairs={{0,1},{1,0},{2,3},{3,2},{4,5},{5,4},{6,7},{7,6},{8,9},{9,8},{10,11... | collective-permute-start | bytes 393224 | tf_op jit(solution)/shard_map/ppermute | solution.py:213
  43.7 3.6 %collective-permute-start.12 = (bf16[32,2048]{1,0:T(8,128)(2,1)S(1)}, bf16[32,2048]{1,0:T(8,128)(2,1)S(1)}, u32[]{:S(2)}, u32[]{:S(2)}) collective-permute-start(bf16[32,2048]{1,0:T(8,128)(2,1)S(1)} %get-tuple-element.39), channel_id=1, source_target_pairs={{0,1},{1,0},{2,3},{3,2},{4,5},{5,4},{6,7},{7,6},{8,9},{9,8},{10,11... | collective-permute-start | bytes 393224 | tf_op jit(solution)/shard_map/ppermute | solution.py:213
  44.2 1.3 %collective-permute-start.11 = (bf16[32,1536]{1,0:T(8,128)(2,1)S(1)}, bf16[32,1536]{1,0:T(8,128)(2,1)S(1)}, u32[]{:S(2)}, u32[]{:S(2)}) collective-permute-start(bf16[32,1536]{1,0:T(8,128)(2,1)S(1)} %get-tuple-element.38.refs_3_), channel_id=1, source_target_pairs={{0,1},{1,0},{2,3},{3,2},{4,5},{5,4},{6,7},{7,6},{8,9},{9,8},{10,11... | collective-permute-start | bytes 294920 | tf_op jit(solution)/shard_map/ppermute | solution.py:213
  44.3 5.5 %collective-permute-start.16 = (bf16[32,3584]{1,0:T(8,128)(2,1)S(1)}, bf16[32,3584]{1,0:T(8,128)(2,1)S(1)}, u32[]{:S(2)}, u32[]{:S(2)}) collective-permute-start(bf16[32,3584]{1,0:T(8,128)(2,1)S(1)} %get-tuple-element.44), channel_id=1, source_target_pairs={{0,1},{1,0},{2,3},{3,2},{4,5},{5,4},{6,7},{7,6},{8,9},{9,8},{10,11... | collective-permute-start | bytes 688136 | tf_op jit(solution)/shard_map/ppermute | solution.py:213
  44.7 6.1 %collective-permute-start.18 = (bf16[32,3584]{1,0:T(8,128)(2,1)S(1)}, bf16[32,3584]{1,0:T(8,128)(2,1)S(1)}, u32[]{:S(2)}, u32[]{:S(2)}) collective-permute-start(bf16[32,3584]{1,0:T(8,128)(2,1)S(1)} %get-tuple-element.51), channel_id=1, source_target_pairs={{0,1},{1,0},{2,3},{3,2},{4,5},{5,4},{6,7},{7,6},{8,9},{9,8},{10,11... | collective-permute-start | bytes 688136 | tf_op jit(solution)/shard_map/ppermute | solution.py:213
  45.5 8.4 %collective-permute-start.19 = (bf16[32,3584]{1,0:T(8,128)(2,1)S(1)}, bf16[32,3584]{1,0:T(8,128)(2,1)S(1)}, u32[]{:S(2)}, u32[]{:S(2)}) collective-permute-start(bf16[32,3584]{1,0:T(8,128)(2,1)S(1)} %shard_map.113.refs_3_), channel_id=1, source_target_pairs={{0,2},{1,3},{2,0},{3,1},{4,6},{5,7},{6,4},{7,5},{8,10},{9,11},{10,... | collective-permute-start | bytes 688136 | tf_op jit(solution)/shard_map/ppermute | solution.py:213
  47.3 6.7 %collective-permute-start.20 = (bf16[32,3584]{1,0:T(8,128)(2,1)S(1)}, bf16[32,3584]{1,0:T(8,128)(2,1)S(1)}, u32[]{:S(2)}, u32[]{:S(2)}) collective-permute-start(bf16[32,3584]{1,0:T(8,128)(2,1)S(1)} %get-tuple-element.53), channel_id=1, source_target_pairs={{0,1},{1,0},{2,3},{3,2},{4,5},{5,4},{6,7},{7,6},{8,9},{9,8},{10,11... | collective-permute-start | bytes 688136 | tf_op jit(solution)/shard_map/ppermute | solution.py:213
  47.4 10.8 %collective-permute-start.21 = (bf16[32,3584]{1,0:T(8,128)(2,1)S(1)}, bf16[32,3584]{1,0:T(8,128)(2,1)S(1)}, u32[]{:S(2)}, u32[]{:S(2)}) collective-permute-start(bf16[32,3584]{1,0:T(8,128)(2,1)S(1)} %shard_map.114.refs_0_), channel_id=1, source_target_pairs={{0,2},{1,3},{2,0},{3,1},{4,6},{5,7},{6,4},{7,5},{8,10},{9,11},{10,... | collective-permute-start | bytes 688136 | tf_op jit(solution)/shard_map/ppermute | solution.py:213

commit v8 on v7

--- a/solution.py
+++ b/solution.py
@@ -12,7 +12,6 @@
 IN_SMEM = pl.BlockSpec(memory_space=pltpu.SMEM)
 ANYWHERE = pl.BlockSpec(memory_space=pl.ANY)
 LANES = 128
-IN_FLIGHT = 4
 
 
 def in_hbm(array):
@@ -146,26 +145,13 @@
 
 
 def product_kernel(pieces, after, narrow, blocks, *refs):
-    tokens, matrix, refs = refs[:pieces], refs[pieces], refs[pieces + 1 + after :]
-    tiles, copies = column_tiles(matrix.shape[1]), []
-    if len(blocks) < len(refs) - (pieces > 1):
-        here, sems = refs[-2:]
-        refs = refs[:-2]
-        for i, cols in enumerate(tiles):
-            copies.append(pltpu.make_async_copy(matrix.at[:, cols], here.at[:, cols], sems.at[i]))
-        matrix = here
-    for copy in copies[:IN_FLIGHT]:
-        copy.start()
+    tokens, matrix, outs = refs[:pieces], refs[pieces], refs[pieces + 1 + after :]
     if pieces > 1:
-        place_rows(tokens, refs[0], narrow)
-        tokens, refs = refs[:1], refs[1:]
-    for i, cols in enumerate(tiles):
-        if copies:
-            copies[i].wait()
-        if i + IN_FLIGHT < len(copies):
-            copies[i + IN_FLIGHT].start()
+        place_rows(tokens, outs[0], narrow)
+        tokens, outs = outs[:1], outs[1:]
+    for cols in column_tiles(matrix.shape[1]):
         total = jnp.dot(tokens[0][...], matrix[:, cols], preferred_element_type=jnp.float32)
-        for out, (row, col) in zip(refs, blocks):
+        for out, (row, col) in zip(outs, blocks):
             if col <= cols.start and cols.stop <= col + out.shape[1]:
                 value = total[row : row + out.shape[0]].astype(out.dtype)
                 out[:, cols.start - col : cols.stop - col] = value
@@ -179,7 +165,7 @@
     return sizes + [left]
 
 
-def product(tokens, matrix, held, narrow, after):
+def product(tokens, matrix, narrow, after):
     placing = len(tokens) > 1
     total = sum(t.shape[0] for t in tokens)
     depth, width = matrix.shape
@@ -190,20 +176,14 @@
     blocks = [(sum(sizes[:k]), first) for k, first, _ in sent]
     blocks += [(total // 2 + sum(sizes[:k]), 0) for k in range(len(sizes))]
     shapes = [(sizes[k], count) for k, _, count in sent] + [(size, width) for size in sizes]
-    stream = [
-        pltpu.VMEM(matrix.shape, matrix.dtype),
-        pltpu.SemaphoreType.DMA((len(column_tiles(width)),)),
-    ]
-    room = 4 + (0 if held else 1 + matrix.size * matrix.dtype.itemsize >> 20)
     found = pl.pallas_call(
         functools.partial(product_kernel, len(tokens), len(after), narrow, blocks),
         out_shape=[jax.ShapeDtypeStruct((total, depth), tokens[0].dtype)] * placing
         + [jax.ShapeDtypeStruct(shape, jnp.bfloat16) for shape in shapes],
-        in_specs=[IN_VMEM] * len(tokens) + [IN_VMEM if held else ANYWHERE] + [ANYWHERE] * len(after),
+        in_specs=[IN_VMEM] * len(tokens) + [IN_VMEM] + [ANYWHERE] * len(after),
         out_specs=[IN_VMEM] * (placing + len(shapes)),
-        scratch_shapes=[] if held else stream,
-        compiler_params=pltpu.CompilerParams(vmem_limit_bytes=room << 20),
-    )(*tokens, (in_vmem if held else in_hbm)(matrix), *after)
+        compiler_params=pltpu.CompilerParams(vmem_limit_bytes=4 << 20),
+    )(*tokens, in_vmem(matrix), *after)
     rows, found = (found[:1], found[1:]) if placing else (tokens, found)
     sends = [(array, k, first) for array, (k, first, _) in zip(found, sent)]
     return rows, sends, found[len(sent) :]
@@ -252,12 +232,12 @@
     return sent, addends(keeps, came, len(keeps) - 1)
 
 
-def target_kernel(starts, live, *refs):
+def target_kernel(places, live, *refs):
     act, out = refs[-2:]
-    count = len(starts[0])
+    count = len(places[0])
     for cols in column_tiles(out.shape[1]):
-        gate = added(refs[:count], starts[0], out.shape[0], cols)
-        upper = added(refs[count:], starts[1], out.shape[0], cols)
+        gate = added(refs[:count], places[0], out.shape[0], cols)
+        upper = added(refs[count:], places[1], out.shape[0], cols)
         value = live[:, :1] * (jax.nn.silu(gate) * upper)
         act[:, cols] = value
         out[:, cols] = value.astype(out.dtype)
@@ -318,18 +298,17 @@
     source_pieces = gather_pieces(source_states, "wide", wide)
     target_up = load(target_up, (target_gate, target_pieces[wide // 2]))
 
-    after = (target_up, source_pieces[1], source_pieces[wide // 2])
-    rows, sends, keeps = product(target_pieces, target_gate, True, narrow, after)
-    _, up_sends, up_keeps = product(rows, target_up, True, narrow, (sends[0][0],))
-    sent, target_g = finish(sends, keeps, narrow, (up_sends[0][0], source_pieces[-1]))
+    after = (target_up,)
+    rows, sends, keeps = product(target_pieces, target_gate, narrow, after)
+    _, up_sends, up_keeps = product(rows, target_up, narrow, (sends[0][0],))
+    sent, target_g = finish(sends, keeps, narrow, (up_sends[0][0], *source_pieces[1:]))
     sent, target_u = finish(up_sends, up_keeps, narrow, (sent,))
 
-    rows, sends, keeps = product(source_pieces, source_gate, False, narrow, (sent,))
+    rows, sends, keeps = product(source_pieces, source_gate, narrow, (sent,))
     after = (sends[0][0], target_g[0][-1])
-    _, up_sends, up_keeps = product(rows, source_up, False, narrow, after)
-    after = (up_sends[0][0], target_u[0][-1])
-    sent, source_g = finish(sends, keeps, narrow, after)
-    sent, source_u = finish(up_sends, up_keeps, narrow, (sent,))
+    _, up_sends, up_keeps = product(rows, source_up, narrow, after)
+    sent, source_g = finish(sends, keeps, narrow, (up_sends[0][0],))
+    sent, source_u = finish(up_sends, up_keeps, narrow, (sent, target_u[0][-1]))
     live, weight = look_up(token_ids, lengths, ratio_weight, (sent,))
     act, target_out = target_end(live, target_g, target_u)
     gated = source_middle(live, weight, source_g)

time: 59.2 us -> 52.7 us (0.89)
  Pallas kernels: 30.9 us -> 23 us
  waiting for transfers between devices: 12 us -> 13.3 us
    pallas_call x4, Pallas kernels: 16.3 us -> 8.36 us  [product(): pl.pallas_call(functools.partial(product_kernel, len(tokens), len(after),...]
    ppermute x16, waiting for transfers between devices: 9.07 us -> 12.3 us  [exchange(): lax.ppermute(array, 'narrow', [(i, i ^ 1 << step) for i in range(size)])]
    ppermute x6, waiting for transfers between devices: 2.97 us -> 1.07 us  [gather_pieces(): pieces.append(lax.ppermute(piece, axis, pairs))]
  transfers between devices with their start and end apart: 22 -> 22, of which waited for: 5 -> 6; matrix products, arithmetic and copies ran while one was open for 0% -> 0% of each run, Pallas kernels for 51% -> 42%
where the time goes in v8:
time: 52.7 us; the launch traced here: 52.5 us
  Pallas kernels  23 us (44%)
  starting transfers between devices  15.3 us (29%)
  waiting for transfers between devices  13.3 us (25%)
  between operations  0.88 us (2%)
    ppermute x16, waiting for transfers between devices, exchange(): lax.ppermute(array, 'narrow', [(i, i ^ 1 << step) for i in range(size)])  12.3 us
    pallas_call x2, Pallas kernels, load(): pl.pallas_call(load_kernel, out_shape=pltpu.VMEM(matrix.shape, matrix.dty...  10.4 us
    pallas_call x4, Pallas kernels, product(): pl.pallas_call(functools.partial(product_kernel, len(tokens), len(after),...  8.36 us
    ppermute x6, starting transfers between devices, gather_pieces(): pieces.append(lax.ppermute(piece, axis, pairs))  8.34 us
    ppermute x16, starting transfers between devices, exchange(): lax.ppermute(array, 'narrow', [(i, i ^ 1 << step) for i in range(size)])  6.92 us
    pallas_call x1, Pallas kernels, look_up(): pl.pallas_call(functools.partial(look_up_kernel, ids.shape[0] // lengths....  2.16 us
    ppermute x6, waiting for transfers between devices, gather_pieces(): pieces.append(lax.ppermute(piece, axis, pairs))  1.07 us
  transfers between devices with their start and end apart: 22, of which 6 were waited for; matrix products, arithmetic and copies ran while one was open for 0% of the time, Pallas kernels for 42%

profile of v8, /device:TPU:0, one launch (start us, length us, event | category | flops | bytes accessed | tf_op | source)
XLA Modules:
  0.0 52.5 jit_solution(8413150546462527540)
XLA Ops:
  0.6 4.1 %collective-permute-start.4 = (bf16[32,2048]{1,0:T(8,128)(2,1)}, bf16[32,2048]{1,0:T(8,128)(2,1)S(1)}, u32[]{:S(2)}, u32[]{:S(2)}) collective-permute-start(bf16[32,2048]{1,0:T(8,128)(2,1)} %refs_0_.2), channel_id=1, source_target_pairs={{0,8},{4,12},{8,0},{12,4},{1,9},{5,13},{9,1},{13,5},{2,10},{6,14},... | collective-permute-start | bytes 393224 | tf_op jit(solution)/shard_map/ppermute | solution.py:47
  4.7 1.6 %collective-permute-start.3 = (bf16[32,2048]{1,0:T(8,128)(2,1)}, bf16[32,2048]{1,0:T(8,128)(2,1)S(1)}, u32[]{:S(2)}, u32[]{:S(2)}) collective-permute-start(bf16[32,2048]{1,0:T(8,128)(2,1)} %refs_0_.2), channel_id=1, source_target_pairs={{0,4},{4,0},{8,12},{12,8},{1,5},{5,1},{9,13},{13,9},{2,6},{6,2},{1... | collective-permute-start | bytes 393224 | tf_op jit(solution)/shard_map/ppermute | solution.py:47
  6.3 0.3 collective-permute-start.1
  6.6 5.2 %shard_map.104.refs_0_.refs_4_ = bf16[2048,3584]{1,0:T(8,128)(2,1)S(1)} custom-call(bf16[2048,3584]{1,0:T(8,128)(2,1)} %matrix.2), custom_call_target="tpu_custom_call" | custom-call | tf_op jit(solution)/shard_map/pallas_call | solution.py:119
  11.8 0.0 copy-start.1
  11.8 1.1 %collective-permute-done.4.piece.refs_1_.refs_2_ = bf16[32,2048]{1,0:T(8,128)(2,1)S(1)} collective-permute-done((bf16[32,2048]{1,0:T(8,128)(2,1)}, bf16[32,2048]{1,0:T(8,128)(2,1)S(1)}, u32[]{:S(2)}, u32[]{:S(2)}) %collective-permute-start.4) | collective-permute-done | bytes 131104 | tf_op jit(solution)/shard_map/ppermute | solution.py:47
  12.9 0.0 copy-start
  12.9 0.2 collective-permute-start.5
  13.2 1.9 %collective-permute-start = (bf16[32,2048]{1,0:T(8,128)(2,1)S(1)}, bf16[32,2048]{1,0:T(8,128)(2,1)S(1)}, u32[]{:S(2)}, u32[]{:S(2)}) collective-permute-start(bf16[32,2048]{1,0:T(8,128)(2,1)S(1)} %copy-done.1), channel_id=1, source_target_pairs={{0,4},{4,0},{8,12},{12,8},{1,5},{5,1},{9,13},{13,9},{2,6},{6,2},{1... | collective-permute-start | bytes 393224 | tf_op jit(solution)/shard_map/ppermute | solution.py:47
  15.0 5.2 %shard_map.106.refs_5_.refs_1_ = bf16[2048,3584]{1,0:T(8,128)(2,1)S(1)} custom-call(bf16[2048,3584]{1,0:T(8,128)(2,1)} %matrix.3, bf16[2048,3584]{1,0:T(8,128)(2,1)S(1)} %shard_map.104.refs_0_.refs_4_, bf16[32,2048]{1,0:T(8,128)(2,1)S(1)} %collective-permute-done.4.piece.refs_1_.refs_2_), custom_call_target="tpu_custom_call" | custom-call | tf_op jit(solution)/shard_map/pallas_call | solution.py:119
  20.2 0.0 collective-permute-done.1.refs_5_.refs_2_
  20.2 0.2 collective-permute-start.2
  20.5 0.0 collective-permute-done.3.refs_1_
  20.5 0.0 collective-permute-done.5.refs_3_
  20.5 0.0 slice-start
  20.5 0.0 slice-start.1
  20.5 0.0 slice-start.2
  20.5 2.1 %shard_map.107 = (bf16[128,2048]{1,0:T(8,128)(2,1)S(1)}, bf16[32,1536]{1,0:T(8,128)(2,1)S(1)}, bf16[32,2048]{1,0:T(8,128)(2,1)S(1)}, bf16[32,3584]{1,0:T(8,128)(...) custom-call(bf16[32,2048]{1,0:T(8,128)(2,1)S(1)} %copy-done, ...), custom_call_target="tpu_custom_call" | custom-call | tf_op jit(solution)/shard_map/pallas_call | solution.py:179
  22.6 0.1 collective-permute-start.9
  22.7 0.5 collective-permute-start.8
  23.2 2.1 %shard_map.108 = (bf16[32,1536]{1,0:T(8,128)(2,1)S(1)}, bf16[32,2048]{1,0:T(8,128)(2,1)S(1)}, bf16[32,3584]{1,0:T(8,128)(2,1)S(1)}, bf16[32,3584]{1,0:T(8,128)(2,1)S(1)}, bf16[32,3584]{1,0:T(8,128)(2,1)S(1)}) custom-call(bf16[128,2048]{1,0:T(8,128)(2,1)S(1)} %get-tuple-element.28.refs_0_, bf16[2048,3584]{1,0:T(8,128)(2,1)S(1)} %shard_map.106.refs_5_.refs_1_, ...), custom_call_target="tpu_custom_call" | custom-call | tf_op jit(solution)/shard_map/pallas_call | solution.py:179
  25.3 0.1 collective-permute-start.7
  25.4 0.0 collective-permute-done.refs_4_.refs_1_
  25.4 0.0 collective-permute-done.2.refs_6_.refs_3_
  25.4 0.0 collective-permute-done.8.refs_1_
  25.4 0.0 collective-permute-done.9.refs_2_
  25.4 0.0 slice-start.6
  25.5 0.1 shard_map.109.refs_3_
  25.5 2.1 %collective-permute-start.10 = (bf16[32,3584]{1,0:T(8,128)(2,1)S(1)}, bf16[32,3584]{1,0:T(8,128)(2,1)S(1)}, u32[]{:S(2)}, u32[]{:S(2)}) collective-permute-start(bf16[32,3584]{1,0:T(8,128)(2,1)S(1)} %shard_map.109.refs_3_), channel_id=1, source_target_pairs={{0,2},{1,3},{2,0},{3,1},{4,6},{5,7},{6,4},{7,5},{8,10},{9,11},{10,... | collective-permute-start | bytes 688136 | tf_op jit(solution)/shard_map/ppermute | solution.py:193
  27.6 0.2 collective-permute-start.6
  27.8 1.1 %collective-permute-done.6.refs_1_ = bf16[32,1536]{1,0:T(8,128)(2,1)S(1)} collective-permute-done((bf16[32,1536]{1,0:T(8,128)(2,1)S(1)}, bf16[32,1536]{1,0:T(8,128)(2,1)S(1)}, u32[]{:S(2)}, u32[]{:S(2)}) %collective-permute-start.6) | collective-permute-done | bytes 98336 | tf_op jit(solution)/shard_map/ppermute | solution.py:193
  28.9 0.0 collective-permute-done.7.refs_2_
  28.9 0.1 shard_map.110.refs_5_
  29.0 0.2 collective-permute-start.15
  29.2 0.1 collective-permute-start.17
  29.3 2.1 %shard_map.111 = (bf16[128,2048]{1,0:T(8,128)(2,1)S(1)}, bf16[32,1536]{1,0:T(8,128)(2,1)S(1)}, bf16[32,2048]{1,0:T(8,128)(2,1)S(1)}, bf16[32,3584]{1,0:T(8,128)(...) custom-call(bf16[32,2048]{1,0:T(8,128)(2,1)S(1)} %copy-done.1, ...), custom_call_target="tpu_custom_call" | custom-call | tf_op jit(solution)/shard_map/pallas_call | solution.py:179
  31.5 0.5 collective-permute-start.13
  31.9 0.1 collective-permute-start.14
  32.0 2.1 %collective-permute-done.10.refs_3_.refs_2_ = bf16[32,3584]{1,0:T(8,128)(2,1)S(1)} collective-permute-done((bf16[32,3584]{1,0:T(8,128)(2,1)S(1)}, bf16[32,3584]{1,0:T(8,128)(2,1)S(1)}, u32[]{:S(2)}, u32[]{:S(2)}) %collective-permute-start.10) | collective-permute-done | bytes 229408 | tf_op jit(solution)/shard_map/ppermute | solution.py:193
  34.1 2.1 %shard_map.112 = (bf16[32,1536]{1,0:T(8,128)(2,1)S(1)}, bf16[32,2048]{1,0:T(8,128)(2,1)S(1)}, bf16[32,3584]{1,0:T(8,128)(2,1)S(1)}, bf16[32,3584]{1,0:T(8,128)(2,1)S(1)}, bf16[32,3584]{1,0:T(8,128)(2,1)S(1)}) custom-call(bf16[128,2048]{1,0:T(8,128)(2,1)S(1)} %get-tuple-element.35.refs_0_, bf16[2048,3584]{1,0:T(8,128)(2,1)S(1)} %bitcast.4, ...), custom_call_target="tpu_custom_call" | custom-call | tf_op jit(solution)/shard_map/pallas_call | solution.py:179
  36.2 0.1 collective-permute-start.12
  36.3 0.0 collective-permute-done.13.refs_1_
  36.3 0.5 collective-permute-start.11
  36.8 0.0 collective-permute-done.14.refs_2_
  36.8 0.1 collective-permute-start.16
  36.9 0.1 shard_map.113.refs_3_
  36.9 1.8 %collective-permute-done.15.refs_4_.refs_5_ = bf16[32,3584]{1,0:T(8,128)(2,1)S(1)} collective-permute-done((bf16[32,3584]{1,0:T(8,128)(2,1)S(1)}, bf16[32,3584]{1,0:T(8,128)(2,1)S(1)}, u32[]{:S(2)}, u32[]{:S(2)}) %collective-permute-start.15) | collective-permute-done | bytes 229408 | tf_op jit(solution)/shard_map/ppermute | solution.py:193
  38.7 0.0 collective-permute-start.18
  38.7 0.0 collective-permute-done.11.refs_1_
  38.7 1.8 %collective-permute-start.19 = (bf16[32,3584]{1,0:T(8,128)(2,1)S(1)}, bf16[32,3584]{1,0:T(8,128)(2,1)S(1)}, u32[]{:S(2)}, u32[]{:S(2)}) collective-permute-start(bf16[32,3584]{1,0:T(8,128)(2,1)S(1)} %shard_map.113.refs_3_), channel_id=1, source_target_pairs={{0,2},{1,3},{2,0},{3,1},{4,6},{5,7},{6,4},{7,5},{8,10},{9,11},{10,... | collective-permute-start | bytes 688136 | tf_op jit(solution)/shard_map/ppermute | solution.py:193
  40.5 0.0 collective-permute-done.12.refs_2_
  40.5 0.2 collective-permute-start.20
  40.7 0.1 shard_map.114.refs_0_
  40.8 0.0 collective-permute-done.17.refs_4_
  40.8 0.4 collective-permute-start.21
  41.2 2.2 %shard_map.115 = (f32[32,128]{1,0:T(8,128)S(1)}, f32[32,128]{1,0:T(8,128)S(1)}) custom-call(s32[32]{0:T(128)} %ids.1, s32[2]{0:T(128)} %lengths.1, f32[1002,128]{1,0:T(8,128)} %bitcast.5, bf16[32,3584]{1,0:T(8,128)(2,1)S(1)} %shard_map.114.refs_0_), custom_call_target="tpu_custom_call" | custom-call | tf_op jit(solution)/shard_map/pallas_call | solution.py:97
  43.4 0.0 collective-permute-done.16.refs_1_
  43.4 0.9 %shard_map.116 = (f32[32,3584]{1,0:T(8,128)S(1)}, bf16[32,3584]{1,0:T(8,128)(2,1)}) custom-call(f32[32,128]{1,0:T(8,128)S(1)} %get-tuple-element.42.live, bf16[32,3584]{1,0:T(8,128)(2,1)S(1)} %get-tuple-element.43.refs_0_, bf16[32,3584]{1,0:T(8,128)(2,1)S(1)} %collective-permute-done.16.refs_1_, ...), custom_call_target="tpu_custom_call" | custom-call | tf_op jit(solution)/shard_map/pallas_call | solution.py:249
  44.3 0.0 collective-permute-done.18.refs_1_
  44.3 2.8 %collective-permute-done.19.refs_2_ = bf16[32,3584]{1,0:T(8,128)(2,1)S(1)} collective-permute-done((bf16[32,3584]{1,0:T(8,128)(2,1)S(1)}, bf16[32,3584]{1,0:T(8,128)(2,1)S(1)}, u32[]{:S(2)}, u32[]{:S(2)}) %collective-permute-start.19) | collective-permute-done | bytes 229408 | tf_op jit(solution)/shard_map/ppermute | solution.py:193
  47.2 0.1 shard_map.117.gated
  47.3 0.0 collective-permute-done.20.refs_1_
  47.3 4.4 %collective-permute-done.21.refs_2_ = bf16[32,3584]{1,0:T(8,128)(2,1)S(1)} collective-permute-done((bf16[32,3584]{1,0:T(8,128)(2,1)S(1)}, bf16[32,3584]{1,0:T(8,128)(2,1)S(1)}, u32[]{:S(2)}, u32[]{:S(2)}) %collective-permute-start.21) | collective-permute-done | bytes 229408 | tf_op jit(solution)/shard_map/ppermute | solution.py:193
  51.7 0.8 %shard_map.118 = bf16[32,3584]{1,0:T(8,128)(2,1)} custom-call(f32[32,3584]{1,0:T(8,128)S(1)} %get-tuple-element.48.act, f32[32,3584]{1,0:T(8,128)S(1)} %shard_map.117.gated, bf16[32,3584]{1,0:T(8,128)(2,1)S(1)} %get-tuple-element.52.refs_0_, bf16[32,3584]{1,0:T(8,128)(2,1)S(1)} %collective-permute-done.20.refs_1_, ...), custom_call_target="tpu_custom_call" | custom-call | tf_op jit(solution)/shard_map/pallas_call | solution.py:285
  (17 shorter events, 0.0 us)
Async XLA Ops:
  0.6 12.3 %collective-permute-start.4 = (bf16[32,2048]{1,0:T(8,128)(2,1)}, bf16[32,2048]{1,0:T(8,128)(2,1)S(1)}, u32[]{:S(2)}, u32[]{:S(2)}) collective-permute-start(bf16[32,2048]{1,0:T(8,128)(2,1)} %refs_0_.2), channel_id=1, source_target_pairs={{0,8},{4,12},{8,0},{12,4},{1,9},{5,13},{9,1},{13,5},{2,10},{6,14},... | collective-permute-start | bytes 393224 | tf_op jit(solution)/shard_map/ppermute | solution.py:47
  4.7 15.7 %collective-permute-start.3 = (bf16[32,2048]{1,0:T(8,128)(2,1)}, bf16[32,2048]{1,0:T(8,128)(2,1)S(1)}, u32[]{:S(2)}, u32[]{:S(2)}) collective-permute-start(bf16[32,2048]{1,0:T(8,128)(2,1)} %refs_0_.2), channel_id=1, source_target_pairs={{0,4},{4,0},{8,12},{12,8},{1,5},{5,1},{9,13},{13,9},{2,6},{6,2},{1... | collective-permute-start | bytes 393224 | tf_op jit(solution)/shard_map/ppermute | solution.py:47
  6.3 13.9 %collective-permute-start.1 = (bf16[32,2048]{1,0:T(8,128)(2,1)}, bf16[32,2048]{1,0:T(8,128)(2,1)S(1)}, u32[]{:S(2)}, u32[]{:S(2)}) collective-permute-start(bf16[32,2048]{1,0:T(8,128)(2,1)} %refs_0_.3), channel_id=1, source_target_pairs={{0,8},{4,12},{8,0},{12,4},{1,9},{5,13},{9,1},{13,5},{2,10},{6,14},... | collective-permute-start | bytes 393224 | tf_op jit(solution)/shard_map/ppermute | solution.py:47
  11.8 1.3 %copy-start.1 = (bf16[32,2048]{1,0:T(8,128)(2,1)S(1)}, bf16[32,2048]{1,0:T(8,128)(2,1)}, u32[]{:S(2)}) copy-start(bf16[32,2048]{1,0:T(8,128)(2,1)} %refs_0_.3) | copy-start | bytes 393220
  12.9 7.6 %copy-start = (bf16[32,2048]{1,0:T(8,128)(2,1)S(1)}, bf16[32,2048]{1,0:T(8,128)(2,1)}, u32[]{:S(2)}) copy-start(bf16[32,2048]{1,0:T(8,128)(2,1)} %refs_0_.2) | copy-start | bytes 393220
  12.9 7.5 %collective-permute-start.5 = (bf16[32,2048]{1,0:T(8,128)(2,1)S(1)}, bf16[32,2048]{1,0:T(8,128)(2,1)S(1)}, u32[]{:S(2)}, u32[]{:S(2)}) collective-permute-start(bf16[32,2048]{1,0:T(8,128)(2,1)S(1)} %shard_map.105), channel_id=1, source_target_pairs={{0,4},{4,0},{8,12},{12,8},{1,5},{5,1},{9,13},{13,9},{2,6},{6,2},{1... | collective-permute-start | bytes 393224 | tf_op jit(solution)/shard_map/ppermute | solution.py:47
  13.2 12.3 %collective-permute-start = (bf16[32,2048]{1,0:T(8,128)(2,1)S(1)}, bf16[32,2048]{1,0:T(8,128)(2,1)S(1)}, u32[]{:S(2)}, u32[]{:S(2)}) collective-permute-start(bf16[32,2048]{1,0:T(8,128)(2,1)S(1)} %copy-done.1), channel_id=1, source_target_pairs={{0,4},{4,0},{8,12},{12,8},{1,5},{5,1},{9,13},{13,9},{2,6},{6,2},{1... | collective-permute-start | bytes 393224 | tf_op jit(solution)/shard_map/ppermute | solution.py:47
  20.2 5.2 %collective-permute-start.2 = (bf16[32,2048]{1,0:T(8,128)(2,1)S(1)}, bf16[32,2048]{1,0:T(8,128)(2,1)S(1)}, u32[]{:S(2)}, u32[]{:S(2)}) collective-permute-start(bf16[32,2048]{1,0:T(8,128)(2,1)S(1)} %collective-permute-done.1.refs_5_.refs_2_), channel_id=1, source_target_pairs={{0,4},{4,0},{8,12},{12,8},{1,5},{5,1},{9,13},{13,9},{2,6},{6,2},{1... | collective-permute-start | bytes 393224 | tf_op jit(solution)/shard_map/ppermute | solution.py:47
  20.5 8.8 %slice-start = ((s8[14680064]{0:T(1024)(128)(4,1)}), s8[4194304]{0:T(1024)(128)(4,1)S(1)}, s32[]{:S(2)}) async-start(s8[14680064]{0:T(1024)(128)(4,1)} %bitcast.1), calls=%async_computation | async-start | bytes 8388608
  20.5 8.8 %slice-start.1 = ((s8[14680064]{0:T(1024)(128)(4,1)}), s8[4194304]{0:T(1024)(128)(4,1)S(1)}, s32[]{:S(2)}) async-start(s8[14680064]{0:T(1024)(128)(4,1)} %bitcast.1), calls=%async_computation.1 | async-start | bytes 8388608
  20.5 8.8 %slice-start.2 = ((s8[14680064]{0:T(1024)(128)(4,1)}), s8[4194304]{0:T(1024)(128)(4,1)S(1)}, s32[]{:S(2)}) async-start(s8[14680064]{0:T(1024)(128)(4,1)} %bitcast.1), calls=%async_computation.2 | async-start | bytes 8388608
  22.6 2.8 %collective-permute-start.9 = (bf16[32,2048]{1,0:T(8,128)(2,1)S(1)}, bf16[32,2048]{1,0:T(8,128)(2,1)S(1)}, u32[]{:S(2)}, u32[]{:S(2)}) collective-permute-start(bf16[32,2048]{1,0:T(8,128)(2,1)S(1)} %get-tuple-element.34), channel_id=1, source_target_pairs={{0,1},{1,0},{2,3},{3,2},{4,5},{5,4},{6,7},{7,6},{8,9},{9,8},{10,11... | collective-permute-start | bytes 393224 | tf_op jit(solution)/shard_map/ppermute | solution.py:193
  22.7 2.7 %collective-permute-start.8 = (bf16[32,1536]{1,0:T(8,128)(2,1)S(1)}, bf16[32,1536]{1,0:T(8,128)(2,1)S(1)}, u32[]{:S(2)}, u32[]{:S(2)}) collective-permute-start(bf16[32,1536]{1,0:T(8,128)(2,1)S(1)} %get-tuple-element.29.refs_2_), channel_id=1, source_target_pairs={{0,1},{1,0},{2,3},{3,2},{4,5},{5,4},{6,7},{7,6},{8,9},{9,8},{10,11... | collective-permute-start | bytes 294920 | tf_op jit(solution)/shard_map/ppermute | solution.py:193
  23.2 6.1 %slice-start.3 = ((s8[14680064]{0:T(1024)(128)(4,1)}), s8[2097152]{0:T(1024)(128)(4,1)S(1)}, s32[]{:S(2)}) async-start(s8[14680064]{0:T(1024)(128)(4,1)} %bitcast.1), calls=%async_computation.3 | async-start | bytes 4194304
  23.2 10.9 %slice-start.4 = ((s8[14680064]{0:T(1024)(128)(4,1)}), s8[4194304]{0:T(1024)(128)(4,1)S(1)}, s32[]{:S(2)}) async-start(s8[14680064]{0:T(1024)(128)(4,1)} %bitcast.3), calls=%async_computation.4 | async-start | bytes 8388608
  23.2 10.9 %slice-start.5 = ((s8[14680064]{0:T(1024)(128)(4,1)}), s8[4194304]{0:T(1024)(128)(4,1)S(1)}, s32[]{:S(2)}) async-start(s8[14680064]{0:T(1024)(128)(4,1)} %bitcast.3), calls=%async_computation.5 | async-start | bytes 8388608
  25.3 3.7 %collective-permute-start.7 = (bf16[32,2048]{1,0:T(8,128)(2,1)S(1)}, bf16[32,2048]{1,0:T(8,128)(2,1)S(1)}, u32[]{:S(2)}, u32[]{:S(2)}) collective-permute-start(bf16[32,2048]{1,0:T(8,128)(2,1)S(1)} %get-tuple-element.32), channel_id=1, source_target_pairs={{0,1},{1,0},{2,3},{3,2},{4,5},{5,4},{6,7},{7,6},{8,9},{9,8},{10,11... | collective-permute-start | bytes 393224 | tf_op jit(solution)/shard_map/ppermute | solution.py:193
  25.4 8.6 %slice-start.6 = ((s8[14680064]{0:T(1024)(128)(4,1)}), s8[4194304]{0:T(1024)(128)(4,1)S(1)}, s32[]{:S(2)}) async-start(s8[14680064]{0:T(1024)(128)(4,1)} %bitcast.3), calls=%async_computation.6 | async-start | bytes 8388608
  25.5 8.6 %collective-permute-start.10 = (bf16[32,3584]{1,0:T(8,128)(2,1)S(1)}, bf16[32,3584]{1,0:T(8,128)(2,1)S(1)}, u32[]{:S(2)}, u32[]{:S(2)}) collective-permute-start(bf16[32,3584]{1,0:T(8,128)(2,1)S(1)} %shard_map.109.refs_3_), channel_id=1, source_target_pairs={{0,2},{1,3},{2,0},{3,1},{4,6},{5,7},{6,4},{7,5},{8,10},{9,11},{10,... | collective-permute-start | bytes 688136 | tf_op jit(solution)/shard_map/ppermute | solution.py:193
  27.6 1.3 %collective-permute-start.6 = (bf16[32,1536]{1,0:T(8,128)(2,1)S(1)}, bf16[32,1536]{1,0:T(8,128)(2,1)S(1)}, u32[]{:S(2)}, u32[]{:S(2)}) collective-permute-start(bf16[32,1536]{1,0:T(8,128)(2,1)S(1)} %get-tuple-element.31.refs_3_), channel_id=1, source_target_pairs={{0,1},{1,0},{2,3},{3,2},{4,5},{5,4},{6,7},{7,6},{8,9},{9,8},{10,11... | collective-permute-start | bytes 294920 | tf_op jit(solution)/shard_map/ppermute | solution.py:193
  29.0 9.8 %collective-permute-start.15 = (bf16[32,3584]{1,0:T(8,128)(2,1)S(1)}, bf16[32,3584]{1,0:T(8,128)(2,1)S(1)}, u32[]{:S(2)}, u32[]{:S(2)}) collective-permute-start(bf16[32,3584]{1,0:T(8,128)(2,1)S(1)} %shard_map.110.refs_5_), channel_id=1, source_target_pairs={{0,2},{1,3},{2,0},{3,1},{4,6},{5,7},{6,4},{7,5},{8,10},{9,11},{10,... | collective-permute-start | bytes 688136 | tf_op jit(solution)/shard_map/ppermute | solution.py:193
  29.2 4.9 %slice-start.7 = ((s8[14680064]{0:T(1024)(128)(4,1)}), s8[2097152]{0:T(1024)(128)(4,1)S(1)}, s32[]{:S(2)}) async-start(s8[14680064]{0:T(1024)(128)(4,1)} %bitcast.3), calls=%async_computation.7 | async-start | bytes 4194304
  29.2 11.6 %collective-permute-start.17 = (bf16[32,3584]{1,0:T(8,128)(2,1)S(1)}, bf16[32,3584]{1,0:T(8,128)(2,1)S(1)}, u32[]{:S(2)}, u32[]{:S(2)}) collective-permute-start(bf16[32,3584]{1,0:T(8,128)(2,1)S(1)} %get-tuple-element.46), channel_id=1, source_target_pairs={{0,1},{1,0},{2,3},{3,2},{4,5},{5,4},{6,7},{7,6},{8,9},{9,8},{10,11... | collective-permute-start | bytes 688136 | tf_op jit(solution)/shard_map/ppermute | solution.py:193
  31.5 4.8 %collective-permute-start.13 = (bf16[32,1536]{1,0:T(8,128)(2,1)S(1)}, bf16[32,1536]{1,0:T(8,128)(2,1)S(1)}, u32[]{:S(2)}, u32[]{:S(2)}) collective-permute-start(bf16[32,1536]{1,0:T(8,128)(2,1)S(1)} %get-tuple-element.36.refs_2_), channel_id=1, source_target_pairs={{0,1},{1,0},{2,3},{3,2},{4,5},{5,4},{6,7},{7,6},{8,9},{9,8},{10,11... | collective-permute-start | bytes 294920 | tf_op jit(solution)/shard_map/ppermute | solution.py:193
  31.9 4.8 %collective-permute-start.14 = (bf16[32,2048]{1,0:T(8,128)(2,1)S(1)}, bf16[32,2048]{1,0:T(8,128)(2,1)S(1)}, u32[]{:S(2)}, u32[]{:S(2)}) collective-permute-start(bf16[32,2048]{1,0:T(8,128)(2,1)S(1)} %get-tuple-element.41), channel_id=1, source_target_pairs={{0,1},{1,0},{2,3},{3,2},{4,5},{5,4},{6,7},{7,6},{8,9},{9,8},{10,11... | collective-permute-start | bytes 393224 | tf_op jit(solution)/shard_map/ppermute | solution.py:193
  36.2 4.3 %collective-permute-start.12 = (bf16[32,2048]{1,0:T(8,128)(2,1)S(1)}, bf16[32,2048]{1,0:T(8,128)(2,1)S(1)}, u32[]{:S(2)}, u32[]{:S(2)}) collective-permute-start(bf16[32,2048]{1,0:T(8,128)(2,1)S(1)} %get-tuple-element.39), channel_id=1, source_target_pairs={{0,1},{1,0},{2,3},{3,2},{4,5},{5,4},{6,7},{7,6},{8,9},{9,8},{10,11... | collective-permute-start | bytes 393224 | tf_op jit(solution)/shard_map/ppermute | solution.py:193
  36.3 2.5 %collective-permute-start.11 = (bf16[32,1536]{1,0:T(8,128)(2,1)S(1)}, bf16[32,1536]{1,0:T(8,128)(2,1)S(1)}, u32[]{:S(2)}, u32[]{:S(2)}) collective-permute-start(bf16[32,1536]{1,0:T(8,128)(2,1)S(1)} %get-tuple-element.38.refs_3_), channel_id=1, source_target_pairs={{0,1},{1,0},{2,3},{3,2},{4,5},{5,4},{6,7},{7,6},{8,9},{9,8},{10,11... | collective-permute-start | bytes 294920 | tf_op jit(solution)/shard_map/ppermute | solution.py:193
  36.8 6.6 %collective-permute-start.16 = (bf16[32,3584]{1,0:T(8,128)(2,1)S(1)}, bf16[32,3584]{1,0:T(8,128)(2,1)S(1)}, u32[]{:S(2)}, u32[]{:S(2)}) collective-permute-start(bf16[32,3584]{1,0:T(8,128)(2,1)S(1)} %get-tuple-element.44), channel_id=1, source_target_pairs={{0,1},{1,0},{2,3},{3,2},{4,5},{5,4},{6,7},{7,6},{8,9},{9,8},{10,11... | collective-permute-start | bytes 688136 | tf_op jit(solution)/shard_map/ppermute | solution.py:193
  38.7 5.6 %collective-permute-start.18 = (bf16[32,3584]{1,0:T(8,128)(2,1)S(1)}, bf16[32,3584]{1,0:T(8,128)(2,1)S(1)}, u32[]{:S(2)}, u32[]{:S(2)}) collective-permute-start(bf16[32,3584]{1,0:T(8,128)(2,1)S(1)} %get-tuple-element.51), channel_id=1, source_target_pairs={{0,1},{1,0},{2,3},{3,2},{4,5},{5,4},{6,7},{7,6},{8,9},{9,8},{10,11... | collective-permute-start | bytes 688136 | tf_op jit(solution)/shard_map/ppermute | solution.py:193
  38.7 8.4 %collective-permute-start.19 = (bf16[32,3584]{1,0:T(8,128)(2,1)S(1)}, bf16[32,3584]{1,0:T(8,128)(2,1)S(1)}, u32[]{:S(2)}, u32[]{:S(2)}) collective-permute-start(bf16[32,3584]{1,0:T(8,128)(2,1)S(1)} %shard_map.113.refs_3_), channel_id=1, source_target_pairs={{0,2},{1,3},{2,0},{3,1},{4,6},{5,7},{6,4},{7,5},{8,10},{9,11},{10,... | collective-permute-start | bytes 688136 | tf_op jit(solution)/shard_map/ppermute | solution.py:193
  40.5 6.8 %collective-permute-start.20 = (bf16[32,3584]{1,0:T(8,128)(2,1)S(1)}, bf16[32,3584]{1,0:T(8,128)(2,1)S(1)}, u32[]{:S(2)}, u32[]{:S(2)}) collective-permute-start(bf16[32,3584]{1,0:T(8,128)(2,1)S(1)} %get-tuple-element.53), channel_id=1, source_target_pairs={{0,1},{1,0},{2,3},{3,2},{4,5},{5,4},{6,7},{7,6},{8,9},{9,8},{10,11... | collective-permute-start | bytes 688136 | tf_op jit(solution)/shard_map/ppermute | solution.py:193
  40.8 10.9 %collective-permute-start.21 = (bf16[32,3584]{1,0:T(8,128)(2,1)S(1)}, bf16[32,3584]{1,0:T(8,128)(2,1)S(1)}, u32[]{:S(2)}, u32[]{:S(2)}) collective-permute-start(bf16[32,3584]{1,0:T(8,128)(2,1)S(1)} %shard_map.114.refs_0_), channel_id=1, source_target_pairs={{0,2},{1,3},{2,0},{3,1},{4,6},{5,7},{6,4},{7,5},{8,10},{9,11},{10,... | collective-permute-start | bytes 688136 | tf_op jit(solution)/shard_map/ppermute | solution.py:193

commit v9 on v8

--- a/solution.py
+++ b/solution.py
@@ -296,10 +296,8 @@
     target_gate = load(target_gate)
     target_pieces = gather_pieces(target_states, "wide", wide, (target_gate,))
     source_pieces = gather_pieces(source_states, "wide", wide)
-    target_up = load(target_up, (target_gate, target_pieces[wide // 2]))
-
-    after = (target_up,)
-    rows, sends, keeps = product(target_pieces, target_gate, narrow, after)
+
+    rows, sends, keeps = product(target_pieces, target_gate, narrow, ())
     _, up_sends, up_keeps = product(rows, target_up, narrow, (sends[0][0],))
     sent, target_g = finish(sends, keeps, narrow, (up_sends[0][0], *source_pieces[1:]))
     sent, target_u = finish(up_sends, up_keeps, narrow, (sent,))

time: 52.7 us -> 51.8 us (0.983)
  Pallas kernels: 23 us -> 17.8 us
  waiting for transfers between devices: 13.3 us -> 17.2 us
    pallas_call x2 -> x1, Pallas kernels: 10.4 us -> 5.18 us  [load(): pl.pallas_call(load_kernel, out_shape=pltpu.VMEM(matrix.shape, matrix.dty...]
    ppermute x6, waiting for transfers between devices: 1.07 us -> 4.99 us  [gather_pieces(): pieces.append(lax.ppermute(piece, axis, pairs))]
  transfers between devices with their start and end apart: 22 -> 22, of which waited for: 6 -> 8; matrix products, arithmetic and copies ran while one was open for 0% -> 0% of each run, Pallas kernels for 42% -> 33%
where the time goes in v9:
time: 51.8 us; the launch traced here: 51.6 us
  Pallas kernels  17.8 us (34%)
  waiting for transfers between devices  17.2 us (33%)
  starting transfers between devices  15.6 us (30%)
  between operations  0.91 us (2%)
    ppermute x16, waiting for transfers between devices, exchange(): lax.ppermute(array, 'narrow', [(i, i ^ 1 << step) for i in range(size)])  12.2 us
    ppermute x6, starting transfers between devices, gather_pieces(): pieces.append(lax.ppermute(piece, axis, pairs))  8.86 us
    pallas_call x4, Pallas kernels, product(): pl.pallas_call(functools.partial(product_kernel, len(tokens), len(after),...  8.35 us
    ppermute x16, starting transfers between devices, exchange(): lax.ppermute(array, 'narrow', [(i, i ^ 1 << step) for i in range(size)])  6.71 us
    pallas_call x1, Pallas kernels, load(): pl.pallas_call(load_kernel, out_shape=pltpu.VMEM(matrix.shape, matrix.dty...  5.18 us
    ppermute x6, waiting for transfers between devices, gather_pieces(): pieces.append(lax.ppermute(piece, axis, pairs))  4.99 us
    pallas_call x1, Pallas kernels, look_up(): pl.pallas_call(functools.partial(look_up_kernel, ids.shape[0] // lengths....  2.16 us
  transfers between devices with their start and end apart: 22, of which 8 were waited for; matrix products, arithmetic and copies ran while one was open for 0% of the time, Pallas kernels for 33%

profile of v9, /device:TPU:0, one launch (start us, length us, event | category | flops | bytes accessed | tf_op | source)
XLA Modules:
  0.0 51.6 jit_solution(579064408114824932)
XLA Ops:
  0.6 4.1 %collective-permute-start.4 = (bf16[32,2048]{1,0:T(8,128)(2,1)}, bf16[32,2048]{1,0:T(8,128)(2,1)S(1)}, u32[]{:S(2)}, u32[]{:S(2)}) collective-permute-start(bf16[32,2048]{1,0:T(8,128)(2,1)} %refs_0_.2), channel_id=1, source_target_pairs={{0,8},{4,12},{8,0},{12,4},{1,9},{5,13},{9,1},{13,5},{2,10},{6,14},... | collective-permute-start | bytes 393224 | tf_op jit(solution)/shard_map/ppermute | solution.py:47
  4.7 1.6 %collective-permute-start.3 = (bf16[32,2048]{1,0:T(8,128)(2,1)}, bf16[32,2048]{1,0:T(8,128)(2,1)S(1)}, u32[]{:S(2)}, u32[]{:S(2)}) collective-permute-start(bf16[32,2048]{1,0:T(8,128)(2,1)} %refs_0_.2), channel_id=1, source_target_pairs={{0,4},{4,0},{8,12},{12,8},{1,5},{5,1},{9,13},{13,9},{2,6},{6,2},{1... | collective-permute-start | bytes 393224 | tf_op jit(solution)/shard_map/ppermute | solution.py:47
  6.3 0.3 collective-permute-start.1
  6.6 5.2 %shard_map.104.refs_0_.refs_4_ = bf16[2048,3584]{1,0:T(8,128)(2,1)S(1)} custom-call(bf16[2048,3584]{1,0:T(8,128)(2,1)} %matrix.1), custom_call_target="tpu_custom_call" | custom-call | tf_op jit(solution)/shard_map/pallas_call | solution.py:119
  11.8 0.0 copy-start
  11.8 0.0 copy-start.1
  11.9 0.0 slice-start
  11.9 0.0 slice-start.1
  11.9 1.0 %collective-permute-done.4.piece.refs_2_ = bf16[32,2048]{1,0:T(8,128)(2,1)S(1)} collective-permute-done((bf16[32,2048]{1,0:T(8,128)(2,1)}, bf16[32,2048]{1,0:T(8,128)(2,1)S(1)}, u32[]{:S(2)}, u32[]{:S(2)}) %collective-permute-start.4) | collective-permute-done | bytes 131104 | tf_op jit(solution)/shard_map/ppermute | solution.py:47
  12.9 0.0 slice-start.2
  12.9 0.0 slice-start.3
  12.9 0.0 slice-start.6
  13.0 0.2 collective-permute-start.5
  13.2 1.9 %collective-permute-start = (bf16[32,2048]{1,0:T(8,128)(2,1)S(1)}, bf16[32,2048]{1,0:T(8,128)(2,1)S(1)}, u32[]{:S(2)}, u32[]{:S(2)}) collective-permute-start(bf16[32,2048]{1,0:T(8,128)(2,1)S(1)} %copy-done), channel_id=1, source_target_pairs={{0,4},{4,0},{8,12},{12,8},{1,5},{5,1},{9,13},{13,9},{2,6},{6,2},{1... | collective-permute-start | bytes 393224 | tf_op jit(solution)/shard_map/ppermute | solution.py:47
  15.1 1.9 %collective-permute-done.1.refs_5_.refs_2_ = bf16[32,2048]{1,0:T(8,128)(2,1)S(1)} collective-permute-done((bf16[32,2048]{1,0:T(8,128)(2,1)}, bf16[32,2048]{1,0:T(8,128)(2,1)S(1)}, u32[]{:S(2)}, u32[]{:S(2)}) %collective-permute-start.1) | collective-permute-done | bytes 131104 | tf_op jit(solution)/shard_map/ppermute | solution.py:47
  17.0 0.8 %collective-permute-start.2 = (bf16[32,2048]{1,0:T(8,128)(2,1)S(1)}, bf16[32,2048]{1,0:T(8,128)(2,1)S(1)}, u32[]{:S(2)}, u32[]{:S(2)}) collective-permute-start(bf16[32,2048]{1,0:T(8,128)(2,1)S(1)} %collective-permute-done.1.refs_5_.refs_2_), channel_id=1, source_target_pairs={{0,4},{4,0},{8,12},{12,8},{1,5},{5,1},{9,13},{13,9},{2,6},{6,2},{1... | collective-permute-start | bytes 393224 | tf_op jit(solution)/shard_map/ppermute | solution.py:47
  17.7 0.0 collective-permute-done.3.refs_1_
  17.7 2.0 %collective-permute-done.5.refs_3_ = bf16[32,2048]{1,0:T(8,128)(2,1)S(1)} collective-permute-done((bf16[32,2048]{1,0:T(8,128)(2,1)S(1)}, bf16[32,2048]{1,0:T(8,128)(2,1)S(1)}, u32[]{:S(2)}, u32[]{:S(2)}) %collective-permute-start.5) | collective-permute-done | bytes 131104 | tf_op jit(solution)/shard_map/ppermute | solution.py:47
  19.8 2.1 %shard_map.106 = (bf16[128,2048]{1,0:T(8,128)(2,1)S(1)}, bf16[32,1536]{1,0:T(8,128)(2,1)S(1)}, bf16[32,2048]{1,0:T(8,128)(2,1)S(1)}, bf16[32,3584]{1,0:T(8,128)(...) custom-call(bf16[32,2048]{1,0:T(8,128)(2,1)S(1)} %copy-done.1, ...), custom_call_target="tpu_custom_call" | custom-call | tf_op jit(solution)/shard_map/pallas_call | solution.py:179
  21.9 0.1 collective-permute-start.9
  22.0 0.5 collective-permute-start.8
  22.5 0.0 slice-start.7
  22.5 0.0 slice-start.8
  22.5 0.0 slice-start.9
  22.5 2.1 %shard_map.107 = (bf16[32,1536]{1,0:T(8,128)(2,1)S(1)}, bf16[32,2048]{1,0:T(8,128)(2,1)S(1)}, bf16[32,3584]{1,0:T(8,128)(2,1)S(1)}, bf16[32,3584]{1,0:T(8,128)(2,1)S(1)}, bf16[32,3584]{1,0:T(8,128)(2,1)S(1)}) custom-call(bf16[128,2048]{1,0:T(8,128)(2,1)S(1)} %get-tuple-element.28.refs_0_, bf16[2048,3584]{1,0:T(8,128)(2,1)S(1)} %bitcast.2, ...), custom_call_target="tpu_custom_call" | custom-call | tf_op jit(solution)/shard_map/pallas_call | solution.py:179
  24.6 0.1 collective-permute-start.7
  24.7 0.0 collective-permute-done.refs_4_.refs_1_
  24.8 0.0 collective-permute-done.2.refs_6_.refs_3_
  24.8 0.0 collective-permute-done.8.refs_1_
  24.8 0.0 collective-permute-done.9.refs_2_
  24.8 0.0 slice-start.10
  24.8 0.1 shard_map.108.refs_3_
  24.8 1.9 %collective-permute-start.10 = (bf16[32,3584]{1,0:T(8,128)(2,1)S(1)}, bf16[32,3584]{1,0:T(8,128)(2,1)S(1)}, u32[]{:S(2)}, u32[]{:S(2)}) collective-permute-start(bf16[32,3584]{1,0:T(8,128)(2,1)S(1)} %shard_map.108.refs_3_), channel_id=1, source_target_pairs={{0,2},{1,3},{2,0},{3,1},{4,6},{5,7},{6,4},{7,5},{8,10},{9,11},{10,... | collective-permute-start | bytes 688136 | tf_op jit(solution)/shard_map/ppermute | solution.py:193
  26.7 0.2 collective-permute-start.6
  26.9 1.1 %collective-permute-done.6.refs_1_ = bf16[32,1536]{1,0:T(8,128)(2,1)S(1)} collective-permute-done((bf16[32,1536]{1,0:T(8,128)(2,1)S(1)}, bf16[32,1536]{1,0:T(8,128)(2,1)S(1)}, u32[]{:S(2)}, u32[]{:S(2)}) %collective-permute-start.6) | collective-permute-done | bytes 98336 | tf_op jit(solution)/shard_map/ppermute | solution.py:193
  28.0 0.0 collective-permute-done.7.refs_2_
  28.0 0.1 shard_map.109.refs_5_
  28.1 0.3 collective-permute-start.15
  28.4 0.0 collective-permute-start.17
  28.4 2.1 %shard_map.110 = (bf16[128,2048]{1,0:T(8,128)(2,1)S(1)}, bf16[32,1536]{1,0:T(8,128)(2,1)S(1)}, bf16[32,2048]{1,0:T(8,128)(2,1)S(1)}, bf16[32,3584]{1,0:T(8,128)(...) custom-call(bf16[32,2048]{1,0:T(8,128)(2,1)S(1)} %copy-done, ...), custom_call_target="tpu_custom_call" | custom-call | tf_op jit(solution)/shard_map/pallas_call | solution.py:179
  30.5 0.5 %collective-permute-start.13 = (bf16[32,1536]{1,0:T(8,128)(2,1)S(1)}, bf16[32,1536]{1,0:T(8,128)(2,1)S(1)}, u32[]{:S(2)}, u32[]{:S(2)}) collective-permute-start(bf16[32,1536]{1,0:T(8,128)(2,1)S(1)} %get-tuple-element.36.refs_2_), channel_id=1, source_target_pairs={{0,1},{1,0},{2,3},{3,2},{4,5},{5,4},{6,7},{7,6},{8,9},{9,8},{10,11... | collective-permute-start | bytes 294920 | tf_op jit(solution)/shard_map/ppermute | solution.py:193
  31.1 0.1 collective-permute-start.14
  31.2 2.2 %collective-permute-done.10.refs_3_.refs_2_ = bf16[32,3584]{1,0:T(8,128)(2,1)S(1)} collective-permute-done((bf16[32,3584]{1,0:T(8,128)(2,1)S(1)}, bf16[32,3584]{1,0:T(8,128)(2,1)S(1)}, u32[]{:S(2)}, u32[]{:S(2)}) %collective-permute-start.10) | collective-permute-done | bytes 229408 | tf_op jit(solution)/shard_map/ppermute | solution.py:193
  33.3 2.1 %shard_map.111 = (bf16[32,1536]{1,0:T(8,128)(2,1)S(1)}, bf16[32,2048]{1,0:T(8,128)(2,1)S(1)}, bf16[32,3584]{1,0:T(8,128)(2,1)S(1)}, bf16[32,3584]{1,0:T(8,128)(2,1)S(1)}, bf16[32,3584]{1,0:T(8,128)(2,1)S(1)}) custom-call(bf16[128,2048]{1,0:T(8,128)(2,1)S(1)} %get-tuple-element.35.refs_0_, bf16[2048,3584]{1,0:T(8,128)(2,1)S(1)} %bitcast.6, ...), custom_call_target="tpu_custom_call" | custom-call | tf_op jit(solution)/shard_map/pallas_call | solution.py:179
  35.4 0.1 collective-permute-start.12
  35.5 0.0 collective-permute-done.13.refs_1_
  35.5 0.5 collective-permute-start.11
  36.0 0.0 collective-permute-done.14.refs_2_
  36.0 0.1 collective-permute-start.16
  36.1 0.1 shard_map.112.refs_3_
  36.1 1.7 %collective-permute-done.15.refs_4_.refs_5_ = bf16[32,3584]{1,0:T(8,128)(2,1)S(1)} collective-permute-done((bf16[32,3584]{1,0:T(8,128)(2,1)S(1)}, bf16[32,3584]{1,0:T(8,128)(2,1)S(1)}, u32[]{:S(2)}, u32[]{:S(2)}) %collective-permute-start.15) | collective-permute-done | bytes 229408 | tf_op jit(solution)/shard_map/ppermute | solution.py:193
  37.8 1.7 %collective-permute-start.19 = (bf16[32,3584]{1,0:T(8,128)(2,1)S(1)}, bf16[32,3584]{1,0:T(8,128)(2,1)S(1)}, u32[]{:S(2)}, u32[]{:S(2)}) collective-permute-start(bf16[32,3584]{1,0:T(8,128)(2,1)S(1)} %shard_map.112.refs_3_), channel_id=1, source_target_pairs={{0,2},{1,3},{2,0},{3,1},{4,6},{5,7},{6,4},{7,5},{8,10},{9,11},{10,... | collective-permute-start | bytes 688136 | tf_op jit(solution)/shard_map/ppermute | solution.py:193
  39.6 0.2 collective-permute-start.20
  39.8 0.1 shard_map.113.refs_0_
  39.9 0.4 collective-permute-start.21
  40.3 2.2 %shard_map.114 = (f32[32,128]{1,0:T(8,128)S(1)}, f32[32,128]{1,0:T(8,128)S(1)}) custom-call(s32[32]{0:T(128)} %ids.1, s32[2]{0:T(128)} %lengths.1, f32[1002,128]{1,0:T(8,128)} %bitcast.7, bf16[32,3584]{1,0:T(8,128)(2,1)S(1)} %shard_map.113.refs_0_), custom_call_target="tpu_custom_call" | custom-call | tf_op jit(solution)/shard_map/pallas_call | solution.py:97
  42.5 0.0 collective-permute-done.16.refs_1_
  42.5 0.9 %shard_map.115 = (f32[32,3584]{1,0:T(8,128)S(1)}, bf16[32,3584]{1,0:T(8,128)(2,1)}) custom-call(f32[32,128]{1,0:T(8,128)S(1)} %get-tuple-element.42.live, bf16[32,3584]{1,0:T(8,128)(2,1)S(1)} %get-tuple-element.43.refs_0_, bf16[32,3584]{1,0:T(8,128)(2,1)S(1)} %collective-permute-done.16.refs_1_, ...), custom_call_target="tpu_custom_call" | custom-call | tf_op jit(solution)/shard_map/pallas_call | solution.py:249
  43.4 0.0 collective-permute-done.18.refs_1_
  43.4 2.8 %collective-permute-done.19.refs_2_ = bf16[32,3584]{1,0:T(8,128)(2,1)S(1)} collective-permute-done((bf16[32,3584]{1,0:T(8,128)(2,1)S(1)}, bf16[32,3584]{1,0:T(8,128)(2,1)S(1)}, u32[]{:S(2)}, u32[]{:S(2)}) %collective-permute-start.19) | collective-permute-done | bytes 229408 | tf_op jit(solution)/shard_map/ppermute | solution.py:193
  46.3 0.1 shard_map.116.gated
  46.4 0.0 collective-permute-done.20.refs_1_
  46.4 4.4 %collective-permute-done.21.refs_2_ = bf16[32,3584]{1,0:T(8,128)(2,1)S(1)} collective-permute-done((bf16[32,3584]{1,0:T(8,128)(2,1)S(1)}, bf16[32,3584]{1,0:T(8,128)(2,1)S(1)}, u32[]{:S(2)}, u32[]{:S(2)}) %collective-permute-start.21) | collective-permute-done | bytes 229408 | tf_op jit(solution)/shard_map/ppermute | solution.py:193
  50.8 0.8 %shard_map.117 = bf16[32,3584]{1,0:T(8,128)(2,1)} custom-call(f32[32,3584]{1,0:T(8,128)S(1)} %get-tuple-element.48.act, f32[32,3584]{1,0:T(8,128)S(1)} %shard_map.116.gated, bf16[32,3584]{1,0:T(8,128)(2,1)S(1)} %get-tuple-element.52.refs_0_, bf16[32,3584]{1,0:T(8,128)(2,1)S(1)} %collective-permute-done.20.refs_1_, ...), custom_call_target="tpu_custom_call" | custom-call | tf_op jit(solution)/shard_map/pallas_call | solution.py:285
  (25 shorter events, 0.1 us)
Async XLA Ops:
  0.6 12.3 %collective-permute-start.4 = (bf16[32,2048]{1,0:T(8,128)(2,1)}, bf16[32,2048]{1,0:T(8,128)(2,1)S(1)}, u32[]{:S(2)}, u32[]{:S(2)}) collective-permute-start(bf16[32,2048]{1,0:T(8,128)(2,1)} %refs_0_.2), channel_id=1, source_target_pairs={{0,8},{4,12},{8,0},{12,4},{1,9},{5,13},{9,1},{13,5},{2,10},{6,14},... | collective-permute-start | bytes 393224 | tf_op jit(solution)/shard_map/ppermute | solution.py:47
  4.7 13.0 %collective-permute-start.3 = (bf16[32,2048]{1,0:T(8,128)(2,1)}, bf16[32,2048]{1,0:T(8,128)(2,1)S(1)}, u32[]{:S(2)}, u32[]{:S(2)}) collective-permute-start(bf16[32,2048]{1,0:T(8,128)(2,1)} %refs_0_.2), channel_id=1, source_target_pairs={{0,4},{4,0},{8,12},{12,8},{1,5},{5,1},{9,13},{13,9},{2,6},{6,2},{1... | collective-permute-start | bytes 393224 | tf_op jit(solution)/shard_map/ppermute | solution.py:47
  6.3 10.7 %collective-permute-start.1 = (bf16[32,2048]{1,0:T(8,128)(2,1)}, bf16[32,2048]{1,0:T(8,128)(2,1)S(1)}, u32[]{:S(2)}, u32[]{:S(2)}) collective-permute-start(bf16[32,2048]{1,0:T(8,128)(2,1)} %refs_0_.3), channel_id=1, source_target_pairs={{0,8},{4,12},{8,0},{12,4},{1,9},{5,13},{9,1},{13,5},{2,10},{6,14},... | collective-permute-start | bytes 393224 | tf_op jit(solution)/shard_map/ppermute | solution.py:47
  11.8 1.4 %copy-start = (bf16[32,2048]{1,0:T(8,128)(2,1)S(1)}, bf16[32,2048]{1,0:T(8,128)(2,1)}, u32[]{:S(2)}) copy-start(bf16[32,2048]{1,0:T(8,128)(2,1)} %refs_0_.3) | copy-start | bytes 393220
  11.8 7.9 %copy-start.1 = (bf16[32,2048]{1,0:T(8,128)(2,1)S(1)}, bf16[32,2048]{1,0:T(8,128)(2,1)}, u32[]{:S(2)}) copy-start(bf16[32,2048]{1,0:T(8,128)(2,1)} %refs_0_.2) | copy-start | bytes 393220
  11.9 10.6 %slice-start = ((s8[14680064]{0:T(1024)(128)(4,1)}), s8[4194304]{0:T(1024)(128)(4,1)S(1)}, s32[]{:S(2)}) async-start(s8[14680064]{0:T(1024)(128)(4,1)} %bitcast.1), calls=%async_computation | async-start | bytes 8388608
  11.9 10.6 %slice-start.1 = ((s8[14680064]{0:T(1024)(128)(4,1)}), s8[4194304]{0:T(1024)(128)(4,1)S(1)}, s32[]{:S(2)}) async-start(s8[14680064]{0:T(1024)(128)(4,1)} %bitcast.1), calls=%async_computation.1 | async-start | bytes 8388608
  12.9 15.5 %slice-start.4 = ((s8[14680064]{0:T(1024)(128)(4,1)}), s8[4194304]{0:T(1024)(128)(4,1)S(1)}, s32[]{:S(2)}) async-start(s8[14680064]{0:T(1024)(128)(4,1)} %bitcast.3), calls=%async_computation.4 | async-start | bytes 8388608
  12.9 15.5 %slice-start.5 = ((s8[14680064]{0:T(1024)(128)(4,1)}), s8[4194304]{0:T(1024)(128)(4,1)S(1)}, s32[]{:S(2)}) async-start(s8[14680064]{0:T(1024)(128)(4,1)} %bitcast.3), calls=%async_computation.5 | async-start | bytes 8388608
  12.9 9.6 %slice-start.2 = ((s8[14680064]{0:T(1024)(128)(4,1)}), s8[4194304]{0:T(1024)(128)(4,1)S(1)}, s32[]{:S(2)}) async-start(s8[14680064]{0:T(1024)(128)(4,1)} %bitcast.1), calls=%async_computation.2 | async-start | bytes 8388608
  12.9 9.5 %slice-start.3 = ((s8[14680064]{0:T(1024)(128)(4,1)}), s8[2097152]{0:T(1024)(128)(4,1)S(1)}, s32[]{:S(2)}) async-start(s8[14680064]{0:T(1024)(128)(4,1)} %bitcast.1), calls=%async_computation.3 | async-start | bytes 4194304
  12.9 15.5 %slice-start.6 = ((s8[14680064]{0:T(1024)(128)(4,1)}), s8[4194304]{0:T(1024)(128)(4,1)S(1)}, s32[]{:S(2)}) async-start(s8[14680064]{0:T(1024)(128)(4,1)} %bitcast.3), calls=%async_computation.6 | async-start | bytes 8388608
  13.0 6.8 %collective-permute-start.5 = (bf16[32,2048]{1,0:T(8,128)(2,1)S(1)}, bf16[32,2048]{1,0:T(8,128)(2,1)S(1)}, u32[]{:S(2)}, u32[]{:S(2)}) collective-permute-start(bf16[32,2048]{1,0:T(8,128)(2,1)S(1)} %shard_map.105), channel_id=1, source_target_pairs={{0,4},{4,0},{8,12},{12,8},{1,5},{5,1},{9,13},{13,9},{2,6},{6,2},{1... | collective-permute-start | bytes 393224 | tf_op jit(solution)/shard_map/ppermute | solution.py:47
  13.2 11.6 %collective-permute-start = (bf16[32,2048]{1,0:T(8,128)(2,1)S(1)}, bf16[32,2048]{1,0:T(8,128)(2,1)S(1)}, u32[]{:S(2)}, u32[]{:S(2)}) collective-permute-start(bf16[32,2048]{1,0:T(8,128)(2,1)S(1)} %copy-done), channel_id=1, source_target_pairs={{0,4},{4,0},{8,12},{12,8},{1,5},{5,1},{9,13},{13,9},{2,6},{6,2},{1... | collective-permute-start | bytes 393224 | tf_op jit(solution)/shard_map/ppermute | solution.py:47
  17.0 7.8 %collective-permute-start.2 = (bf16[32,2048]{1,0:T(8,128)(2,1)S(1)}, bf16[32,2048]{1,0:T(8,128)(2,1)S(1)}, u32[]{:S(2)}, u32[]{:S(2)}) collective-permute-start(bf16[32,2048]{1,0:T(8,128)(2,1)S(1)} %collective-permute-done.1.refs_5_.refs_2_), channel_id=1, source_target_pairs={{0,4},{4,0},{8,12},{12,8},{1,5},{5,1},{9,13},{13,9},{2,6},{6,2},{1... | collective-permute-start | bytes 393224 | tf_op jit(solution)/shard_map/ppermute | solution.py:47
  21.9 2.9 %collective-permute-start.9 = (bf16[32,2048]{1,0:T(8,128)(2,1)S(1)}, bf16[32,2048]{1,0:T(8,128)(2,1)S(1)}, u32[]{:S(2)}, u32[]{:S(2)}) collective-permute-start(bf16[32,2048]{1,0:T(8,128)(2,1)S(1)} %get-tuple-element.34), channel_id=1, source_target_pairs={{0,1},{1,0},{2,3},{3,2},{4,5},{5,4},{6,7},{7,6},{8,9},{9,8},{10,11... | collective-permute-start | bytes 393224 | tf_op jit(solution)/shard_map/ppermute | solution.py:193
  22.0 2.8 %collective-permute-start.8 = (bf16[32,1536]{1,0:T(8,128)(2,1)S(1)}, bf16[32,1536]{1,0:T(8,128)(2,1)S(1)}, u32[]{:S(2)}, u32[]{:S(2)}) collective-permute-start(bf16[32,1536]{1,0:T(8,128)(2,1)S(1)} %get-tuple-element.29.refs_2_), channel_id=1, source_target_pairs={{0,1},{1,0},{2,3},{3,2},{4,5},{5,4},{6,7},{7,6},{8,9},{9,8},{10,11... | collective-permute-start | bytes 294920 | tf_op jit(solution)/shard_map/ppermute | solution.py:193
  22.5 5.9 %slice-start.7 = ((s8[14680064]{0:T(1024)(128)(4,1)}), s8[2097152]{0:T(1024)(128)(4,1)S(1)}, s32[]{:S(2)}) async-start(s8[14680064]{0:T(1024)(128)(4,1)} %bitcast.3), calls=%async_computation.7 | async-start | bytes 4194304
  22.5 10.8 %slice-start.8 = ((s8[14680064]{0:T(1024)(128)(4,1)}), s8[4194304]{0:T(1024)(128)(4,1)S(1)}, s32[]{:S(2)}) async-start(s8[14680064]{0:T(1024)(128)(4,1)} %bitcast.5), calls=%async_computation.8 | async-start | bytes 8388608
  22.5 10.8 %slice-start.9 = ((s8[14680064]{0:T(1024)(128)(4,1)}), s8[4194304]{0:T(1024)(128)(4,1)S(1)}, s32[]{:S(2)}) async-start(s8[14680064]{0:T(1024)(128)(4,1)} %bitcast.5), calls=%async_computation.9 | async-start | bytes 8388608
  24.6 3.4 %collective-permute-start.7 = (bf16[32,2048]{1,0:T(8,128)(2,1)S(1)}, bf16[32,2048]{1,0:T(8,128)(2,1)S(1)}, u32[]{:S(2)}, u32[]{:S(2)}) collective-permute-start(bf16[32,2048]{1,0:T(8,128)(2,1)S(1)} %get-tuple-element.32), channel_id=1, source_target_pairs={{0,1},{1,0},{2,3},{3,2},{4,5},{5,4},{6,7},{7,6},{8,9},{9,8},{10,11... | collective-permute-start | bytes 393224 | tf_op jit(solution)/shard_map/ppermute | solution.py:193
  24.8 8.5 %slice-start.10 = ((s8[14680064]{0:T(1024)(128)(4,1)}), s8[4194304]{0:T(1024)(128)(4,1)S(1)}, s32[]{:S(2)}) async-start(s8[14680064]{0:T(1024)(128)(4,1)} %bitcast.5), calls=%async_computation.10 | async-start | bytes 8388608
  24.8 8.5 %collective-permute-start.10 = (bf16[32,3584]{1,0:T(8,128)(2,1)S(1)}, bf16[32,3584]{1,0:T(8,128)(2,1)S(1)}, u32[]{:S(2)}, u32[]{:S(2)}) collective-permute-start(bf16[32,3584]{1,0:T(8,128)(2,1)S(1)} %shard_map.108.refs_3_), channel_id=1, source_target_pairs={{0,2},{1,3},{2,0},{3,1},{4,6},{5,7},{6,4},{7,5},{8,10},{9,11},{10,... | collective-permute-start | bytes 688136 | tf_op jit(solution)/shard_map/ppermute | solution.py:193
  26.7 1.3 %collective-permute-start.6 = (bf16[32,1536]{1,0:T(8,128)(2,1)S(1)}, bf16[32,1536]{1,0:T(8,128)(2,1)S(1)}, u32[]{:S(2)}, u32[]{:S(2)}) collective-permute-start(bf16[32,1536]{1,0:T(8,128)(2,1)S(1)} %get-tuple-element.31.refs_3_), channel_id=1, source_target_pairs={{0,1},{1,0},{2,3},{3,2},{4,5},{5,4},{6,7},{7,6},{8,9},{9,8},{10,11... | collective-permute-start | bytes 294920 | tf_op jit(solution)/shard_map/ppermute | solution.py:193
  28.1 9.8 %collective-permute-start.15 = (bf16[32,3584]{1,0:T(8,128)(2,1)S(1)}, bf16[32,3584]{1,0:T(8,128)(2,1)S(1)}, u32[]{:S(2)}, u32[]{:S(2)}) collective-permute-start(bf16[32,3584]{1,0:T(8,128)(2,1)S(1)} %shard_map.109.refs_5_), channel_id=1, source_target_pairs={{0,2},{1,3},{2,0},{3,1},{4,6},{5,7},{6,4},{7,5},{8,10},{9,11},{10,... | collective-permute-start | bytes 688136 | tf_op jit(solution)/shard_map/ppermute | solution.py:193
  28.4 5.0 %slice-start.11 = ((s8[14680064]{0:T(1024)(128)(4,1)}), s8[2097152]{0:T(1024)(128)(4,1)S(1)}, s32[]{:S(2)}) async-start(s8[14680064]{0:T(1024)(128)(4,1)} %bitcast.5), calls=%async_computation.11 | async-start | bytes 4194304
  28.4 11.5 %collective-permute-start.17 = (bf16[32,3584]{1,0:T(8,128)(2,1)S(1)}, bf16[32,3584]{1,0:T(8,128)(2,1)S(1)}, u32[]{:S(2)}, u32[]{:S(2)}) collective-permute-start(bf16[32,3584]{1,0:T(8,128)(2,1)S(1)} %get-tuple-element.46), channel_id=1, source_target_pairs={{0,1},{1,0},{2,3},{3,2},{4,5},{5,4},{6,7},{7,6},{8,9},{9,8},{10,11... | collective-permute-start | bytes 688136 | tf_op jit(solution)/shard_map/ppermute | solution.py:193
  30.5 5.0 %collective-permute-start.13 = (bf16[32,1536]{1,0:T(8,128)(2,1)S(1)}, bf16[32,1536]{1,0:T(8,128)(2,1)S(1)}, u32[]{:S(2)}, u32[]{:S(2)}) collective-permute-start(bf16[32,1536]{1,0:T(8,128)(2,1)S(1)} %get-tuple-element.36.refs_2_), channel_id=1, source_target_pairs={{0,1},{1,0},{2,3},{3,2},{4,5},{5,4},{6,7},{7,6},{8,9},{9,8},{10,11... | collective-permute-start | bytes 294920 | tf_op jit(solution)/shard_map/ppermute | solution.py:193
  31.1 4.9 %collective-permute-start.14 = (bf16[32,2048]{1,0:T(8,128)(2,1)S(1)}, bf16[32,2048]{1,0:T(8,128)(2,1)S(1)}, u32[]{:S(2)}, u32[]{:S(2)}) collective-permute-start(bf16[32,2048]{1,0:T(8,128)(2,1)S(1)} %get-tuple-element.41), channel_id=1, source_target_pairs={{0,1},{1,0},{2,3},{3,2},{4,5},{5,4},{6,7},{7,6},{8,9},{9,8},{10,11... | collective-permute-start | bytes 393224 | tf_op jit(solution)/shard_map/ppermute | solution.py:193
  35.4 4.2 %collective-permute-start.12 = (bf16[32,2048]{1,0:T(8,128)(2,1)S(1)}, bf16[32,2048]{1,0:T(8,128)(2,1)S(1)}, u32[]{:S(2)}, u32[]{:S(2)}) collective-permute-start(bf16[32,2048]{1,0:T(8,128)(2,1)S(1)} %get-tuple-element.39), channel_id=1, source_target_pairs={{0,1},{1,0},{2,3},{3,2},{4,5},{5,4},{6,7},{7,6},{8,9},{9,8},{10,11... | collective-permute-start | bytes 393224 | tf_op jit(solution)/shard_map/ppermute | solution.py:193
  35.5 2.3 %collective-permute-start.11 = (bf16[32,1536]{1,0:T(8,128)(2,1)S(1)}, bf16[32,1536]{1,0:T(8,128)(2,1)S(1)}, u32[]{:S(2)}, u32[]{:S(2)}) collective-permute-start(bf16[32,1536]{1,0:T(8,128)(2,1)S(1)} %get-tuple-element.38.refs_3_), channel_id=1, source_target_pairs={{0,1},{1,0},{2,3},{3,2},{4,5},{5,4},{6,7},{7,6},{8,9},{9,8},{10,11... | collective-permute-start | bytes 294920 | tf_op jit(solution)/shard_map/ppermute | solution.py:193
  36.0 6.5 %collective-permute-start.16 = (bf16[32,3584]{1,0:T(8,128)(2,1)S(1)}, bf16[32,3584]{1,0:T(8,128)(2,1)S(1)}, u32[]{:S(2)}, u32[]{:S(2)}) collective-permute-start(bf16[32,3584]{1,0:T(8,128)(2,1)S(1)} %get-tuple-element.44), channel_id=1, source_target_pairs={{0,1},{1,0},{2,3},{3,2},{4,5},{5,4},{6,7},{7,6},{8,9},{9,8},{10,11... | collective-permute-start | bytes 688136 | tf_op jit(solution)/shard_map/ppermute | solution.py:193
  37.8 5.6 %collective-permute-start.18 = (bf16[32,3584]{1,0:T(8,128)(2,1)S(1)}, bf16[32,3584]{1,0:T(8,128)(2,1)S(1)}, u32[]{:S(2)}, u32[]{:S(2)}) collective-permute-start(bf16[32,3584]{1,0:T(8,128)(2,1)S(1)} %get-tuple-element.51), channel_id=1, source_target_pairs={{0,1},{1,0},{2,3},{3,2},{4,5},{5,4},{6,7},{7,6},{8,9},{9,8},{10,11... | collective-permute-start | bytes 688136 | tf_op jit(solution)/shard_map/ppermute | solution.py:193
  37.8 8.4 %collective-permute-start.19 = (bf16[32,3584]{1,0:T(8,128)(2,1)S(1)}, bf16[32,3584]{1,0:T(8,128)(2,1)S(1)}, u32[]{:S(2)}, u32[]{:S(2)}) collective-permute-start(bf16[32,3584]{1,0:T(8,128)(2,1)S(1)} %shard_map.112.refs_3_), channel_id=1, source_target_pairs={{0,2},{1,3},{2,0},{3,1},{4,6},{5,7},{6,4},{7,5},{8,10},{9,11},{10,... | collective-permute-start | bytes 688136 | tf_op jit(solution)/shard_map/ppermute | solution.py:193
  39.6 6.8 %collective-permute-start.20 = (bf16[32,3584]{1,0:T(8,128)(2,1)S(1)}, bf16[32,3584]{1,0:T(8,128)(2,1)S(1)}, u32[]{:S(2)}, u32[]{:S(2)}) collective-permute-start(bf16[32,3584]{1,0:T(8,128)(2,1)S(1)} %get-tuple-element.53), channel_id=1, source_target_pairs={{0,1},{1,0},{2,3},{3,2},{4,5},{5,4},{6,7},{7,6},{8,9},{9,8},{10,11... | collective-permute-start | bytes 688136 | tf_op jit(solution)/shard_map/ppermute | solution.py:193
  39.9 10.9 %collective-permute-start.21 = (bf16[32,3584]{1,0:T(8,128)(2,1)S(1)}, bf16[32,3584]{1,0:T(8,128)(2,1)S(1)}, u32[]{:S(2)}, u32[]{:S(2)}) collective-permute-start(bf16[32,3584]{1,0:T(8,128)(2,1)S(1)} %shard_map.113.refs_0_), channel_id=1, source_target_pairs={{0,2},{1,3},{2,0},{3,1},{4,6},{5,7},{6,4},{7,5},{8,10},{9,11},{10,... | collective-permute-start | bytes 688136 | tf_op jit(solution)/shard_map/ppermute | solution.py:193

commit v10 on v9

--- a/solution.py
+++ b/solution.py
@@ -36,15 +36,18 @@
     )(piece, *after)
 
 
-def gather_pieces(piece, axis, size, after=()):
-    pieces = [piece]
-    for offset in range(1, size):
+def gather_pieces(piece, axis, size, after=None, relays_after=None):
+    pieces = [piece] + [None] * (size - 1)
+    near = [1 << b for b in range(size.bit_length() - 1)]
+    for offset in near[::-1] + [o for o in range(size) if o & (o - 1)]:
         low = offset & -offset
-        pairs = [(i, i ^ low) for i in range(size)]
-        piece = pieces[offset ^ low]
-        if after and offset != low:
-            piece = passed(piece, after)
-        pieces.append(lax.ppermute(piece, axis, pairs))
+        source = pieces[offset ^ low]
+        if after is not None and offset == low:
+            source = passed(piece, (after,))
+        if relays_after is not None and offset != low:
+            source = passed(source, (relays_after,))
+        pieces[offset] = lax.ppermute(source, axis, [(i, i ^ low) for i in range(size)])
+        after = pieces[offset] if after is not None else None
     return pieces
 
 
@@ -145,10 +148,14 @@
 
 
 def product_kernel(pieces, after, narrow, blocks, *refs):
-    tokens, matrix, outs = refs[:pieces], refs[pieces], refs[pieces + 1 + after :]
+    tokens, matrix = refs[:pieces], refs[pieces]
+    beside, outs = refs[pieces + 1 : len(refs) - len(blocks) - (pieces > 1) - after], refs[-len(blocks) :]
     if pieces > 1:
-        place_rows(tokens, outs[0], narrow)
-        tokens, outs = outs[:1], outs[1:]
+        rows = refs[-len(blocks) - 1]
+        place_rows(tokens, rows, narrow)
+        tokens = [rows]
+    for earlier in beside:
+        outs[-1][:, : earlier.shape[1]] = earlier[...]
     for cols in column_tiles(matrix.shape[1]):
         total = jnp.dot(tokens[0][...], matrix[:, cols], preferred_element_type=jnp.float32)
         for out, (row, col) in zip(outs, blocks):
@@ -165,28 +172,29 @@
     return sizes + [left]
 
 
-def product(tokens, matrix, narrow, after):
+def product(tokens, matrix, narrow, after, beside=(), split=True):
     placing = len(tokens) > 1
     total = sum(t.shape[0] for t in tokens)
     depth, width = matrix.shape
     sizes = part_sizes(total, narrow)
-    sent = []
-    for k in range(len(sizes)):
-        sent += [(k, *chunk) for chunk in (column_chunks(width) if k + 1 < len(sizes) else [(0, width)])]
+    sent = [(k, *cols) for k in range(len(sizes) - 1) for cols in (column_chunks(width) if split else [(0, width)])]
+    ahead = sum(b.shape[1] for b in beside)
     blocks = [(sum(sizes[:k]), first) for k, first, _ in sent]
     blocks += [(total // 2 + sum(sizes[:k]), 0) for k in range(len(sizes))]
+    blocks += [(sum(sizes[:-1]), -ahead)]
     shapes = [(sizes[k], count) for k, _, count in sent] + [(size, width) for size in sizes]
+    shapes += [(sizes[-1], ahead + width)]
     found = pl.pallas_call(
         functools.partial(product_kernel, len(tokens), len(after), narrow, blocks),
         out_shape=[jax.ShapeDtypeStruct((total, depth), tokens[0].dtype)] * placing
         + [jax.ShapeDtypeStruct(shape, jnp.bfloat16) for shape in shapes],
-        in_specs=[IN_VMEM] * len(tokens) + [IN_VMEM] + [ANYWHERE] * len(after),
+        in_specs=[IN_VMEM] * (len(tokens) + 1 + len(beside)) + [ANYWHERE] * len(after),
         out_specs=[IN_VMEM] * (placing + len(shapes)),
         compiler_params=pltpu.CompilerParams(vmem_limit_bytes=4 << 20),
-    )(*tokens, in_vmem(matrix), *after)
+    )(*tokens, in_vmem(matrix), *beside, *after)
     rows, found = (found[:1], found[1:]) if placing else (tokens, found)
     sends = [(array, k, first) for array, (k, first, _) in zip(found, sent)]
-    return rows, sends, found[len(sent) :]
+    return rows, sends, found[-1], found[len(sent) : -1]
 
 
 def exchange(array, step, size):
@@ -216,10 +224,12 @@
         out[:, cols] = added(refs, places, out.shape[0], cols).astype(out.dtype)
 
 
-def finish(sends, keeps, narrow, after):
+def finish(sends, keeps, own, narrow, after):
+    last = len(keeps) - 1
     came = [(exchange(array, 0, narrow), k, k + 1, col) for array, k, col in sends]
-    sent = sends[0][0]
-    for k in range(len(keeps) - 1):
+    came.append((own[0], last, last + 1, own[1]))
+    sent = keeps[-1]
+    for k in range(last):
         arrays, places = addends(keeps, came, k)
         sent = pl.pallas_call(
             functools.partial(next_kernel, places),
@@ -294,19 +304,23 @@
 def local(mesh_shape, target_states, source_states, target_gate, target_up, source_gate, source_up, token_ids, lengths, ratio_weight):
     wide, narrow = mesh_shape["wide"], mesh_shape["narrow"]
     target_gate = load(target_gate)
-    target_pieces = gather_pieces(target_states, "wide", wide, (target_gate,))
-    source_pieces = gather_pieces(source_states, "wide", wide)
-
-    rows, sends, keeps = product(target_pieces, target_gate, narrow, ())
-    _, up_sends, up_keeps = product(rows, target_up, narrow, (sends[0][0],))
-    sent, target_g = finish(sends, keeps, narrow, (up_sends[0][0], *source_pieces[1:]))
-    sent, target_u = finish(up_sends, up_keeps, narrow, (sent,))
-
-    rows, sends, keeps = product(source_pieces, source_gate, narrow, (sent,))
-    after = (sends[0][0], target_g[0][-1])
-    _, up_sends, up_keeps = product(rows, source_up, narrow, after)
-    sent, source_g = finish(sends, keeps, narrow, (up_sends[0][0],))
-    sent, source_u = finish(up_sends, up_keeps, narrow, (sent, target_u[0][-1]))
+    target_pieces = gather_pieces(target_states, "wide", wide, relays_after=target_gate)
+    source_pieces = gather_pieces(source_states, "wide", wide, target_pieces[wide // 2])
+    width = target_gate.shape[1]
+
+    rows, sends, own, keeps = product(target_pieces, target_gate, narrow, (), split=False)
+    _, up_sends, own, up_keeps = product(rows, target_up, narrow, (keeps[0],), (own,))
+    target_own = exchange(own, 0, narrow)
+    after = (up_keeps[0], *source_pieces[1:])
+    sent, target_g = finish(sends, keeps, (target_own, 0), narrow, after)
+    sent, target_u = finish(up_sends, up_keeps, (target_own, -width), narrow, (sent,))
+
+    rows, sends, own, keeps = product(source_pieces, source_gate, narrow, (sent,))
+    after = (keeps[0], target_g[0][-1])
+    _, up_sends, own, up_keeps = product(rows, source_up, narrow, after, (own,))
+    own = exchange(own, 0, narrow)
+    sent, source_g = finish(sends, keeps, (own, 0), narrow, (up_keeps[0], target_own))
+    sent, source_u = finish(up_sends, up_keeps, (own, -width), narrow, (sent, target_u[0][-1]))
     live, weight = look_up(token_ids, lengths, ratio_weight, (sent,))
     act, target_out = target_end(live, target_g, target_u)
     gated = source_middle(live, weight, source_g)

time: 51.8 us -> 53.7 us (1.037)
  starting transfers between devices: 15.6 us -> 18.4 us
  waiting for transfers between devices: 17.2 us -> 16 us
    ppermute x16 -> x13, waiting for transfers between devices: 12.2 us -> 8.24 us  [exchange(): lax.ppermute(array, 'narrow', [(i, i ^ 1 << step) for i in range(size)])]
    ppermute x6, waiting for transfers between devices: 4.99 us -> 7.71 us  [gather_pieces(): lax.ppermute(source, axis, [(i, i ^ low) for i in range(size)])]
    ppermute x6, starting transfers between devices: 8.86 us -> 11.4 us  [gather_pieces(): lax.ppermute(source, axis, [(i, i ^ low) for i in range(size)])]
    ppermute x16 -> x13, starting transfers between devices: 6.71 us -> 6.99 us  [exchange(): lax.ppermute(array, 'narrow', [(i, i ^ 1 << step) for i in range(size)])]
  transfers between devices with their start and end apart: 22 -> 19, of which waited for: 8 -> 7; matrix products, arithmetic and copies ran while one was open for 0% -> 0% of each run, Pallas kernels for 33% -> 32%
where the time goes in v10:
time: 53.7 us; the launch traced here: 53.5 us
  starting transfers between devices  18.4 us (34%)
  Pallas kernels  17.8 us (33%)
  waiting for transfers between devices  16 us (30%)
  between operations  0.92 us (2%)
    ppermute x6, starting transfers between devices, gather_pieces(): lax.ppermute(source, axis, [(i, i ^ low) for i in range(size)])  11.4 us
    pallas_call x4, Pallas kernels, product(): pl.pallas_call(functools.partial(product_kernel, len(tokens), len(after),...  8.35 us
    ppermute x13, waiting for transfers between devices, exchange(): lax.ppermute(array, 'narrow', [(i, i ^ 1 << step) for i in range(size)])  8.24 us
    ppermute x6, waiting for transfers between devices, gather_pieces(): lax.ppermute(source, axis, [(i, i ^ low) for i in range(size)])  7.71 us
    ppermute x13, starting transfers between devices, exchange(): lax.ppermute(array, 'narrow', [(i, i ^ 1 << step) for i in range(size)])  6.99 us
    pallas_call x1, Pallas kernels, load(): pl.pallas_call(load_kernel, out_shape=pltpu.VMEM(matrix.shape, matrix.dty...  5.18 us
    pallas_call x1, Pallas kernels, look_up(): pl.pallas_call(functools.partial(look_up_kernel, ids.shape[0] // lengths....  2.16 us
  transfers between devices with their start and end apart: 19, of which 7 were waited for; matrix products, arithmetic and copies ran while one was open for 0% of the time, Pallas kernels for 32%

profile of v10, /device:TPU:0, one launch (start us, length us, event | category | flops | bytes accessed | tf_op | source)
XLA Modules:
  0.0 53.5 jit_solution(3164146274773070319)
XLA Ops:
  0.6 4.1 %collective-permute-start = (bf16[32,2048]{1,0:T(8,128)(2,1)}, bf16[32,2048]{1,0:T(8,128)(2,1)S(1)}, u32[]{:S(2)}, u32[]{:S(2)}) collective-permute-start(bf16[32,2048]{1,0:T(8,128)(2,1)} %refs_0_.2), channel_id=1, source_target_pairs={{0,8},{4,12},{8,0},{12,4},{1,9},{5,13},{9,1},{13,5},{2,10},{6,14},... | collective-permute-start | bytes 393224 | tf_op jit(solution)/shard_map/ppermute | solution.py:49
  4.7 1.6 %collective-permute-start.4 = (bf16[32,2048]{1,0:T(8,128)(2,1)}, bf16[32,2048]{1,0:T(8,128)(2,1)S(1)}, u32[]{:S(2)}, u32[]{:S(2)}) collective-permute-start(bf16[32,2048]{1,0:T(8,128)(2,1)} %refs_0_.2), channel_id=1, source_target_pairs={{0,4},{4,0},{8,12},{12,8},{1,5},{5,1},{9,13},{13,9},{2,6},{6,2},{1... | collective-permute-start | bytes 393224 | tf_op jit(solution)/shard_map/ppermute | solution.py:49
  6.3 5.2 %shard_map.106.refs_0_.refs_4_ = bf16[2048,3584]{1,0:T(8,128)(2,1)S(1)} custom-call(bf16[2048,3584]{1,0:T(8,128)(2,1)} %matrix.1), custom_call_target="tpu_custom_call" | custom-call | tf_op jit(solution)/shard_map/pallas_call | solution.py:122
  11.5 0.0 copy-start
  11.5 0.0 copy-start.1
  11.5 0.0 slice-start
  11.5 0.0 slice-start.1
  11.5 0.0 collective-permute-done.refs_0_.piece.refs_2_
  11.6 0.6 %collective-permute-start.5 = (bf16[32,2048]{1,0:T(8,128)(2,1)S(1)}, bf16[32,2048]{1,0:T(8,128)(2,1)S(1)}, u32[]{:S(2)}, u32[]{:S(2)}) collective-permute-start(bf16[32,2048]{1,0:T(8,128)(2,1)S(1)} %shard_map.107), channel_id=1, source_target_pairs={{0,4},{4,0},{8,12},{12,8},{1,5},{5,1},{9,13},{13,9},{2,6},{6,2},{1... | collective-permute-start | bytes 393224 | tf_op jit(solution)/shard_map/ppermute | solution.py:49
  12.2 0.3 copy-done
  12.4 0.0 slice-start.2
  12.4 0.0 slice-start.3
  12.4 0.0 slice-start.4
  12.5 0.0 slice-start.5
  12.5 3.1 %collective-permute-start.1 = (bf16[32,2048]{1,0:T(8,128)(2,1)S(1)}, bf16[32,2048]{1,0:T(8,128)(2,1)S(1)}, u32[]{:S(2)}, u32[]{:S(2)}) collective-permute-start(bf16[32,2048]{1,0:T(8,128)(2,1)S(1)} %shard_map.104), channel_id=1, source_target_pairs={{0,8},{4,12},{8,0},{12,4},{1,9},{5,13},{9,1},{13,5},{2,10},{6,14},... | collective-permute-start | bytes 393224 | tf_op jit(solution)/shard_map/ppermute | solution.py:49
  15.6 0.0 collective-permute-done.4.refs_1_
  15.6 3.2 %collective-permute-done.5.refs_3_ = bf16[32,2048]{1,0:T(8,128)(2,1)S(1)} collective-permute-done((bf16[32,2048]{1,0:T(8,128)(2,1)S(1)}, bf16[32,2048]{1,0:T(8,128)(2,1)S(1)}, u32[]{:S(2)}, u32[]{:S(2)}) %collective-permute-start.5) | collective-permute-done | bytes 131104 | tf_op jit(solution)/shard_map/ppermute | solution.py:49
  18.7 2.1 %shard_map.108 = (bf16[128,2048]{1,0:T(8,128)(2,1)S(1)}, bf16[32,3584]{1,0:T(8,128)(2,1)S(1)}, bf16[32,3584]{1,0:T(8,128)(2,1)S(1)}, bf16[32,3584]{1,0:T(8,128)(2,1)S(1)}, bf16[32,3584]{1,0:T(8,128)(2,1)S(1)}) custom-call(bf16[32,2048]{1,0:T(8,128)(2,1)S(1)} %copy-done.1, bf16[32,2048]{1,0:T(8,128)(2,1)S(1)} %collective-permute-done.4.refs_1_, ...), custom_call_target="tpu_custom_call" | custom-call | tf_op jit(solution)/shard_map/pallas_call | solution.py:187
  20.8 0.1 collective-permute-start.8
  20.9 0.9 %collective-permute-done.1.refs_0_.refs_4_.refs_2_ = bf16[32,2048]{1,0:T(8,128)(2,1)S(1)} collective-permute-done((bf16[32,2048]{1,0:T(8,128)(2,1)S(1)}, bf16[32,2048]{1,0:T(8,128)(2,1)S(1)}, u32[]{:S(2)}, u32[]{:S(2)}) %collective-permute-start.1) | collective-permute-done | bytes 131104 | tf_op jit(solution)/shard_map/ppermute | solution.py:49
  21.8 0.3 collective-permute-start.2
  22.1 1.8 %collective-permute-start.3 = (bf16[32,2048]{1,0:T(8,128)(2,1)S(1)}, bf16[32,2048]{1,0:T(8,128)(2,1)S(1)}, u32[]{:S(2)}, u32[]{:S(2)}) collective-permute-start(bf16[32,2048]{1,0:T(8,128)(2,1)S(1)} %collective-permute-done.1.refs_0_.refs_4_.refs_2_), channel_id=1, source_target_pairs={{0,4},{4,0},{8,12},{12,8},{1,5},{5,1},{9,13},{13,9},{2,6},{6,2},{1... | collective-permute-start | bytes 393224 | tf_op jit(solution)/shard_map/ppermute | solution.py:49
  23.9 0.0 slice-start.6
  24.0 0.0 slice-start.7
  24.0 0.0 slice-start.8
  24.0 0.0 slice-start.9
  24.0 2.1 %shard_map.109 = (bf16[32,1536]{1,0:T(8,128)(2,1)S(1)}, bf16[32,2048]{1,0:T(8,128)(2,1)S(1)}, bf16[32,3584]{1,0:T(8,128)(2,1)S(1)}, bf16[32,3584]{1,0:T(8,128)(2,1)S(1)}, bf16[32,7168]{1,0:T(8,128)(2,1)S(1)}) custom-call(bf16[128,2048]{1,0:T(8,128)(2,1)S(1)} %get-tuple-element.27.refs_0_, bf16[2048,3584]{1,0:T(8,128)(2,1)S(1)} %bitcast.2, ...), custom_call_target="tpu_custom_call" | custom-call | tf_op jit(solution)/shard_map/pallas_call | solution.py:187
  26.1 2.2 %collective-permute-done.2.refs_3_.refs_1_ = bf16[32,2048]{1,0:T(8,128)(2,1)S(1)} collective-permute-done((bf16[32,2048]{1,0:T(8,128)(2,1)S(1)}, bf16[32,2048]{1,0:T(8,128)(2,1)S(1)}, u32[]{:S(2)}, u32[]{:S(2)}) %collective-permute-start.2) | collective-permute-done | bytes 131104 | tf_op jit(solution)/shard_map/ppermute | solution.py:49
  28.3 1.4 %collective-permute-done.3.refs_5_.refs_3_ = bf16[32,2048]{1,0:T(8,128)(2,1)S(1)} collective-permute-done((bf16[32,2048]{1,0:T(8,128)(2,1)S(1)}, bf16[32,2048]{1,0:T(8,128)(2,1)S(1)}, u32[]{:S(2)}, u32[]{:S(2)}) %collective-permute-start.3) | collective-permute-done | bytes 131104 | tf_op jit(solution)/shard_map/ppermute | solution.py:49
  29.7 0.0 collective-permute-done.8.refs_1_
  29.7 0.1 shard_map.110.refs_3_
  29.8 1.6 %collective-permute-start.9 = (bf16[32,3584]{1,0:T(8,128)(2,1)S(1)}, bf16[32,3584]{1,0:T(8,128)(2,1)S(1)}, u32[]{:S(2)}, u32[]{:S(2)}) collective-permute-start(bf16[32,3584]{1,0:T(8,128)(2,1)S(1)} %shard_map.110.refs_3_), channel_id=1, source_target_pairs={{0,2},{1,3},{2,0},{3,1},{4,6},{5,7},{6,4},{7,5},{8,10},{9,11},{10,... | collective-permute-start | bytes 688136 | tf_op jit(solution)/shard_map/ppermute | solution.py:201
  31.3 0.0 collective-permute-start.14
  31.3 0.5 collective-permute-start.7
  31.8 0.0 collective-permute-start.6
  31.9 1.6 %collective-permute-done.6.refs_1_ = bf16[32,1536]{1,0:T(8,128)(2,1)S(1)} collective-permute-done((bf16[32,1536]{1,0:T(8,128)(2,1)S(1)}, bf16[32,1536]{1,0:T(8,128)(2,1)S(1)}, u32[]{:S(2)}, u32[]{:S(2)}) %collective-permute-start.6) | collective-permute-done | bytes 98336 | tf_op jit(solution)/shard_map/ppermute | solution.py:201
  33.5 0.0 collective-permute-done.7.refs_2_
  33.5 0.1 shard_map.111.refs_5_
  33.5 0.0 slice-start.11
  33.6 0.6 %collective-permute-start.15 = (bf16[32,3584]{1,0:T(8,128)(2,1)S(1)}, bf16[32,3584]{1,0:T(8,128)(2,1)S(1)}, u32[]{:S(2)}, u32[]{:S(2)}) collective-permute-start(bf16[32,3584]{1,0:T(8,128)(2,1)S(1)} %shard_map.111.refs_5_), channel_id=1, source_target_pairs={{0,2},{1,3},{2,0},{3,1},{4,6},{5,7},{6,4},{7,5},{8,10},{9,11},{10,... | collective-permute-start | bytes 688136 | tf_op jit(solution)/shard_map/ppermute | solution.py:201
  34.2 2.1 %shard_map.112 = (bf16[128,2048]{1,0:T(8,128)(2,1)S(1)}, bf16[32,1536]{1,0:T(8,128)(2,1)S(1)}, bf16[32,2048]{1,0:T(8,128)(2,1)S(1)}, bf16[32,3584]{1,0:T(8,128)(...) custom-call(bf16[32,2048]{1,0:T(8,128)(2,1)S(1)} %copy-done, ...), custom_call_target="tpu_custom_call" | custom-call | tf_op jit(solution)/shard_map/pallas_call | solution.py:187
  36.3 0.1 collective-permute-start.13
  36.4 0.5 collective-permute-start.12
  36.9 0.0 collective-permute-done.9.refs_4_.refs_2_
  36.9 2.1 %shard_map.113 = (bf16[32,1536]{1,0:T(8,128)(2,1)S(1)}, bf16[32,2048]{1,0:T(8,128)(2,1)S(1)}, bf16[32,3584]{1,0:T(8,128)(2,1)S(1)}, bf16[32,3584]{1,0:T(8,128)(2,1)S(1)}, bf16[32,7168]{1,0:T(8,128)(2,1)S(1)}) custom-call(bf16[128,2048]{1,0:T(8,128)(2,1)S(1)} %get-tuple-element.34.refs_0_, bf16[2048,3584]{1,0:T(8,128)(2,1)S(1)} %bitcast.6, ...), custom_call_target="tpu_custom_call" | custom-call | tf_op jit(solution)/shard_map/pallas_call | solution.py:187
  39.0 0.1 collective-permute-start.16
  39.1 0.0 collective-permute-done.12.refs_1_
  39.1 0.4 collective-permute-start.11
  39.6 0.0 collective-permute-done.13.refs_2_
  39.6 0.1 collective-permute-start.10
  39.7 0.0 collective-permute-done.14.refs_4_.refs_1_
  39.7 0.1 shard_map.114.refs_3_
  39.7 1.6 %collective-permute-start.17 = (bf16[32,3584]{1,0:T(8,128)(2,1)S(1)}, bf16[32,3584]{1,0:T(8,128)(2,1)S(1)}, u32[]{:S(2)}, u32[]{:S(2)}) collective-permute-start(bf16[32,3584]{1,0:T(8,128)(2,1)S(1)} %shard_map.114.refs_3_), channel_id=1, source_target_pairs={{0,2},{1,3},{2,0},{3,1},{4,6},{5,7},{6,4},{7,5},{8,10},{9,11},{10,... | collective-permute-start | bytes 688136 | tf_op jit(solution)/shard_map/ppermute | solution.py:201
  41.3 0.0 collective-permute-done.15.refs_4_.refs_5_
  41.3 0.0 collective-permute-done.10.refs_1_
  41.3 0.1 shard_map.115.refs_0_
  41.4 1.5 %collective-permute-start.18 = (bf16[32,3584]{1,0:T(8,128)(2,1)S(1)}, bf16[32,3584]{1,0:T(8,128)(2,1)S(1)}, u32[]{:S(2)}, u32[]{:S(2)}) collective-permute-start(bf16[32,3584]{1,0:T(8,128)(2,1)S(1)} %shard_map.115.refs_0_), channel_id=1, source_target_pairs={{0,2},{1,3},{2,0},{3,1},{4,6},{5,7},{6,4},{7,5},{8,10},{9,11},{10,... | collective-permute-start | bytes 688136 | tf_op jit(solution)/shard_map/ppermute | solution.py:201
  42.8 2.2 %shard_map.116 = (f32[32,128]{1,0:T(8,128)S(1)}, f32[32,128]{1,0:T(8,128)S(1)}) custom-call(s32[32]{0:T(128)} %ids.1, s32[2]{0:T(128)} %lengths.1, f32[1002,128]{1,0:T(8,128)} %bitcast.7, bf16[32,3584]{1,0:T(8,128)(2,1)S(1)} %shard_map.115.refs_0_), custom_call_target="tpu_custom_call" | custom-call | tf_op jit(solution)/shard_map/pallas_call | solution.py:100
  45.0 0.9 %shard_map.117 = (f32[32,3584]{1,0:T(8,128)S(1)}, bf16[32,3584]{1,0:T(8,128)(2,1)}) custom-call(f32[32,128]{1,0:T(8,128)S(1)} %get-tuple-element.43.live, bf16[32,3584]{1,0:T(8,128)(2,1)S(1)} %get-tuple-element.44.refs_0_, bf16[32,7168]{1,0:T(8,128)(2,1)S(1)} %collective-permute-done.14.refs_4_.refs_1_, ...), custom_call_target="tpu_custom_call" | custom-call | tf_op jit(solution)/shard_map/pallas_call | solution.py:259
  45.9 2.3 %collective-permute-done.17.refs_2_ = bf16[32,3584]{1,0:T(8,128)(2,1)S(1)} collective-permute-done((bf16[32,3584]{1,0:T(8,128)(2,1)S(1)}, bf16[32,3584]{1,0:T(8,128)(2,1)S(1)}, u32[]{:S(2)}, u32[]{:S(2)}) %collective-permute-start.17) | collective-permute-done | bytes 229408 | tf_op jit(solution)/shard_map/ppermute | solution.py:201
  48.2 0.0 collective-permute-done.16.refs_1_
  48.2 0.1 shard_map.118.gated
  48.3 4.3 %collective-permute-done.18.refs_2_ = bf16[32,3584]{1,0:T(8,128)(2,1)S(1)} collective-permute-done((bf16[32,3584]{1,0:T(8,128)(2,1)S(1)}, bf16[32,3584]{1,0:T(8,128)(2,1)S(1)}, u32[]{:S(2)}, u32[]{:S(2)}) %collective-permute-start.18) | collective-permute-done | bytes 229408 | tf_op jit(solution)/shard_map/ppermute | solution.py:201
  52.6 0.8 %shard_map.119 = bf16[32,3584]{1,0:T(8,128)(2,1)} custom-call(f32[32,3584]{1,0:T(8,128)S(1)} %get-tuple-element.47.act, f32[32,3584]{1,0:T(8,128)S(1)} %shard_map.118.gated, bf16[32,3584]{1,0:T(8,128)(2,1)S(1)} %get-tuple-element.51.refs_0_, bf16[32,7168]{1,0:T(8,128)(2,1)S(1)} %collective-permute-done.16.refs_1_, ...), custom_call_target="tpu_custom_call" | custom-call | tf_op jit(solution)/shard_map/pallas_call | solution.py:295
  (21 shorter events, 0.1 us)
Async XLA Ops:
  0.6 10.9 %collective-permute-start = (bf16[32,2048]{1,0:T(8,128)(2,1)}, bf16[32,2048]{1,0:T(8,128)(2,1)S(1)}, u32[]{:S(2)}, u32[]{:S(2)}) collective-permute-start(bf16[32,2048]{1,0:T(8,128)(2,1)} %refs_0_.2), channel_id=1, source_target_pairs={{0,8},{4,12},{8,0},{12,4},{1,9},{5,13},{9,1},{13,5},{2,10},{6,14},... | collective-permute-start | bytes 393224 | tf_op jit(solution)/shard_map/ppermute | solution.py:49
  4.7 10.8 %collective-permute-start.4 = (bf16[32,2048]{1,0:T(8,128)(2,1)}, bf16[32,2048]{1,0:T(8,128)(2,1)S(1)}, u32[]{:S(2)}, u32[]{:S(2)}) collective-permute-start(bf16[32,2048]{1,0:T(8,128)(2,1)} %refs_0_.2), channel_id=1, source_target_pairs={{0,4},{4,0},{8,12},{12,8},{1,5},{5,1},{9,13},{13,9},{2,6},{6,2},{1... | collective-permute-start | bytes 393224 | tf_op jit(solution)/shard_map/ppermute | solution.py:49
  11.5 0.9 %copy-start = (bf16[32,2048]{1,0:T(8,128)(2,1)S(1)}, bf16[32,2048]{1,0:T(8,128)(2,1)}, u32[]{:S(2)}) copy-start(bf16[32,2048]{1,0:T(8,128)(2,1)} %refs_0_.3) | copy-start | bytes 393220
  11.5 7.2 %copy-start.1 = (bf16[32,2048]{1,0:T(8,128)(2,1)S(1)}, bf16[32,2048]{1,0:T(8,128)(2,1)}, u32[]{:S(2)}) copy-start(bf16[32,2048]{1,0:T(8,128)(2,1)} %refs_0_.2) | copy-start | bytes 393220
  11.5 12.4 %slice-start = ((s8[14680064]{0:T(1024)(128)(4,1)}), s8[4194304]{0:T(1024)(128)(4,1)S(1)}, s32[]{:S(2)}) async-start(s8[14680064]{0:T(1024)(128)(4,1)} %bitcast.1), calls=%async_computation | async-start | bytes 8388608
  11.5 12.4 %slice-start.1 = ((s8[14680064]{0:T(1024)(128)(4,1)}), s8[4194304]{0:T(1024)(128)(4,1)S(1)}, s32[]{:S(2)}) async-start(s8[14680064]{0:T(1024)(128)(4,1)} %bitcast.1), calls=%async_computation.1 | async-start | bytes 8388608
  11.6 7.2 %collective-permute-start.5 = (bf16[32,2048]{1,0:T(8,128)(2,1)S(1)}, bf16[32,2048]{1,0:T(8,128)(2,1)S(1)}, u32[]{:S(2)}, u32[]{:S(2)}) collective-permute-start(bf16[32,2048]{1,0:T(8,128)(2,1)S(1)} %shard_map.107), channel_id=1, source_target_pairs={{0,4},{4,0},{8,12},{12,8},{1,5},{5,1},{9,13},{13,9},{2,6},{6,2},{1... | collective-permute-start | bytes 393224 | tf_op jit(solution)/shard_map/ppermute | solution.py:49
  12.4 11.5 %slice-start.2 = ((s8[14680064]{0:T(1024)(128)(4,1)}), s8[4194304]{0:T(1024)(128)(4,1)S(1)}, s32[]{:S(2)}) async-start(s8[14680064]{0:T(1024)(128)(4,1)} %bitcast.1), calls=%async_computation.2 | async-start | bytes 8388608
  12.4 11.5 %slice-start.3 = ((s8[14680064]{0:T(1024)(128)(4,1)}), s8[2097152]{0:T(1024)(128)(4,1)S(1)}, s32[]{:S(2)}) async-start(s8[14680064]{0:T(1024)(128)(4,1)} %bitcast.1), calls=%async_computation.3 | async-start | bytes 4194304
  12.4 21.7 %slice-start.4 = ((s8[14680064]{0:T(1024)(128)(4,1)}), s8[4194304]{0:T(1024)(128)(4,1)S(1)}, s32[]{:S(2)}) async-start(s8[14680064]{0:T(1024)(128)(4,1)} %bitcast.3), calls=%async_computation.4 | async-start | bytes 8388608
  12.5 21.7 %slice-start.5 = ((s8[14680064]{0:T(1024)(128)(4,1)}), s8[4194304]{0:T(1024)(128)(4,1)S(1)}, s32[]{:S(2)}) async-start(s8[14680064]{0:T(1024)(128)(4,1)} %bitcast.3), calls=%async_computation.5 | async-start | bytes 8388608
  12.5 9.3 %collective-permute-start.1 = (bf16[32,2048]{1,0:T(8,128)(2,1)S(1)}, bf16[32,2048]{1,0:T(8,128)(2,1)S(1)}, u32[]{:S(2)}, u32[]{:S(2)}) collective-permute-start(bf16[32,2048]{1,0:T(8,128)(2,1)S(1)} %shard_map.104), channel_id=1, source_target_pairs={{0,8},{4,12},{8,0},{12,4},{1,9},{5,13},{9,1},{13,5},{2,10},{6,14},... | collective-permute-start | bytes 393224 | tf_op jit(solution)/shard_map/ppermute | solution.py:49
  20.8 8.9 %collective-permute-start.8 = (bf16[32,3584]{1,0:T(8,128)(2,1)S(1)}, bf16[32,3584]{1,0:T(8,128)(2,1)S(1)}, u32[]{:S(2)}, u32[]{:S(2)}) collective-permute-start(bf16[32,3584]{1,0:T(8,128)(2,1)S(1)} %get-tuple-element.33), channel_id=1, source_target_pairs={{0,1},{1,0},{2,3},{3,2},{4,5},{5,4},{6,7},{7,6},{8,9},{9,8},{10,11... | collective-permute-start | bytes 688136 | tf_op jit(solution)/shard_map/ppermute | solution.py:201
  21.8 6.5 %collective-permute-start.2 = (bf16[32,2048]{1,0:T(8,128)(2,1)S(1)}, bf16[32,2048]{1,0:T(8,128)(2,1)S(1)}, u32[]{:S(2)}, u32[]{:S(2)}) collective-permute-start(bf16[32,2048]{1,0:T(8,128)(2,1)S(1)} %shard_map.105), channel_id=1, source_target_pairs={{0,4},{4,0},{8,12},{12,8},{1,5},{5,1},{9,13},{13,9},{2,6},{6,2},{1... | collective-permute-start | bytes 393224 | tf_op jit(solution)/shard_map/ppermute | solution.py:49
  22.1 7.6 %collective-permute-start.3 = (bf16[32,2048]{1,0:T(8,128)(2,1)S(1)}, bf16[32,2048]{1,0:T(8,128)(2,1)S(1)}, u32[]{:S(2)}, u32[]{:S(2)}) collective-permute-start(bf16[32,2048]{1,0:T(8,128)(2,1)S(1)} %collective-permute-done.1.refs_0_.refs_4_.refs_2_), channel_id=1, source_target_pairs={{0,4},{4,0},{8,12},{12,8},{1,5},{5,1},{9,13},{13,9},{2,6},{6,2},{1... | collective-permute-start | bytes 393224 | tf_op jit(solution)/shard_map/ppermute | solution.py:49
  23.9 10.2 %slice-start.6 = ((s8[14680064]{0:T(1024)(128)(4,1)}), s8[4194304]{0:T(1024)(128)(4,1)S(1)}, s32[]{:S(2)}) async-start(s8[14680064]{0:T(1024)(128)(4,1)} %bitcast.3), calls=%async_computation.6 | async-start | bytes 8388608
  24.0 10.2 %slice-start.7 = ((s8[14680064]{0:T(1024)(128)(4,1)}), s8[2097152]{0:T(1024)(128)(4,1)S(1)}, s32[]{:S(2)}) async-start(s8[14680064]{0:T(1024)(128)(4,1)} %bitcast.3), calls=%async_computation.7 | async-start | bytes 4194304
  24.0 12.9 %slice-start.8 = ((s8[14680064]{0:T(1024)(128)(4,1)}), s8[4194304]{0:T(1024)(128)(4,1)S(1)}, s32[]{:S(2)}) async-start(s8[14680064]{0:T(1024)(128)(4,1)} %bitcast.5), calls=%async_computation.8 | async-start | bytes 8388608
  24.0 12.9 %slice-start.9 = ((s8[14680064]{0:T(1024)(128)(4,1)}), s8[4194304]{0:T(1024)(128)(4,1)S(1)}, s32[]{:S(2)}) async-start(s8[14680064]{0:T(1024)(128)(4,1)} %bitcast.5), calls=%async_computation.9 | async-start | bytes 8388608
  29.7 7.2 %slice-start.10 = ((s8[14680064]{0:T(1024)(128)(4,1)}), s8[4194304]{0:T(1024)(128)(4,1)S(1)}, s32[]{:S(2)}) async-start(s8[14680064]{0:T(1024)(128)(4,1)} %bitcast.5), calls=%async_computation.10 | async-start | bytes 8388608
  29.8 7.1 %collective-permute-start.9 = (bf16[32,3584]{1,0:T(8,128)(2,1)S(1)}, bf16[32,3584]{1,0:T(8,128)(2,1)S(1)}, u32[]{:S(2)}, u32[]{:S(2)}) collective-permute-start(bf16[32,3584]{1,0:T(8,128)(2,1)S(1)} %shard_map.110.refs_3_), channel_id=1, source_target_pairs={{0,2},{1,3},{2,0},{3,1},{4,6},{5,7},{6,4},{7,5},{8,10},{9,11},{10,... | collective-permute-start | bytes 688136 | tf_op jit(solution)/shard_map/ppermute | solution.py:201
  31.3 8.3 %collective-permute-start.14 = (bf16[32,7168]{1,0:T(8,128)(2,1)S(1)}, bf16[32,7168]{1,0:T(8,128)(2,1)S(1)}, u32[]{:S(2)}, u32[]{:S(2)}) collective-permute-start(bf16[32,7168]{1,0:T(8,128)(2,1)S(1)} %get-tuple-element.42), channel_id=1, source_target_pairs={{0,1},{1,0},{2,3},{3,2},{4,5},{5,4},{6,7},{7,6},{8,9},{9,8},{10,11... | collective-permute-start | bytes 1376264 | tf_op jit(solution)/shard_map/ppermute | solution.py:201
  31.3 2.1 %collective-permute-start.7 = (bf16[32,2048]{1,0:T(8,128)(2,1)S(1)}, bf16[32,2048]{1,0:T(8,128)(2,1)S(1)}, u32[]{:S(2)}, u32[]{:S(2)}) collective-permute-start(bf16[32,2048]{1,0:T(8,128)(2,1)S(1)} %get-tuple-element.32), channel_id=1, source_target_pairs={{0,1},{1,0},{2,3},{3,2},{4,5},{5,4},{6,7},{7,6},{8,9},{9,8},{10,11... | collective-permute-start | bytes 393224 | tf_op jit(solution)/shard_map/ppermute | solution.py:201
  31.8 1.6 %collective-permute-start.6 = (bf16[32,1536]{1,0:T(8,128)(2,1)S(1)}, bf16[32,1536]{1,0:T(8,128)(2,1)S(1)}, u32[]{:S(2)}, u32[]{:S(2)}) collective-permute-start(bf16[32,1536]{1,0:T(8,128)(2,1)S(1)} %get-tuple-element.31), channel_id=1, source_target_pairs={{0,1},{1,0},{2,3},{3,2},{4,5},{5,4},{6,7},{7,6},{8,9},{9,8},{10,11... | collective-permute-start | bytes 294920 | tf_op jit(solution)/shard_map/ppermute | solution.py:201
  33.5 3.3 %slice-start.11 = ((s8[14680064]{0:T(1024)(128)(4,1)}), s8[2097152]{0:T(1024)(128)(4,1)S(1)}, s32[]{:S(2)}) async-start(s8[14680064]{0:T(1024)(128)(4,1)} %bitcast.5), calls=%async_computation.11 | async-start | bytes 4194304
  33.6 7.7 %collective-permute-start.15 = (bf16[32,3584]{1,0:T(8,128)(2,1)S(1)}, bf16[32,3584]{1,0:T(8,128)(2,1)S(1)}, u32[]{:S(2)}, u32[]{:S(2)}) collective-permute-start(bf16[32,3584]{1,0:T(8,128)(2,1)S(1)} %shard_map.111.refs_5_), channel_id=1, source_target_pairs={{0,2},{1,3},{2,0},{3,1},{4,6},{5,7},{6,4},{7,5},{8,10},{9,11},{10,... | collective-permute-start | bytes 688136 | tf_op jit(solution)/shard_map/ppermute | solution.py:201
  36.3 3.3 %collective-permute-start.13 = (bf16[32,2048]{1,0:T(8,128)(2,1)S(1)}, bf16[32,2048]{1,0:T(8,128)(2,1)S(1)}, u32[]{:S(2)}, u32[]{:S(2)}) collective-permute-start(bf16[32,2048]{1,0:T(8,128)(2,1)S(1)} %get-tuple-element.41), channel_id=1, source_target_pairs={{0,1},{1,0},{2,3},{3,2},{4,5},{5,4},{6,7},{7,6},{8,9},{9,8},{10,11... | collective-permute-start | bytes 393224 | tf_op jit(solution)/shard_map/ppermute | solution.py:201
  36.4 2.8 %collective-permute-start.12 = (bf16[32,1536]{1,0:T(8,128)(2,1)S(1)}, bf16[32,1536]{1,0:T(8,128)(2,1)S(1)}, u32[]{:S(2)}, u32[]{:S(2)}) collective-permute-start(bf16[32,1536]{1,0:T(8,128)(2,1)S(1)} %get-tuple-element.40), channel_id=1, source_target_pairs={{0,1},{1,0},{2,3},{3,2},{4,5},{5,4},{6,7},{7,6},{8,9},{9,8},{10,11... | collective-permute-start | bytes 294920 | tf_op jit(solution)/shard_map/ppermute | solution.py:201
  39.0 9.2 %collective-permute-start.16 = (bf16[32,7168]{1,0:T(8,128)(2,1)S(1)}, bf16[32,7168]{1,0:T(8,128)(2,1)S(1)}, u32[]{:S(2)}, u32[]{:S(2)}) collective-permute-start(bf16[32,7168]{1,0:T(8,128)(2,1)S(1)} %get-tuple-element.50), channel_id=1, source_target_pairs={{0,1},{1,0},{2,3},{3,2},{4,5},{5,4},{6,7},{7,6},{8,9},{9,8},{10,11... | collective-permute-start | bytes 1376264 | tf_op jit(solution)/shard_map/ppermute | solution.py:201
  39.1 2.1 %collective-permute-start.11 = (bf16[32,2048]{1,0:T(8,128)(2,1)S(1)}, bf16[32,2048]{1,0:T(8,128)(2,1)S(1)}, u32[]{:S(2)}, u32[]{:S(2)}) collective-permute-start(bf16[32,2048]{1,0:T(8,128)(2,1)S(1)} %get-tuple-element.39), channel_id=1, source_target_pairs={{0,1},{1,0},{2,3},{3,2},{4,5},{5,4},{6,7},{7,6},{8,9},{9,8},{10,11... | collective-permute-start | bytes 393224 | tf_op jit(solution)/shard_map/ppermute | solution.py:201
  39.6 1.7 %collective-permute-start.10 = (bf16[32,1536]{1,0:T(8,128)(2,1)S(1)}, bf16[32,1536]{1,0:T(8,128)(2,1)S(1)}, u32[]{:S(2)}, u32[]{:S(2)}) collective-permute-start(bf16[32,1536]{1,0:T(8,128)(2,1)S(1)} %get-tuple-element.38), channel_id=1, source_target_pairs={{0,1},{1,0},{2,3},{3,2},{4,5},{5,4},{6,7},{7,6},{8,9},{9,8},{10,11... | collective-permute-start | bytes 294920 | tf_op jit(solution)/shard_map/ppermute | solution.py:201
  39.7 8.5 %collective-permute-start.17 = (bf16[32,3584]{1,0:T(8,128)(2,1)S(1)}, bf16[32,3584]{1,0:T(8,128)(2,1)S(1)}, u32[]{:S(2)}, u32[]{:S(2)}) collective-permute-start(bf16[32,3584]{1,0:T(8,128)(2,1)S(1)} %shard_map.114.refs_3_), channel_id=1, source_target_pairs={{0,2},{1,3},{2,0},{3,1},{4,6},{5,7},{6,4},{7,5},{8,10},{9,11},{10,... | collective-permute-start | bytes 688136 | tf_op jit(solution)/shard_map/ppermute | solution.py:201
  41.4 11.3 %collective-permute-start.18 = (bf16[32,3584]{1,0:T(8,128)(2,1)S(1)}, bf16[32,3584]{1,0:T(8,128)(2,1)S(1)}, u32[]{:S(2)}, u32[]{:S(2)}) collective-permute-start(bf16[32,3584]{1,0:T(8,128)(2,1)S(1)} %shard_map.115.refs_0_), channel_id=1, source_target_pairs={{0,2},{1,3},{2,0},{3,1},{4,6},{5,7},{6,4},{7,5},{8,10},{9,11},{10,... | collective-permute-start | bytes 688136 | tf_op jit(solution)/shard_map/ppermute | solution.py:201

commit v11 on v10

--- a/solution.py
+++ b/solution.py
@@ -36,9 +36,9 @@
     )(piece, *after)
 
 
-def gather_pieces(piece, axis, size, after=None, relays_after=None):
+def gather_pieces(piece, axis, size, chained=False, relays_after=None):
     pieces = [piece] + [None] * (size - 1)
-    near = [1 << b for b in range(size.bit_length() - 1)]
+    after, near = None, [1 << b for b in range(size.bit_length() - 1)]
     for offset in near[::-1] + [o for o in range(size) if o & (o - 1)]:
         low = offset & -offset
         source = pieces[offset ^ low]
@@ -47,7 +47,7 @@
         if relays_after is not None and offset != low:
             source = passed(source, (relays_after,))
         pieces[offset] = lax.ppermute(source, axis, [(i, i ^ low) for i in range(size)])
-        after = pieces[offset] if after is not None else None
+        after = pieces[offset] if chained else None
     return pieces
 
 
@@ -305,10 +305,10 @@
     wide, narrow = mesh_shape["wide"], mesh_shape["narrow"]
     target_gate = load(target_gate)
     target_pieces = gather_pieces(target_states, "wide", wide, relays_after=target_gate)
-    source_pieces = gather_pieces(source_states, "wide", wide, target_pieces[wide // 2])
+    source_pieces = gather_pieces(source_states, "wide", wide, chained=True)
     width = target_gate.shape[1]
 
-    rows, sends, own, keeps = product(target_pieces, target_gate, narrow, (), split=False)
+    rows, sends, own, keeps = product(target_pieces, target_gate, narrow, ())
     _, up_sends, own, up_keeps = product(rows, target_up, narrow, (keeps[0],), (own,))
     target_own = exchange(own, 0, narrow)
     after = (up_keeps[0], *source_pieces[1:])

time: 53.7 us -> 49.6 us (0.924)
  waiting for transfers between devices: 16 us -> 13.9 us
  starting transfers between devices: 18.4 us -> 16.6 us
    ppermute x6, starting transfers between devices: 11.4 us -> 8.34 us  [gather_pieces(): lax.ppermute(source, axis, [(i, i ^ low) for i in range(size)])]
    ppermute x6, waiting for transfers between devices: 7.71 us -> 5.33 us  [gather_pieces(): lax.ppermute(source, axis, [(i, i ^ low) for i in range(size)])]
    ppermute x13 -> x14, starting transfers between devices: 6.99 us -> 8.29 us  [exchange(): lax.ppermute(array, 'narrow', [(i, i ^ 1 << step) for i in range(size)])]
    ppermute x13 -> x14, waiting for transfers between devices: 8.24 us -> 8.57 us  [exchange(): lax.ppermute(array, 'narrow', [(i, i ^ 1 << step) for i in range(size)])]
  transfers between devices with their start and end apart: 19 -> 20, of which waited for: 7 -> 7; matrix products, arithmetic and copies ran while one was open for 0% -> 0% of each run, Pallas kernels for 32% -> 34%
where the time goes in v11:
time: 49.6 us; the launch traced here: 49.4 us
  Pallas kernels  17.8 us (36%)
  starting transfers between devices  16.6 us (33%)
  waiting for transfers between devices  13.9 us (28%)
  between operations  0.93 us (2%)
    ppermute x14, waiting for transfers between devices, exchange(): lax.ppermute(array, 'narrow', [(i, i ^ 1 << step) for i in range(size)])  8.57 us
    pallas_call x4, Pallas kernels, product(): pl.pallas_call(functools.partial(product_kernel, len(tokens), len(after),...  8.36 us
    ppermute x6, starting transfers between devices, gather_pieces(): lax.ppermute(source, axis, [(i, i ^ low) for i in range(size)])  8.34 us
    ppermute x14, starting transfers between devices, exchange(): lax.ppermute(array, 'narrow', [(i, i ^ 1 << step) for i in range(size)])  8.29 us
    ppermute x6, waiting for transfers between devices, gather_pieces(): lax.ppermute(source, axis, [(i, i ^ low) for i in range(size)])  5.33 us
    pallas_call x1, Pallas kernels, load(): pl.pallas_call(load_kernel, out_shape=pltpu.VMEM(matrix.shape, matrix.dty...  5.18 us
    pallas_call x1, Pallas kernels, look_up(): pl.pallas_call(functools.partial(look_up_kernel, ids.shape[0] // lengths....  2.16 us
  transfers between devices with their start and end apart: 20, of which 7 were waited for; matrix products, arithmetic and copies ran while one was open for 0% of the time, Pallas kernels for 34%

profile of v11, /device:TPU:0, one launch (start us, length us, event | category | flops | bytes accessed | tf_op | source)
XLA Modules:
  0.0 49.4 jit_solution(13877103833669834337)
XLA Ops:
  0.6 4.1 %collective-permute-start.4 = (bf16[32,2048]{1,0:T(8,128)(2,1)}, bf16[32,2048]{1,0:T(8,128)(2,1)S(1)}, u32[]{:S(2)}, u32[]{:S(2)}) collective-permute-start(bf16[32,2048]{1,0:T(8,128)(2,1)} %refs_0_.2), channel_id=1, source_target_pairs={{0,8},{4,12},{8,0},{12,4},{1,9},{5,13},{9,1},{13,5},{2,10},{6,14},... | collective-permute-start | bytes 393224 | tf_op jit(solution)/shard_map/ppermute | solution.py:49
  4.7 1.6 %collective-permute-start.3 = (bf16[32,2048]{1,0:T(8,128)(2,1)}, bf16[32,2048]{1,0:T(8,128)(2,1)S(1)}, u32[]{:S(2)}, u32[]{:S(2)}) collective-permute-start(bf16[32,2048]{1,0:T(8,128)(2,1)} %refs_0_.2), channel_id=1, source_target_pairs={{0,4},{4,0},{8,12},{12,8},{1,5},{5,1},{9,13},{13,9},{2,6},{6,2},{1... | collective-permute-start | bytes 393224 | tf_op jit(solution)/shard_map/ppermute | solution.py:49
  6.3 0.3 collective-permute-start
  6.6 5.2 %shard_map.105.refs_0_.refs_4_ = bf16[2048,3584]{1,0:T(8,128)(2,1)S(1)} custom-call(bf16[2048,3584]{1,0:T(8,128)(2,1)} %matrix.1), custom_call_target="tpu_custom_call" | custom-call | tf_op jit(solution)/shard_map/pallas_call | solution.py:122
  11.8 0.0 copy-start
  11.8 0.0 copy-start.1
  11.9 0.0 slice-start
  11.9 0.0 slice-start.1
  11.9 1.0 %collective-permute-done.4.piece.refs_2_ = bf16[32,2048]{1,0:T(8,128)(2,1)S(1)} collective-permute-done((bf16[32,2048]{1,0:T(8,128)(2,1)}, bf16[32,2048]{1,0:T(8,128)(2,1)S(1)}, u32[]{:S(2)}, u32[]{:S(2)}) %collective-permute-start.4) | collective-permute-done | bytes 131104 | tf_op jit(solution)/shard_map/ppermute | solution.py:49
  12.9 0.0 slice-start.2
  12.9 0.2 collective-permute-start.5
  13.2 3.7 %collective-permute-done.refs_0_.refs_5_.refs_2_ = bf16[32,2048]{1,0:T(8,128)(2,1)S(1)} collective-permute-done((bf16[32,2048]{1,0:T(8,128)(2,1)}, bf16[32,2048]{1,0:T(8,128)(2,1)S(1)}, u32[]{:S(2)}, u32[]{:S(2)}) %collective-permute-start) | collective-permute-done | bytes 131104 | tf_op jit(solution)/shard_map/ppermute | solution.py:49
  16.9 0.0 slice-start.3
  16.9 0.0 slice-start.4
  16.9 0.0 slice-start.5
  17.0 0.9 %collective-permute-start.1 = (bf16[32,2048]{1,0:T(8,128)(2,1)S(1)}, bf16[32,2048]{1,0:T(8,128)(2,1)S(1)}, u32[]{:S(2)}, u32[]{:S(2)}) collective-permute-start(bf16[32,2048]{1,0:T(8,128)(2,1)S(1)} %shard_map.104), channel_id=1, source_target_pairs={{0,4},{4,0},{8,12},{12,8},{1,5},{5,1},{9,13},{13,9},{2,6},{6,2},{1... | collective-permute-start | bytes 393224 | tf_op jit(solution)/shard_map/ppermute | solution.py:49
  17.9 1.2 %collective-permute-start.2 = (bf16[32,2048]{1,0:T(8,128)(2,1)S(1)}, bf16[32,2048]{1,0:T(8,128)(2,1)S(1)}, u32[]{:S(2)}, u32[]{:S(2)}) collective-permute-start(bf16[32,2048]{1,0:T(8,128)(2,1)S(1)} %collective-permute-done.refs_0_.refs_5_.refs_2_), channel_id=1, source_target_pairs={{0,4},{4,0},{8,12},{12,8},{1,5},{5,1},{9,13},{13,9},{2,6},{6,2},{1... | collective-permute-start | bytes 393224 | tf_op jit(solution)/shard_map/ppermute | solution.py:49
  19.0 0.0 collective-permute-done.3.refs_1_
  19.0 0.0 collective-permute-done.5.refs_3_
  19.1 2.1 %shard_map.107 = (bf16[128,2048]{1,0:T(8,128)(2,1)S(1)}, bf16[32,1536]{1,0:T(8,128)(2,1)S(1)}, bf16[32,2048]{1,0:T(8,128)(2,1)S(1)}, bf16[32,3584]{1,0:T(8,128)(...) custom-call(bf16[32,2048]{1,0:T(8,128)(2,1)S(1)} %copy-done.1, ...), custom_call_target="tpu_custom_call" | custom-call | tf_op jit(solution)/shard_map/pallas_call | solution.py:187
  21.2 0.1 collective-permute-start.9
  21.2 0.5 %collective-permute-start.8 = (bf16[32,1536]{1,0:T(8,128)(2,1)S(1)}, bf16[32,1536]{1,0:T(8,128)(2,1)S(1)}, u32[]{:S(2)}, u32[]{:S(2)}) collective-permute-start(bf16[32,1536]{1,0:T(8,128)(2,1)S(1)} %get-tuple-element.34), channel_id=1, source_target_pairs={{0,1},{1,0},{2,3},{3,2},{4,5},{5,4},{6,7},{7,6},{8,9},{9,8},{10,11... | collective-permute-start | bytes 294920 | tf_op jit(solution)/shard_map/ppermute | solution.py:201
  21.8 0.0 slice-start.6
  21.8 0.0 slice-start.7
  21.8 0.0 slice-start.8
  21.8 0.0 slice-start.9
  21.8 2.1 %shard_map.108 = (bf16[32,1536]{1,0:T(8,128)(2,1)S(1)}, bf16[32,2048]{1,0:T(8,128)(2,1)S(1)}, bf16[32,3584]{1,0:T(8,128)(2,1)S(1)}, bf16[32,3584]{1,0:T(8,128)(2,1)S(1)}, bf16[32,7168]{1,0:T(8,128)(2,1)S(1)}) custom-call(bf16[128,2048]{1,0:T(8,128)(2,1)S(1)} %get-tuple-element.28.refs_0_, bf16[2048,3584]{1,0:T(8,128)(2,1)S(1)} %bitcast.2, ...), custom_call_target="tpu_custom_call" | custom-call | tf_op jit(solution)/shard_map/pallas_call | solution.py:187
  23.9 0.0 collective-permute-done.1.refs_4_.refs_1_
  23.9 0.6 %collective-permute-done.2.refs_6_.refs_3_ = bf16[32,2048]{1,0:T(8,128)(2,1)S(1)} collective-permute-done((bf16[32,2048]{1,0:T(8,128)(2,1)S(1)}, bf16[32,2048]{1,0:T(8,128)(2,1)S(1)}, u32[]{:S(2)}, u32[]{:S(2)}) %collective-permute-start.2) | collective-permute-done | bytes 131104 | tf_op jit(solution)/shard_map/ppermute | solution.py:49
  24.5 0.0 collective-permute-done.8.refs_1_
  24.5 0.0 collective-permute-done.9.refs_2_
  24.5 0.1 shard_map.109.refs_3_
  24.6 1.5 %collective-permute-start.10 = (bf16[32,3584]{1,0:T(8,128)(2,1)S(1)}, bf16[32,3584]{1,0:T(8,128)(2,1)S(1)}, u32[]{:S(2)}, u32[]{:S(2)}) collective-permute-start(bf16[32,3584]{1,0:T(8,128)(2,1)S(1)} %shard_map.109.refs_3_), channel_id=1, source_target_pairs={{0,2},{1,3},{2,0},{3,1},{4,6},{5,7},{6,4},{7,5},{8,10},{9,11},{10,... | collective-permute-start | bytes 688136 | tf_op jit(solution)/shard_map/ppermute | solution.py:201
  26.0 0.0 collective-permute-start.15
  26.0 0.5 %collective-permute-start.7 = (bf16[32,2048]{1,0:T(8,128)(2,1)S(1)}, bf16[32,2048]{1,0:T(8,128)(2,1)S(1)}, u32[]{:S(2)}, u32[]{:S(2)}) collective-permute-start(bf16[32,2048]{1,0:T(8,128)(2,1)S(1)} %get-tuple-element.33), channel_id=1, source_target_pairs={{0,1},{1,0},{2,3},{3,2},{4,5},{5,4},{6,7},{7,6},{8,9},{9,8},{10,11... | collective-permute-start | bytes 393224 | tf_op jit(solution)/shard_map/ppermute | solution.py:201
  26.5 0.0 collective-permute-start.6
  26.5 1.6 %collective-permute-done.6.refs_1_ = bf16[32,1536]{1,0:T(8,128)(2,1)S(1)} collective-permute-done((bf16[32,1536]{1,0:T(8,128)(2,1)S(1)}, bf16[32,1536]{1,0:T(8,128)(2,1)S(1)}, u32[]{:S(2)}, u32[]{:S(2)}) %collective-permute-start.6) | collective-permute-done | bytes 98336 | tf_op jit(solution)/shard_map/ppermute | solution.py:201
  28.2 0.0 collective-permute-done.7.refs_2_
  28.2 0.1 shard_map.110.refs_5_
  28.2 0.0 slice-start.11
  28.2 0.7 %collective-permute-start.16 = (bf16[32,3584]{1,0:T(8,128)(2,1)S(1)}, bf16[32,3584]{1,0:T(8,128)(2,1)S(1)}, u32[]{:S(2)}, u32[]{:S(2)}) collective-permute-start(bf16[32,3584]{1,0:T(8,128)(2,1)S(1)} %shard_map.110.refs_5_), channel_id=1, source_target_pairs={{0,2},{1,3},{2,0},{3,1},{4,6},{5,7},{6,4},{7,5},{8,10},{9,11},{10,... | collective-permute-start | bytes 688136 | tf_op jit(solution)/shard_map/ppermute | solution.py:201
  29.0 2.1 %shard_map.111 = (bf16[128,2048]{1,0:T(8,128)(2,1)S(1)}, bf16[32,1536]{1,0:T(8,128)(2,1)S(1)}, bf16[32,2048]{1,0:T(8,128)(2,1)S(1)}, bf16[32,3584]{1,0:T(8,128)(...) custom-call(bf16[32,2048]{1,0:T(8,128)(2,1)S(1)} %copy-done, ...), custom_call_target="tpu_custom_call" | custom-call | tf_op jit(solution)/shard_map/pallas_call | solution.py:187
  31.1 0.1 collective-permute-start.14
  31.1 0.5 %collective-permute-start.13 = (bf16[32,1536]{1,0:T(8,128)(2,1)S(1)}, bf16[32,1536]{1,0:T(8,128)(2,1)S(1)}, u32[]{:S(2)}, u32[]{:S(2)}) collective-permute-start(bf16[32,1536]{1,0:T(8,128)(2,1)S(1)} %get-tuple-element.42), channel_id=1, source_target_pairs={{0,1},{1,0},{2,3},{3,2},{4,5},{5,4},{6,7},{7,6},{8,9},{9,8},{10,11... | collective-permute-start | bytes 294920 | tf_op jit(solution)/shard_map/ppermute | solution.py:201
  31.6 0.6 %collective-permute-done.10.refs_4_.refs_2_ = bf16[32,3584]{1,0:T(8,128)(2,1)S(1)} collective-permute-done((bf16[32,3584]{1,0:T(8,128)(2,1)S(1)}, bf16[32,3584]{1,0:T(8,128)(2,1)S(1)}, u32[]{:S(2)}, u32[]{:S(2)}) %collective-permute-start.10) | collective-permute-done | bytes 229408 | tf_op jit(solution)/shard_map/ppermute | solution.py:201
  32.3 2.1 %shard_map.112 = (bf16[32,1536]{1,0:T(8,128)(2,1)S(1)}, bf16[32,2048]{1,0:T(8,128)(2,1)S(1)}, bf16[32,3584]{1,0:T(8,128)(2,1)S(1)}, bf16[32,3584]{1,0:T(8,128)(2,1)S(1)}, bf16[32,7168]{1,0:T(8,128)(2,1)S(1)}) custom-call(bf16[128,2048]{1,0:T(8,128)(2,1)S(1)} %get-tuple-element.36.refs_0_, bf16[2048,3584]{1,0:T(8,128)(2,1)S(1)} %bitcast.6, ...), custom_call_target="tpu_custom_call" | custom-call | tf_op jit(solution)/shard_map/pallas_call | solution.py:187
  34.3 0.1 collective-permute-start.17
  34.4 0.0 collective-permute-done.13.refs_1_
  34.4 0.5 collective-permute-start.12
  34.9 0.0 collective-permute-done.14.refs_2_
  34.9 0.1 collective-permute-start.11
  35.0 0.0 collective-permute-done.15.refs_4_.refs_1_
  35.0 0.1 shard_map.113.refs_3_
  35.1 2.4 %collective-permute-start.18 = (bf16[32,3584]{1,0:T(8,128)(2,1)S(1)}, bf16[32,3584]{1,0:T(8,128)(2,1)S(1)}, u32[]{:S(2)}, u32[]{:S(2)}) collective-permute-start(bf16[32,3584]{1,0:T(8,128)(2,1)S(1)} %shard_map.113.refs_3_), channel_id=1, source_target_pairs={{0,2},{1,3},{2,0},{3,1},{4,6},{5,7},{6,4},{7,5},{8,10},{9,11},{10,... | collective-permute-start | bytes 688136 | tf_op jit(solution)/shard_map/ppermute | solution.py:201
  37.4 0.0 collective-permute-done.16.refs_4_.refs_5_
  37.5 0.1 shard_map.114.refs_0_
  37.5 1.5 %collective-permute-start.19 = (bf16[32,3584]{1,0:T(8,128)(2,1)S(1)}, bf16[32,3584]{1,0:T(8,128)(2,1)S(1)}, u32[]{:S(2)}, u32[]{:S(2)}) collective-permute-start(bf16[32,3584]{1,0:T(8,128)(2,1)S(1)} %shard_map.114.refs_0_), channel_id=1, source_target_pairs={{0,2},{1,3},{2,0},{3,1},{4,6},{5,7},{6,4},{7,5},{8,10},{9,11},{10,... | collective-permute-start | bytes 688136 | tf_op jit(solution)/shard_map/ppermute | solution.py:201
  39.0 2.2 %shard_map.115 = (f32[32,128]{1,0:T(8,128)S(1)}, f32[32,128]{1,0:T(8,128)S(1)}) custom-call(s32[32]{0:T(128)} %ids.1, s32[2]{0:T(128)} %lengths.1, f32[1002,128]{1,0:T(8,128)} %bitcast.7, bf16[32,3584]{1,0:T(8,128)(2,1)S(1)} %shard_map.114.refs_0_), custom_call_target="tpu_custom_call" | custom-call | tf_op jit(solution)/shard_map/pallas_call | solution.py:100
  41.2 0.9 %shard_map.116 = (f32[32,3584]{1,0:T(8,128)S(1)}, bf16[32,3584]{1,0:T(8,128)(2,1)}) custom-call(f32[32,128]{1,0:T(8,128)S(1)} %get-tuple-element.45.live, bf16[32,3584]{1,0:T(8,128)(2,1)S(1)} %get-tuple-element.46.refs_0_, bf16[32,7168]{1,0:T(8,128)(2,1)S(1)} %collective-permute-done.15.refs_4_.refs_1_, ...), custom_call_target="tpu_custom_call" | custom-call | tf_op jit(solution)/shard_map/pallas_call | solution.py:259
  42.1 1.8 %collective-permute-done.18.refs_2_ = bf16[32,3584]{1,0:T(8,128)(2,1)S(1)} collective-permute-done((bf16[32,3584]{1,0:T(8,128)(2,1)S(1)}, bf16[32,3584]{1,0:T(8,128)(2,1)S(1)}, u32[]{:S(2)}, u32[]{:S(2)}) %collective-permute-start.18) | collective-permute-done | bytes 229408 | tf_op jit(solution)/shard_map/ppermute | solution.py:201
  43.9 0.0 collective-permute-done.17.refs_1_
  43.9 0.1 shard_map.117.gated
  44.1 4.5 %collective-permute-done.19.refs_2_ = bf16[32,3584]{1,0:T(8,128)(2,1)S(1)} collective-permute-done((bf16[32,3584]{1,0:T(8,128)(2,1)S(1)}, bf16[32,3584]{1,0:T(8,128)(2,1)S(1)}, u32[]{:S(2)}, u32[]{:S(2)}) %collective-permute-start.19) | collective-permute-done | bytes 229408 | tf_op jit(solution)/shard_map/ppermute | solution.py:201
  48.6 0.8 %shard_map.118 = bf16[32,3584]{1,0:T(8,128)(2,1)} custom-call(f32[32,3584]{1,0:T(8,128)S(1)} %get-tuple-element.49.act, f32[32,3584]{1,0:T(8,128)S(1)} %shard_map.117.gated, bf16[32,3584]{1,0:T(8,128)(2,1)S(1)} %get-tuple-element.53.refs_0_, bf16[32,7168]{1,0:T(8,128)(2,1)S(1)} %collective-permute-done.17.refs_1_, ...), custom_call_target="tpu_custom_call" | custom-call | tf_op jit(solution)/shard_map/pallas_call | solution.py:295
  (22 shorter events, 0.1 us)
Async XLA Ops:
  0.6 12.3 %collective-permute-start.4 = (bf16[32,2048]{1,0:T(8,128)(2,1)}, bf16[32,2048]{1,0:T(8,128)(2,1)S(1)}, u32[]{:S(2)}, u32[]{:S(2)}) collective-permute-start(bf16[32,2048]{1,0:T(8,128)(2,1)} %refs_0_.2), channel_id=1, source_target_pairs={{0,8},{4,12},{8,0},{12,4},{1,9},{5,13},{9,1},{13,5},{2,10},{6,14},... | collective-permute-start | bytes 393224 | tf_op jit(solution)/shard_map/ppermute | solution.py:49
  4.7 14.3 %collective-permute-start.3 = (bf16[32,2048]{1,0:T(8,128)(2,1)}, bf16[32,2048]{1,0:T(8,128)(2,1)S(1)}, u32[]{:S(2)}, u32[]{:S(2)}) collective-permute-start(bf16[32,2048]{1,0:T(8,128)(2,1)} %refs_0_.2), channel_id=1, source_target_pairs={{0,4},{4,0},{8,12},{12,8},{1,5},{5,1},{9,13},{13,9},{2,6},{6,2},{1... | collective-permute-start | bytes 393224 | tf_op jit(solution)/shard_map/ppermute | solution.py:49
  6.3 10.6 %collective-permute-start = (bf16[32,2048]{1,0:T(8,128)(2,1)}, bf16[32,2048]{1,0:T(8,128)(2,1)S(1)}, u32[]{:S(2)}, u32[]{:S(2)}) collective-permute-start(bf16[32,2048]{1,0:T(8,128)(2,1)} %refs_0_.3), channel_id=1, source_target_pairs={{0,8},{4,12},{8,0},{12,4},{1,9},{5,13},{9,1},{13,5},{2,10},{6,14},... | collective-permute-start | bytes 393224 | tf_op jit(solution)/shard_map/ppermute | solution.py:49
  11.8 5.1 %copy-start = (bf16[32,2048]{1,0:T(8,128)(2,1)S(1)}, bf16[32,2048]{1,0:T(8,128)(2,1)}, u32[]{:S(2)}) copy-start(bf16[32,2048]{1,0:T(8,128)(2,1)} %refs_0_.3) | copy-start | bytes 393220
  11.8 7.2 %copy-start.1 = (bf16[32,2048]{1,0:T(8,128)(2,1)S(1)}, bf16[32,2048]{1,0:T(8,128)(2,1)}, u32[]{:S(2)}) copy-start(bf16[32,2048]{1,0:T(8,128)(2,1)} %refs_0_.2) | copy-start | bytes 393220
  11.9 9.9 %slice-start = ((s8[14680064]{0:T(1024)(128)(4,1)}), s8[4194304]{0:T(1024)(128)(4,1)S(1)}, s32[]{:S(2)}) async-start(s8[14680064]{0:T(1024)(128)(4,1)} %bitcast.1), calls=%async_computation | async-start | bytes 8388608
  11.9 9.9 %slice-start.1 = ((s8[14680064]{0:T(1024)(128)(4,1)}), s8[4194304]{0:T(1024)(128)(4,1)S(1)}, s32[]{:S(2)}) async-start(s8[14680064]{0:T(1024)(128)(4,1)} %bitcast.1), calls=%async_computation.1 | async-start | bytes 8388608
  12.9 8.8 %slice-start.2 = ((s8[14680064]{0:T(1024)(128)(4,1)}), s8[4194304]{0:T(1024)(128)(4,1)S(1)}, s32[]{:S(2)}) async-start(s8[14680064]{0:T(1024)(128)(4,1)} %bitcast.1), calls=%async_computation.2 | async-start | bytes 8388608
  12.9 6.1 %collective-permute-start.5 = (bf16[32,2048]{1,0:T(8,128)(2,1)S(1)}, bf16[32,2048]{1,0:T(8,128)(2,1)S(1)}, u32[]{:S(2)}, u32[]{:S(2)}) collective-permute-start(bf16[32,2048]{1,0:T(8,128)(2,1)S(1)} %shard_map.106), channel_id=1, source_target_pairs={{0,4},{4,0},{8,12},{12,8},{1,5},{5,1},{9,13},{13,9},{2,6},{6,2},{1... | collective-permute-start | bytes 393224 | tf_op jit(solution)/shard_map/ppermute | solution.py:49
  16.9 4.8 %slice-start.3 = ((s8[14680064]{0:T(1024)(128)(4,1)}), s8[2097152]{0:T(1024)(128)(4,1)S(1)}, s32[]{:S(2)}) async-start(s8[14680064]{0:T(1024)(128)(4,1)} %bitcast.1), calls=%async_computation.3 | async-start | bytes 4194304
  16.9 12.0 %slice-start.4 = ((s8[14680064]{0:T(1024)(128)(4,1)}), s8[4194304]{0:T(1024)(128)(4,1)S(1)}, s32[]{:S(2)}) async-start(s8[14680064]{0:T(1024)(128)(4,1)} %bitcast.3), calls=%async_computation.4 | async-start | bytes 8388608
  16.9 12.0 %slice-start.5 = ((s8[14680064]{0:T(1024)(128)(4,1)}), s8[4194304]{0:T(1024)(128)(4,1)S(1)}, s32[]{:S(2)}) async-start(s8[14680064]{0:T(1024)(128)(4,1)} %bitcast.3), calls=%async_computation.5 | async-start | bytes 8388608
  17.0 6.9 %collective-permute-start.1 = (bf16[32,2048]{1,0:T(8,128)(2,1)S(1)}, bf16[32,2048]{1,0:T(8,128)(2,1)S(1)}, u32[]{:S(2)}, u32[]{:S(2)}) collective-permute-start(bf16[32,2048]{1,0:T(8,128)(2,1)S(1)} %shard_map.104), channel_id=1, source_target_pairs={{0,4},{4,0},{8,12},{12,8},{1,5},{5,1},{9,13},{13,9},{2,6},{6,2},{1... | collective-permute-start | bytes 393224 | tf_op jit(solution)/shard_map/ppermute | solution.py:49
  17.9 6.6 %collective-permute-start.2 = (bf16[32,2048]{1,0:T(8,128)(2,1)S(1)}, bf16[32,2048]{1,0:T(8,128)(2,1)S(1)}, u32[]{:S(2)}, u32[]{:S(2)}) collective-permute-start(bf16[32,2048]{1,0:T(8,128)(2,1)S(1)} %collective-permute-done.refs_0_.refs_5_.refs_2_), channel_id=1, source_target_pairs={{0,4},{4,0},{8,12},{12,8},{1,5},{5,1},{9,13},{13,9},{2,6},{6,2},{1... | collective-permute-start | bytes 393224 | tf_op jit(solution)/shard_map/ppermute | solution.py:49
  21.2 3.3 %collective-permute-start.9 = (bf16[32,2048]{1,0:T(8,128)(2,1)S(1)}, bf16[32,2048]{1,0:T(8,128)(2,1)S(1)}, u32[]{:S(2)}, u32[]{:S(2)}) collective-permute-start(bf16[32,2048]{1,0:T(8,128)(2,1)S(1)} %get-tuple-element.35), channel_id=1, source_target_pairs={{0,1},{1,0},{2,3},{3,2},{4,5},{5,4},{6,7},{7,6},{8,9},{9,8},{10,11... | collective-permute-start | bytes 393224 | tf_op jit(solution)/shard_map/ppermute | solution.py:201
  21.2 3.2 %collective-permute-start.8 = (bf16[32,1536]{1,0:T(8,128)(2,1)S(1)}, bf16[32,1536]{1,0:T(8,128)(2,1)S(1)}, u32[]{:S(2)}, u32[]{:S(2)}) collective-permute-start(bf16[32,1536]{1,0:T(8,128)(2,1)S(1)} %get-tuple-element.34), channel_id=1, source_target_pairs={{0,1},{1,0},{2,3},{3,2},{4,5},{5,4},{6,7},{7,6},{8,9},{9,8},{10,11... | collective-permute-start | bytes 294920 | tf_op jit(solution)/shard_map/ppermute | solution.py:201
  21.8 7.2 %slice-start.6 = ((s8[14680064]{0:T(1024)(128)(4,1)}), s8[4194304]{0:T(1024)(128)(4,1)S(1)}, s32[]{:S(2)}) async-start(s8[14680064]{0:T(1024)(128)(4,1)} %bitcast.3), calls=%async_computation.6 | async-start | bytes 8388608
  21.8 7.2 %slice-start.7 = ((s8[14680064]{0:T(1024)(128)(4,1)}), s8[2097152]{0:T(1024)(128)(4,1)S(1)}, s32[]{:S(2)}) async-start(s8[14680064]{0:T(1024)(128)(4,1)} %bitcast.3), calls=%async_computation.7 | async-start | bytes 4194304
  21.8 10.4 %slice-start.8 = ((s8[14680064]{0:T(1024)(128)(4,1)}), s8[4194304]{0:T(1024)(128)(4,1)S(1)}, s32[]{:S(2)}) async-start(s8[14680064]{0:T(1024)(128)(4,1)} %bitcast.5), calls=%async_computation.8 | async-start | bytes 8388608
  21.8 10.4 %slice-start.9 = ((s8[14680064]{0:T(1024)(128)(4,1)}), s8[4194304]{0:T(1024)(128)(4,1)S(1)}, s32[]{:S(2)}) async-start(s8[14680064]{0:T(1024)(128)(4,1)} %bitcast.5), calls=%async_computation.9 | async-start | bytes 8388608
  24.5 7.8 %slice-start.10 = ((s8[14680064]{0:T(1024)(128)(4,1)}), s8[4194304]{0:T(1024)(128)(4,1)S(1)}, s32[]{:S(2)}) async-start(s8[14680064]{0:T(1024)(128)(4,1)} %bitcast.5), calls=%async_computation.10 | async-start | bytes 8388608
  24.6 7.7 %collective-permute-start.10 = (bf16[32,3584]{1,0:T(8,128)(2,1)S(1)}, bf16[32,3584]{1,0:T(8,128)(2,1)S(1)}, u32[]{:S(2)}, u32[]{:S(2)}) collective-permute-start(bf16[32,3584]{1,0:T(8,128)(2,1)S(1)} %shard_map.109.refs_3_), channel_id=1, source_target_pairs={{0,2},{1,3},{2,0},{3,1},{4,6},{5,7},{6,4},{7,5},{8,10},{9,11},{10,... | collective-permute-start | bytes 688136 | tf_op jit(solution)/shard_map/ppermute | solution.py:201
  26.0 9.0 %collective-permute-start.15 = (bf16[32,7168]{1,0:T(8,128)(2,1)S(1)}, bf16[32,7168]{1,0:T(8,128)(2,1)S(1)}, u32[]{:S(2)}, u32[]{:S(2)}) collective-permute-start(bf16[32,7168]{1,0:T(8,128)(2,1)S(1)} %get-tuple-element.44), channel_id=1, source_target_pairs={{0,1},{1,0},{2,3},{3,2},{4,5},{5,4},{6,7},{7,6},{8,9},{9,8},{10,11... | collective-permute-start | bytes 1376264 | tf_op jit(solution)/shard_map/ppermute | solution.py:201
  26.0 2.1 %collective-permute-start.7 = (bf16[32,2048]{1,0:T(8,128)(2,1)S(1)}, bf16[32,2048]{1,0:T(8,128)(2,1)S(1)}, u32[]{:S(2)}, u32[]{:S(2)}) collective-permute-start(bf16[32,2048]{1,0:T(8,128)(2,1)S(1)} %get-tuple-element.33), channel_id=1, source_target_pairs={{0,1},{1,0},{2,3},{3,2},{4,5},{5,4},{6,7},{7,6},{8,9},{9,8},{10,11... | collective-permute-start | bytes 393224 | tf_op jit(solution)/shard_map/ppermute | solution.py:201
  26.5 1.6 %collective-permute-start.6 = (bf16[32,1536]{1,0:T(8,128)(2,1)S(1)}, bf16[32,1536]{1,0:T(8,128)(2,1)S(1)}, u32[]{:S(2)}, u32[]{:S(2)}) collective-permute-start(bf16[32,1536]{1,0:T(8,128)(2,1)S(1)} %get-tuple-element.32), channel_id=1, source_target_pairs={{0,1},{1,0},{2,3},{3,2},{4,5},{5,4},{6,7},{7,6},{8,9},{9,8},{10,11... | collective-permute-start | bytes 294920 | tf_op jit(solution)/shard_map/ppermute | solution.py:201
  28.2 4.0 %slice-start.11 = ((s8[14680064]{0:T(1024)(128)(4,1)}), s8[2097152]{0:T(1024)(128)(4,1)S(1)}, s32[]{:S(2)}) async-start(s8[14680064]{0:T(1024)(128)(4,1)} %bitcast.5), calls=%async_computation.11 | async-start | bytes 4194304
  28.2 9.2 %collective-permute-start.16 = (bf16[32,3584]{1,0:T(8,128)(2,1)S(1)}, bf16[32,3584]{1,0:T(8,128)(2,1)S(1)}, u32[]{:S(2)}, u32[]{:S(2)}) collective-permute-start(bf16[32,3584]{1,0:T(8,128)(2,1)S(1)} %shard_map.110.refs_5_), channel_id=1, source_target_pairs={{0,2},{1,3},{2,0},{3,1},{4,6},{5,7},{6,4},{7,5},{8,10},{9,11},{10,... | collective-permute-start | bytes 688136 | tf_op jit(solution)/shard_map/ppermute | solution.py:201
  31.1 3.9 %collective-permute-start.14 = (bf16[32,2048]{1,0:T(8,128)(2,1)S(1)}, bf16[32,2048]{1,0:T(8,128)(2,1)S(1)}, u32[]{:S(2)}, u32[]{:S(2)}) collective-permute-start(bf16[32,2048]{1,0:T(8,128)(2,1)S(1)} %get-tuple-element.43), channel_id=1, source_target_pairs={{0,1},{1,0},{2,3},{3,2},{4,5},{5,4},{6,7},{7,6},{8,9},{9,8},{10,11... | collective-permute-start | bytes 393224 | tf_op jit(solution)/shard_map/ppermute | solution.py:201
  31.1 3.3 %collective-permute-start.13 = (bf16[32,1536]{1,0:T(8,128)(2,1)S(1)}, bf16[32,1536]{1,0:T(8,128)(2,1)S(1)}, u32[]{:S(2)}, u32[]{:S(2)}) collective-permute-start(bf16[32,1536]{1,0:T(8,128)(2,1)S(1)} %get-tuple-element.42), channel_id=1, source_target_pairs={{0,1},{1,0},{2,3},{3,2},{4,5},{5,4},{6,7},{7,6},{8,9},{9,8},{10,11... | collective-permute-start | bytes 294920 | tf_op jit(solution)/shard_map/ppermute | solution.py:201
  34.3 9.6 %collective-permute-start.17 = (bf16[32,7168]{1,0:T(8,128)(2,1)S(1)}, bf16[32,7168]{1,0:T(8,128)(2,1)S(1)}, u32[]{:S(2)}, u32[]{:S(2)}) collective-permute-start(bf16[32,7168]{1,0:T(8,128)(2,1)S(1)} %get-tuple-element.52), channel_id=1, source_target_pairs={{0,1},{1,0},{2,3},{3,2},{4,5},{5,4},{6,7},{7,6},{8,9},{9,8},{10,11... | collective-permute-start | bytes 1376264 | tf_op jit(solution)/shard_map/ppermute | solution.py:201
  34.4 3.0 %collective-permute-start.12 = (bf16[32,2048]{1,0:T(8,128)(2,1)S(1)}, bf16[32,2048]{1,0:T(8,128)(2,1)S(1)}, u32[]{:S(2)}, u32[]{:S(2)}) collective-permute-start(bf16[32,2048]{1,0:T(8,128)(2,1)S(1)} %get-tuple-element.41), channel_id=1, source_target_pairs={{0,1},{1,0},{2,3},{3,2},{4,5},{5,4},{6,7},{7,6},{8,9},{9,8},{10,11... | collective-permute-start | bytes 393224 | tf_op jit(solution)/shard_map/ppermute | solution.py:201
  34.9 2.5 %collective-permute-start.11 = (bf16[32,1536]{1,0:T(8,128)(2,1)S(1)}, bf16[32,1536]{1,0:T(8,128)(2,1)S(1)}, u32[]{:S(2)}, u32[]{:S(2)}) collective-permute-start(bf16[32,1536]{1,0:T(8,128)(2,1)S(1)} %get-tuple-element.40), channel_id=1, source_target_pairs={{0,1},{1,0},{2,3},{3,2},{4,5},{5,4},{6,7},{7,6},{8,9},{9,8},{10,11... | collective-permute-start | bytes 294920 | tf_op jit(solution)/shard_map/ppermute | solution.py:201
  35.1 8.8 %collective-permute-start.18 = (bf16[32,3584]{1,0:T(8,128)(2,1)S(1)}, bf16[32,3584]{1,0:T(8,128)(2,1)S(1)}, u32[]{:S(2)}, u32[]{:S(2)}) collective-permute-start(bf16[32,3584]{1,0:T(8,128)(2,1)S(1)} %shard_map.113.refs_3_), channel_id=1, source_target_pairs={{0,2},{1,3},{2,0},{3,1},{4,6},{5,7},{6,4},{7,5},{8,10},{9,11},{10,... | collective-permute-start | bytes 688136 | tf_op jit(solution)/shard_map/ppermute | solution.py:201
  37.5 11.0 %collective-permute-start.19 = (bf16[32,3584]{1,0:T(8,128)(2,1)S(1)}, bf16[32,3584]{1,0:T(8,128)(2,1)S(1)}, u32[]{:S(2)}, u32[]{:S(2)}) collective-permute-start(bf16[32,3584]{1,0:T(8,128)(2,1)S(1)} %shard_map.114.refs_0_), channel_id=1, source_target_pairs={{0,2},{1,3},{2,0},{3,1},{4,6},{5,7},{6,4},{7,5},{8,10},{9,11},{10,... | collective-permute-start | bytes 688136 | tf_op jit(solution)/shard_map/ppermute | solution.py:201

commit v12 on v11

--- a/solution.py
+++ b/solution.py
@@ -22,33 +22,60 @@
     return pltpu.with_memory_space_constraint(array, pltpu.VMEM)
 
 
-def pass_kernel(piece, *refs):
-    refs[-1][...] = piece[...]
-
-
-def passed(piece, after):
-    return pl.pallas_call(
-        pass_kernel,
-        out_shape=jax.ShapeDtypeStruct(piece.shape, piece.dtype),
-        in_specs=[IN_VMEM] + [ANYWHERE] * len(after),
+def pass_kernel(count, *refs):
+    for source, dest in zip(refs[:count], refs[-count:]):
+        dest[...] = source[...]
+
+
+def passed(arrays, after):
+    return pl.pallas_call(
+        functools.partial(pass_kernel, len(arrays)),
+        out_shape=[jax.ShapeDtypeStruct(a.shape, a.dtype) for a in arrays],
+        in_specs=[IN_VMEM] * len(arrays) + [ANYWHERE] * len(after),
+        out_specs=[IN_VMEM] * len(arrays),
+        compiler_params=pltpu.CompilerParams(vmem_limit_bytes=2 << 20),
+    )(*arrays, *after)
+
+
+def stack_kernel(*refs):
+    row = 0
+    for source in refs[:-1]:
+        refs[-1][row : row + source.shape[0], :] = source[...]
+        row += source.shape[0]
+
+
+def stacked(arrays):
+    rows = sum(a.shape[0] for a in arrays)
+    return pl.pallas_call(
+        stack_kernel,
+        out_shape=jax.ShapeDtypeStruct((rows, arrays[0].shape[1]), arrays[0].dtype),
+        in_specs=[IN_VMEM] * len(arrays),
         out_specs=IN_VMEM,
-        compiler_params=pltpu.CompilerParams(vmem_limit_bytes=1 << 20),
-    )(piece, *after)
-
-
-def gather_pieces(piece, axis, size, chained=False, relays_after=None):
-    pieces = [piece] + [None] * (size - 1)
-    after, near = None, [1 << b for b in range(size.bit_length() - 1)]
-    for offset in near[::-1] + [o for o in range(size) if o & (o - 1)]:
+        compiler_params=pltpu.CompilerParams(vmem_limit_bytes=2 << 20),
+    )(*arrays)
+
+
+def gather_pieces(piece, axis, size, relays_after):
+    pieces = [piece]
+    for offset in range(1, size):
         low = offset & -offset
         source = pieces[offset ^ low]
-        if after is not None and offset == low:
-            source = passed(piece, (after,))
-        if relays_after is not None and offset != low:
-            source = passed(source, (relays_after,))
-        pieces[offset] = lax.ppermute(source, axis, [(i, i ^ low) for i in range(size)])
-        after = pieces[offset] if chained else None
-    return pieces
+        if offset != low:
+            (source,) = passed([source], (relays_after,))
+        pieces.append(lax.ppermute(source, axis, [(i, i ^ low) for i in range(size)]))
+    return pieces, [(i, 0) for i in range(size)]
+
+
+def gather_doubling(piece, axis, size):
+    arrays, order, spots, low = [piece], [0], {0: (0, 0)}, size // 2
+    while low:
+        send = stacked(arrays) if len(arrays) > 1 else piece
+        arrays.append(lax.ppermute(send, axis, [(i, i ^ low) for i in range(size)]))
+        for place, offset in enumerate(order):
+            spots[offset ^ low] = (len(arrays) - 1, place * piece.shape[0])
+        order += [offset ^ low for offset in order]
+        low //= 2
+    return arrays, [spots[offset] for offset in range(size)]
 
 
 def halving_order(size):
@@ -57,12 +84,12 @@
     return reverse[::-1]
 
 
-def place_rows(pieces, rows, narrow):
+def place_rows(arrays, spots, rows, narrow):
     me_wide, me_narrow = lax.axis_index("wide"), lax.axis_index("narrow")
-    piece_rows = pieces[0].shape[0]
-    block_rows = piece_rows * len(pieces) // narrow
+    piece_rows = rows.shape[0] // len(spots)
+    block_rows = rows.shape[0] // narrow
     size = math.gcd(piece_rows, block_rows)
-    for offset, piece in enumerate(pieces):
+    for offset, (index, first) in enumerate(spots):
         for start in range(0, piece_rows, size):
             row = (me_wide ^ offset) * piece_rows + start
             block = (row // block_rows) ^ me_narrow
@@ -71,7 +98,7 @@
                 for position, known in enumerate(halving_order(narrow))
             )
             spot = pl.multiple_of(place * block_rows + row % block_rows, size)
-            rows[pl.ds(spot, size), :] = piece[start : start + size, :]
+            rows[pl.ds(spot, size), :] = arrays[index][first + start : first + start + size, :]
 
 
 def look_up_kernel(slots, ids, lengths, table, *refs):
@@ -147,12 +174,12 @@
     return [(0, first), (first, width - first)] if first else [(0, width)]
 
 
-def product_kernel(pieces, after, narrow, blocks, *refs):
+def product_kernel(pieces, spots, after, narrow, blocks, *refs):
     tokens, matrix = refs[:pieces], refs[pieces]
     beside, outs = refs[pieces + 1 : len(refs) - len(blocks) - (pieces > 1) - after], refs[-len(blocks) :]
     if pieces > 1:
         rows = refs[-len(blocks) - 1]
-        place_rows(tokens, rows, narrow)
+        place_rows(tokens, spots, rows, narrow)
         tokens = [rows]
     for earlier in beside:
         outs[-1][:, : earlier.shape[1]] = earlier[...]
@@ -172,12 +199,12 @@
     return sizes + [left]
 
 
-def product(tokens, matrix, narrow, after, beside=(), split=True):
+def product(tokens, matrix, narrow, after, beside=(), spots=()):
     placing = len(tokens) > 1
     total = sum(t.shape[0] for t in tokens)
     depth, width = matrix.shape
     sizes = part_sizes(total, narrow)
-    sent = [(k, *cols) for k in range(len(sizes) - 1) for cols in (column_chunks(width) if split else [(0, width)])]
+    sent = [(k, *cols) for k in range(len(sizes) - 1) for cols in column_chunks(width)]
     ahead = sum(b.shape[1] for b in beside)
     blocks = [(sum(sizes[:k]), first) for k, first, _ in sent]
     blocks += [(total // 2 + sum(sizes[:k]), 0) for k in range(len(sizes))]
@@ -185,7 +212,7 @@
     shapes = [(sizes[k], count) for k, _, count in sent] + [(size, width) for size in sizes]
     shapes += [(sizes[-1], ahead + width)]
     found = pl.pallas_call(
-        functools.partial(product_kernel, len(tokens), len(after), narrow, blocks),
+        functools.partial(product_kernel, len(tokens), spots, len(after), narrow, blocks),
         out_shape=[jax.ShapeDtypeStruct((total, depth), tokens[0].dtype)] * placing
         + [jax.ShapeDtypeStruct(shape, jnp.bfloat16) for shape in shapes],
         in_specs=[IN_VMEM] * (len(tokens) + 1 + len(beside)) + [ANYWHERE] * len(after),
@@ -195,6 +222,13 @@
     rows, found = (found[:1], found[1:]) if placing else (tokens, found)
     sends = [(array, k, first) for array, (k, first, _) in zip(found, sent)]
     return rows, sends, found[-1], found[len(sent) : -1]
+
+
+def resent(sends, after):
+    if not sends:
+        return sends
+    arrays = passed([array for array, _, _ in sends], after)
+    return [(array, k, col) for array, (_, k, col) in zip(arrays, sends)]
 
 
 def exchange(array, step, size):
@@ -304,23 +338,23 @@
 def local(mesh_shape, target_states, source_states, target_gate, target_up, source_gate, source_up, token_ids, lengths, ratio_weight):
     wide, narrow = mesh_shape["wide"], mesh_shape["narrow"]
     target_gate = load(target_gate)
-    target_pieces = gather_pieces(target_states, "wide", wide, relays_after=target_gate)
-    source_pieces = gather_pieces(source_states, "wide", wide, chained=True)
+    target_pieces, target_spots = gather_pieces(target_states, "wide", wide, target_gate)
+    source_pieces, source_spots = gather_doubling(source_states, "wide", wide)
     width = target_gate.shape[1]
 
-    rows, sends, own, keeps = product(target_pieces, target_gate, narrow, ())
+    rows, sends, own, keeps = product(target_pieces, target_gate, narrow, (), spots=target_spots)
     _, up_sends, own, up_keeps = product(rows, target_up, narrow, (keeps[0],), (own,))
     target_own = exchange(own, 0, narrow)
     after = (up_keeps[0], *source_pieces[1:])
     sent, target_g = finish(sends, keeps, (target_own, 0), narrow, after)
-    sent, target_u = finish(up_sends, up_keeps, (target_own, -width), narrow, (sent,))
-
-    rows, sends, own, keeps = product(source_pieces, source_gate, narrow, (sent,))
-    after = (keeps[0], target_g[0][-1])
-    _, up_sends, own, up_keeps = product(rows, source_up, narrow, after, (own,))
+    rows, gate_sends, own, gate_keeps = product(source_pieces, source_gate, narrow, (sent,), spots=source_spots)
+    after = (gate_keeps[0],)
+    sent, target_u = finish(up_sends, up_keeps, (target_own, -width), narrow, after)
+    _, sends, own, keeps = product(rows, source_up, narrow, (sent,), (own,))
+    sends = resent(sends, (target_g[0][-1],))
     own = exchange(own, 0, narrow)
-    sent, source_g = finish(sends, keeps, (own, 0), narrow, (up_keeps[0], target_own))
-    sent, source_u = finish(up_sends, up_keeps, (own, -width), narrow, (sent, target_u[0][-1]))
+    sent, source_g = finish(gate_sends, gate_keeps, (own, 0), narrow, (keeps[0], target_own))
+    sent, source_u = finish(sends, keeps, (own, -width), narrow, (sent, target_u[0][-1]))
     live, weight = look_up(token_ids, lengths, ratio_weight, (sent,))
     act, target_out = target_end(live, target_g, target_u)
     gated = source_middle(live, weight, source_g)

time: 49.6 us -> 50.5 us (1.018)
  waiting for transfers between devices: 13.9 us -> 15.9 us
  starting transfers between devices: 16.6 us -> 15.6 us
    ppermute x6 -> x3, starting transfers between devices: 8.34 us -> 6.09 us  [gather_pieces(): lax.ppermute(source, axis, [(i, i ^ low) for i in range(size)])]
    ppermute x0 -> x2, waiting for transfers between devices: none -> 1.9 us  [gather_doubling(): arrays.append(lax.ppermute(send, axis, [(i, i ^ low) for i in range(size)]))]
    ppermute x6 -> x3, waiting for transfers between devices: 5.33 us -> 6.21 us  [gather_pieces(): lax.ppermute(source, axis, [(i, i ^ low) for i in range(size)])]
    ppermute x0 -> x2, starting transfers between devices: none -> 0.87 us  [gather_doubling(): arrays.append(lax.ppermute(send, axis, [(i, i ^ low) for i in range(size)]))]
    ppermute x14, waiting for transfers between devices: 8.57 us -> 7.83 us  [exchange(): lax.ppermute(array, 'narrow', [(i, i ^ 1 << step) for i in range(size)])]
    pallas_call x6 -> x7, Pallas kernels: 8.37 us -> 8.4 us  [the longest x4 8.35 us: product(): pl.pallas_call(functools.partial(product_kernel, len(tokens), spots, len(...]
  transfers between devices with their start and end apart: 20 -> 19, of which waited for: 7 -> 8; matrix products, arithmetic and copies ran while one was open for 0% -> 0% of each run, Pallas kernels for 34% -> 34%
where the time goes in v12:
time: 50.5 us; the launch traced here: 50.3 us
  Pallas kernels  17.8 us (35%)
  waiting for transfers between devices  15.9 us (31%)
  starting transfers between devices  15.6 us (31%)
  between operations  0.88 us (2%)
    ppermute x14, starting transfers between devices, exchange(): lax.ppermute(array, 'narrow', [(i, i ^ 1 << step) for i in range(size)])  8.62 us
    pallas_call x4, Pallas kernels, product(): pl.pallas_call(functools.partial(product_kernel, len(tokens), spots, len(...  8.35 us
    ppermute x14, waiting for transfers between devices, exchange(): lax.ppermute(array, 'narrow', [(i, i ^ 1 << step) for i in range(size)])  7.83 us
    ppermute x3, waiting for transfers between devices, gather_pieces(): lax.ppermute(source, axis, [(i, i ^ low) for i in range(size)])  6.21 us
    ppermute x3, starting transfers between devices, gather_pieces(): lax.ppermute(source, axis, [(i, i ^ low) for i in range(size)])  6.09 us
    pallas_call x1, Pallas kernels, load(): pl.pallas_call(load_kernel, out_shape=pltpu.VMEM(matrix.shape, matrix.dty...  5.18 us
    pallas_call x1, Pallas kernels, look_up(): pl.pallas_call(functools.partial(look_up_kernel, ids.shape[0] // lengths....  2.16 us
    ppermute x2, waiting for transfers between devices, gather_doubling(): arrays.append(lax.ppermute(send, axis, [(i, i ^ low) for i in range(size)]))  1.9 us
  transfers between devices with their start and end apart: 19, of which 8 were waited for; matrix products, arithmetic and copies ran while one was open for 0% of the time, Pallas kernels for 34%

profile of v12, /device:TPU:0, one launch (start us, length us, event | category | flops | bytes accessed | tf_op | source)
XLA Modules:
  0.0 50.3 jit_solution(5388428735519363819)
XLA Ops:
  0.6 4.1 %collective-permute-start.3 = (bf16[32,2048]{1,0:T(8,128)(2,1)}, bf16[32,2048]{1,0:T(8,128)(2,1)S(1)}, u32[]{:S(2)}, u32[]{:S(2)}) collective-permute-start(bf16[32,2048]{1,0:T(8,128)(2,1)} %refs_0_.4), channel_id=1, source_target_pairs={{0,8},{4,12},{8,0},{12,4},{1,9},{5,13},{9,1},{13,5},{2,10},{6,14},... | collective-permute-start | bytes 393224 | tf_op jit(solution)/shard_map/ppermute | solution.py:65
  4.7 0.1 collective-permute-start
  4.8 1.8 %collective-permute-start.2 = (bf16[32,2048]{1,0:T(8,128)(2,1)}, bf16[32,2048]{1,0:T(8,128)(2,1)S(1)}, u32[]{:S(2)}, u32[]{:S(2)}) collective-permute-start(bf16[32,2048]{1,0:T(8,128)(2,1)} %refs_0_.4), channel_id=1, source_target_pairs={{0,4},{4,0},{8,12},{12,8},{1,5},{5,1},{9,13},{13,9},{2,6},{6,2},{1... | collective-permute-start | bytes 393224 | tf_op jit(solution)/shard_map/ppermute | solution.py:65
  6.6 5.2 %shard_map.105.refs_1_.refs_4_ = bf16[2048,3584]{1,0:T(8,128)(2,1)S(1)} custom-call(bf16[2048,3584]{1,0:T(8,128)(2,1)} %matrix.1), custom_call_target="tpu_custom_call" | custom-call | tf_op jit(solution)/shard_map/pallas_call | solution.py:149
  11.8 0.0 copy-start
  11.8 0.0 copy-start.1
  11.9 0.0 slice-start
  11.9 0.0 slice-start.1
  11.9 3.0 %collective-permute-done.3.refs_0_.refs_2_ = bf16[32,2048]{1,0:T(8,128)(2,1)S(1)} collective-permute-done((bf16[32,2048]{1,0:T(8,128)(2,1)}, bf16[32,2048]{1,0:T(8,128)(2,1)S(1)}, u32[]{:S(2)}, u32[]{:S(2)}) %collective-permute-start.3) | collective-permute-done | bytes 131104 | tf_op jit(solution)/shard_map/ppermute | solution.py:65
  14.9 0.0 slice-start.2
  14.9 0.2 collective-permute-start.4
  15.1 1.9 %collective-permute-done.refs_1_.refs_4_ = bf16[32,2048]{1,0:T(8,128)(2,1)S(1)} collective-permute-done((bf16[32,2048]{1,0:T(8,128)(2,1)}, bf16[32,2048]{1,0:T(8,128)(2,1)S(1)}, u32[]{:S(2)}, u32[]{:S(2)}) %collective-permute-start) | collective-permute-done | bytes 131104 | tf_op jit(solution)/shard_map/ppermute | solution.py:73
  17.0 0.0 slice-start.3
  17.0 0.0 slice-start.4
  17.0 0.0 slice-start.5
  17.0 0.8 %collective-permute-start.1 = (bf16[64,2048]{1,0:T(8,128)(2,1)S(1)}, bf16[64,2048]{1,0:T(8,128)(2,1)S(1)}, u32[]{:S(2)}, u32[]{:S(2)}) collective-permute-start(bf16[64,2048]{1,0:T(8,128)(2,1)S(1)} %shard_map.104), channel_id=1, source_target_pairs={{0,4},{4,0},{8,12},{12,8},{1,5},{5,1},{9,13},{13,9},{2,6},{6,2},{1... | collective-permute-start | bytes 786440 | tf_op jit(solution)/shard_map/ppermute | solution.py:73
  17.8 0.0 collective-permute-done.2.refs_1_
  17.8 3.2 %collective-permute-done.4.refs_3_ = bf16[32,2048]{1,0:T(8,128)(2,1)S(1)} collective-permute-done((bf16[32,2048]{1,0:T(8,128)(2,1)S(1)}, bf16[32,2048]{1,0:T(8,128)(2,1)S(1)}, u32[]{:S(2)}, u32[]{:S(2)}) %collective-permute-start.4) | collective-permute-done | bytes 131104 | tf_op jit(solution)/shard_map/ppermute | solution.py:65
  21.0 2.1 %shard_map.107 = (bf16[128,2048]{1,0:T(8,128)(2,1)S(1)}, bf16[32,1536]{1,0:T(8,128)(2,1)S(1)}, bf16[32,2048]{1,0:T(8,128)(2,1)S(1)}, bf16[32,3584]{1,0:T(8,128)(...) custom-call(bf16[32,2048]{1,0:T(8,128)(2,1)S(1)} %copy-done.1, ...), custom_call_target="tpu_custom_call" | custom-call | tf_op jit(solution)/shard_map/pallas_call | solution.py:214
  23.1 0.1 collective-permute-start.6
  23.2 0.5 collective-permute-start.5
  23.7 0.0 slice-start.6
  23.7 0.0 slice-start.7
  23.8 0.0 slice-start.8
  23.8 0.0 slice-start.9
  23.8 2.1 %shard_map.108 = (bf16[32,1536]{1,0:T(8,128)(2,1)S(1)}, bf16[32,2048]{1,0:T(8,128)(2,1)S(1)}, bf16[32,3584]{1,0:T(8,128)(2,1)S(1)}, bf16[32,3584]{1,0:T(8,128)(2,1)S(1)}, bf16[32,7168]{1,0:T(8,128)(2,1)S(1)}) custom-call(bf16[128,2048]{1,0:T(8,128)(2,1)S(1)} %get-tuple-element.33.refs_0_, bf16[2048,3584]{1,0:T(8,128)(2,1)S(1)} %bitcast.2, ...), custom_call_target="tpu_custom_call" | custom-call | tf_op jit(solution)/shard_map/pallas_call | solution.py:214
  25.9 0.1 collective-permute-start.14
  26.0 0.0 collective-permute-done.5.refs_1_
  26.0 0.0 collective-permute-done.6.refs_2_
  26.0 0.0 collective-permute-done.1.refs_5_.refs_2_
  26.0 0.0 slice-start.10
  26.0 0.1 shard_map.109.refs_4_
  26.1 2.2 %collective-permute-start.9 = (bf16[32,3584]{1,0:T(8,128)(2,1)S(1)}, bf16[32,3584]{1,0:T(8,128)(2,1)S(1)}, u32[]{:S(2)}, u32[]{:S(2)}) collective-permute-start(bf16[32,3584]{1,0:T(8,128)(2,1)S(1)} %shard_map.109.refs_4_), channel_id=1, source_target_pairs={{0,2},{1,3},{2,0},{3,1},{4,6},{5,7},{6,4},{7,5},{8,10},{9,11},{10,... | collective-permute-start | bytes 688136 | tf_op jit(solution)/shard_map/ppermute | solution.py:235
  28.3 0.2 collective-permute-start.8
  28.5 0.3 collective-permute-start.7
  28.9 2.1 %shard_map.110 = (bf16[128,2048]{1,0:T(8,128)(2,1)S(1)}, bf16[32,1536]{1,0:T(8,128)(2,1)S(1)}, bf16[32,2048]{1,0:T(8,128)(2,1)S(1)}, bf16[32,3584]{1,0:T(8,128)(...) custom-call(bf16[32,2048]{1,0:T(8,128)(2,1)S(1)} %copy-done, ...), custom_call_target="tpu_custom_call" | custom-call | tf_op jit(solution)/shard_map/pallas_call | solution.py:214
  31.0 0.2 collective-permute-start.13
  31.2 0.0 collective-permute-done.7.refs_1_
  31.2 0.0 collective-permute-done.8.refs_2_
  31.2 0.1 shard_map.111.refs_3_
  31.3 0.4 collective-permute-start.15
  31.7 2.1 %shard_map.112 = (bf16[32,1536]{1,0:T(8,128)(2,1)S(1)}, bf16[32,2048]{1,0:T(8,128)(2,1)S(1)}, bf16[32,3584]{1,0:T(8,128)(2,1)S(1)}, bf16[32,3584]{1,0:T(8,128)(2,1)S(1)}, bf16[32,7168]{1,0:T(8,128)(2,1)S(1)}) custom-call(bf16[128,2048]{1,0:T(8,128)(2,1)S(1)} %get-tuple-element.36.refs_0_, bf16[2048,3584]{1,0:T(8,128)(2,1)S(1)} %bitcast.6, ...), custom_call_target="tpu_custom_call" | custom-call | tf_op jit(solution)/shard_map/pallas_call | solution.py:214
  33.8 0.1 collective-permute-start.16
  33.9 0.8 %collective-permute-done.9.refs_2_ = bf16[32,3584]{1,0:T(8,128)(2,1)S(1)} collective-permute-done((bf16[32,3584]{1,0:T(8,128)(2,1)S(1)}, bf16[32,3584]{1,0:T(8,128)(2,1)S(1)}, u32[]{:S(2)}, u32[]{:S(2)}) %collective-permute-start.9) | collective-permute-done | bytes 229408 | tf_op jit(solution)/shard_map/ppermute | solution.py:235
  34.7 0.0 collective-permute-start.12
  34.7 1.3 %collective-permute-done.12.refs_1_ = bf16[32,1536]{1,0:T(8,128)(2,1)S(1)} collective-permute-done((bf16[32,1536]{1,0:T(8,128)(2,1)S(1)}, bf16[32,1536]{1,0:T(8,128)(2,1)S(1)}, u32[]{:S(2)}, u32[]{:S(2)}) %collective-permute-start.12) | collective-permute-done | bytes 98336 | tf_op jit(solution)/shard_map/ppermute | solution.py:235
  36.0 0.2 collective-permute-start.11
  36.2 0.0 collective-permute-done.13.refs_2_
  36.2 0.4 collective-permute-start.10
  36.5 0.0 collective-permute-done.14.refs_4_.refs_1_
  36.5 0.1 shard_map.114.refs_3_
  36.6 2.1 %collective-permute-start.17 = (bf16[32,3584]{1,0:T(8,128)(2,1)S(1)}, bf16[32,3584]{1,0:T(8,128)(2,1)S(1)}, u32[]{:S(2)}, u32[]{:S(2)}) collective-permute-start(bf16[32,3584]{1,0:T(8,128)(2,1)S(1)} %shard_map.114.refs_3_), channel_id=1, source_target_pairs={{0,2},{1,3},{2,0},{3,1},{4,6},{5,7},{6,4},{7,5},{8,10},{9,11},{10,... | collective-permute-start | bytes 688136 | tf_op jit(solution)/shard_map/ppermute | solution.py:235
  38.7 0.8 %collective-permute-done.15.refs_4_.refs_5_ = bf16[32,3584]{1,0:T(8,128)(2,1)S(1)} collective-permute-done((bf16[32,3584]{1,0:T(8,128)(2,1)S(1)}, bf16[32,3584]{1,0:T(8,128)(2,1)S(1)}, u32[]{:S(2)}, u32[]{:S(2)}) %collective-permute-start.15) | collective-permute-done | bytes 229408 | tf_op jit(solution)/shard_map/ppermute | solution.py:235
  39.4 0.0 collective-permute-done.10.refs_1_
  39.4 0.0 collective-permute-done.11.refs_2_
  39.4 0.1 shard_map.115.refs_0_
  39.5 1.8 %collective-permute-start.18 = (bf16[32,3584]{1,0:T(8,128)(2,1)S(1)}, bf16[32,3584]{1,0:T(8,128)(2,1)S(1)}, u32[]{:S(2)}, u32[]{:S(2)}) collective-permute-start(bf16[32,3584]{1,0:T(8,128)(2,1)S(1)} %shard_map.115.refs_0_), channel_id=1, source_target_pairs={{0,2},{1,3},{2,0},{3,1},{4,6},{5,7},{6,4},{7,5},{8,10},{9,11},{10,... | collective-permute-start | bytes 688136 | tf_op jit(solution)/shard_map/ppermute | solution.py:235
  41.3 2.2 %shard_map.116 = (f32[32,128]{1,0:T(8,128)S(1)}, f32[32,128]{1,0:T(8,128)S(1)}) custom-call(s32[32]{0:T(128)} %ids.1, s32[2]{0:T(128)} %lengths.1, f32[1002,128]{1,0:T(8,128)} %bitcast.7, bf16[32,3584]{1,0:T(8,128)(2,1)S(1)} %shard_map.115.refs_0_), custom_call_target="tpu_custom_call" | custom-call | tf_op jit(solution)/shard_map/pallas_call | solution.py:127
  43.5 0.9 %shard_map.117 = (f32[32,3584]{1,0:T(8,128)S(1)}, bf16[32,3584]{1,0:T(8,128)(2,1)}) custom-call(f32[32,128]{1,0:T(8,128)S(1)} %get-tuple-element.49.live, bf16[32,3584]{1,0:T(8,128)(2,1)S(1)} %get-tuple-element.50.refs_0_, bf16[32,7168]{1,0:T(8,128)(2,1)S(1)} %collective-permute-done.14.refs_4_.refs_1_, bf16[32,3584]{1,0:T(8,128)(2,1)S(1)} %collective-permute-done.9.refs_2_, ...), custom_call_target="tpu_custom_call" | custom-call | tf_op jit(solution)/shard_map/pallas_call | solution.py:293
  44.4 0.0 collective-permute-done.16.refs_1_
  44.4 0.6 %collective-permute-done.17.refs_2_ = bf16[32,3584]{1,0:T(8,128)(2,1)S(1)} collective-permute-done((bf16[32,3584]{1,0:T(8,128)(2,1)S(1)}, bf16[32,3584]{1,0:T(8,128)(2,1)S(1)}, u32[]{:S(2)}, u32[]{:S(2)}) %collective-permute-start.17) | collective-permute-done | bytes 229408 | tf_op jit(solution)/shard_map/ppermute | solution.py:235
  45.1 0.1 shard_map.118.gated
  45.2 4.3 %collective-permute-done.18.refs_2_ = bf16[32,3584]{1,0:T(8,128)(2,1)S(1)} collective-permute-done((bf16[32,3584]{1,0:T(8,128)(2,1)S(1)}, bf16[32,3584]{1,0:T(8,128)(2,1)S(1)}, u32[]{:S(2)}, u32[]{:S(2)}) %collective-permute-start.18) | collective-permute-done | bytes 229408 | tf_op jit(solution)/shard_map/ppermute | solution.py:235
  49.5 0.8 %shard_map.119 = bf16[32,3584]{1,0:T(8,128)(2,1)} custom-call(f32[32,3584]{1,0:T(8,128)S(1)} %get-tuple-element.53.act, f32[32,3584]{1,0:T(8,128)S(1)} %shard_map.118.gated, bf16[32,3584]{1,0:T(8,128)(2,1)S(1)} %get-tuple-element.57.refs_0_, bf16[32,7168]{1,0:T(8,128)(2,1)S(1)} %collective-permute-done.16.refs_1_, ...), custom_call_target="tpu_custom_call" | custom-call | tf_op jit(solution)/shard_map/pallas_call | solution.py:329
  (21 shorter events, 0.1 us)
Async XLA Ops:
  0.6 14.3 %collective-permute-start.3 = (bf16[32,2048]{1,0:T(8,128)(2,1)}, bf16[32,2048]{1,0:T(8,128)(2,1)S(1)}, u32[]{:S(2)}, u32[]{:S(2)}) collective-permute-start(bf16[32,2048]{1,0:T(8,128)(2,1)} %refs_0_.4), channel_id=1, source_target_pairs={{0,8},{4,12},{8,0},{12,4},{1,9},{5,13},{9,1},{13,5},{2,10},{6,14},... | collective-permute-start | bytes 393224 | tf_op jit(solution)/shard_map/ppermute | solution.py:65
  4.7 12.2 %collective-permute-start = (bf16[32,2048]{1,0:T(8,128)(2,1)}, bf16[32,2048]{1,0:T(8,128)(2,1)S(1)}, u32[]{:S(2)}, u32[]{:S(2)}) collective-permute-start(bf16[32,2048]{1,0:T(8,128)(2,1)} %refs_0_.5), channel_id=1, source_target_pairs={{0,8},{4,12},{8,0},{12,4},{1,9},{5,13},{9,1},{13,5},{2,10},{6,14},... | collective-permute-start | bytes 393224 | tf_op jit(solution)/shard_map/ppermute | solution.py:73
  4.8 13.0 %collective-permute-start.2 = (bf16[32,2048]{1,0:T(8,128)(2,1)}, bf16[32,2048]{1,0:T(8,128)(2,1)S(1)}, u32[]{:S(2)}, u32[]{:S(2)}) collective-permute-start(bf16[32,2048]{1,0:T(8,128)(2,1)} %refs_0_.4), channel_id=1, source_target_pairs={{0,4},{4,0},{8,12},{12,8},{1,5},{5,1},{9,13},{13,9},{2,6},{6,2},{1... | collective-permute-start | bytes 393224 | tf_op jit(solution)/shard_map/ppermute | solution.py:65
  11.8 5.1 %copy-start = (bf16[32,2048]{1,0:T(8,128)(2,1)S(1)}, bf16[32,2048]{1,0:T(8,128)(2,1)}, u32[]{:S(2)}) copy-start(bf16[32,2048]{1,0:T(8,128)(2,1)} %refs_0_.5) | copy-start | bytes 393220
  11.8 9.2 %copy-start.1 = (bf16[32,2048]{1,0:T(8,128)(2,1)S(1)}, bf16[32,2048]{1,0:T(8,128)(2,1)}, u32[]{:S(2)}) copy-start(bf16[32,2048]{1,0:T(8,128)(2,1)} %refs_0_.4) | copy-start | bytes 393220
  11.9 11.9 %slice-start = ((s8[14680064]{0:T(1024)(128)(4,1)}), s8[4194304]{0:T(1024)(128)(4,1)S(1)}, s32[]{:S(2)}) async-start(s8[14680064]{0:T(1024)(128)(4,1)} %bitcast.1), calls=%async_computation | async-start | bytes 8388608
  11.9 11.8 %slice-start.1 = ((s8[14680064]{0:T(1024)(128)(4,1)}), s8[4194304]{0:T(1024)(128)(4,1)S(1)}, s32[]{:S(2)}) async-start(s8[14680064]{0:T(1024)(128)(4,1)} %bitcast.1), calls=%async_computation.1 | async-start | bytes 8388608
  14.9 8.8 %slice-start.2 = ((s8[14680064]{0:T(1024)(128)(4,1)}), s8[4194304]{0:T(1024)(128)(4,1)S(1)}, s32[]{:S(2)}) async-start(s8[14680064]{0:T(1024)(128)(4,1)} %bitcast.1), calls=%async_computation.2 | async-start | bytes 8388608
  14.9 6.1 %collective-permute-start.4 = (bf16[32,2048]{1,0:T(8,128)(2,1)S(1)}, bf16[32,2048]{1,0:T(8,128)(2,1)S(1)}, u32[]{:S(2)}, u32[]{:S(2)}) collective-permute-start(bf16[32,2048]{1,0:T(8,128)(2,1)S(1)} %shard_map.106), channel_id=1, source_target_pairs={{0,4},{4,0},{8,12},{12,8},{1,5},{5,1},{9,13},{13,9},{2,6},{6,2},{1... | collective-permute-start | bytes 393224 | tf_op jit(solution)/shard_map/ppermute | solution.py:65
  17.0 6.7 %slice-start.3 = ((s8[14680064]{0:T(1024)(128)(4,1)}), s8[2097152]{0:T(1024)(128)(4,1)S(1)}, s32[]{:S(2)}) async-start(s8[14680064]{0:T(1024)(128)(4,1)} %bitcast.1), calls=%async_computation.3 | async-start | bytes 4194304
  17.0 11.8 %slice-start.4 = ((s8[14680064]{0:T(1024)(128)(4,1)}), s8[4194304]{0:T(1024)(128)(4,1)S(1)}, s32[]{:S(2)}) async-start(s8[14680064]{0:T(1024)(128)(4,1)} %bitcast.3), calls=%async_computation.4 | async-start | bytes 8388608
  17.0 11.8 %slice-start.5 = ((s8[14680064]{0:T(1024)(128)(4,1)}), s8[4194304]{0:T(1024)(128)(4,1)S(1)}, s32[]{:S(2)}) async-start(s8[14680064]{0:T(1024)(128)(4,1)} %bitcast.3), calls=%async_computation.5 | async-start | bytes 8388608
  17.0 9.0 %collective-permute-start.1 = (bf16[64,2048]{1,0:T(8,128)(2,1)S(1)}, bf16[64,2048]{1,0:T(8,128)(2,1)S(1)}, u32[]{:S(2)}, u32[]{:S(2)}) collective-permute-start(bf16[64,2048]{1,0:T(8,128)(2,1)S(1)} %shard_map.104), channel_id=1, source_target_pairs={{0,4},{4,0},{8,12},{12,8},{1,5},{5,1},{9,13},{13,9},{2,6},{6,2},{1... | collective-permute-start | bytes 786440 | tf_op jit(solution)/shard_map/ppermute | solution.py:73
  23.1 2.9 %collective-permute-start.6 = (bf16[32,2048]{1,0:T(8,128)(2,1)S(1)}, bf16[32,2048]{1,0:T(8,128)(2,1)S(1)}, u32[]{:S(2)}, u32[]{:S(2)}) collective-permute-start(bf16[32,2048]{1,0:T(8,128)(2,1)S(1)} %get-tuple-element.32), channel_id=1, source_target_pairs={{0,1},{1,0},{2,3},{3,2},{4,5},{5,4},{6,7},{7,6},{8,9},{9,8},{10,11... | collective-permute-start | bytes 393224 | tf_op jit(solution)/shard_map/ppermute | solution.py:235
  23.2 2.8 %collective-permute-start.5 = (bf16[32,1536]{1,0:T(8,128)(2,1)S(1)}, bf16[32,1536]{1,0:T(8,128)(2,1)S(1)}, u32[]{:S(2)}, u32[]{:S(2)}) collective-permute-start(bf16[32,1536]{1,0:T(8,128)(2,1)S(1)} %get-tuple-element.31), channel_id=1, source_target_pairs={{0,1},{1,0},{2,3},{3,2},{4,5},{5,4},{6,7},{7,6},{8,9},{9,8},{10,11... | collective-permute-start | bytes 294920 | tf_op jit(solution)/shard_map/ppermute | solution.py:235
  23.7 5.1 %slice-start.6 = ((s8[14680064]{0:T(1024)(128)(4,1)}), s8[4194304]{0:T(1024)(128)(4,1)S(1)}, s32[]{:S(2)}) async-start(s8[14680064]{0:T(1024)(128)(4,1)} %bitcast.3), calls=%async_computation.6 | async-start | bytes 8388608
  23.7 5.1 %slice-start.7 = ((s8[14680064]{0:T(1024)(128)(4,1)}), s8[2097152]{0:T(1024)(128)(4,1)S(1)}, s32[]{:S(2)}) async-start(s8[14680064]{0:T(1024)(128)(4,1)} %bitcast.3), calls=%async_computation.7 | async-start | bytes 4194304
  23.8 7.9 %slice-start.8 = ((s8[14680064]{0:T(1024)(128)(4,1)}), s8[4194304]{0:T(1024)(128)(4,1)S(1)}, s32[]{:S(2)}) async-start(s8[14680064]{0:T(1024)(128)(4,1)} %bitcast.5), calls=%async_computation.8 | async-start | bytes 8388608
  23.8 7.9 %slice-start.9 = ((s8[14680064]{0:T(1024)(128)(4,1)}), s8[4194304]{0:T(1024)(128)(4,1)S(1)}, s32[]{:S(2)}) async-start(s8[14680064]{0:T(1024)(128)(4,1)} %bitcast.5), calls=%async_computation.9 | async-start | bytes 8388608
  25.9 10.7 %collective-permute-start.14 = (bf16[32,7168]{1,0:T(8,128)(2,1)S(1)}, bf16[32,7168]{1,0:T(8,128)(2,1)S(1)}, u32[]{:S(2)}, u32[]{:S(2)}) collective-permute-start(bf16[32,7168]{1,0:T(8,128)(2,1)S(1)} %get-tuple-element.48), channel_id=1, source_target_pairs={{0,1},{1,0},{2,3},{3,2},{4,5},{5,4},{6,7},{7,6},{8,9},{9,8},{10,11... | collective-permute-start | bytes 1376264 | tf_op jit(solution)/shard_map/ppermute | solution.py:235
  26.0 5.7 %slice-start.10 = ((s8[14680064]{0:T(1024)(128)(4,1)}), s8[4194304]{0:T(1024)(128)(4,1)S(1)}, s32[]{:S(2)}) async-start(s8[14680064]{0:T(1024)(128)(4,1)} %bitcast.5), calls=%async_computation.10 | async-start | bytes 8388608
  26.1 8.6 %collective-permute-start.9 = (bf16[32,3584]{1,0:T(8,128)(2,1)S(1)}, bf16[32,3584]{1,0:T(8,128)(2,1)S(1)}, u32[]{:S(2)}, u32[]{:S(2)}) collective-permute-start(bf16[32,3584]{1,0:T(8,128)(2,1)S(1)} %shard_map.109.refs_4_), channel_id=1, source_target_pairs={{0,2},{1,3},{2,0},{3,1},{4,6},{5,7},{6,4},{7,5},{8,10},{9,11},{10,... | collective-permute-start | bytes 688136 | tf_op jit(solution)/shard_map/ppermute | solution.py:235
  28.3 2.9 %collective-permute-start.8 = (bf16[32,2048]{1,0:T(8,128)(2,1)S(1)}, bf16[32,2048]{1,0:T(8,128)(2,1)S(1)}, u32[]{:S(2)}, u32[]{:S(2)}) collective-permute-start(bf16[32,2048]{1,0:T(8,128)(2,1)S(1)} %get-tuple-element.39), channel_id=1, source_target_pairs={{0,1},{1,0},{2,3},{3,2},{4,5},{5,4},{6,7},{7,6},{8,9},{9,8},{10,11... | collective-permute-start | bytes 393224 | tf_op jit(solution)/shard_map/ppermute | solution.py:235
  28.5 3.2 %slice-start.11 = ((s8[14680064]{0:T(1024)(128)(4,1)}), s8[2097152]{0:T(1024)(128)(4,1)S(1)}, s32[]{:S(2)}) async-start(s8[14680064]{0:T(1024)(128)(4,1)} %bitcast.5), calls=%async_computation.11 | async-start | bytes 4194304
  28.5 2.7 %collective-permute-start.7 = (bf16[32,1536]{1,0:T(8,128)(2,1)S(1)}, bf16[32,1536]{1,0:T(8,128)(2,1)S(1)}, u32[]{:S(2)}, u32[]{:S(2)}) collective-permute-start(bf16[32,1536]{1,0:T(8,128)(2,1)S(1)} %get-tuple-element.38), channel_id=1, source_target_pairs={{0,1},{1,0},{2,3},{3,2},{4,5},{5,4},{6,7},{7,6},{8,9},{9,8},{10,11... | collective-permute-start | bytes 294920 | tf_op jit(solution)/shard_map/ppermute | solution.py:235
  31.0 5.2 %collective-permute-start.13 = (bf16[32,2048]{1,0:T(8,128)(2,1)S(1)}, bf16[32,2048]{1,0:T(8,128)(2,1)S(1)}, u32[]{:S(2)}, u32[]{:S(2)}) collective-permute-start(bf16[32,2048]{1,0:T(8,128)(2,1)S(1)} %get-tuple-element.47), channel_id=1, source_target_pairs={{0,1},{1,0},{2,3},{3,2},{4,5},{5,4},{6,7},{7,6},{8,9},{9,8},{10,11... | collective-permute-start | bytes 393224 | tf_op jit(solution)/shard_map/ppermute | solution.py:235
  31.3 8.2 %collective-permute-start.15 = (bf16[32,3584]{1,0:T(8,128)(2,1)S(1)}, bf16[32,3584]{1,0:T(8,128)(2,1)S(1)}, u32[]{:S(2)}, u32[]{:S(2)}) collective-permute-start(bf16[32,3584]{1,0:T(8,128)(2,1)S(1)} %shard_map.111.refs_3_), channel_id=1, source_target_pairs={{0,2},{1,3},{2,0},{3,1},{4,6},{5,7},{6,4},{7,5},{8,10},{9,11},{10,... | collective-permute-start | bytes 688136 | tf_op jit(solution)/shard_map/ppermute | solution.py:235
  33.8 10.6 %collective-permute-start.16 = (bf16[32,7168]{1,0:T(8,128)(2,1)S(1)}, bf16[32,7168]{1,0:T(8,128)(2,1)S(1)}, u32[]{:S(2)}, u32[]{:S(2)}) collective-permute-start(bf16[32,7168]{1,0:T(8,128)(2,1)S(1)} %get-tuple-element.56), channel_id=1, source_target_pairs={{0,1},{1,0},{2,3},{3,2},{4,5},{5,4},{6,7},{7,6},{8,9},{9,8},{10,11... | collective-permute-start | bytes 1376264 | tf_op jit(solution)/shard_map/ppermute | solution.py:235
  34.7 1.3 %collective-permute-start.12 = (bf16[32,1536]{1,0:T(8,128)(2,1)S(1)}, bf16[32,1536]{1,0:T(8,128)(2,1)S(1)}, u32[]{:S(2)}, u32[]{:S(2)}) collective-permute-start(bf16[32,1536]{1,0:T(8,128)(2,1)S(1)} %get-tuple-element.46), channel_id=1, source_target_pairs={{0,1},{1,0},{2,3},{3,2},{4,5},{5,4},{6,7},{7,6},{8,9},{9,8},{10,11... | collective-permute-start | bytes 294920 | tf_op jit(solution)/shard_map/ppermute | solution.py:235
  36.0 3.4 %collective-permute-start.11 = (bf16[32,2048]{1,0:T(8,128)(2,1)S(1)}, bf16[32,2048]{1,0:T(8,128)(2,1)S(1)}, u32[]{:S(2)}, u32[]{:S(2)}) collective-permute-start(bf16[32,2048]{1,0:T(8,128)(2,1)S(1)} %get-tuple-element.45), channel_id=1, source_target_pairs={{0,1},{1,0},{2,3},{3,2},{4,5},{5,4},{6,7},{7,6},{8,9},{9,8},{10,11... | collective-permute-start | bytes 393224 | tf_op jit(solution)/shard_map/ppermute | solution.py:235
  36.2 3.3 %collective-permute-start.10 = (bf16[32,1536]{1,0:T(8,128)(2,1)S(1)}, bf16[32,1536]{1,0:T(8,128)(2,1)S(1)}, u32[]{:S(2)}, u32[]{:S(2)}) collective-permute-start(bf16[32,1536]{1,0:T(8,128)(2,1)S(1)} %get-tuple-element.44), channel_id=1, source_target_pairs={{0,1},{1,0},{2,3},{3,2},{4,5},{5,4},{6,7},{7,6},{8,9},{9,8},{10,11... | collective-permute-start | bytes 294920 | tf_op jit(solution)/shard_map/ppermute | solution.py:235
  36.6 8.5 %collective-permute-start.17 = (bf16[32,3584]{1,0:T(8,128)(2,1)S(1)}, bf16[32,3584]{1,0:T(8,128)(2,1)S(1)}, u32[]{:S(2)}, u32[]{:S(2)}) collective-permute-start(bf16[32,3584]{1,0:T(8,128)(2,1)S(1)} %shard_map.114.refs_3_), channel_id=1, source_target_pairs={{0,2},{1,3},{2,0},{3,1},{4,6},{5,7},{6,4},{7,5},{8,10},{9,11},{10,... | collective-permute-start | bytes 688136 | tf_op jit(solution)/shard_map/ppermute | solution.py:235
  39.5 10.0 %collective-permute-start.18 = (bf16[32,3584]{1,0:T(8,128)(2,1)S(1)}, bf16[32,3584]{1,0:T(8,128)(2,1)S(1)}, u32[]{:S(2)}, u32[]{:S(2)}) collective-permute-start(bf16[32,3584]{1,0:T(8,128)(2,1)S(1)} %shard_map.115.refs_0_), channel_id=1, source_target_pairs={{0,2},{1,3},{2,0},{3,1},{4,6},{5,7},{6,4},{7,5},{8,10},{9,11},{10,... | collective-permute-start | bytes 688136 | tf_op jit(solution)/shard_map/ppermute | solution.py:235

commit v13 on v12

--- a/solution.py
+++ b/solution.py
@@ -138,22 +138,24 @@
     )(*map(in_hbm, (ids, lengths, table)), *after)
 
 
-def load_kernel(matrix, *refs):
+def load_kernel(first, matrix, *refs):
     dest, sem = refs[-2:]
-    copy = pltpu.make_async_copy(matrix, dest, sem)
+    copy = pltpu.make_async_copy(matrix.at[pl.ds(first, dest.shape[0]), :], dest, sem)
     copy.start()
     copy.wait()
 
 
-def load(matrix, after=()):
-    return pl.pallas_call(
-        load_kernel,
-        out_shape=pltpu.VMEM(matrix.shape, matrix.dtype),
-        in_specs=[ANYWHERE] * (1 + len(after)),
-        out_specs=IN_VMEM,
-        scratch_shapes=[pltpu.SemaphoreType.DMA],
-        compiler_params=pltpu.CompilerParams(vmem_limit_bytes=1 << 20),
-    )(in_hbm(matrix), *after)
+def load(matrix, first, rows, after=()):
+    return in_vmem(
+        pl.pallas_call(
+            functools.partial(load_kernel, first),
+            out_shape=pltpu.VMEM((rows, matrix.shape[1]), matrix.dtype),
+            in_specs=[ANYWHERE] * (1 + len(after)),
+            out_specs=IN_VMEM,
+            scratch_shapes=[pltpu.SemaphoreType.DMA],
+            compiler_params=pltpu.CompilerParams(vmem_limit_bytes=1 << 20),
+        )(in_hbm(matrix), *after)
+    )
 
 
 def tile_of(cols):
@@ -174,17 +176,22 @@
     return [(0, first), (first, width - first)] if first else [(0, width)]
 
 
-def product_kernel(pieces, spots, after, narrow, blocks, *refs):
-    tokens, matrix = refs[:pieces], refs[pieces]
-    beside, outs = refs[pieces + 1 : len(refs) - len(blocks) - (pieces > 1) - after], refs[-len(blocks) :]
+def product_kernel(pieces, parts, spots, after, narrow, blocks, *refs):
+    tokens, matrices = refs[:pieces], refs[pieces : pieces + parts]
+    beside, outs = refs[pieces + parts : len(refs) - len(blocks) - (pieces > 1) - after], refs[-len(blocks) :]
     if pieces > 1:
         rows = refs[-len(blocks) - 1]
         place_rows(tokens, spots, rows, narrow)
         tokens = [rows]
     for earlier in beside:
         outs[-1][:, : earlier.shape[1]] = earlier[...]
-    for cols in column_tiles(matrix.shape[1]):
-        total = jnp.dot(tokens[0][...], matrix[:, cols], preferred_element_type=jnp.float32)
+    for cols in column_tiles(matrices[0].shape[1]):
+        total, depth = None, 0
+        for matrix in matrices:
+            part = tokens[0][:, depth : depth + matrix.shape[0]]
+            term = jnp.dot(part, matrix[:, cols], preferred_element_type=jnp.float32)
+            total = term if total is None else total + term
+            depth += matrix.shape[0]
         for out, (row, col) in zip(outs, blocks):
             if col <= cols.start and cols.stop <= col + out.shape[1]:
                 value = total[row : row + out.shape[0]].astype(out.dtype)
@@ -199,12 +206,12 @@
     return sizes + [left]
 
 
-def product(tokens, matrix, narrow, after, beside=(), spots=()):
+def product(tokens, matrices, narrow, after, beside=(), spots=(), split=True):
     placing = len(tokens) > 1
     total = sum(t.shape[0] for t in tokens)
-    depth, width = matrix.shape
+    depth, width = tokens[0].shape[1], matrices[0].shape[1]
     sizes = part_sizes(total, narrow)
-    sent = [(k, *cols) for k in range(len(sizes) - 1) for cols in column_chunks(width)]
+    sent = [(k, *cols) for k in range(len(sizes) - 1) for cols in (column_chunks(width) if split else [(0, width)])]
     ahead = sum(b.shape[1] for b in beside)
     blocks = [(sum(sizes[:k]), first) for k, first, _ in sent]
     blocks += [(total // 2 + sum(sizes[:k]), 0) for k in range(len(sizes))]
@@ -212,13 +219,13 @@
     shapes = [(sizes[k], count) for k, _, count in sent] + [(size, width) for size in sizes]
     shapes += [(sizes[-1], ahead + width)]
     found = pl.pallas_call(
-        functools.partial(product_kernel, len(tokens), spots, len(after), narrow, blocks),
+        functools.partial(product_kernel, len(tokens), len(matrices), spots, len(after), narrow, blocks),
         out_shape=[jax.ShapeDtypeStruct((total, depth), tokens[0].dtype)] * placing
         + [jax.ShapeDtypeStruct(shape, jnp.bfloat16) for shape in shapes],
-        in_specs=[IN_VMEM] * (len(tokens) + 1 + len(beside)) + [ANYWHERE] * len(after),
+        in_specs=[IN_VMEM] * (len(tokens) + len(matrices) + len(beside)) + [ANYWHERE] * len(after),
         out_specs=[IN_VMEM] * (placing + len(shapes)),
         compiler_params=pltpu.CompilerParams(vmem_limit_bytes=4 << 20),
-    )(*tokens, in_vmem(matrix), *beside, *after)
+    )(*tokens, *matrices, *beside, *after)
     rows, found = (found[:1], found[1:]) if placing else (tokens, found)
     sends = [(array, k, first) for array, (k, first, _) in zip(found, sent)]
     return rows, sends, found[-1], found[len(sent) : -1]
@@ -337,20 +344,26 @@
 
 def local(mesh_shape, target_states, source_states, target_gate, target_up, source_gate, source_up, token_ids, lengths, ratio_weight):
     wide, narrow = mesh_shape["wide"], mesh_shape["narrow"]
-    target_gate = load(target_gate)
-    target_pieces, target_spots = gather_pieces(target_states, "wide", wide, target_gate)
+    depth, width = target_gate.shape
+    half = depth // 2
+    gate_top = load(target_gate, 0, half)
+    gate_bottom = load(target_gate, half, depth - half, (gate_top,))
+    target_pieces, target_spots = gather_pieces(target_states, "wide", wide, gate_bottom)
+    (source_states,) = passed([source_states], (gate_top,))
     source_pieces, source_spots = gather_doubling(source_states, "wide", wide)
-    width = target_gate.shape[1]
-
-    rows, sends, own, keeps = product(target_pieces, target_gate, narrow, (), spots=target_spots)
-    _, up_sends, own, up_keeps = product(rows, target_up, narrow, (keeps[0],), (own,))
+
+    gate = (gate_top, gate_bottom)
+    rows, sends, own, keeps = product(target_pieces, gate, narrow, (), spots=target_spots)
+    after = (keeps[0],)
+    _, up_sends, own, up_keeps = product(rows, (in_vmem(target_up),), narrow, after, (own,))
     target_own = exchange(own, 0, narrow)
-    after = (up_keeps[0], *source_pieces[1:])
-    sent, target_g = finish(sends, keeps, (target_own, 0), narrow, after)
-    rows, gate_sends, own, gate_keeps = product(source_pieces, source_gate, narrow, (sent,), spots=source_spots)
+    sent, target_g = finish(sends, keeps, (target_own, 0), narrow, (up_keeps[0], source_pieces[-1]))
+    rows, gate_sends, own, gate_keeps = product(
+        source_pieces, (in_vmem(source_gate),), narrow, (sent,), spots=source_spots
+    )
     after = (gate_keeps[0],)
     sent, target_u = finish(up_sends, up_keeps, (target_own, -width), narrow, after)
-    _, sends, own, keeps = product(rows, source_up, narrow, (sent,), (own,))
+    _, sends, own, keeps = product(rows, (in_vmem(source_up),), narrow, (sent,), (own,))
     sends = resent(sends, (target_g[0][-1],))
     own = exchange(own, 0, narrow)
     sent, source_g = finish(gate_sends, gate_keeps, (own, 0), narrow, (keeps[0], target_own))

time: 50.5 us -> 49.8 us (0.986); the launches traced: 50.3 us -> 49 us
  waiting for transfers between devices: 15.9 us -> 12.1 us
  starting transfers between devices: 15.6 us -> 17 us
  Pallas kernels: 17.8 us -> 19 us
    ppermute x3, waiting for transfers between devices: 6.21 us -> 2.11 us  [gather_pieces(): lax.ppermute(source, axis, [(i, i ^ low) for i in range(size)])]
    ppermute x3, starting transfers between devices: 6.09 us -> 7.94 us  [gather_pieces(): lax.ppermute(source, axis, [(i, i ^ low) for i in range(size)])]
    pallas_call x5 -> x6, Pallas kernels: 13.5 us -> 14.7 us  [the longest x4 8.35 us: product(): pl.pallas_call(functools.partial(product_kernel, len(tokens), len(matrice...]
  transfers between devices with their start and end apart: 19 -> 19, of which waited for: 8 -> 8; matrix products, arithmetic and copies ran while one was open for 0% -> 0% of each run, Pallas kernels for 34% -> 37%
where the time goes in v13:
time: 49.8 us; the launch traced here: 49 us
  Pallas kernels  19 us (38%)
  starting transfers between devices  17 us (34%)
  waiting for transfers between devices  12.1 us (24%)
  between operations  0.89 us (2%)
    pallas_call x4, Pallas kernels, product(): pl.pallas_call(functools.partial(product_kernel, len(tokens), len(matrice...  8.35 us
    ppermute x14, starting transfers between devices, exchange(): lax.ppermute(array, 'narrow', [(i, i ^ 1 << step) for i in range(size)])  8.24 us
    ppermute x3, starting transfers between devices, gather_pieces(): lax.ppermute(source, axis, [(i, i ^ low) for i in range(size)])  7.94 us
    ppermute x14, waiting for transfers between devices, exchange(): lax.ppermute(array, 'narrow', [(i, i ^ 1 << step) for i in range(size)])  7.63 us
    pallas_call x2, Pallas kernels, load(): pl.pallas_call(functools.partial(load_kernel, first), out_shape=pltpu.VME...  6.33 us
    ppermute x2, waiting for transfers between devices, gather_doubling(): arrays.append(lax.ppermute(send, axis, [(i, i ^ low) for i in range(size)]))  2.34 us
    pallas_call x1, Pallas kernels, look_up(): pl.pallas_call(functools.partial(look_up_kernel, ids.shape[0] // lengths....  2.16 us
    ppermute x3, waiting for transfers between devices, gather_pieces(): lax.ppermute(source, axis, [(i, i ^ low) for i in range(size)])  2.11 us
  transfers between devices with their start and end apart: 19, of which 8 were waited for; matrix products, arithmetic and copies ran while one was open for 0% of the time, Pallas kernels for 37%

profile of v13, /device:TPU:0, one launch (start us, length us, event | category | flops | bytes accessed | tf_op | source)
XLA Modules:
  0.0 49.0 jit_solution(13982217143575743451)
XLA Ops:
  0.6 0.0 copy-start.1
  0.6 0.0 copy-start
  0.6 4.1 %collective-permute-start.3 = (bf16[32,2048]{1,0:T(8,128)(2,1)}, bf16[32,2048]{1,0:T(8,128)(2,1)S(1)}, u32[]{:S(2)}, u32[]{:S(2)}) collective-permute-start(bf16[32,2048]{1,0:T(8,128)(2,1)} %refs_0_.3), channel_id=1, source_target_pairs={{0,8},{4,12},{8,0},{12,4},{1,9},{5,13},{9,1},{13,5},{2,10},{6,14},... | collective-permute-start | bytes 393224 | tf_op jit(solution)/shard_map/ppermute | solution.py:65
  4.8 3.1 %shard_map.104.refs_1_.refs_0_.refs_4_ = bf16[1024,3584]{1,0:T(8,128)(2,1)S(1)} custom-call(bf16[2048,3584]{1,0:T(8,128)(2,1)} %matrix.3), custom_call_target="tpu_custom_call" | custom-call | tf_op jit(solution)/shard_map/pallas_call | solution.py:150
  7.8 0.0 copy-done
  7.9 0.1 collective-permute-start
  8.0 1.9 %collective-permute-start.2 = (bf16[32,2048]{1,0:T(8,128)(2,1)S(1)}, bf16[32,2048]{1,0:T(8,128)(2,1)S(1)}, u32[]{:S(2)}, u32[]{:S(2)}) collective-permute-start(bf16[32,2048]{1,0:T(8,128)(2,1)S(1)} %copy-done.1), channel_id=1, source_target_pairs={{0,4},{4,0},{8,12},{12,8},{1,5},{5,1},{9,13},{13,9},{2,6},{6,2},{1... | collective-permute-start | bytes 393224 | tf_op jit(solution)/shard_map/ppermute | solution.py:65
  9.9 3.2 %shard_map.107.refs_1_.refs_5_ = bf16[1024,3584]{1,0:T(8,128)(2,1)S(1)} custom-call(bf16[2048,3584]{1,0:T(8,128)(2,1)} %matrix.3, bf16[1024,3584]{1,0:T(8,128)(2,1)S(1)} %shard_map.104.refs_1_.refs_0_.refs_4_), custom_call_target="tpu_custom_call" | custom-call | tf_op jit(solution)/shard_map/pallas_call | solution.py:150
  13.1 0.0 collective-permute-done.3.refs_0_.refs_2_
  13.1 2.0 %collective-permute-start.4 = (bf16[32,2048]{1,0:T(8,128)(2,1)S(1)}, bf16[32,2048]{1,0:T(8,128)(2,1)S(1)}, u32[]{:S(2)}, u32[]{:S(2)}) collective-permute-start(bf16[32,2048]{1,0:T(8,128)(2,1)S(1)} %shard_map.108), channel_id=1, source_target_pairs={{0,4},{4,0},{8,12},{12,8},{1,5},{5,1},{9,13},{13,9},{2,6},{6,2},{1... | collective-permute-start | bytes 393224 | tf_op jit(solution)/shard_map/ppermute | solution.py:65
  15.1 1.9 %collective-permute-done.refs_1_ = bf16[32,2048]{1,0:T(8,128)(2,1)S(1)} collective-permute-done((bf16[32,2048]{1,0:T(8,128)(2,1)S(1)}, bf16[32,2048]{1,0:T(8,128)(2,1)S(1)}, u32[]{:S(2)}, u32[]{:S(2)}) %collective-permute-start) | collective-permute-done | bytes 131104 | tf_op jit(solution)/shard_map/ppermute | solution.py:73
  17.0 0.0 slice-start.3
  17.1 0.0 slice-start.4
  17.1 0.0 slice-start.5
  17.1 0.7 %collective-permute-start.1 = (bf16[64,2048]{1,0:T(8,128)(2,1)S(1)}, bf16[64,2048]{1,0:T(8,128)(2,1)S(1)}, u32[]{:S(2)}, u32[]{:S(2)}) collective-permute-start(bf16[64,2048]{1,0:T(8,128)(2,1)S(1)} %shard_map.106), channel_id=1, source_target_pairs={{0,4},{4,0},{8,12},{12,8},{1,5},{5,1},{9,13},{13,9},{2,6},{6,2},{1... | collective-permute-start | bytes 786440 | tf_op jit(solution)/shard_map/ppermute | solution.py:73
  17.8 0.0 collective-permute-done.2.refs_1_
  17.8 2.1 %collective-permute-done.4.refs_3_ = bf16[32,2048]{1,0:T(8,128)(2,1)S(1)} collective-permute-done((bf16[32,2048]{1,0:T(8,128)(2,1)S(1)}, bf16[32,2048]{1,0:T(8,128)(2,1)S(1)}, u32[]{:S(2)}, u32[]{:S(2)}) %collective-permute-start.4) | collective-permute-done | bytes 131104 | tf_op jit(solution)/shard_map/ppermute | solution.py:65
  19.9 2.1 %shard_map.109 = (bf16[128,2048]{1,0:T(8,128)(2,1)S(1)}, bf16[32,1536]{1,0:T(8,128)(2,1)S(1)}, bf16[32,2048]{1,0:T(8,128)(2,1)S(1)}, bf16[32,3584]{1,0:T(8,128)(...) custom-call(bf16[32,2048]{1,0:T(8,128)(2,1)S(1)} %copy-done.1, ...), custom_call_target="tpu_custom_call" | custom-call | tf_op jit(solution)/shard_map/pallas_call | solution.py:221
  22.0 0.1 collective-permute-start.6
  22.1 0.5 %collective-permute-start.5 = (bf16[32,1536]{1,0:T(8,128)(2,1)S(1)}, bf16[32,1536]{1,0:T(8,128)(2,1)S(1)}, u32[]{:S(2)}, u32[]{:S(2)}) collective-permute-start(bf16[32,1536]{1,0:T(8,128)(2,1)S(1)} %get-tuple-element.31), channel_id=1, source_target_pairs={{0,1},{1,0},{2,3},{3,2},{4,5},{5,4},{6,7},{7,6},{8,9},{9,8},{10,11... | collective-permute-start | bytes 294920 | tf_op jit(solution)/shard_map/ppermute | solution.py:242
  22.6 0.0 slice-done.3
  22.6 0.0 slice-start.6
  22.6 0.0 slice-start.7
  22.6 0.0 slice-start.8
  22.6 0.0 slice-start.9
  22.6 2.1 %shard_map.110 = (bf16[32,1536]{1,0:T(8,128)(2,1)S(1)}, bf16[32,2048]{1,0:T(8,128)(2,1)S(1)}, bf16[32,3584]{1,0:T(8,128)(2,1)S(1)}, bf16[32,3584]{1,0:T(8,128)(2,1)S(1)}, bf16[32,7168]{1,0:T(8,128)(2,1)S(1)}) custom-call(bf16[128,2048]{1,0:T(8,128)(2,1)S(1)} %get-tuple-element.33.refs_0_, bf16[2048,3584]{1,0:T(8,128)(2,1)S(1)} %bitcast.2, ...), custom_call_target="tpu_custom_call" | custom-call | tf_op jit(solution)/shard_map/pallas_call | solution.py:221
  24.7 0.1 collective-permute-start.14
  24.9 0.0 collective-permute-done.5.refs_1_
  24.9 0.0 collective-permute-done.6.refs_2_
  24.9 0.4 collective-permute-done.1.refs_4_.refs_2_
  25.3 0.1 shard_map.111.refs_4_
  25.4 1.6 %collective-permute-start.9 = (bf16[32,3584]{1,0:T(8,128)(2,1)S(1)}, bf16[32,3584]{1,0:T(8,128)(2,1)S(1)}, u32[]{:S(2)}, u32[]{:S(2)}) collective-permute-start(bf16[32,3584]{1,0:T(8,128)(2,1)S(1)} %shard_map.111.refs_4_), channel_id=1, source_target_pairs={{0,2},{1,3},{2,0},{3,1},{4,6},{5,7},{6,4},{7,5},{8,10},{9,11},{10,... | collective-permute-start | bytes 688136 | tf_op jit(solution)/shard_map/ppermute | solution.py:242
  27.0 0.0 collective-permute-start.8
  27.0 0.5 %collective-permute-start.7 = (bf16[32,1536]{1,0:T(8,128)(2,1)S(1)}, bf16[32,1536]{1,0:T(8,128)(2,1)S(1)}, u32[]{:S(2)}, u32[]{:S(2)}) collective-permute-start(bf16[32,1536]{1,0:T(8,128)(2,1)S(1)} %get-tuple-element.38), channel_id=1, source_target_pairs={{0,1},{1,0},{2,3},{3,2},{4,5},{5,4},{6,7},{7,6},{8,9},{9,8},{10,11... | collective-permute-start | bytes 294920 | tf_op jit(solution)/shard_map/ppermute | solution.py:242
  27.5 0.0 slice-done.7
  27.5 2.1 %shard_map.112 = (bf16[128,2048]{1,0:T(8,128)(2,1)S(1)}, bf16[32,1536]{1,0:T(8,128)(2,1)S(1)}, bf16[32,2048]{1,0:T(8,128)(2,1)S(1)}, bf16[32,3584]{1,0:T(8,128)(...) custom-call(bf16[32,2048]{1,0:T(8,128)(2,1)S(1)} %shard_map.105.refs_0_, ...), custom_call_target="tpu_custom_call" | custom-call | tf_op jit(solution)/shard_map/pallas_call | solution.py:221
  29.6 0.1 collective-permute-start.13
  29.7 0.0 collective-permute-done.7.refs_1_
  29.7 0.0 collective-permute-done.8.refs_2_
  29.7 0.1 shard_map.113.refs_3_
  29.8 0.6 %collective-permute-start.15 = (bf16[32,3584]{1,0:T(8,128)(2,1)S(1)}, bf16[32,3584]{1,0:T(8,128)(2,1)S(1)}, u32[]{:S(2)}, u32[]{:S(2)}) collective-permute-start(bf16[32,3584]{1,0:T(8,128)(2,1)S(1)} %shard_map.113.refs_3_), channel_id=1, source_target_pairs={{0,2},{1,3},{2,0},{3,1},{4,6},{5,7},{6,4},{7,5},{8,10},{9,11},{10,... | collective-permute-start | bytes 688136 | tf_op jit(solution)/shard_map/ppermute | solution.py:242
  30.4 2.1 %shard_map.114 = (bf16[32,1536]{1,0:T(8,128)(2,1)S(1)}, bf16[32,2048]{1,0:T(8,128)(2,1)S(1)}, bf16[32,3584]{1,0:T(8,128)(2,1)S(1)}, bf16[32,3584]{1,0:T(8,128)(2,1)S(1)}, bf16[32,7168]{1,0:T(8,128)(2,1)S(1)}) custom-call(bf16[128,2048]{1,0:T(8,128)(2,1)S(1)} %get-tuple-element.36.refs_0_, bf16[2048,3584]{1,0:T(8,128)(2,1)S(1)} %bitcast.6, ...), custom_call_target="tpu_custom_call" | custom-call | tf_op jit(solution)/shard_map/pallas_call | solution.py:221
  32.4 0.3 collective-permute-start.16
  32.7 0.3 collective-permute-done.9.refs_2_
  33.0 0.1 collective-permute-start.12
  33.0 1.4 %collective-permute-done.12.refs_1_ = bf16[32,1536]{1,0:T(8,128)(2,1)S(1)} collective-permute-done((bf16[32,1536]{1,0:T(8,128)(2,1)S(1)}, bf16[32,1536]{1,0:T(8,128)(2,1)S(1)}, u32[]{:S(2)}, u32[]{:S(2)}) %collective-permute-start.12) | collective-permute-done | bytes 98336 | tf_op jit(solution)/shard_map/ppermute | solution.py:242
  34.5 0.2 collective-permute-start.11
  34.7 0.0 collective-permute-done.13.refs_2_
  34.7 0.3 collective-permute-start.10
  35.0 0.0 collective-permute-done.14.refs_4_.refs_1_
  35.0 0.1 shard_map.116.refs_3_
  35.0 2.3 %collective-permute-start.17 = (bf16[32,3584]{1,0:T(8,128)(2,1)S(1)}, bf16[32,3584]{1,0:T(8,128)(2,1)S(1)}, u32[]{:S(2)}, u32[]{:S(2)}) collective-permute-start(bf16[32,3584]{1,0:T(8,128)(2,1)S(1)} %shard_map.116.refs_3_), channel_id=1, source_target_pairs={{0,2},{1,3},{2,0},{3,1},{4,6},{5,7},{6,4},{7,5},{8,10},{9,11},{10,... | collective-permute-start | bytes 688136 | tf_op jit(solution)/shard_map/ppermute | solution.py:242
  37.4 0.5 collective-permute-done.15.refs_4_.refs_5_
  37.9 0.0 collective-permute-done.10.refs_1_
  37.9 0.0 collective-permute-done.11.refs_2_
  37.9 0.1 shard_map.117.refs_0_
  37.9 1.6 %collective-permute-start.18 = (bf16[32,3584]{1,0:T(8,128)(2,1)S(1)}, bf16[32,3584]{1,0:T(8,128)(2,1)S(1)}, u32[]{:S(2)}, u32[]{:S(2)}) collective-permute-start(bf16[32,3584]{1,0:T(8,128)(2,1)S(1)} %shard_map.117.refs_0_), channel_id=1, source_target_pairs={{0,2},{1,3},{2,0},{3,1},{4,6},{5,7},{6,4},{7,5},{8,10},{9,11},{10,... | collective-permute-start | bytes 688136 | tf_op jit(solution)/shard_map/ppermute | solution.py:242
  39.5 2.2 %shard_map.118 = (f32[32,128]{1,0:T(8,128)S(1)}, f32[32,128]{1,0:T(8,128)S(1)}) custom-call(s32[32]{0:T(128)} %ids.1, s32[2]{0:T(128)} %lengths.1, f32[1002,128]{1,0:T(8,128)} %bitcast.7, bf16[32,3584]{1,0:T(8,128)(2,1)S(1)} %shard_map.117.refs_0_), custom_call_target="tpu_custom_call" | custom-call | tf_op jit(solution)/shard_map/pallas_call | solution.py:127
  41.7 0.9 %shard_map.119 = (f32[32,3584]{1,0:T(8,128)S(1)}, bf16[32,3584]{1,0:T(8,128)(2,1)}) custom-call(f32[32,128]{1,0:T(8,128)S(1)} %get-tuple-element.49.live, bf16[32,3584]{1,0:T(8,128)(2,1)S(1)} %get-tuple-element.50.refs_0_, bf16[32,7168]{1,0:T(8,128)(2,1)S(1)} %collective-permute-done.14.refs_4_.refs_1_, bf16[32,3584]{1,0:T(8,128)(2,1)S(1)} %collective-permute-done.9.refs_2_, ...), custom_call_target="tpu_custom_call" | custom-call | tf_op jit(solution)/shard_map/pallas_call | solution.py:300
  42.6 0.0 collective-permute-done.16.refs_1_
  42.6 1.1 %collective-permute-done.17.refs_2_ = bf16[32,3584]{1,0:T(8,128)(2,1)S(1)} collective-permute-done((bf16[32,3584]{1,0:T(8,128)(2,1)S(1)}, bf16[32,3584]{1,0:T(8,128)(2,1)S(1)}, u32[]{:S(2)}, u32[]{:S(2)}) %collective-permute-start.17) | collective-permute-done | bytes 229408 | tf_op jit(solution)/shard_map/ppermute | solution.py:242
  43.8 0.1 shard_map.120.gated
  43.9 4.3 %collective-permute-done.18.refs_2_ = bf16[32,3584]{1,0:T(8,128)(2,1)S(1)} collective-permute-done((bf16[32,3584]{1,0:T(8,128)(2,1)S(1)}, bf16[32,3584]{1,0:T(8,128)(2,1)S(1)}, u32[]{:S(2)}, u32[]{:S(2)}) %collective-permute-start.18) | collective-permute-done | bytes 229408 | tf_op jit(solution)/shard_map/ppermute | solution.py:242
  48.2 0.8 %shard_map.121 = bf16[32,3584]{1,0:T(8,128)(2,1)} custom-call(f32[32,3584]{1,0:T(8,128)S(1)} %get-tuple-element.53.act, f32[32,3584]{1,0:T(8,128)S(1)} %shard_map.120.gated, bf16[32,3584]{1,0:T(8,128)(2,1)S(1)} %get-tuple-element.57.refs_0_, bf16[32,7168]{1,0:T(8,128)(2,1)S(1)} %collective-permute-done.16.refs_1_, ...), custom_call_target="tpu_custom_call" | custom-call | tf_op jit(solution)/shard_map/pallas_call | solution.py:336
  (23 shorter events, 0.1 us)
Async XLA Ops:
  0.6 7.4 %copy-start.1 = (bf16[32,2048]{1,0:T(8,128)(2,1)S(1)}, bf16[32,2048]{1,0:T(8,128)(2,1)}, u32[]{:S(2)}) copy-start(bf16[32,2048]{1,0:T(8,128)(2,1)} %refs_0_.3) | copy-start | bytes 393220
  0.6 7.2 %copy-start = (bf16[32,2048]{1,0:T(8,128)(2,1)S(1)}, bf16[32,2048]{1,0:T(8,128)(2,1)}, u32[]{:S(2)}) copy-start(bf16[32,2048]{1,0:T(8,128)(2,1)} %refs_0_.2) | copy-start | bytes 393220
  0.6 12.5 %collective-permute-start.3 = (bf16[32,2048]{1,0:T(8,128)(2,1)}, bf16[32,2048]{1,0:T(8,128)(2,1)S(1)}, u32[]{:S(2)}, u32[]{:S(2)}) collective-permute-start(bf16[32,2048]{1,0:T(8,128)(2,1)} %refs_0_.3), channel_id=1, source_target_pairs={{0,8},{4,12},{8,0},{12,4},{1,9},{5,13},{9,1},{13,5},{2,10},{6,14},... | collective-permute-start | bytes 393224 | tf_op jit(solution)/shard_map/ppermute | solution.py:65
  7.9 9.1 %collective-permute-start = (bf16[32,2048]{1,0:T(8,128)(2,1)S(1)}, bf16[32,2048]{1,0:T(8,128)(2,1)S(1)}, u32[]{:S(2)}, u32[]{:S(2)}) collective-permute-start(bf16[32,2048]{1,0:T(8,128)(2,1)S(1)} %shard_map.105.refs_0_), channel_id=1, source_target_pairs={{0,8},{4,12},{8,0},{12,4},{1,9},{5,13},{9,1},{13,5},{2,10},{6,14},... | collective-permute-start | bytes 393224 | tf_op jit(solution)/shard_map/ppermute | solution.py:73
  8.0 9.8 %collective-permute-start.2 = (bf16[32,2048]{1,0:T(8,128)(2,1)S(1)}, bf16[32,2048]{1,0:T(8,128)(2,1)S(1)}, u32[]{:S(2)}, u32[]{:S(2)}) collective-permute-start(bf16[32,2048]{1,0:T(8,128)(2,1)S(1)} %copy-done.1), channel_id=1, source_target_pairs={{0,4},{4,0},{8,12},{12,8},{1,5},{5,1},{9,13},{13,9},{2,6},{6,2},{1... | collective-permute-start | bytes 393224 | tf_op jit(solution)/shard_map/ppermute | solution.py:65
  9.9 12.7 %slice-start = ((s8[14680064]{0:T(1024)(128)(4,1)}), s8[4194304]{0:T(1024)(128)(4,1)S(1)}, s32[]{:S(2)}) async-start(s8[14680064]{0:T(1024)(128)(4,1)} %bitcast.1), calls=%async_computation | async-start | bytes 8388608
  9.9 12.7 %slice-start.1 = ((s8[14680064]{0:T(1024)(128)(4,1)}), s8[4194304]{0:T(1024)(128)(4,1)S(1)}, s32[]{:S(2)}) async-start(s8[14680064]{0:T(1024)(128)(4,1)} %bitcast.1), calls=%async_computation.1 | async-start | bytes 8388608
  9.9 12.7 %slice-start.2 = ((s8[14680064]{0:T(1024)(128)(4,1)}), s8[4194304]{0:T(1024)(128)(4,1)S(1)}, s32[]{:S(2)}) async-start(s8[14680064]{0:T(1024)(128)(4,1)} %bitcast.1), calls=%async_computation.2 | async-start | bytes 8388608
  13.1 6.7 %collective-permute-start.4 = (bf16[32,2048]{1,0:T(8,128)(2,1)S(1)}, bf16[32,2048]{1,0:T(8,128)(2,1)S(1)}, u32[]{:S(2)}, u32[]{:S(2)}) collective-permute-start(bf16[32,2048]{1,0:T(8,128)(2,1)S(1)} %shard_map.108), channel_id=1, source_target_pairs={{0,4},{4,0},{8,12},{12,8},{1,5},{5,1},{9,13},{13,9},{2,6},{6,2},{1... | collective-permute-start | bytes 393224 | tf_op jit(solution)/shard_map/ppermute | solution.py:65
  17.0 5.5 %slice-start.3 = ((s8[14680064]{0:T(1024)(128)(4,1)}), s8[2097152]{0:T(1024)(128)(4,1)S(1)}, s32[]{:S(2)}) async-start(s8[14680064]{0:T(1024)(128)(4,1)} %bitcast.1), calls=%async_computation.3 | async-start | bytes 4194304
  17.1 10.4 %slice-start.4 = ((s8[14680064]{0:T(1024)(128)(4,1)}), s8[4194304]{0:T(1024)(128)(4,1)S(1)}, s32[]{:S(2)}) async-start(s8[14680064]{0:T(1024)(128)(4,1)} %bitcast.3), calls=%async_computation.4 | async-start | bytes 8388608
  17.1 10.4 %slice-start.5 = ((s8[14680064]{0:T(1024)(128)(4,1)}), s8[4194304]{0:T(1024)(128)(4,1)S(1)}, s32[]{:S(2)}) async-start(s8[14680064]{0:T(1024)(128)(4,1)} %bitcast.3), calls=%async_computation.5 | async-start | bytes 8388608
  17.1 8.2 %collective-permute-start.1 = (bf16[64,2048]{1,0:T(8,128)(2,1)S(1)}, bf16[64,2048]{1,0:T(8,128)(2,1)S(1)}, u32[]{:S(2)}, u32[]{:S(2)}) collective-permute-start(bf16[64,2048]{1,0:T(8,128)(2,1)S(1)} %shard_map.106), channel_id=1, source_target_pairs={{0,4},{4,0},{8,12},{12,8},{1,5},{5,1},{9,13},{13,9},{2,6},{6,2},{1... | collective-permute-start | bytes 786440 | tf_op jit(solution)/shard_map/ppermute | solution.py:73
  22.0 2.9 %collective-permute-start.6 = (bf16[32,2048]{1,0:T(8,128)(2,1)S(1)}, bf16[32,2048]{1,0:T(8,128)(2,1)S(1)}, u32[]{:S(2)}, u32[]{:S(2)}) collective-permute-start(bf16[32,2048]{1,0:T(8,128)(2,1)S(1)} %get-tuple-element.32), channel_id=1, source_target_pairs={{0,1},{1,0},{2,3},{3,2},{4,5},{5,4},{6,7},{7,6},{8,9},{9,8},{10,11... | collective-permute-start | bytes 393224 | tf_op jit(solution)/shard_map/ppermute | solution.py:242
  22.1 2.8 %collective-permute-start.5 = (bf16[32,1536]{1,0:T(8,128)(2,1)S(1)}, bf16[32,1536]{1,0:T(8,128)(2,1)S(1)}, u32[]{:S(2)}, u32[]{:S(2)}) collective-permute-start(bf16[32,1536]{1,0:T(8,128)(2,1)S(1)} %get-tuple-element.31), channel_id=1, source_target_pairs={{0,1},{1,0},{2,3},{3,2},{4,5},{5,4},{6,7},{7,6},{8,9},{9,8},{10,11... | collective-permute-start | bytes 294920 | tf_op jit(solution)/shard_map/ppermute | solution.py:242
  22.6 4.9 %slice-start.6 = ((s8[14680064]{0:T(1024)(128)(4,1)}), s8[4194304]{0:T(1024)(128)(4,1)S(1)}, s32[]{:S(2)}) async-start(s8[14680064]{0:T(1024)(128)(4,1)} %bitcast.3), calls=%async_computation.6 | async-start | bytes 8388608
  22.6 4.9 %slice-start.7 = ((s8[14680064]{0:T(1024)(128)(4,1)}), s8[2097152]{0:T(1024)(128)(4,1)S(1)}, s32[]{:S(2)}) async-start(s8[14680064]{0:T(1024)(128)(4,1)} %bitcast.3), calls=%async_computation.7 | async-start | bytes 4194304
  22.6 7.7 %slice-start.8 = ((s8[14680064]{0:T(1024)(128)(4,1)}), s8[4194304]{0:T(1024)(128)(4,1)S(1)}, s32[]{:S(2)}) async-start(s8[14680064]{0:T(1024)(128)(4,1)} %bitcast.5), calls=%async_computation.8 | async-start | bytes 8388608
  22.6 7.7 %slice-start.9 = ((s8[14680064]{0:T(1024)(128)(4,1)}), s8[4194304]{0:T(1024)(128)(4,1)S(1)}, s32[]{:S(2)}) async-start(s8[14680064]{0:T(1024)(128)(4,1)} %bitcast.5), calls=%async_computation.9 | async-start | bytes 8388608
  24.7 10.3 %collective-permute-start.14 = (bf16[32,7168]{1,0:T(8,128)(2,1)S(1)}, bf16[32,7168]{1,0:T(8,128)(2,1)S(1)}, u32[]{:S(2)}, u32[]{:S(2)}) collective-permute-start(bf16[32,7168]{1,0:T(8,128)(2,1)S(1)} %get-tuple-element.48), channel_id=1, source_target_pairs={{0,1},{1,0},{2,3},{3,2},{4,5},{5,4},{6,7},{7,6},{8,9},{9,8},{10,11... | collective-permute-start | bytes 1376264 | tf_op jit(solution)/shard_map/ppermute | solution.py:242
  25.3 5.0 %slice-start.10 = ((s8[14680064]{0:T(1024)(128)(4,1)}), s8[4194304]{0:T(1024)(128)(4,1)S(1)}, s32[]{:S(2)}) async-start(s8[14680064]{0:T(1024)(128)(4,1)} %bitcast.5), calls=%async_computation.10 | async-start | bytes 8388608
  25.4 7.6 %collective-permute-start.9 = (bf16[32,3584]{1,0:T(8,128)(2,1)S(1)}, bf16[32,3584]{1,0:T(8,128)(2,1)S(1)}, u32[]{:S(2)}, u32[]{:S(2)}) collective-permute-start(bf16[32,3584]{1,0:T(8,128)(2,1)S(1)} %shard_map.111.refs_4_), channel_id=1, source_target_pairs={{0,2},{1,3},{2,0},{3,1},{4,6},{5,7},{6,4},{7,5},{8,10},{9,11},{10,... | collective-permute-start | bytes 688136 | tf_op jit(solution)/shard_map/ppermute | solution.py:242
  27.0 2.7 %collective-permute-start.8 = (bf16[32,2048]{1,0:T(8,128)(2,1)S(1)}, bf16[32,2048]{1,0:T(8,128)(2,1)S(1)}, u32[]{:S(2)}, u32[]{:S(2)}) collective-permute-start(bf16[32,2048]{1,0:T(8,128)(2,1)S(1)} %get-tuple-element.39), channel_id=1, source_target_pairs={{0,1},{1,0},{2,3},{3,2},{4,5},{5,4},{6,7},{7,6},{8,9},{9,8},{10,11... | collective-permute-start | bytes 393224 | tf_op jit(solution)/shard_map/ppermute | solution.py:242
  27.0 3.4 %slice-start.11 = ((s8[14680064]{0:T(1024)(128)(4,1)}), s8[2097152]{0:T(1024)(128)(4,1)S(1)}, s32[]{:S(2)}) async-start(s8[14680064]{0:T(1024)(128)(4,1)} %bitcast.5), calls=%async_computation.11 | async-start | bytes 4194304
  27.0 2.7 %collective-permute-start.7 = (bf16[32,1536]{1,0:T(8,128)(2,1)S(1)}, bf16[32,1536]{1,0:T(8,128)(2,1)S(1)}, u32[]{:S(2)}, u32[]{:S(2)}) collective-permute-start(bf16[32,1536]{1,0:T(8,128)(2,1)S(1)} %get-tuple-element.38), channel_id=1, source_target_pairs={{0,1},{1,0},{2,3},{3,2},{4,5},{5,4},{6,7},{7,6},{8,9},{9,8},{10,11... | collective-permute-start | bytes 294920 | tf_op jit(solution)/shard_map/ppermute | solution.py:242
  29.6 5.0 %collective-permute-start.13 = (bf16[32,2048]{1,0:T(8,128)(2,1)S(1)}, bf16[32,2048]{1,0:T(8,128)(2,1)S(1)}, u32[]{:S(2)}, u32[]{:S(2)}) collective-permute-start(bf16[32,2048]{1,0:T(8,128)(2,1)S(1)} %get-tuple-element.47), channel_id=1, source_target_pairs={{0,1},{1,0},{2,3},{3,2},{4,5},{5,4},{6,7},{7,6},{8,9},{9,8},{10,11... | collective-permute-start | bytes 393224 | tf_op jit(solution)/shard_map/ppermute | solution.py:242
  29.8 8.1 %collective-permute-start.15 = (bf16[32,3584]{1,0:T(8,128)(2,1)S(1)}, bf16[32,3584]{1,0:T(8,128)(2,1)S(1)}, u32[]{:S(2)}, u32[]{:S(2)}) collective-permute-start(bf16[32,3584]{1,0:T(8,128)(2,1)S(1)} %shard_map.113.refs_3_), channel_id=1, source_target_pairs={{0,2},{1,3},{2,0},{3,1},{4,6},{5,7},{6,4},{7,5},{8,10},{9,11},{10,... | collective-permute-start | bytes 688136 | tf_op jit(solution)/shard_map/ppermute | solution.py:242
  32.4 10.2 %collective-permute-start.16 = (bf16[32,7168]{1,0:T(8,128)(2,1)S(1)}, bf16[32,7168]{1,0:T(8,128)(2,1)S(1)}, u32[]{:S(2)}, u32[]{:S(2)}) collective-permute-start(bf16[32,7168]{1,0:T(8,128)(2,1)S(1)} %get-tuple-element.56), channel_id=1, source_target_pairs={{0,1},{1,0},{2,3},{3,2},{4,5},{5,4},{6,7},{7,6},{8,9},{9,8},{10,11... | collective-permute-start | bytes 1376264 | tf_op jit(solution)/shard_map/ppermute | solution.py:242
  33.0 1.5 %collective-permute-start.12 = (bf16[32,1536]{1,0:T(8,128)(2,1)S(1)}, bf16[32,1536]{1,0:T(8,128)(2,1)S(1)}, u32[]{:S(2)}, u32[]{:S(2)}) collective-permute-start(bf16[32,1536]{1,0:T(8,128)(2,1)S(1)} %get-tuple-element.46), channel_id=1, source_target_pairs={{0,1},{1,0},{2,3},{3,2},{4,5},{5,4},{6,7},{7,6},{8,9},{9,8},{10,11... | collective-permute-start | bytes 294920 | tf_op jit(solution)/shard_map/ppermute | solution.py:242
  34.5 3.4 %collective-permute-start.11 = (bf16[32,2048]{1,0:T(8,128)(2,1)S(1)}, bf16[32,2048]{1,0:T(8,128)(2,1)S(1)}, u32[]{:S(2)}, u32[]{:S(2)}) collective-permute-start(bf16[32,2048]{1,0:T(8,128)(2,1)S(1)} %get-tuple-element.45), channel_id=1, source_target_pairs={{0,1},{1,0},{2,3},{3,2},{4,5},{5,4},{6,7},{7,6},{8,9},{9,8},{10,11... | collective-permute-start | bytes 393224 | tf_op jit(solution)/shard_map/ppermute | solution.py:242
  34.7 3.2 %collective-permute-start.10 = (bf16[32,1536]{1,0:T(8,128)(2,1)S(1)}, bf16[32,1536]{1,0:T(8,128)(2,1)S(1)}, u32[]{:S(2)}, u32[]{:S(2)}) collective-permute-start(bf16[32,1536]{1,0:T(8,128)(2,1)S(1)} %get-tuple-element.44), channel_id=1, source_target_pairs={{0,1},{1,0},{2,3},{3,2},{4,5},{5,4},{6,7},{7,6},{8,9},{9,8},{10,11... | collective-permute-start | bytes 294920 | tf_op jit(solution)/shard_map/ppermute | solution.py:242
  35.0 8.7 %collective-permute-start.17 = (bf16[32,3584]{1,0:T(8,128)(2,1)S(1)}, bf16[32,3584]{1,0:T(8,128)(2,1)S(1)}, u32[]{:S(2)}, u32[]{:S(2)}) collective-permute-start(bf16[32,3584]{1,0:T(8,128)(2,1)S(1)} %shard_map.116.refs_3_), channel_id=1, source_target_pairs={{0,2},{1,3},{2,0},{3,1},{4,6},{5,7},{6,4},{7,5},{8,10},{9,11},{10,... | collective-permute-start | bytes 688136 | tf_op jit(solution)/shard_map/ppermute | solution.py:242
  37.9 10.3 %collective-permute-start.18 = (bf16[32,3584]{1,0:T(8,128)(2,1)S(1)}, bf16[32,3584]{1,0:T(8,128)(2,1)S(1)}, u32[]{:S(2)}, u32[]{:S(2)}) collective-permute-start(bf16[32,3584]{1,0:T(8,128)(2,1)S(1)} %shard_map.117.refs_0_), channel_id=1, source_target_pairs={{0,2},{1,3},{2,0},{3,1},{4,6},{5,7},{6,4},{7,5},{8,10},{9,11},{10,... | collective-permute-start | bytes 688136 | tf_op jit(solution)/shard_map/ppermute | solution.py:242

commit v14 on v13

--- a/solution.py
+++ b/solution.py
@@ -359,15 +359,16 @@
     target_own = exchange(own, 0, narrow)
     sent, target_g = finish(sends, keeps, (target_own, 0), narrow, (up_keeps[0], source_pieces[-1]))
     rows, gate_sends, own, gate_keeps = product(
-        source_pieces, (in_vmem(source_gate),), narrow, (sent,), spots=source_spots
+        source_pieces, (in_vmem(source_gate),), narrow, (sent,), spots=source_spots, split=False
     )
+    gate_own = exchange(own, 0, narrow)
     after = (gate_keeps[0],)
     sent, target_u = finish(up_sends, up_keeps, (target_own, -width), narrow, after)
-    _, sends, own, keeps = product(rows, (in_vmem(source_up),), narrow, (sent,), (own,))
+    _, sends, own, keeps = product(rows, (in_vmem(source_up),), narrow, (sent,))
     sends = resent(sends, (target_g[0][-1],))
     own = exchange(own, 0, narrow)
-    sent, source_g = finish(gate_sends, gate_keeps, (own, 0), narrow, (keeps[0], target_own))
-    sent, source_u = finish(sends, keeps, (own, -width), narrow, (sent, target_u[0][-1]))
+    sent, source_g = finish(gate_sends, gate_keeps, (gate_own, 0), narrow, (keeps[0], target_own))
+    sent, source_u = finish(sends, keeps, (own, 0), narrow, (sent, target_u[0][-1]))
     live, weight = look_up(token_ids, lengths, ratio_weight, (sent,))
     act, target_out = target_end(live, target_g, target_u)
     gated = source_middle(live, weight, source_g)

time: 49.8 us -> 49.6 us (level)
  the two profiles are of different devices: /device:TPU:0 before, /device:TPU:24 now
where the time goes in v14:
time: 49.6 us; the launch traced here: 49.4 us
  Pallas kernels  19 us (38%)
  waiting for transfers between devices  18.5 us (37%)
  starting transfers between devices  10.9 us (22%)
  between operations  0.93 us (2%)
    ppermute x14, waiting for transfers between devices, exchange(): lax.ppermute(array, 'narrow', [(i, i ^ 1 << step) for i in range(size)])  8.54 us
    pallas_call x4, Pallas kernels, product(): pl.pallas_call(functools.partial(product_kernel, len(tokens), len(matrice...  8.35 us
    ppermute x3, waiting for transfers between devices, gather_pieces(): lax.ppermute(source, axis, [(i, i ^ low) for i in range(size)])  7.29 us
    ppermute x14, starting transfers between devices, exchange(): lax.ppermute(array, 'narrow', [(i, i ^ 1 << step) for i in range(size)])  7.29 us
    pallas_call x2, Pallas kernels, load(): pl.pallas_call(functools.partial(load_kernel, first), out_shape=pltpu.VME...  6.33 us
    ppermute x2, starting transfers between devices, gather_doubling(): arrays.append(lax.ppermute(send, axis, [(i, i ^ low) for i in range(size)]))  2.73 us
    ppermute x2, waiting for transfers between devices, gather_doubling(): arrays.append(lax.ppermute(send, axis, [(i, i ^ low) for i in range(size)]))  2.63 us
    pallas_call x1, Pallas kernels, look_up(): pl.pallas_call(functools.partial(look_up_kernel, ids.shape[0] // lengths....  2.16 us
  transfers between devices with their start and end apart: 19, of which 8 were waited for; matrix products, arithmetic and copies ran while one was open for 0% of the time, Pallas kernels for 37%

profile of v14, /device:TPU:24, one launch (start us, length us, event | category | flops | bytes accessed | tf_op | source)
XLA Modules:
  0.0 49.4 jit_solution(1947275930813961710)
XLA Ops:
  0.6 0.0 copy-start.1
  0.6 0.0 copy-start
  0.6 0.4 collective-permute-start.3
  1.1 3.1 %shard_map.104.refs_1_.refs_0_.refs_4_ = bf16[1024,3584]{1,0:T(8,128)(2,1)S(1)} custom-call(bf16[2048,3584]{1,0:T(8,128)(2,1)} %matrix.3), custom_call_target="tpu_custom_call" | custom-call | tf_op jit(solution)/shard_map/pallas_call | solution.py:150
  4.2 2.7 %collective-permute-start = (bf16[32,2048]{1,0:T(8,128)(2,1)S(1)}, bf16[32,2048]{1,0:T(8,128)(2,1)S(1)}, u32[]{:S(2)}, u32[]{:S(2)}) collective-permute-start(bf16[32,2048]{1,0:T(8,128)(2,1)S(1)} %shard_map.105.refs_0_), channel_id=1, source_target_pairs={{0,8},{4,12},{8,0},{12,4},{1,9},{5,13},{9,1},{13,5},{2,10},{6,14},... | collective-permute-start | bytes 393224 | tf_op jit(solution)/shard_map/ppermute | solution.py:73
  6.8 0.4 collective-permute-start.2
  7.3 3.2 %shard_map.107.refs_1_.refs_5_ = bf16[1024,3584]{1,0:T(8,128)(2,1)S(1)} custom-call(bf16[2048,3584]{1,0:T(8,128)(2,1)} %matrix.3, bf16[1024,3584]{1,0:T(8,128)(2,1)S(1)} %shard_map.104.refs_1_.refs_0_.refs_4_), custom_call_target="tpu_custom_call" | custom-call | tf_op jit(solution)/shard_map/pallas_call | solution.py:150
  10.5 2.2 %collective-permute-done.3.refs_0_.refs_2_ = bf16[32,2048]{1,0:T(8,128)(2,1)S(1)} collective-permute-done((bf16[32,2048]{1,0:T(8,128)(2,1)}, bf16[32,2048]{1,0:T(8,128)(2,1)S(1)}, u32[]{:S(2)}, u32[]{:S(2)}) %collective-permute-start.3) | collective-permute-done | bytes 131104 | tf_op jit(solution)/shard_map/ppermute | solution.py:65
  12.8 0.1 collective-permute-start.4
  12.8 2.6 %collective-permute-done.refs_1_ = bf16[32,2048]{1,0:T(8,128)(2,1)S(1)} collective-permute-done((bf16[32,2048]{1,0:T(8,128)(2,1)S(1)}, bf16[32,2048]{1,0:T(8,128)(2,1)S(1)}, u32[]{:S(2)}, u32[]{:S(2)}) %collective-permute-start) | collective-permute-done | bytes 131104 | tf_op jit(solution)/shard_map/ppermute | solution.py:73
  15.5 0.0 slice-start.3
  15.5 0.0 slice-start.4
  15.5 0.0 slice-start.5
  15.5 0.1 collective-permute-start.1
  15.6 2.3 %collective-permute-done.2.refs_1_ = bf16[32,2048]{1,0:T(8,128)(2,1)S(1)} collective-permute-done((bf16[32,2048]{1,0:T(8,128)(2,1)S(1)}, bf16[32,2048]{1,0:T(8,128)(2,1)S(1)}, u32[]{:S(2)}, u32[]{:S(2)}) %collective-permute-start.2) | collective-permute-done | bytes 131104 | tf_op jit(solution)/shard_map/ppermute | solution.py:65
  17.9 2.8 %collective-permute-done.4.refs_3_ = bf16[32,2048]{1,0:T(8,128)(2,1)S(1)} collective-permute-done((bf16[32,2048]{1,0:T(8,128)(2,1)S(1)}, bf16[32,2048]{1,0:T(8,128)(2,1)S(1)}, u32[]{:S(2)}, u32[]{:S(2)}) %collective-permute-start.4) | collective-permute-done | bytes 131104 | tf_op jit(solution)/shard_map/ppermute | solution.py:65
  20.7 2.1 %shard_map.109 = (bf16[128,2048]{1,0:T(8,128)(2,1)S(1)}, bf16[32,1536]{1,0:T(8,128)(2,1)S(1)}, bf16[32,2048]{1,0:T(8,128)(2,1)S(1)}, bf16[32,3584]{1,0:T(8,128)(...) custom-call(bf16[32,2048]{1,0:T(8,128)(2,1)S(1)} %copy-done.1, ...), custom_call_target="tpu_custom_call" | custom-call | tf_op jit(solution)/shard_map/pallas_call | solution.py:221
  22.8 0.1 collective-permute-start.6
  22.9 0.5 %collective-permute-start.5 = (bf16[32,1536]{1,0:T(8,128)(2,1)S(1)}, bf16[32,1536]{1,0:T(8,128)(2,1)S(1)}, u32[]{:S(2)}, u32[]{:S(2)}) collective-permute-start(bf16[32,1536]{1,0:T(8,128)(2,1)S(1)} %get-tuple-element.30), channel_id=1, source_target_pairs={{0,1},{1,0},{2,3},{3,2},{4,5},{5,4},{6,7},{7,6},{8,9},{9,8},{10,11... | collective-permute-start | bytes 294920 | tf_op jit(solution)/shard_map/ppermute | solution.py:242
  23.4 0.0 slice-done.3
  23.4 0.0 slice-start.6
  23.4 0.0 slice-start.7
  23.4 0.0 slice-start.8
  23.4 0.0 slice-start.9
  23.4 2.1 %shard_map.110 = (bf16[32,1536]{1,0:T(8,128)(2,1)S(1)}, bf16[32,2048]{1,0:T(8,128)(2,1)S(1)}, bf16[32,3584]{1,0:T(8,128)(2,1)S(1)}, bf16[32,3584]{1,0:T(8,128)(2,1)S(1)}, bf16[32,7168]{1,0:T(8,128)(2,1)S(1)}) custom-call(bf16[128,2048]{1,0:T(8,128)(2,1)S(1)} %get-tuple-element.32.refs_0_, bf16[2048,3584]{1,0:T(8,128)(2,1)S(1)} %bitcast.2, ...), custom_call_target="tpu_custom_call" | custom-call | tf_op jit(solution)/shard_map/pallas_call | solution.py:221
  25.5 0.1 collective-permute-start.13
  25.7 0.4 collective-permute-start.8
  26.1 0.0 collective-permute-done.5.refs_1_
  26.1 0.0 collective-permute-done.6.refs_2_
  26.1 0.0 collective-permute-done.1.refs_4_.refs_2_
  26.1 0.0 slice-start.10
  26.1 0.1 shard_map.111.refs_4_
  26.2 1.4 %collective-permute-start.9 = (bf16[32,3584]{1,0:T(8,128)(2,1)S(1)}, bf16[32,3584]{1,0:T(8,128)(2,1)S(1)}, u32[]{:S(2)}, u32[]{:S(2)}) collective-permute-start(bf16[32,3584]{1,0:T(8,128)(2,1)S(1)} %shard_map.111.refs_4_), channel_id=1, source_target_pairs={{0,2},{1,3},{2,0},{3,1},{4,6},{5,7},{6,4},{7,5},{8,10},{9,11},{10,... | collective-permute-start | bytes 688136 | tf_op jit(solution)/shard_map/ppermute | solution.py:242
  27.6 0.0 collective-permute-start.7
  27.6 2.1 %shard_map.112 = (bf16[128,2048]{1,0:T(8,128)(2,1)S(1)}, bf16[32,3584]{1,0:T(8,128)(2,1)S(1)}, bf16[32,3584]{1,0:T(8,128)(2,1)S(1)}, bf16[32,3584]{1,0:T(8,128)(2,1)S(1)}, bf16[32,3584]{1,0:T(8,128)(2,1)S(1)}) custom-call(bf16[32,2048]{1,0:T(8,128)(2,1)S(1)} %shard_map.105.refs_0_, bf16[32,2048]{1,0:T(8,128)(2,1)S(1)} %collective-permute-done.refs_1_, ...), custom_call_target="tpu_custom_call" | custom-call | tf_op jit(solution)/shard_map/pallas_call | solution.py:221
  29.7 0.6 %collective-permute-start.12 = (bf16[32,3584]{1,0:T(8,128)(2,1)S(1)}, bf16[32,3584]{1,0:T(8,128)(2,1)S(1)}, u32[]{:S(2)}, u32[]{:S(2)}) collective-permute-start(bf16[32,3584]{1,0:T(8,128)(2,1)S(1)} %get-tuple-element.44), channel_id=1, source_target_pairs={{0,1},{1,0},{2,3},{3,2},{4,5},{5,4},{6,7},{7,6},{8,9},{9,8},{10,11... | collective-permute-start | bytes 688136 | tf_op jit(solution)/shard_map/ppermute | solution.py:242
  30.3 0.0 collective-permute-done.7.refs_1_
  30.3 0.0 collective-permute-done.8.refs_2_
  30.3 0.1 shard_map.113.refs_2_
  30.4 0.8 %collective-permute-start.14 = (bf16[32,3584]{1,0:T(8,128)(2,1)S(1)}, bf16[32,3584]{1,0:T(8,128)(2,1)S(1)}, u32[]{:S(2)}, u32[]{:S(2)}) collective-permute-start(bf16[32,3584]{1,0:T(8,128)(2,1)S(1)} %shard_map.113.refs_2_), channel_id=1, source_target_pairs={{0,2},{1,3},{2,0},{3,1},{4,6},{5,7},{6,4},{7,5},{8,10},{9,11},{10,... | collective-permute-start | bytes 688136 | tf_op jit(solution)/shard_map/ppermute | solution.py:242
  31.1 0.0 slice-done.8
  31.2 2.1 %shard_map.114 = (bf16[32,1536]{1,0:T(8,128)(2,1)S(1)}, bf16[32,2048]{1,0:T(8,128)(2,1)S(1)}, bf16[32,3584]{1,0:T(8,128)(2,1)S(1)}, bf16[32,3584]{1,0:T(8,128)(2,1)S(1)}, bf16[32,3584]{1,0:T(8,128)(2,1)S(1)}) custom-call(bf16[128,2048]{1,0:T(8,128)(2,1)S(1)} %get-tuple-element.35.refs_0_, bf16[2048,3584]{1,0:T(8,128)(2,1)S(1)} %bitcast.6, ...), custom_call_target="tpu_custom_call" | custom-call | tf_op jit(solution)/shard_map/pallas_call | solution.py:221
  33.2 1.3 %collective-permute-done.9.refs_2_ = bf16[32,3584]{1,0:T(8,128)(2,1)S(1)} collective-permute-done((bf16[32,3584]{1,0:T(8,128)(2,1)S(1)}, bf16[32,3584]{1,0:T(8,128)(2,1)S(1)}, u32[]{:S(2)}, u32[]{:S(2)}) %collective-permute-start.9) | collective-permute-done | bytes 229408 | tf_op jit(solution)/shard_map/ppermute | solution.py:242
  34.6 0.1 collective-permute-start.11
  34.7 0.5 %collective-permute-start.10 = (bf16[32,1536]{1,0:T(8,128)(2,1)S(1)}, bf16[32,1536]{1,0:T(8,128)(2,1)S(1)}, u32[]{:S(2)}, u32[]{:S(2)}) collective-permute-start(bf16[32,1536]{1,0:T(8,128)(2,1)S(1)} %get-tuple-element.42), channel_id=1, source_target_pairs={{0,1},{1,0},{2,3},{3,2},{4,5},{5,4},{6,7},{7,6},{8,9},{9,8},{10,11... | collective-permute-start | bytes 294920 | tf_op jit(solution)/shard_map/ppermute | solution.py:242
  35.2 0.0 collective-permute-done.12.refs_1_
  35.2 0.1 collective-permute-start.15
  35.3 0.0 collective-permute-done.13.refs_3_.refs_1_.refs_4_
  35.3 0.1 shard_map.116.refs_3_
  35.3 1.5 %collective-permute-start.16 = (bf16[32,3584]{1,0:T(8,128)(2,1)S(1)}, bf16[32,3584]{1,0:T(8,128)(2,1)S(1)}, u32[]{:S(2)}, u32[]{:S(2)}) collective-permute-start(bf16[32,3584]{1,0:T(8,128)(2,1)S(1)} %shard_map.116.refs_3_), channel_id=1, source_target_pairs={{0,2},{1,3},{2,0},{3,1},{4,6},{5,7},{6,4},{7,5},{8,10},{9,11},{10,... | collective-permute-start | bytes 688136 | tf_op jit(solution)/shard_map/ppermute | solution.py:242
  36.8 2.2 %collective-permute-done.14.refs_4_.refs_5_ = bf16[32,3584]{1,0:T(8,128)(2,1)S(1)} collective-permute-done((bf16[32,3584]{1,0:T(8,128)(2,1)S(1)}, bf16[32,3584]{1,0:T(8,128)(2,1)S(1)}, u32[]{:S(2)}, u32[]{:S(2)}) %collective-permute-start.14) | collective-permute-done | bytes 229408 | tf_op jit(solution)/shard_map/ppermute | solution.py:242
  39.0 0.0 collective-permute-start.17
  39.0 0.0 collective-permute-done.10.refs_1_
  39.0 0.0 collective-permute-done.11.refs_2_
  39.1 0.1 shard_map.117.refs_0_
  39.1 1.2 %collective-permute-start.18 = (bf16[32,3584]{1,0:T(8,128)(2,1)S(1)}, bf16[32,3584]{1,0:T(8,128)(2,1)S(1)}, u32[]{:S(2)}, u32[]{:S(2)}) collective-permute-start(bf16[32,3584]{1,0:T(8,128)(2,1)S(1)} %shard_map.117.refs_0_), channel_id=1, source_target_pairs={{0,2},{1,3},{2,0},{3,1},{4,6},{5,7},{6,4},{7,5},{8,10},{9,11},{10,... | collective-permute-start | bytes 688136 | tf_op jit(solution)/shard_map/ppermute | solution.py:242
  40.4 2.2 %shard_map.118 = (f32[32,128]{1,0:T(8,128)S(1)}, f32[32,128]{1,0:T(8,128)S(1)}) custom-call(s32[32]{0:T(128)} %ids.1, s32[2]{0:T(128)} %lengths.1, f32[1002,128]{1,0:T(8,128)} %bitcast.7, bf16[32,3584]{1,0:T(8,128)(2,1)S(1)} %shard_map.117.refs_0_), custom_call_target="tpu_custom_call" | custom-call | tf_op jit(solution)/shard_map/pallas_call | solution.py:127
  42.5 0.9 %shard_map.119 = (f32[32,3584]{1,0:T(8,128)S(1)}, bf16[32,3584]{1,0:T(8,128)(2,1)}) custom-call(f32[32,128]{1,0:T(8,128)S(1)} %get-tuple-element.46.live, bf16[32,3584]{1,0:T(8,128)(2,1)S(1)} %get-tuple-element.47.refs_0_, bf16[32,7168]{1,0:T(8,128)(2,1)S(1)} %collective-permute-done.13.refs_3_.refs_1_.refs_4_, ...), custom_call_target="tpu_custom_call" | custom-call | tf_op jit(solution)/shard_map/pallas_call | solution.py:300
  43.5 0.0 collective-permute-done.15.refs_1_
  43.5 0.5 %collective-permute-done.16.refs_2_ = bf16[32,3584]{1,0:T(8,128)(2,1)S(1)} collective-permute-done((bf16[32,3584]{1,0:T(8,128)(2,1)S(1)}, bf16[32,3584]{1,0:T(8,128)(2,1)S(1)}, u32[]{:S(2)}, u32[]{:S(2)}) %collective-permute-start.16) | collective-permute-done | bytes 229408 | tf_op jit(solution)/shard_map/ppermute | solution.py:242
  44.0 0.1 shard_map.120.gated
  44.1 0.0 collective-permute-done.17.refs_1_
  44.1 4.5 %collective-permute-done.18.refs_2_ = bf16[32,3584]{1,0:T(8,128)(2,1)S(1)} collective-permute-done((bf16[32,3584]{1,0:T(8,128)(2,1)S(1)}, bf16[32,3584]{1,0:T(8,128)(2,1)S(1)}, u32[]{:S(2)}, u32[]{:S(2)}) %collective-permute-start.18) | collective-permute-done | bytes 229408 | tf_op jit(solution)/shard_map/ppermute | solution.py:242
  48.6 0.8 %shard_map.121 = bf16[32,3584]{1,0:T(8,128)(2,1)} custom-call(f32[32,3584]{1,0:T(8,128)S(1)} %get-tuple-element.50.act, f32[32,3584]{1,0:T(8,128)S(1)} %shard_map.120.gated, bf16[32,3584]{1,0:T(8,128)(2,1)S(1)} %get-tuple-element.54.refs_0_, bf16[32,3584]{1,0:T(8,128)(2,1)S(1)} %collective-permute-done.17.refs_1_, ...), custom_call_target="tpu_custom_call" | custom-call | tf_op jit(solution)/shard_map/pallas_call | solution.py:336
  (23 shorter events, 0.1 us)
Async XLA Ops:
  0.6 6.2 %copy-start.1 = (bf16[32,2048]{1,0:T(8,128)(2,1)S(1)}, bf16[32,2048]{1,0:T(8,128)(2,1)}, u32[]{:S(2)}) copy-start(bf16[32,2048]{1,0:T(8,128)(2,1)} %refs_0_.3) | copy-start | bytes 393220
  0.6 3.5 %copy-start = (bf16[32,2048]{1,0:T(8,128)(2,1)S(1)}, bf16[32,2048]{1,0:T(8,128)(2,1)}, u32[]{:S(2)}) copy-start(bf16[32,2048]{1,0:T(8,128)(2,1)} %refs_0_.2) | copy-start | bytes 393220
  0.6 12.1 %collective-permute-start.3 = (bf16[32,2048]{1,0:T(8,128)(2,1)}, bf16[32,2048]{1,0:T(8,128)(2,1)S(1)}, u32[]{:S(2)}, u32[]{:S(2)}) collective-permute-start(bf16[32,2048]{1,0:T(8,128)(2,1)} %refs_0_.3), channel_id=1, source_target_pairs={{0,8},{4,12},{8,0},{12,4},{1,9},{5,13},{9,1},{13,5},{2,10},{6,14},... | collective-permute-start | bytes 393224 | tf_op jit(solution)/shard_map/ppermute | solution.py:65
  4.2 11.3 %collective-permute-start = (bf16[32,2048]{1,0:T(8,128)(2,1)S(1)}, bf16[32,2048]{1,0:T(8,128)(2,1)S(1)}, u32[]{:S(2)}, u32[]{:S(2)}) collective-permute-start(bf16[32,2048]{1,0:T(8,128)(2,1)S(1)} %shard_map.105.refs_0_), channel_id=1, source_target_pairs={{0,8},{4,12},{8,0},{12,4},{1,9},{5,13},{9,1},{13,5},{2,10},{6,14},... | collective-permute-start | bytes 393224 | tf_op jit(solution)/shard_map/ppermute | solution.py:73
  6.8 11.0 %collective-permute-start.2 = (bf16[32,2048]{1,0:T(8,128)(2,1)S(1)}, bf16[32,2048]{1,0:T(8,128)(2,1)S(1)}, u32[]{:S(2)}, u32[]{:S(2)}) collective-permute-start(bf16[32,2048]{1,0:T(8,128)(2,1)S(1)} %copy-done.1), channel_id=1, source_target_pairs={{0,4},{4,0},{8,12},{12,8},{1,5},{5,1},{9,13},{13,9},{2,6},{6,2},{1... | collective-permute-start | bytes 393224 | tf_op jit(solution)/shard_map/ppermute | solution.py:65
  7.3 16.1 %slice-start = ((s8[14680064]{0:T(1024)(128)(4,1)}), s8[4194304]{0:T(1024)(128)(4,1)S(1)}, s32[]{:S(2)}) async-start(s8[14680064]{0:T(1024)(128)(4,1)} %bitcast.1), calls=%async_computation | async-start | bytes 8388608
  7.3 16.1 %slice-start.1 = ((s8[14680064]{0:T(1024)(128)(4,1)}), s8[4194304]{0:T(1024)(128)(4,1)S(1)}, s32[]{:S(2)}) async-start(s8[14680064]{0:T(1024)(128)(4,1)} %bitcast.1), calls=%async_computation.1 | async-start | bytes 8388608
  7.3 16.1 %slice-start.2 = ((s8[14680064]{0:T(1024)(128)(4,1)}), s8[4194304]{0:T(1024)(128)(4,1)S(1)}, s32[]{:S(2)}) async-start(s8[14680064]{0:T(1024)(128)(4,1)} %bitcast.1), calls=%async_computation.2 | async-start | bytes 8388608
  12.8 7.9 %collective-permute-start.4 = (bf16[32,2048]{1,0:T(8,128)(2,1)S(1)}, bf16[32,2048]{1,0:T(8,128)(2,1)S(1)}, u32[]{:S(2)}, u32[]{:S(2)}) collective-permute-start(bf16[32,2048]{1,0:T(8,128)(2,1)S(1)} %shard_map.108), channel_id=1, source_target_pairs={{0,4},{4,0},{8,12},{12,8},{1,5},{5,1},{9,13},{13,9},{2,6},{6,2},{1... | collective-permute-start | bytes 393224 | tf_op jit(solution)/shard_map/ppermute | solution.py:65
  15.5 7.9 %slice-start.3 = ((s8[14680064]{0:T(1024)(128)(4,1)}), s8[2097152]{0:T(1024)(128)(4,1)S(1)}, s32[]{:S(2)}) async-start(s8[14680064]{0:T(1024)(128)(4,1)} %bitcast.1), calls=%async_computation.3 | async-start | bytes 4194304
  15.5 12.1 %slice-start.4 = ((s8[14680064]{0:T(1024)(128)(4,1)}), s8[4194304]{0:T(1024)(128)(4,1)S(1)}, s32[]{:S(2)}) async-start(s8[14680064]{0:T(1024)(128)(4,1)} %bitcast.3), calls=%async_computation.4 | async-start | bytes 8388608
  15.5 12.1 %slice-start.5 = ((s8[14680064]{0:T(1024)(128)(4,1)}), s8[4194304]{0:T(1024)(128)(4,1)S(1)}, s32[]{:S(2)}) async-start(s8[14680064]{0:T(1024)(128)(4,1)} %bitcast.3), calls=%async_computation.5 | async-start | bytes 8388608
  15.5 10.6 %collective-permute-start.1 = (bf16[64,2048]{1,0:T(8,128)(2,1)S(1)}, bf16[64,2048]{1,0:T(8,128)(2,1)S(1)}, u32[]{:S(2)}, u32[]{:S(2)}) collective-permute-start(bf16[64,2048]{1,0:T(8,128)(2,1)S(1)} %shard_map.106), channel_id=1, source_target_pairs={{0,4},{4,0},{8,12},{12,8},{1,5},{5,1},{9,13},{13,9},{2,6},{6,2},{1... | collective-permute-start | bytes 786440 | tf_op jit(solution)/shard_map/ppermute | solution.py:73
  22.8 3.3 %collective-permute-start.6 = (bf16[32,2048]{1,0:T(8,128)(2,1)S(1)}, bf16[32,2048]{1,0:T(8,128)(2,1)S(1)}, u32[]{:S(2)}, u32[]{:S(2)}) collective-permute-start(bf16[32,2048]{1,0:T(8,128)(2,1)S(1)} %get-tuple-element.31), channel_id=1, source_target_pairs={{0,1},{1,0},{2,3},{3,2},{4,5},{5,4},{6,7},{7,6},{8,9},{9,8},{10,11... | collective-permute-start | bytes 393224 | tf_op jit(solution)/shard_map/ppermute | solution.py:242
  22.9 3.2 %collective-permute-start.5 = (bf16[32,1536]{1,0:T(8,128)(2,1)S(1)}, bf16[32,1536]{1,0:T(8,128)(2,1)S(1)}, u32[]{:S(2)}, u32[]{:S(2)}) collective-permute-start(bf16[32,1536]{1,0:T(8,128)(2,1)S(1)} %get-tuple-element.30), channel_id=1, source_target_pairs={{0,1},{1,0},{2,3},{3,2},{4,5},{5,4},{6,7},{7,6},{8,9},{9,8},{10,11... | collective-permute-start | bytes 294920 | tf_op jit(solution)/shard_map/ppermute | solution.py:242
  23.4 4.2 %slice-start.6 = ((s8[14680064]{0:T(1024)(128)(4,1)}), s8[4194304]{0:T(1024)(128)(4,1)S(1)}, s32[]{:S(2)}) async-start(s8[14680064]{0:T(1024)(128)(4,1)} %bitcast.3), calls=%async_computation.6 | async-start | bytes 8388608
  23.4 4.2 %slice-start.7 = ((s8[14680064]{0:T(1024)(128)(4,1)}), s8[2097152]{0:T(1024)(128)(4,1)S(1)}, s32[]{:S(2)}) async-start(s8[14680064]{0:T(1024)(128)(4,1)} %bitcast.3), calls=%async_computation.7 | async-start | bytes 4194304
  23.4 7.7 %slice-start.8 = ((s8[14680064]{0:T(1024)(128)(4,1)}), s8[2097152]{0:T(1024)(128)(4,1)S(1)}, s32[]{:S(2)}) async-start(s8[14680064]{0:T(1024)(128)(4,1)} %bitcast.5), calls=%async_computation.8 | async-start | bytes 4194304
  23.4 7.7 %slice-start.9 = ((s8[14680064]{0:T(1024)(128)(4,1)}), s8[4194304]{0:T(1024)(128)(4,1)S(1)}, s32[]{:S(2)}) async-start(s8[14680064]{0:T(1024)(128)(4,1)} %bitcast.5), calls=%async_computation.9 | async-start | bytes 8388608
  25.5 9.7 %collective-permute-start.13 = (bf16[32,7168]{1,0:T(8,128)(2,1)S(1)}, bf16[32,7168]{1,0:T(8,128)(2,1)S(1)}, u32[]{:S(2)}, u32[]{:S(2)}) collective-permute-start(bf16[32,7168]{1,0:T(8,128)(2,1)S(1)} %get-tuple-element.45), channel_id=1, source_target_pairs={{0,1},{1,0},{2,3},{3,2},{4,5},{5,4},{6,7},{7,6},{8,9},{9,8},{10,11... | collective-permute-start | bytes 1376264 | tf_op jit(solution)/shard_map/ppermute | solution.py:242
  25.7 4.6 %collective-permute-start.8 = (bf16[32,2048]{1,0:T(8,128)(2,1)S(1)}, bf16[32,2048]{1,0:T(8,128)(2,1)S(1)}, u32[]{:S(2)}, u32[]{:S(2)}) collective-permute-start(bf16[32,2048]{1,0:T(8,128)(2,1)S(1)} %get-tuple-element.37), channel_id=1, source_target_pairs={{0,1},{1,0},{2,3},{3,2},{4,5},{5,4},{6,7},{7,6},{8,9},{9,8},{10,11... | collective-permute-start | bytes 393224 | tf_op jit(solution)/shard_map/ppermute | solution.py:242
  26.1 5.0 %slice-start.10 = ((s8[14680064]{0:T(1024)(128)(4,1)}), s8[4194304]{0:T(1024)(128)(4,1)S(1)}, s32[]{:S(2)}) async-start(s8[14680064]{0:T(1024)(128)(4,1)} %bitcast.5), calls=%async_computation.10 | async-start | bytes 8388608
  26.2 8.4 %collective-permute-start.9 = (bf16[32,3584]{1,0:T(8,128)(2,1)S(1)}, bf16[32,3584]{1,0:T(8,128)(2,1)S(1)}, u32[]{:S(2)}, u32[]{:S(2)}) collective-permute-start(bf16[32,3584]{1,0:T(8,128)(2,1)S(1)} %shard_map.111.refs_4_), channel_id=1, source_target_pairs={{0,2},{1,3},{2,0},{3,1},{4,6},{5,7},{6,4},{7,5},{8,10},{9,11},{10,... | collective-permute-start | bytes 688136 | tf_op jit(solution)/shard_map/ppermute | solution.py:242
  27.6 3.6 %slice-start.11 = ((s8[14680064]{0:T(1024)(128)(4,1)}), s8[4194304]{0:T(1024)(128)(4,1)S(1)}, s32[]{:S(2)}) async-start(s8[14680064]{0:T(1024)(128)(4,1)} %bitcast.5), calls=%async_computation.11 | async-start | bytes 8388608
  27.6 2.7 %collective-permute-start.7 = (bf16[32,1536]{1,0:T(8,128)(2,1)S(1)}, bf16[32,1536]{1,0:T(8,128)(2,1)S(1)}, u32[]{:S(2)}, u32[]{:S(2)}) collective-permute-start(bf16[32,1536]{1,0:T(8,128)(2,1)S(1)} %get-tuple-element.36), channel_id=1, source_target_pairs={{0,1},{1,0},{2,3},{3,2},{4,5},{5,4},{6,7},{7,6},{8,9},{9,8},{10,11... | collective-permute-start | bytes 294920 | tf_op jit(solution)/shard_map/ppermute | solution.py:242
  29.7 5.4 %collective-permute-start.12 = (bf16[32,3584]{1,0:T(8,128)(2,1)S(1)}, bf16[32,3584]{1,0:T(8,128)(2,1)S(1)}, u32[]{:S(2)}, u32[]{:S(2)}) collective-permute-start(bf16[32,3584]{1,0:T(8,128)(2,1)S(1)} %get-tuple-element.44), channel_id=1, source_target_pairs={{0,1},{1,0},{2,3},{3,2},{4,5},{5,4},{6,7},{7,6},{8,9},{9,8},{10,11... | collective-permute-start | bytes 688136 | tf_op jit(solution)/shard_map/ppermute | solution.py:242
  30.4 8.7 %collective-permute-start.14 = (bf16[32,3584]{1,0:T(8,128)(2,1)S(1)}, bf16[32,3584]{1,0:T(8,128)(2,1)S(1)}, u32[]{:S(2)}, u32[]{:S(2)}) collective-permute-start(bf16[32,3584]{1,0:T(8,128)(2,1)S(1)} %shard_map.113.refs_2_), channel_id=1, source_target_pairs={{0,2},{1,3},{2,0},{3,1},{4,6},{5,7},{6,4},{7,5},{8,10},{9,11},{10,... | collective-permute-start | bytes 688136 | tf_op jit(solution)/shard_map/ppermute | solution.py:242
  34.6 4.5 %collective-permute-start.11 = (bf16[32,2048]{1,0:T(8,128)(2,1)S(1)}, bf16[32,2048]{1,0:T(8,128)(2,1)S(1)}, u32[]{:S(2)}, u32[]{:S(2)}) collective-permute-start(bf16[32,2048]{1,0:T(8,128)(2,1)S(1)} %get-tuple-element.43), channel_id=1, source_target_pairs={{0,1},{1,0},{2,3},{3,2},{4,5},{5,4},{6,7},{7,6},{8,9},{9,8},{10,11... | collective-permute-start | bytes 393224 | tf_op jit(solution)/shard_map/ppermute | solution.py:242
  34.7 4.4 %collective-permute-start.10 = (bf16[32,1536]{1,0:T(8,128)(2,1)S(1)}, bf16[32,1536]{1,0:T(8,128)(2,1)S(1)}, u32[]{:S(2)}, u32[]{:S(2)}) collective-permute-start(bf16[32,1536]{1,0:T(8,128)(2,1)S(1)} %get-tuple-element.42), channel_id=1, source_target_pairs={{0,1},{1,0},{2,3},{3,2},{4,5},{5,4},{6,7},{7,6},{8,9},{9,8},{10,11... | collective-permute-start | bytes 294920 | tf_op jit(solution)/shard_map/ppermute | solution.py:242
  35.2 8.3 %collective-permute-start.15 = (bf16[32,3584]{1,0:T(8,128)(2,1)S(1)}, bf16[32,3584]{1,0:T(8,128)(2,1)S(1)}, u32[]{:S(2)}, u32[]{:S(2)}) collective-permute-start(bf16[32,3584]{1,0:T(8,128)(2,1)S(1)} %get-tuple-element.53), channel_id=1, source_target_pairs={{0,1},{1,0},{2,3},{3,2},{4,5},{5,4},{6,7},{7,6},{8,9},{9,8},{10,11... | collective-permute-start | bytes 688136 | tf_op jit(solution)/shard_map/ppermute | solution.py:242
  35.3 8.6 %collective-permute-start.16 = (bf16[32,3584]{1,0:T(8,128)(2,1)S(1)}, bf16[32,3584]{1,0:T(8,128)(2,1)S(1)}, u32[]{:S(2)}, u32[]{:S(2)}) collective-permute-start(bf16[32,3584]{1,0:T(8,128)(2,1)S(1)} %shard_map.116.refs_3_), channel_id=1, source_target_pairs={{0,2},{1,3},{2,0},{3,1},{4,6},{5,7},{6,4},{7,5},{8,10},{9,11},{10,... | collective-permute-start | bytes 688136 | tf_op jit(solution)/shard_map/ppermute | solution.py:242
  39.0 5.1 %collective-permute-start.17 = (bf16[32,3584]{1,0:T(8,128)(2,1)S(1)}, bf16[32,3584]{1,0:T(8,128)(2,1)S(1)}, u32[]{:S(2)}, u32[]{:S(2)}) collective-permute-start(bf16[32,3584]{1,0:T(8,128)(2,1)S(1)} %get-tuple-element.55), channel_id=1, source_target_pairs={{0,1},{1,0},{2,3},{3,2},{4,5},{5,4},{6,7},{7,6},{8,9},{9,8},{10,11... | collective-permute-start | bytes 688136 | tf_op jit(solution)/shard_map/ppermute | solution.py:242
  39.1 9.5 %collective-permute-start.18 = (bf16[32,3584]{1,0:T(8,128)(2,1)S(1)}, bf16[32,3584]{1,0:T(8,128)(2,1)S(1)}, u32[]{:S(2)}, u32[]{:S(2)}) collective-permute-start(bf16[32,3584]{1,0:T(8,128)(2,1)S(1)} %shard_map.117.refs_0_), channel_id=1, source_target_pairs={{0,2},{1,3},{2,0},{3,1},{4,6},{5,7},{6,4},{7,5},{8,10},{9,11},{10,... | collective-permute-start | bytes 688136 | tf_op jit(solution)/shard_map/ppermute | solution.py:242

commit v15 on v14

--- a/solution.py
+++ b/solution.py
@@ -35,24 +35,6 @@
         out_specs=[IN_VMEM] * len(arrays),
         compiler_params=pltpu.CompilerParams(vmem_limit_bytes=2 << 20),
     )(*arrays, *after)
-
-
-def stack_kernel(*refs):
-    row = 0
-    for source in refs[:-1]:
-        refs[-1][row : row + source.shape[0], :] = source[...]
-        row += source.shape[0]
-
-
-def stacked(arrays):
-    rows = sum(a.shape[0] for a in arrays)
-    return pl.pallas_call(
-        stack_kernel,
-        out_shape=jax.ShapeDtypeStruct((rows, arrays[0].shape[1]), arrays[0].dtype),
-        in_specs=[IN_VMEM] * len(arrays),
-        out_specs=IN_VMEM,
-        compiler_params=pltpu.CompilerParams(vmem_limit_bytes=2 << 20),
-    )(*arrays)
 
 
 def gather_pieces(piece, axis, size, relays_after):
@@ -66,16 +48,17 @@
     return pieces, [(i, 0) for i in range(size)]
 
 
-def gather_doubling(piece, axis, size):
-    arrays, order, spots, low = [piece], [0], {0: (0, 0)}, size // 2
-    while low:
-        send = stacked(arrays) if len(arrays) > 1 else piece
-        arrays.append(lax.ppermute(send, axis, [(i, i ^ low) for i in range(size)]))
-        for place, offset in enumerate(order):
-            spots[offset ^ low] = (len(arrays) - 1, place * piece.shape[0])
-        order += [offset ^ low for offset in order]
-        low //= 2
-    return arrays, [spots[offset] for offset in range(size)]
+def gather_chained(piece, axis, size):
+    pieces, after = [piece] + [None] * (size - 1), None
+    near = [1 << b for b in range(size.bit_length() - 1)]
+    for offset in near[::-1] + [o for o in range(size) if o & (o - 1)]:
+        low = offset & -offset
+        source = pieces[offset ^ low]
+        if after is not None and offset == low:
+            (source,) = passed([piece], (after,))
+        pieces[offset] = lax.ppermute(source, axis, [(i, i ^ low) for i in range(size)])
+        after = pieces[offset]
+    return pieces, [(i, 0) for i in range(size)]
 
 
 def halving_order(size):
@@ -345,19 +328,15 @@
 def local(mesh_shape, target_states, source_states, target_gate, target_up, source_gate, source_up, token_ids, lengths, ratio_weight):
     wide, narrow = mesh_shape["wide"], mesh_shape["narrow"]
     depth, width = target_gate.shape
-    half = depth // 2
-    gate_top = load(target_gate, 0, half)
-    gate_bottom = load(target_gate, half, depth - half, (gate_top,))
-    target_pieces, target_spots = gather_pieces(target_states, "wide", wide, gate_bottom)
-    (source_states,) = passed([source_states], (gate_top,))
-    source_pieces, source_spots = gather_doubling(source_states, "wide", wide)
-
-    gate = (gate_top, gate_bottom)
-    rows, sends, own, keeps = product(target_pieces, gate, narrow, (), spots=target_spots)
+    gate = load(target_gate, 0, depth)
+    target_pieces, target_spots = gather_pieces(target_states, "wide", wide, gate)
+    source_pieces, source_spots = gather_chained(source_states, "wide", wide)
+
+    rows, sends, own, keeps = product(target_pieces, (gate,), narrow, (), spots=target_spots)
     after = (keeps[0],)
     _, up_sends, own, up_keeps = product(rows, (in_vmem(target_up),), narrow, after, (own,))
     target_own = exchange(own, 0, narrow)
-    sent, target_g = finish(sends, keeps, (target_own, 0), narrow, (up_keeps[0], source_pieces[-1]))
+    sent, target_g = finish(sends, keeps, (target_own, 0), narrow, (up_keeps[0], *source_pieces[1:]))
     rows, gate_sends, own, gate_keeps = product(
         source_pieces, (in_vmem(source_gate),), narrow, (sent,), spots=source_spots, split=False
     )

time: 49.6 us -> 48 us (0.968)
  the two profiles are of different devices: /device:TPU:24 before, /device:TPU:0 now
where the time goes in v15:
time: 48 us; the launch traced here: 47.7 us
  Pallas kernels  17.8 us (37%)
  starting transfers between devices  16.1 us (34%)
  waiting for transfers between devices  12.8 us (27%)
  between operations  0.9 us (2%)
    pallas_call x4, Pallas kernels, product(): pl.pallas_call(functools.partial(product_kernel, len(tokens), len(matrice...  8.35 us
    ppermute x14, waiting for transfers between devices, exchange(): lax.ppermute(array, 'narrow', [(i, i ^ 1 << step) for i in range(size)])  8.06 us
    ppermute x14, starting transfers between devices, exchange(): lax.ppermute(array, 'narrow', [(i, i ^ 1 << step) for i in range(size)])  7.77 us
    ppermute x3, starting transfers between devices, gather_pieces(): lax.ppermute(source, axis, [(i, i ^ low) for i in range(size)])  5.91 us
    pallas_call x1, Pallas kernels, load(): pl.pallas_call(functools.partial(load_kernel, first), out_shape=pltpu.VME...  5.18 us
    ppermute x3, waiting for transfers between devices, gather_chained(): lax.ppermute(source, axis, [(i, i ^ low) for i in range(size)])  3.75 us
    ppermute x3, starting transfers between devices, gather_chained(): lax.ppermute(source, axis, [(i, i ^ low) for i in range(size)])  2.43 us
    pallas_call x1, Pallas kernels, look_up(): pl.pallas_call(functools.partial(look_up_kernel, ids.shape[0] // lengths....  2.16 us
  transfers between devices with their start and end apart: 20, of which 6 were waited for; matrix products, arithmetic and copies ran while one was open for 0% of the time, Pallas kernels for 36%

profile of v15, /device:TPU:0, one launch (start us, length us, event | category | flops | bytes accessed | tf_op | source)
XLA Modules:
  0.0 47.7 jit_solution(8954849898107359984)
XLA Ops:
  0.6 4.1 %collective-permute-start.4 = (bf16[32,2048]{1,0:T(8,128)(2,1)}, bf16[32,2048]{1,0:T(8,128)(2,1)S(1)}, u32[]{:S(2)}, u32[]{:S(2)}) collective-permute-start(bf16[32,2048]{1,0:T(8,128)(2,1)} %refs_0_.4), channel_id=1, source_target_pairs={{0,8},{4,12},{8,0},{12,4},{1,9},{5,13},{9,1},{13,5},{2,10},{6,14},... | collective-permute-start | bytes 393224 | tf_op jit(solution)/shard_map/ppermute | solution.py:47
  4.7 1.6 %collective-permute-start.3 = (bf16[32,2048]{1,0:T(8,128)(2,1)}, bf16[32,2048]{1,0:T(8,128)(2,1)S(1)}, u32[]{:S(2)}, u32[]{:S(2)}) collective-permute-start(bf16[32,2048]{1,0:T(8,128)(2,1)} %refs_0_.4), channel_id=1, source_target_pairs={{0,4},{4,0},{8,12},{12,8},{1,5},{5,1},{9,13},{13,9},{2,6},{6,2},{1... | collective-permute-start | bytes 393224 | tf_op jit(solution)/shard_map/ppermute | solution.py:47
  6.3 0.3 collective-permute-start
  6.6 5.2 %shard_map.105.refs_1_.refs_4_ = bf16[2048,3584]{1,0:T(8,128)(2,1)S(1)} custom-call(bf16[2048,3584]{1,0:T(8,128)(2,1)} %matrix.1), custom_call_target="tpu_custom_call" | custom-call | tf_op jit(solution)/shard_map/pallas_call | solution.py:133
  11.8 0.0 copy-start
  11.8 0.0 copy-start.1
  11.9 0.0 slice-start
  11.9 0.0 slice-start.1
  11.9 1.0 %collective-permute-done.4.refs_0_.refs_2_ = bf16[32,2048]{1,0:T(8,128)(2,1)S(1)} collective-permute-done((bf16[32,2048]{1,0:T(8,128)(2,1)}, bf16[32,2048]{1,0:T(8,128)(2,1)S(1)}, u32[]{:S(2)}, u32[]{:S(2)}) %collective-permute-start.4) | collective-permute-done | bytes 131104 | tf_op jit(solution)/shard_map/ppermute | solution.py:47
  12.9 0.0 slice-start.2
  12.9 0.2 collective-permute-start.5
  13.2 3.7 %collective-permute-done.refs_1_.refs_5_.refs_2_ = bf16[32,2048]{1,0:T(8,128)(2,1)S(1)} collective-permute-done((bf16[32,2048]{1,0:T(8,128)(2,1)}, bf16[32,2048]{1,0:T(8,128)(2,1)S(1)}, u32[]{:S(2)}, u32[]{:S(2)}) %collective-permute-start) | collective-permute-done | bytes 131104 | tf_op jit(solution)/shard_map/ppermute | solution.py:59
  16.9 0.0 slice-start.3
  16.9 0.0 slice-start.6
  16.9 0.9 %collective-permute-start.1 = (bf16[32,2048]{1,0:T(8,128)(2,1)S(1)}, bf16[32,2048]{1,0:T(8,128)(2,1)S(1)}, u32[]{:S(2)}, u32[]{:S(2)}) collective-permute-start(bf16[32,2048]{1,0:T(8,128)(2,1)S(1)} %shard_map.104), channel_id=1, source_target_pairs={{0,4},{4,0},{8,12},{12,8},{1,5},{5,1},{9,13},{13,9},{2,6},{6,2},{1... | collective-permute-start | bytes 393224 | tf_op jit(solution)/shard_map/ppermute | solution.py:59
  17.8 1.2 %collective-permute-start.2 = (bf16[32,2048]{1,0:T(8,128)(2,1)S(1)}, bf16[32,2048]{1,0:T(8,128)(2,1)S(1)}, u32[]{:S(2)}, u32[]{:S(2)}) collective-permute-start(bf16[32,2048]{1,0:T(8,128)(2,1)S(1)} %collective-permute-done.refs_1_.refs_5_.refs_2_), channel_id=1, source_target_pairs={{0,4},{4,0},{8,12},{12,8},{1,5},{5,1},{9,13},{13,9},{2,6},{6,2},{1... | collective-permute-start | bytes 393224 | tf_op jit(solution)/shard_map/ppermute | solution.py:59
  19.0 0.0 collective-permute-done.3.refs_1_
  19.0 0.0 collective-permute-done.5.refs_3_
  19.0 2.1 %shard_map.107 = (bf16[128,2048]{1,0:T(8,128)(2,1)S(1)}, bf16[32,1536]{1,0:T(8,128)(2,1)S(1)}, bf16[32,2048]{1,0:T(8,128)(2,1)S(1)}, bf16[32,3584]{1,0:T(8,128)(...) custom-call(bf16[32,2048]{1,0:T(8,128)(2,1)S(1)} %copy-done.1, ...), custom_call_target="tpu_custom_call" | custom-call | tf_op jit(solution)/shard_map/pallas_call | solution.py:204
  21.2 0.1 collective-permute-start.7
  21.2 0.5 %collective-permute-start.6 = (bf16[32,1536]{1,0:T(8,128)(2,1)S(1)}, bf16[32,1536]{1,0:T(8,128)(2,1)S(1)}, u32[]{:S(2)}, u32[]{:S(2)}) collective-permute-start(bf16[32,1536]{1,0:T(8,128)(2,1)S(1)} %get-tuple-element.30), channel_id=1, source_target_pairs={{0,1},{1,0},{2,3},{3,2},{4,5},{5,4},{6,7},{7,6},{8,9},{9,8},{10,11... | collective-permute-start | bytes 294920 | tf_op jit(solution)/shard_map/ppermute | solution.py:225
  21.7 0.0 slice-done.2
  21.8 0.0 slice-start.7
  21.8 0.0 slice-start.8
  21.8 0.0 slice-start.9
  21.8 2.1 %shard_map.108 = (bf16[32,1536]{1,0:T(8,128)(2,1)S(1)}, bf16[32,2048]{1,0:T(8,128)(2,1)S(1)}, bf16[32,3584]{1,0:T(8,128)(2,1)S(1)}, bf16[32,3584]{1,0:T(8,128)(2,1)S(1)}, bf16[32,7168]{1,0:T(8,128)(2,1)S(1)}) custom-call(bf16[128,2048]{1,0:T(8,128)(2,1)S(1)} %get-tuple-element.32.refs_0_, bf16[2048,3584]{1,0:T(8,128)(2,1)S(1)} %bitcast.2, ...), custom_call_target="tpu_custom_call" | custom-call | tf_op jit(solution)/shard_map/pallas_call | solution.py:204
  23.9 0.1 collective-permute-start.14
  24.0 0.0 collective-permute-done.1.refs_4_.refs_1_
  24.0 0.4 collective-permute-start.9
  24.4 0.0 collective-permute-done.2.refs_6_.refs_3_
  24.5 0.0 collective-permute-done.6.refs_1_
  24.5 0.0 collective-permute-done.7.refs_2_
  24.5 0.1 shard_map.109.refs_5_
  24.5 1.6 %collective-permute-start.10 = (bf16[32,3584]{1,0:T(8,128)(2,1)S(1)}, bf16[32,3584]{1,0:T(8,128)(2,1)S(1)}, u32[]{:S(2)}, u32[]{:S(2)}) collective-permute-start(bf16[32,3584]{1,0:T(8,128)(2,1)S(1)} %shard_map.109.refs_5_), channel_id=1, source_target_pairs={{0,2},{1,3},{2,0},{3,1},{4,6},{5,7},{6,4},{7,5},{8,10},{9,11},{10,... | collective-permute-start | bytes 688136 | tf_op jit(solution)/shard_map/ppermute | solution.py:225
  26.1 0.0 collective-permute-start.8
  26.2 2.1 %shard_map.110 = (bf16[128,2048]{1,0:T(8,128)(2,1)S(1)}, bf16[32,3584]{1,0:T(8,128)(2,1)S(1)}, bf16[32,3584]{1,0:T(8,128)(2,1)S(1)}, bf16[32,3584]{1,0:T(8,128)(2,1)S(1)}, bf16[32,3584]{1,0:T(8,128)(2,1)S(1)}) custom-call(bf16[32,2048]{1,0:T(8,128)(2,1)S(1)} %copy-done, bf16[32,2048]{1,0:T(8,128)(2,1)S(1)} %collective-permute-done.1.refs_4_.refs_1_, ...), custom_call_target="tpu_custom_call" | custom-call | tf_op jit(solution)/shard_map/pallas_call | solution.py:204
  28.3 0.6 %collective-permute-start.13 = (bf16[32,3584]{1,0:T(8,128)(2,1)S(1)}, bf16[32,3584]{1,0:T(8,128)(2,1)S(1)}, u32[]{:S(2)}, u32[]{:S(2)}) collective-permute-start(bf16[32,3584]{1,0:T(8,128)(2,1)S(1)} %get-tuple-element.44), channel_id=1, source_target_pairs={{0,1},{1,0},{2,3},{3,2},{4,5},{5,4},{6,7},{7,6},{8,9},{9,8},{10,11... | collective-permute-start | bytes 688136 | tf_op jit(solution)/shard_map/ppermute | solution.py:225
  28.8 0.0 collective-permute-done.8.refs_1_
  28.8 0.0 collective-permute-done.9.refs_2_
  28.8 0.1 shard_map.111.refs_2_
  28.9 0.6 %collective-permute-start.15 = (bf16[32,3584]{1,0:T(8,128)(2,1)S(1)}, bf16[32,3584]{1,0:T(8,128)(2,1)S(1)}, u32[]{:S(2)}, u32[]{:S(2)}) collective-permute-start(bf16[32,3584]{1,0:T(8,128)(2,1)S(1)} %shard_map.111.refs_2_), channel_id=1, source_target_pairs={{0,2},{1,3},{2,0},{3,1},{4,6},{5,7},{6,4},{7,5},{8,10},{9,11},{10,... | collective-permute-start | bytes 688136 | tf_op jit(solution)/shard_map/ppermute | solution.py:225
  29.5 2.1 %shard_map.112 = (bf16[32,1536]{1,0:T(8,128)(2,1)S(1)}, bf16[32,2048]{1,0:T(8,128)(2,1)S(1)}, bf16[32,3584]{1,0:T(8,128)(2,1)S(1)}, bf16[32,3584]{1,0:T(8,128)(2,1)S(1)}, bf16[32,3584]{1,0:T(8,128)(2,1)S(1)}) custom-call(bf16[128,2048]{1,0:T(8,128)(2,1)S(1)} %get-tuple-element.35.refs_0_, bf16[2048,3584]{1,0:T(8,128)(2,1)S(1)} %bitcast.6, ...), custom_call_target="tpu_custom_call" | custom-call | tf_op jit(solution)/shard_map/pallas_call | solution.py:204
  31.6 1.2 %collective-permute-done.10.refs_2_ = bf16[32,3584]{1,0:T(8,128)(2,1)S(1)} collective-permute-done((bf16[32,3584]{1,0:T(8,128)(2,1)S(1)}, bf16[32,3584]{1,0:T(8,128)(2,1)S(1)}, u32[]{:S(2)}, u32[]{:S(2)}) %collective-permute-start.10) | collective-permute-done | bytes 229408 | tf_op jit(solution)/shard_map/ppermute | solution.py:225
  32.8 0.1 collective-permute-start.12
  32.8 0.5 %collective-permute-start.11 = (bf16[32,1536]{1,0:T(8,128)(2,1)S(1)}, bf16[32,1536]{1,0:T(8,128)(2,1)S(1)}, u32[]{:S(2)}, u32[]{:S(2)}) collective-permute-start(bf16[32,1536]{1,0:T(8,128)(2,1)S(1)} %get-tuple-element.42), channel_id=1, source_target_pairs={{0,1},{1,0},{2,3},{3,2},{4,5},{5,4},{6,7},{7,6},{8,9},{9,8},{10,11... | collective-permute-start | bytes 294920 | tf_op jit(solution)/shard_map/ppermute | solution.py:225
  33.3 0.0 collective-permute-done.13.refs_1_
  33.3 0.1 collective-permute-start.16
  33.4 0.0 collective-permute-done.14.refs_3_.refs_1_.refs_4_
  33.4 0.1 shard_map.114.refs_3_
  33.5 1.9 %collective-permute-start.17 = (bf16[32,3584]{1,0:T(8,128)(2,1)S(1)}, bf16[32,3584]{1,0:T(8,128)(2,1)S(1)}, u32[]{:S(2)}, u32[]{:S(2)}) collective-permute-start(bf16[32,3584]{1,0:T(8,128)(2,1)S(1)} %shard_map.114.refs_3_), channel_id=1, source_target_pairs={{0,2},{1,3},{2,0},{3,1},{4,6},{5,7},{6,4},{7,5},{8,10},{9,11},{10,... | collective-permute-start | bytes 688136 | tf_op jit(solution)/shard_map/ppermute | solution.py:225
  35.4 2.1 %collective-permute-done.15.refs_4_.refs_5_ = bf16[32,3584]{1,0:T(8,128)(2,1)S(1)} collective-permute-done((bf16[32,3584]{1,0:T(8,128)(2,1)S(1)}, bf16[32,3584]{1,0:T(8,128)(2,1)S(1)}, u32[]{:S(2)}, u32[]{:S(2)}) %collective-permute-start.15) | collective-permute-done | bytes 229408 | tf_op jit(solution)/shard_map/ppermute | solution.py:225
  37.5 0.0 collective-permute-start.18
  37.5 0.0 collective-permute-done.11.refs_1_
  37.5 0.0 collective-permute-done.12.refs_2_
  37.5 0.1 shard_map.115.refs_0_
  37.6 1.3 %collective-permute-start.19 = (bf16[32,3584]{1,0:T(8,128)(2,1)S(1)}, bf16[32,3584]{1,0:T(8,128)(2,1)S(1)}, u32[]{:S(2)}, u32[]{:S(2)}) collective-permute-start(bf16[32,3584]{1,0:T(8,128)(2,1)S(1)} %shard_map.115.refs_0_), channel_id=1, source_target_pairs={{0,2},{1,3},{2,0},{3,1},{4,6},{5,7},{6,4},{7,5},{8,10},{9,11},{10,... | collective-permute-start | bytes 688136 | tf_op jit(solution)/shard_map/ppermute | solution.py:225
  38.9 2.2 %shard_map.116 = (f32[32,128]{1,0:T(8,128)S(1)}, f32[32,128]{1,0:T(8,128)S(1)}) custom-call(s32[32]{0:T(128)} %ids.1, s32[2]{0:T(128)} %lengths.1, f32[1002,128]{1,0:T(8,128)} %bitcast.7, bf16[32,3584]{1,0:T(8,128)(2,1)S(1)} %shard_map.115.refs_0_), custom_call_target="tpu_custom_call" | custom-call | tf_op jit(solution)/shard_map/pallas_call | solution.py:110
  41.1 0.9 %shard_map.117 = (f32[32,3584]{1,0:T(8,128)S(1)}, bf16[32,3584]{1,0:T(8,128)(2,1)}) custom-call(f32[32,128]{1,0:T(8,128)S(1)} %get-tuple-element.46.live, bf16[32,3584]{1,0:T(8,128)(2,1)S(1)} %get-tuple-element.47.refs_0_, bf16[32,7168]{1,0:T(8,128)(2,1)S(1)} %collective-permute-done.14.refs_3_.refs_1_.refs_4_, ...), custom_call_target="tpu_custom_call" | custom-call | tf_op jit(solution)/shard_map/pallas_call | solution.py:283
  42.0 0.0 collective-permute-done.16.refs_1_
  42.0 0.4 collective-permute-done.17.refs_2_
  42.4 0.1 shard_map.118.gated
  42.5 0.0 collective-permute-done.18.refs_1_
  42.6 4.4 %collective-permute-done.19.refs_2_ = bf16[32,3584]{1,0:T(8,128)(2,1)S(1)} collective-permute-done((bf16[32,3584]{1,0:T(8,128)(2,1)S(1)}, bf16[32,3584]{1,0:T(8,128)(2,1)S(1)}, u32[]{:S(2)}, u32[]{:S(2)}) %collective-permute-start.19) | collective-permute-done | bytes 229408 | tf_op jit(solution)/shard_map/ppermute | solution.py:225
  46.9 0.8 %shard_map.119 = bf16[32,3584]{1,0:T(8,128)(2,1)} custom-call(f32[32,3584]{1,0:T(8,128)S(1)} %get-tuple-element.50.act, f32[32,3584]{1,0:T(8,128)S(1)} %shard_map.118.gated, bf16[32,3584]{1,0:T(8,128)(2,1)S(1)} %get-tuple-element.54.refs_0_, bf16[32,3584]{1,0:T(8,128)(2,1)S(1)} %collective-permute-done.18.refs_1_, ...), custom_call_target="tpu_custom_call" | custom-call | tf_op jit(solution)/shard_map/pallas_call | solution.py:319
  (23 shorter events, 0.1 us)
Async XLA Ops:
  0.6 12.3 %collective-permute-start.4 = (bf16[32,2048]{1,0:T(8,128)(2,1)}, bf16[32,2048]{1,0:T(8,128)(2,1)S(1)}, u32[]{:S(2)}, u32[]{:S(2)}) collective-permute-start(bf16[32,2048]{1,0:T(8,128)(2,1)} %refs_0_.4), channel_id=1, source_target_pairs={{0,8},{4,12},{8,0},{12,4},{1,9},{5,13},{9,1},{13,5},{2,10},{6,14},... | collective-permute-start | bytes 393224 | tf_op jit(solution)/shard_map/ppermute | solution.py:47
  4.7 14.3 %collective-permute-start.3 = (bf16[32,2048]{1,0:T(8,128)(2,1)}, bf16[32,2048]{1,0:T(8,128)(2,1)S(1)}, u32[]{:S(2)}, u32[]{:S(2)}) collective-permute-start(bf16[32,2048]{1,0:T(8,128)(2,1)} %refs_0_.4), channel_id=1, source_target_pairs={{0,4},{4,0},{8,12},{12,8},{1,5},{5,1},{9,13},{13,9},{2,6},{6,2},{1... | collective-permute-start | bytes 393224 | tf_op jit(solution)/shard_map/ppermute | solution.py:47
  6.3 10.6 %collective-permute-start = (bf16[32,2048]{1,0:T(8,128)(2,1)}, bf16[32,2048]{1,0:T(8,128)(2,1)S(1)}, u32[]{:S(2)}, u32[]{:S(2)}) collective-permute-start(bf16[32,2048]{1,0:T(8,128)(2,1)} %refs_0_.5), channel_id=1, source_target_pairs={{0,8},{4,12},{8,0},{12,4},{1,9},{5,13},{9,1},{13,5},{2,10},{6,14},... | collective-permute-start | bytes 393224 | tf_op jit(solution)/shard_map/ppermute | solution.py:59
  11.8 5.1 %copy-start = (bf16[32,2048]{1,0:T(8,128)(2,1)S(1)}, bf16[32,2048]{1,0:T(8,128)(2,1)}, u32[]{:S(2)}) copy-start(bf16[32,2048]{1,0:T(8,128)(2,1)} %refs_0_.5) | copy-start | bytes 393220
  11.8 7.2 %copy-start.1 = (bf16[32,2048]{1,0:T(8,128)(2,1)S(1)}, bf16[32,2048]{1,0:T(8,128)(2,1)}, u32[]{:S(2)}) copy-start(bf16[32,2048]{1,0:T(8,128)(2,1)} %refs_0_.4) | copy-start | bytes 393220
  11.9 9.9 %slice-start = ((s8[14680064]{0:T(1024)(128)(4,1)}), s8[4194304]{0:T(1024)(128)(4,1)S(1)}, s32[]{:S(2)}) async-start(s8[14680064]{0:T(1024)(128)(4,1)} %bitcast.1), calls=%async_computation | async-start | bytes 8388608
  11.9 9.9 %slice-start.1 = ((s8[14680064]{0:T(1024)(128)(4,1)}), s8[4194304]{0:T(1024)(128)(4,1)S(1)}, s32[]{:S(2)}) async-start(s8[14680064]{0:T(1024)(128)(4,1)} %bitcast.1), calls=%async_computation.1 | async-start | bytes 8388608
  12.9 13.2 %slice-start.4 = ((s8[14680064]{0:T(1024)(128)(4,1)}), s8[4194304]{0:T(1024)(128)(4,1)S(1)}, s32[]{:S(2)}) async-start(s8[14680064]{0:T(1024)(128)(4,1)} %bitcast.3), calls=%async_computation.4 | async-start | bytes 8388608
  12.9 13.2 %slice-start.5 = ((s8[14680064]{0:T(1024)(128)(4,1)}), s8[4194304]{0:T(1024)(128)(4,1)S(1)}, s32[]{:S(2)}) async-start(s8[14680064]{0:T(1024)(128)(4,1)} %bitcast.3), calls=%async_computation.5 | async-start | bytes 8388608
  12.9 8.8 %slice-start.2 = ((s8[14680064]{0:T(1024)(128)(4,1)}), s8[4194304]{0:T(1024)(128)(4,1)S(1)}, s32[]{:S(2)}) async-start(s8[14680064]{0:T(1024)(128)(4,1)} %bitcast.1), calls=%async_computation.2 | async-start | bytes 8388608
  12.9 6.1 %collective-permute-start.5 = (bf16[32,2048]{1,0:T(8,128)(2,1)S(1)}, bf16[32,2048]{1,0:T(8,128)(2,1)S(1)}, u32[]{:S(2)}, u32[]{:S(2)}) collective-permute-start(bf16[32,2048]{1,0:T(8,128)(2,1)S(1)} %shard_map.106), channel_id=1, source_target_pairs={{0,4},{4,0},{8,12},{12,8},{1,5},{5,1},{9,13},{13,9},{2,6},{6,2},{1... | collective-permute-start | bytes 393224 | tf_op jit(solution)/shard_map/ppermute | solution.py:47
  16.9 4.8 %slice-start.3 = ((s8[14680064]{0:T(1024)(128)(4,1)}), s8[2097152]{0:T(1024)(128)(4,1)S(1)}, s32[]{:S(2)}) async-start(s8[14680064]{0:T(1024)(128)(4,1)} %bitcast.1), calls=%async_computation.3 | async-start | bytes 4194304
  16.9 9.2 %slice-start.6 = ((s8[14680064]{0:T(1024)(128)(4,1)}), s8[4194304]{0:T(1024)(128)(4,1)S(1)}, s32[]{:S(2)}) async-start(s8[14680064]{0:T(1024)(128)(4,1)} %bitcast.3), calls=%async_computation.6 | async-start | bytes 8388608
  16.9 7.1 %collective-permute-start.1 = (bf16[32,2048]{1,0:T(8,128)(2,1)S(1)}, bf16[32,2048]{1,0:T(8,128)(2,1)S(1)}, u32[]{:S(2)}, u32[]{:S(2)}) collective-permute-start(bf16[32,2048]{1,0:T(8,128)(2,1)S(1)} %shard_map.104), channel_id=1, source_target_pairs={{0,4},{4,0},{8,12},{12,8},{1,5},{5,1},{9,13},{13,9},{2,6},{6,2},{1... | collective-permute-start | bytes 393224 | tf_op jit(solution)/shard_map/ppermute | solution.py:59
  17.8 6.6 %collective-permute-start.2 = (bf16[32,2048]{1,0:T(8,128)(2,1)S(1)}, bf16[32,2048]{1,0:T(8,128)(2,1)S(1)}, u32[]{:S(2)}, u32[]{:S(2)}) collective-permute-start(bf16[32,2048]{1,0:T(8,128)(2,1)S(1)} %collective-permute-done.refs_1_.refs_5_.refs_2_), channel_id=1, source_target_pairs={{0,4},{4,0},{8,12},{12,8},{1,5},{5,1},{9,13},{13,9},{2,6},{6,2},{1... | collective-permute-start | bytes 393224 | tf_op jit(solution)/shard_map/ppermute | solution.py:59
  21.2 3.3 %collective-permute-start.7 = (bf16[32,2048]{1,0:T(8,128)(2,1)S(1)}, bf16[32,2048]{1,0:T(8,128)(2,1)S(1)}, u32[]{:S(2)}, u32[]{:S(2)}) collective-permute-start(bf16[32,2048]{1,0:T(8,128)(2,1)S(1)} %get-tuple-element.31), channel_id=1, source_target_pairs={{0,1},{1,0},{2,3},{3,2},{4,5},{5,4},{6,7},{7,6},{8,9},{9,8},{10,11... | collective-permute-start | bytes 393224 | tf_op jit(solution)/shard_map/ppermute | solution.py:225
  21.2 3.2 %collective-permute-start.6 = (bf16[32,1536]{1,0:T(8,128)(2,1)S(1)}, bf16[32,1536]{1,0:T(8,128)(2,1)S(1)}, u32[]{:S(2)}, u32[]{:S(2)}) collective-permute-start(bf16[32,1536]{1,0:T(8,128)(2,1)S(1)} %get-tuple-element.30), channel_id=1, source_target_pairs={{0,1},{1,0},{2,3},{3,2},{4,5},{5,4},{6,7},{7,6},{8,9},{9,8},{10,11... | collective-permute-start | bytes 294920 | tf_op jit(solution)/shard_map/ppermute | solution.py:225
  21.8 4.4 %slice-start.7 = ((s8[14680064]{0:T(1024)(128)(4,1)}), s8[2097152]{0:T(1024)(128)(4,1)S(1)}, s32[]{:S(2)}) async-start(s8[14680064]{0:T(1024)(128)(4,1)} %bitcast.3), calls=%async_computation.7 | async-start | bytes 4194304
  21.8 7.7 %slice-start.8 = ((s8[14680064]{0:T(1024)(128)(4,1)}), s8[2097152]{0:T(1024)(128)(4,1)S(1)}, s32[]{:S(2)}) async-start(s8[14680064]{0:T(1024)(128)(4,1)} %bitcast.5), calls=%async_computation.8 | async-start | bytes 4194304
  21.8 7.7 %slice-start.9 = ((s8[14680064]{0:T(1024)(128)(4,1)}), s8[4194304]{0:T(1024)(128)(4,1)S(1)}, s32[]{:S(2)}) async-start(s8[14680064]{0:T(1024)(128)(4,1)} %bitcast.5), calls=%async_computation.9 | async-start | bytes 8388608
  23.9 9.5 %collective-permute-start.14 = (bf16[32,7168]{1,0:T(8,128)(2,1)S(1)}, bf16[32,7168]{1,0:T(8,128)(2,1)S(1)}, u32[]{:S(2)}, u32[]{:S(2)}) collective-permute-start(bf16[32,7168]{1,0:T(8,128)(2,1)S(1)} %get-tuple-element.45), channel_id=1, source_target_pairs={{0,1},{1,0},{2,3},{3,2},{4,5},{5,4},{6,7},{7,6},{8,9},{9,8},{10,11... | collective-permute-start | bytes 1376264 | tf_op jit(solution)/shard_map/ppermute | solution.py:225
  24.0 4.8 %collective-permute-start.9 = (bf16[32,2048]{1,0:T(8,128)(2,1)S(1)}, bf16[32,2048]{1,0:T(8,128)(2,1)S(1)}, u32[]{:S(2)}, u32[]{:S(2)}) collective-permute-start(bf16[32,2048]{1,0:T(8,128)(2,1)S(1)} %get-tuple-element.37), channel_id=1, source_target_pairs={{0,1},{1,0},{2,3},{3,2},{4,5},{5,4},{6,7},{7,6},{8,9},{9,8},{10,11... | collective-permute-start | bytes 393224 | tf_op jit(solution)/shard_map/ppermute | solution.py:225
  24.5 5.0 %slice-start.10 = ((s8[14680064]{0:T(1024)(128)(4,1)}), s8[4194304]{0:T(1024)(128)(4,1)S(1)}, s32[]{:S(2)}) async-start(s8[14680064]{0:T(1024)(128)(4,1)} %bitcast.5), calls=%async_computation.10 | async-start | bytes 8388608
  24.5 8.2 %collective-permute-start.10 = (bf16[32,3584]{1,0:T(8,128)(2,1)S(1)}, bf16[32,3584]{1,0:T(8,128)(2,1)S(1)}, u32[]{:S(2)}, u32[]{:S(2)}) collective-permute-start(bf16[32,3584]{1,0:T(8,128)(2,1)S(1)} %shard_map.109.refs_5_), channel_id=1, source_target_pairs={{0,2},{1,3},{2,0},{3,1},{4,6},{5,7},{6,4},{7,5},{8,10},{9,11},{10,... | collective-permute-start | bytes 688136 | tf_op jit(solution)/shard_map/ppermute | solution.py:225
  26.1 3.4 %slice-start.11 = ((s8[14680064]{0:T(1024)(128)(4,1)}), s8[4194304]{0:T(1024)(128)(4,1)S(1)}, s32[]{:S(2)}) async-start(s8[14680064]{0:T(1024)(128)(4,1)} %bitcast.5), calls=%async_computation.11 | async-start | bytes 8388608
  26.1 2.7 %collective-permute-start.8 = (bf16[32,1536]{1,0:T(8,128)(2,1)S(1)}, bf16[32,1536]{1,0:T(8,128)(2,1)S(1)}, u32[]{:S(2)}, u32[]{:S(2)}) collective-permute-start(bf16[32,1536]{1,0:T(8,128)(2,1)S(1)} %get-tuple-element.36), channel_id=1, source_target_pairs={{0,1},{1,0},{2,3},{3,2},{4,5},{5,4},{6,7},{7,6},{8,9},{9,8},{10,11... | collective-permute-start | bytes 294920 | tf_op jit(solution)/shard_map/ppermute | solution.py:225
  28.3 5.1 %collective-permute-start.13 = (bf16[32,3584]{1,0:T(8,128)(2,1)S(1)}, bf16[32,3584]{1,0:T(8,128)(2,1)S(1)}, u32[]{:S(2)}, u32[]{:S(2)}) collective-permute-start(bf16[32,3584]{1,0:T(8,128)(2,1)S(1)} %get-tuple-element.44), channel_id=1, source_target_pairs={{0,1},{1,0},{2,3},{3,2},{4,5},{5,4},{6,7},{7,6},{8,9},{9,8},{10,11... | collective-permute-start | bytes 688136 | tf_op jit(solution)/shard_map/ppermute | solution.py:225
  28.9 8.6 %collective-permute-start.15 = (bf16[32,3584]{1,0:T(8,128)(2,1)S(1)}, bf16[32,3584]{1,0:T(8,128)(2,1)S(1)}, u32[]{:S(2)}, u32[]{:S(2)}) collective-permute-start(bf16[32,3584]{1,0:T(8,128)(2,1)S(1)} %shard_map.111.refs_2_), channel_id=1, source_target_pairs={{0,2},{1,3},{2,0},{3,1},{4,6},{5,7},{6,4},{7,5},{8,10},{9,11},{10,... | collective-permute-start | bytes 688136 | tf_op jit(solution)/shard_map/ppermute | solution.py:225
  32.8 4.7 %collective-permute-start.12 = (bf16[32,2048]{1,0:T(8,128)(2,1)S(1)}, bf16[32,2048]{1,0:T(8,128)(2,1)S(1)}, u32[]{:S(2)}, u32[]{:S(2)}) collective-permute-start(bf16[32,2048]{1,0:T(8,128)(2,1)S(1)} %get-tuple-element.43), channel_id=1, source_target_pairs={{0,1},{1,0},{2,3},{3,2},{4,5},{5,4},{6,7},{7,6},{8,9},{9,8},{10,11... | collective-permute-start | bytes 393224 | tf_op jit(solution)/shard_map/ppermute | solution.py:225
  32.8 4.7 %collective-permute-start.11 = (bf16[32,1536]{1,0:T(8,128)(2,1)S(1)}, bf16[32,1536]{1,0:T(8,128)(2,1)S(1)}, u32[]{:S(2)}, u32[]{:S(2)}) collective-permute-start(bf16[32,1536]{1,0:T(8,128)(2,1)S(1)} %get-tuple-element.42), channel_id=1, source_target_pairs={{0,1},{1,0},{2,3},{3,2},{4,5},{5,4},{6,7},{7,6},{8,9},{9,8},{10,11... | collective-permute-start | bytes 294920 | tf_op jit(solution)/shard_map/ppermute | solution.py:225
  33.3 8.7 %collective-permute-start.16 = (bf16[32,3584]{1,0:T(8,128)(2,1)S(1)}, bf16[32,3584]{1,0:T(8,128)(2,1)S(1)}, u32[]{:S(2)}, u32[]{:S(2)}) collective-permute-start(bf16[32,3584]{1,0:T(8,128)(2,1)S(1)} %get-tuple-element.53), channel_id=1, source_target_pairs={{0,1},{1,0},{2,3},{3,2},{4,5},{5,4},{6,7},{7,6},{8,9},{9,8},{10,11... | collective-permute-start | bytes 688136 | tf_op jit(solution)/shard_map/ppermute | solution.py:225
  33.5 8.9 %collective-permute-start.17 = (bf16[32,3584]{1,0:T(8,128)(2,1)S(1)}, bf16[32,3584]{1,0:T(8,128)(2,1)S(1)}, u32[]{:S(2)}, u32[]{:S(2)}) collective-permute-start(bf16[32,3584]{1,0:T(8,128)(2,1)S(1)} %shard_map.114.refs_3_), channel_id=1, source_target_pairs={{0,2},{1,3},{2,0},{3,1},{4,6},{5,7},{6,4},{7,5},{8,10},{9,11},{10,... | collective-permute-start | bytes 688136 | tf_op jit(solution)/shard_map/ppermute | solution.py:225
  37.5 5.1 %collective-permute-start.18 = (bf16[32,3584]{1,0:T(8,128)(2,1)S(1)}, bf16[32,3584]{1,0:T(8,128)(2,1)S(1)}, u32[]{:S(2)}, u32[]{:S(2)}) collective-permute-start(bf16[32,3584]{1,0:T(8,128)(2,1)S(1)} %get-tuple-element.55), channel_id=1, source_target_pairs={{0,1},{1,0},{2,3},{3,2},{4,5},{5,4},{6,7},{7,6},{8,9},{9,8},{10,11... | collective-permute-start | bytes 688136 | tf_op jit(solution)/shard_map/ppermute | solution.py:225
  37.6 9.4 %collective-permute-start.19 = (bf16[32,3584]{1,0:T(8,128)(2,1)S(1)}, bf16[32,3584]{1,0:T(8,128)(2,1)S(1)}, u32[]{:S(2)}, u32[]{:S(2)}) collective-permute-start(bf16[32,3584]{1,0:T(8,128)(2,1)S(1)} %shard_map.115.refs_0_), channel_id=1, source_target_pairs={{0,2},{1,3},{2,0},{3,1},{4,6},{5,7},{6,4},{7,5},{8,10},{9,11},{10,... | collective-permute-start | bytes 688136 | tf_op jit(solution)/shard_map/ppermute | solution.py:225

commit v16 on v14

--- a/solution.py
+++ b/solution.py
@@ -56,13 +56,14 @@
 
 
 def gather_pieces(piece, axis, size, relays_after):
-    pieces = [piece]
-    for offset in range(1, size):
+    pieces = [piece] + [None] * (size - 1)
+    near = [1 << b for b in range(size.bit_length() - 1)]
+    for offset in near[::-1] + [o for o in range(size) if o & (o - 1)]:
         low = offset & -offset
         source = pieces[offset ^ low]
         if offset != low:
-            (source,) = passed([source], (relays_after,))
-        pieces.append(lax.ppermute(source, axis, [(i, i ^ low) for i in range(size)]))
+            (source,) = passed([source], (relays_after, pieces[low]))
+        pieces[offset] = lax.ppermute(source, axis, [(i, i ^ low) for i in range(size)])
     return pieces, [(i, 0) for i in range(size)]
 
 
@@ -345,15 +346,11 @@
 def local(mesh_shape, target_states, source_states, target_gate, target_up, source_gate, source_up, token_ids, lengths, ratio_weight):
     wide, narrow = mesh_shape["wide"], mesh_shape["narrow"]
     depth, width = target_gate.shape
-    half = depth // 2
-    gate_top = load(target_gate, 0, half)
-    gate_bottom = load(target_gate, half, depth - half, (gate_top,))
-    target_pieces, target_spots = gather_pieces(target_states, "wide", wide, gate_bottom)
-    (source_states,) = passed([source_states], (gate_top,))
+    gate = load(target_gate, 0, depth)
+    target_pieces, target_spots = gather_pieces(target_states, "wide", wide, gate)
     source_pieces, source_spots = gather_doubling(source_states, "wide", wide)
 
-    gate = (gate_top, gate_bottom)
-    rows, sends, own, keeps = product(target_pieces, gate, narrow, (), spots=target_spots)
+    rows, sends, own, keeps = product(target_pieces, (gate,), narrow, (), spots=target_spots)
     after = (keeps[0],)
     _, up_sends, own, up_keeps = product(rows, (in_vmem(target_up),), narrow, after, (own,))
     target_own = exchange(own, 0, narrow)

time: 49.6 us -> 51.8 us (1.044)
  the two profiles are of different devices: /device:TPU:24 before, /device:TPU:0 now
where the time goes in v16:
time: 51.8 us; the launch traced here: 51.6 us
  waiting for transfers between devices  18.7 us (36%)
  Pallas kernels  17.8 us (34%)
  starting transfers between devices  14.1 us (27%)
  between operations  0.92 us (2%)
    ppermute x3, waiting for transfers between devices, gather_pieces(): lax.ppermute(source, axis, [(i, i ^ low) for i in range(size)])  8.78 us
    pallas_call x4, Pallas kernels, product(): pl.pallas_call(functools.partial(product_kernel, len(tokens), len(matrice...  8.36 us
    ppermute x14, waiting for transfers between devices, exchange(): lax.ppermute(array, 'narrow', [(i, i ^ 1 << step) for i in range(size)])  8.17 us
    ppermute x14, starting transfers between devices, exchange(): lax.ppermute(array, 'narrow', [(i, i ^ 1 << step) for i in range(size)])  7.66 us
    ppermute x3, starting transfers between devices, gather_pieces(): lax.ppermute(source, axis, [(i, i ^ low) for i in range(size)])  5.75 us
    pallas_call x1, Pallas kernels, load(): pl.pallas_call(functools.partial(load_kernel, first), out_shape=pltpu.VME...  5.18 us
    pallas_call x1, Pallas kernels, look_up(): pl.pallas_call(functools.partial(look_up_kernel, ids.shape[0] // lengths....  2.16 us
    ppermute x2, waiting for transfers between devices, gather_doubling(): arrays.append(lax.ppermute(send, axis, [(i, i ^ low) for i in range(size)]))  1.71 us
  transfers between devices with their start and end apart: 19, of which 7 were waited for; matrix products, arithmetic and copies ran while one was open for 0% of the time, Pallas kernels for 33%

profile of v16, /device:TPU:0, one launch (start us, length us, event | category | flops | bytes accessed | tf_op | source)
XLA Modules:
  0.0 51.6 jit_solution(8199819996897635453)
XLA Ops:
  0.6 3.1 %collective-permute-start.2 = (bf16[32,2048]{1,0:T(8,128)(2,1)}, bf16[32,2048]{1,0:T(8,128)(2,1)S(1)}, u32[]{:S(2)}, u32[]{:S(2)}) collective-permute-start(bf16[32,2048]{1,0:T(8,128)(2,1)} %refs_0_.4), channel_id=1, source_target_pairs={{0,4},{4,0},{8,12},{12,8},{1,5},{5,1},{9,13},{13,9},{2,6},{6,2},{1... | collective-permute-start | bytes 393224 | tf_op jit(solution)/shard_map/ppermute | solution.py:66
  3.7 2.6 %collective-permute-start.3 = (bf16[32,2048]{1,0:T(8,128)(2,1)}, bf16[32,2048]{1,0:T(8,128)(2,1)S(1)}, u32[]{:S(2)}, u32[]{:S(2)}) collective-permute-start(bf16[32,2048]{1,0:T(8,128)(2,1)} %refs_0_.4), channel_id=1, source_target_pairs={{0,8},{4,12},{8,0},{12,4},{1,9},{5,13},{9,1},{13,5},{2,10},{6,14},... | collective-permute-start | bytes 393224 | tf_op jit(solution)/shard_map/ppermute | solution.py:66
  6.3 0.3 collective-permute-start
  6.6 5.2 %shard_map.105.refs_1_.refs_4_ = bf16[2048,3584]{1,0:T(8,128)(2,1)S(1)} custom-call(bf16[2048,3584]{1,0:T(8,128)(2,1)} %matrix.1), custom_call_target="tpu_custom_call" | custom-call | tf_op jit(solution)/shard_map/pallas_call | solution.py:151
  11.8 0.0 copy-start
  11.8 0.0 copy-start.1
  11.9 0.0 slice-start
  11.9 0.0 slice-start.1
  11.9 0.0 collective-permute-done.2.refs_2_.refs_1_
  11.9 4.6 %collective-permute-done.3.refs_0_.refs_2_ = bf16[32,2048]{1,0:T(8,128)(2,1)S(1)} collective-permute-done((bf16[32,2048]{1,0:T(8,128)(2,1)}, bf16[32,2048]{1,0:T(8,128)(2,1)S(1)}, u32[]{:S(2)}, u32[]{:S(2)}) %collective-permute-start.3) | collective-permute-done | bytes 131104 | tf_op jit(solution)/shard_map/ppermute | solution.py:66
  16.5 0.0 slice-start.2
  16.5 0.1 collective-permute-start.4
  16.6 1.7 %collective-permute-done.refs_1_ = bf16[32,2048]{1,0:T(8,128)(2,1)S(1)} collective-permute-done((bf16[32,2048]{1,0:T(8,128)(2,1)}, bf16[32,2048]{1,0:T(8,128)(2,1)S(1)}, u32[]{:S(2)}, u32[]{:S(2)}) %collective-permute-start) | collective-permute-done | bytes 131104 | tf_op jit(solution)/shard_map/ppermute | solution.py:74
  18.3 0.0 slice-start.3
  18.3 0.0 slice-start.6
  18.3 0.4 collective-permute-start.1
  18.7 4.2 %collective-permute-done.4.refs_3_ = bf16[32,2048]{1,0:T(8,128)(2,1)S(1)} collective-permute-done((bf16[32,2048]{1,0:T(8,128)(2,1)S(1)}, bf16[32,2048]{1,0:T(8,128)(2,1)S(1)}, u32[]{:S(2)}, u32[]{:S(2)}) %collective-permute-start.4) | collective-permute-done | bytes 131104 | tf_op jit(solution)/shard_map/ppermute | solution.py:66
  22.9 2.1 %shard_map.107 = (bf16[128,2048]{1,0:T(8,128)(2,1)S(1)}, bf16[32,1536]{1,0:T(8,128)(2,1)S(1)}, bf16[32,2048]{1,0:T(8,128)(2,1)S(1)}, bf16[32,3584]{1,0:T(8,128)(...) custom-call(bf16[32,2048]{1,0:T(8,128)(2,1)S(1)} %copy-done.1, ...), custom_call_target="tpu_custom_call" | custom-call | tf_op jit(solution)/shard_map/pallas_call | solution.py:222
  25.0 0.1 collective-permute-start.6
  25.1 0.5 collective-permute-start.5
  25.6 0.0 slice-done.3
  25.6 0.0 slice-start.7
  25.6 0.0 slice-start.8
  25.7 0.0 slice-start.9
  25.7 2.1 %shard_map.108 = (bf16[32,1536]{1,0:T(8,128)(2,1)S(1)}, bf16[32,2048]{1,0:T(8,128)(2,1)S(1)}, bf16[32,3584]{1,0:T(8,128)(2,1)S(1)}, bf16[32,3584]{1,0:T(8,128)(2,1)S(1)}, bf16[32,7168]{1,0:T(8,128)(2,1)S(1)}) custom-call(bf16[128,2048]{1,0:T(8,128)(2,1)S(1)} %get-tuple-element.32.refs_0_, bf16[2048,3584]{1,0:T(8,128)(2,1)S(1)} %bitcast.2, ...), custom_call_target="tpu_custom_call" | custom-call | tf_op jit(solution)/shard_map/pallas_call | solution.py:222
  27.7 0.1 collective-permute-start.13
  27.9 0.4 collective-permute-start.8
  28.3 0.0 collective-permute-done.5.refs_1_
  28.3 0.0 collective-permute-done.6.refs_2_
  28.3 0.0 collective-permute-done.1.refs_4_.refs_2_
  28.3 0.0 slice-start.10
  28.3 0.1 shard_map.109.refs_4_
  28.4 1.6 %collective-permute-start.9 = (bf16[32,3584]{1,0:T(8,128)(2,1)S(1)}, bf16[32,3584]{1,0:T(8,128)(2,1)S(1)}, u32[]{:S(2)}, u32[]{:S(2)}) collective-permute-start(bf16[32,3584]{1,0:T(8,128)(2,1)S(1)} %shard_map.109.refs_4_), channel_id=1, source_target_pairs={{0,2},{1,3},{2,0},{3,1},{4,6},{5,7},{6,4},{7,5},{8,10},{9,11},{10,... | collective-permute-start | bytes 688136 | tf_op jit(solution)/shard_map/ppermute | solution.py:243
  30.0 0.0 collective-permute-start.7
  30.0 2.1 %shard_map.110 = (bf16[128,2048]{1,0:T(8,128)(2,1)S(1)}, bf16[32,3584]{1,0:T(8,128)(2,1)S(1)}, bf16[32,3584]{1,0:T(8,128)(2,1)S(1)}, bf16[32,3584]{1,0:T(8,128)(2,1)S(1)}, bf16[32,3584]{1,0:T(8,128)(2,1)S(1)}) custom-call(bf16[32,2048]{1,0:T(8,128)(2,1)S(1)} %copy-done, bf16[32,2048]{1,0:T(8,128)(2,1)S(1)} %collective-permute-done.refs_1_, ...), custom_call_target="tpu_custom_call" | custom-call | tf_op jit(solution)/shard_map/pallas_call | solution.py:222
  32.1 0.6 %collective-permute-start.12 = (bf16[32,3584]{1,0:T(8,128)(2,1)S(1)}, bf16[32,3584]{1,0:T(8,128)(2,1)S(1)}, u32[]{:S(2)}, u32[]{:S(2)}) collective-permute-start(bf16[32,3584]{1,0:T(8,128)(2,1)S(1)} %get-tuple-element.44), channel_id=1, source_target_pairs={{0,1},{1,0},{2,3},{3,2},{4,5},{5,4},{6,7},{7,6},{8,9},{9,8},{10,11... | collective-permute-start | bytes 688136 | tf_op jit(solution)/shard_map/ppermute | solution.py:243
  32.7 0.0 collective-permute-done.7.refs_1_
  32.7 0.0 collective-permute-done.8.refs_2_
  32.7 0.1 shard_map.111.refs_2_
  32.7 0.6 %collective-permute-start.14 = (bf16[32,3584]{1,0:T(8,128)(2,1)S(1)}, bf16[32,3584]{1,0:T(8,128)(2,1)S(1)}, u32[]{:S(2)}, u32[]{:S(2)}) collective-permute-start(bf16[32,3584]{1,0:T(8,128)(2,1)S(1)} %shard_map.111.refs_2_), channel_id=1, source_target_pairs={{0,2},{1,3},{2,0},{3,1},{4,6},{5,7},{6,4},{7,5},{8,10},{9,11},{10,... | collective-permute-start | bytes 688136 | tf_op jit(solution)/shard_map/ppermute | solution.py:243
  33.3 0.0 slice-done.8
  33.4 2.1 %shard_map.112 = (bf16[32,1536]{1,0:T(8,128)(2,1)S(1)}, bf16[32,2048]{1,0:T(8,128)(2,1)S(1)}, bf16[32,3584]{1,0:T(8,128)(2,1)S(1)}, bf16[32,3584]{1,0:T(8,128)(2,1)S(1)}, bf16[32,3584]{1,0:T(8,128)(2,1)S(1)}) custom-call(bf16[128,2048]{1,0:T(8,128)(2,1)S(1)} %get-tuple-element.35.refs_0_, bf16[2048,3584]{1,0:T(8,128)(2,1)S(1)} %bitcast.6, ...), custom_call_target="tpu_custom_call" | custom-call | tf_op jit(solution)/shard_map/pallas_call | solution.py:222
  35.4 1.2 %collective-permute-done.9.refs_2_ = bf16[32,3584]{1,0:T(8,128)(2,1)S(1)} collective-permute-done((bf16[32,3584]{1,0:T(8,128)(2,1)S(1)}, bf16[32,3584]{1,0:T(8,128)(2,1)S(1)}, u32[]{:S(2)}, u32[]{:S(2)}) %collective-permute-start.9) | collective-permute-done | bytes 229408 | tf_op jit(solution)/shard_map/ppermute | solution.py:243
  36.7 0.1 collective-permute-start.11
  36.7 0.5 collective-permute-start.10
  37.2 0.0 collective-permute-done.12.refs_1_
  37.2 0.1 collective-permute-start.15
  37.3 0.0 collective-permute-done.13.refs_3_.refs_1_.refs_4_
  37.3 0.1 shard_map.114.refs_3_
  37.4 1.9 %collective-permute-start.16 = (bf16[32,3584]{1,0:T(8,128)(2,1)S(1)}, bf16[32,3584]{1,0:T(8,128)(2,1)S(1)}, u32[]{:S(2)}, u32[]{:S(2)}) collective-permute-start(bf16[32,3584]{1,0:T(8,128)(2,1)S(1)} %shard_map.114.refs_3_), channel_id=1, source_target_pairs={{0,2},{1,3},{2,0},{3,1},{4,6},{5,7},{6,4},{7,5},{8,10},{9,11},{10,... | collective-permute-start | bytes 688136 | tf_op jit(solution)/shard_map/ppermute | solution.py:243
  39.2 2.2 %collective-permute-done.14.refs_4_.refs_5_ = bf16[32,3584]{1,0:T(8,128)(2,1)S(1)} collective-permute-done((bf16[32,3584]{1,0:T(8,128)(2,1)S(1)}, bf16[32,3584]{1,0:T(8,128)(2,1)S(1)}, u32[]{:S(2)}, u32[]{:S(2)}) %collective-permute-start.14) | collective-permute-done | bytes 229408 | tf_op jit(solution)/shard_map/ppermute | solution.py:243
  41.4 0.0 collective-permute-start.17
  41.4 0.0 collective-permute-done.10.refs_1_
  41.4 0.0 collective-permute-done.11.refs_2_
  41.4 0.1 shard_map.115.refs_0_
  41.5 1.3 %collective-permute-start.18 = (bf16[32,3584]{1,0:T(8,128)(2,1)S(1)}, bf16[32,3584]{1,0:T(8,128)(2,1)S(1)}, u32[]{:S(2)}, u32[]{:S(2)}) collective-permute-start(bf16[32,3584]{1,0:T(8,128)(2,1)S(1)} %shard_map.115.refs_0_), channel_id=1, source_target_pairs={{0,2},{1,3},{2,0},{3,1},{4,6},{5,7},{6,4},{7,5},{8,10},{9,11},{10,... | collective-permute-start | bytes 688136 | tf_op jit(solution)/shard_map/ppermute | solution.py:243
  42.8 2.2 %shard_map.116 = (f32[32,128]{1,0:T(8,128)S(1)}, f32[32,128]{1,0:T(8,128)S(1)}) custom-call(s32[32]{0:T(128)} %ids.1, s32[2]{0:T(128)} %lengths.1, f32[1002,128]{1,0:T(8,128)} %bitcast.7, bf16[32,3584]{1,0:T(8,128)(2,1)S(1)} %shard_map.115.refs_0_), custom_call_target="tpu_custom_call" | custom-call | tf_op jit(solution)/shard_map/pallas_call | solution.py:128
  44.9 0.9 %shard_map.117 = (f32[32,3584]{1,0:T(8,128)S(1)}, bf16[32,3584]{1,0:T(8,128)(2,1)}) custom-call(f32[32,128]{1,0:T(8,128)S(1)} %get-tuple-element.46.live, bf16[32,3584]{1,0:T(8,128)(2,1)S(1)} %get-tuple-element.47.refs_0_, bf16[32,7168]{1,0:T(8,128)(2,1)S(1)} %collective-permute-done.13.refs_3_.refs_1_.refs_4_, ...), custom_call_target="tpu_custom_call" | custom-call | tf_op jit(solution)/shard_map/pallas_call | solution.py:301
  45.8 0.0 collective-permute-done.15.refs_1_
  45.8 0.5 collective-permute-done.16.refs_2_
  46.3 0.1 shard_map.118.gated
  46.4 0.0 collective-permute-done.17.refs_1_
  46.5 4.4 %collective-permute-done.18.refs_2_ = bf16[32,3584]{1,0:T(8,128)(2,1)S(1)} collective-permute-done((bf16[32,3584]{1,0:T(8,128)(2,1)S(1)}, bf16[32,3584]{1,0:T(8,128)(2,1)S(1)}, u32[]{:S(2)}, u32[]{:S(2)}) %collective-permute-start.18) | collective-permute-done | bytes 229408 | tf_op jit(solution)/shard_map/ppermute | solution.py:243
  50.8 0.8 %shard_map.119 = bf16[32,3584]{1,0:T(8,128)(2,1)} custom-call(f32[32,3584]{1,0:T(8,128)S(1)} %get-tuple-element.50.act, f32[32,3584]{1,0:T(8,128)S(1)} %shard_map.118.gated, bf16[32,3584]{1,0:T(8,128)(2,1)S(1)} %get-tuple-element.54.refs_0_, bf16[32,3584]{1,0:T(8,128)(2,1)S(1)} %collective-permute-done.17.refs_1_, ...), custom_call_target="tpu_custom_call" | custom-call | tf_op jit(solution)/shard_map/pallas_call | solution.py:337
  (21 shorter events, 0.1 us)
Async XLA Ops:
  0.6 11.3 %collective-permute-start.2 = (bf16[32,2048]{1,0:T(8,128)(2,1)}, bf16[32,2048]{1,0:T(8,128)(2,1)S(1)}, u32[]{:S(2)}, u32[]{:S(2)}) collective-permute-start(bf16[32,2048]{1,0:T(8,128)(2,1)} %refs_0_.4), channel_id=1, source_target_pairs={{0,4},{4,0},{8,12},{12,8},{1,5},{5,1},{9,13},{13,9},{2,6},{6,2},{1... | collective-permute-start | bytes 393224 | tf_op jit(solution)/shard_map/ppermute | solution.py:66
  3.7 12.7 %collective-permute-start.3 = (bf16[32,2048]{1,0:T(8,128)(2,1)}, bf16[32,2048]{1,0:T(8,128)(2,1)S(1)}, u32[]{:S(2)}, u32[]{:S(2)}) collective-permute-start(bf16[32,2048]{1,0:T(8,128)(2,1)} %refs_0_.4), channel_id=1, source_target_pairs={{0,8},{4,12},{8,0},{12,4},{1,9},{5,13},{9,1},{13,5},{2,10},{6,14},... | collective-permute-start | bytes 393224 | tf_op jit(solution)/shard_map/ppermute | solution.py:66
  6.3 12.0 %collective-permute-start = (bf16[32,2048]{1,0:T(8,128)(2,1)}, bf16[32,2048]{1,0:T(8,128)(2,1)S(1)}, u32[]{:S(2)}, u32[]{:S(2)}) collective-permute-start(bf16[32,2048]{1,0:T(8,128)(2,1)} %refs_0_.5), channel_id=1, source_target_pairs={{0,8},{4,12},{8,0},{12,4},{1,9},{5,13},{9,1},{13,5},{2,10},{6,14},... | collective-permute-start | bytes 393224 | tf_op jit(solution)/shard_map/ppermute | solution.py:74
  11.8 6.4 %copy-start = (bf16[32,2048]{1,0:T(8,128)(2,1)S(1)}, bf16[32,2048]{1,0:T(8,128)(2,1)}, u32[]{:S(2)}) copy-start(bf16[32,2048]{1,0:T(8,128)(2,1)} %refs_0_.5) | copy-start | bytes 393220
  11.8 11.1 %copy-start.1 = (bf16[32,2048]{1,0:T(8,128)(2,1)S(1)}, bf16[32,2048]{1,0:T(8,128)(2,1)}, u32[]{:S(2)}) copy-start(bf16[32,2048]{1,0:T(8,128)(2,1)} %refs_0_.4) | copy-start | bytes 393220
  11.9 13.7 %slice-start = ((s8[14680064]{0:T(1024)(128)(4,1)}), s8[4194304]{0:T(1024)(128)(4,1)S(1)}, s32[]{:S(2)}) async-start(s8[14680064]{0:T(1024)(128)(4,1)} %bitcast.1), calls=%async_computation | async-start | bytes 8388608
  11.9 13.7 %slice-start.1 = ((s8[14680064]{0:T(1024)(128)(4,1)}), s8[4194304]{0:T(1024)(128)(4,1)S(1)}, s32[]{:S(2)}) async-start(s8[14680064]{0:T(1024)(128)(4,1)} %bitcast.1), calls=%async_computation.1 | async-start | bytes 8388608
  16.5 13.5 %slice-start.4 = ((s8[14680064]{0:T(1024)(128)(4,1)}), s8[4194304]{0:T(1024)(128)(4,1)S(1)}, s32[]{:S(2)}) async-start(s8[14680064]{0:T(1024)(128)(4,1)} %bitcast.3), calls=%async_computation.4 | async-start | bytes 8388608
  16.5 13.5 %slice-start.5 = ((s8[14680064]{0:T(1024)(128)(4,1)}), s8[4194304]{0:T(1024)(128)(4,1)S(1)}, s32[]{:S(2)}) async-start(s8[14680064]{0:T(1024)(128)(4,1)} %bitcast.3), calls=%async_computation.5 | async-start | bytes 8388608
  16.5 9.1 %slice-start.2 = ((s8[14680064]{0:T(1024)(128)(4,1)}), s8[4194304]{0:T(1024)(128)(4,1)S(1)}, s32[]{:S(2)}) async-start(s8[14680064]{0:T(1024)(128)(4,1)} %bitcast.1), calls=%async_computation.2 | async-start | bytes 8388608
  16.5 6.4 %collective-permute-start.4 = (bf16[32,2048]{1,0:T(8,128)(2,1)S(1)}, bf16[32,2048]{1,0:T(8,128)(2,1)S(1)}, u32[]{:S(2)}, u32[]{:S(2)}) collective-permute-start(bf16[32,2048]{1,0:T(8,128)(2,1)S(1)} %shard_map.106), channel_id=1, source_target_pairs={{0,4},{4,0},{8,12},{12,8},{1,5},{5,1},{9,13},{13,9},{2,6},{6,2},{1... | collective-permute-start | bytes 393224 | tf_op jit(solution)/shard_map/ppermute | solution.py:66
  18.3 7.3 %slice-start.3 = ((s8[14680064]{0:T(1024)(128)(4,1)}), s8[2097152]{0:T(1024)(128)(4,1)S(1)}, s32[]{:S(2)}) async-start(s8[14680064]{0:T(1024)(128)(4,1)} %bitcast.1), calls=%async_computation.3 | async-start | bytes 4194304
  18.3 11.7 %slice-start.6 = ((s8[14680064]{0:T(1024)(128)(4,1)}), s8[4194304]{0:T(1024)(128)(4,1)S(1)}, s32[]{:S(2)}) async-start(s8[14680064]{0:T(1024)(128)(4,1)} %bitcast.3), calls=%async_computation.6 | async-start | bytes 8388608
  18.3 10.0 %collective-permute-start.1 = (bf16[64,2048]{1,0:T(8,128)(2,1)S(1)}, bf16[64,2048]{1,0:T(8,128)(2,1)S(1)}, u32[]{:S(2)}, u32[]{:S(2)}) collective-permute-start(bf16[64,2048]{1,0:T(8,128)(2,1)S(1)} %shard_map.104), channel_id=1, source_target_pairs={{0,4},{4,0},{8,12},{12,8},{1,5},{5,1},{9,13},{13,9},{2,6},{6,2},{1... | collective-permute-start | bytes 786440 | tf_op jit(solution)/shard_map/ppermute | solution.py:74
  25.0 3.3 %collective-permute-start.6 = (bf16[32,2048]{1,0:T(8,128)(2,1)S(1)}, bf16[32,2048]{1,0:T(8,128)(2,1)S(1)}, u32[]{:S(2)}, u32[]{:S(2)}) collective-permute-start(bf16[32,2048]{1,0:T(8,128)(2,1)S(1)} %get-tuple-element.31), channel_id=1, source_target_pairs={{0,1},{1,0},{2,3},{3,2},{4,5},{5,4},{6,7},{7,6},{8,9},{9,8},{10,11... | collective-permute-start | bytes 393224 | tf_op jit(solution)/shard_map/ppermute | solution.py:243
  25.1 3.2 %collective-permute-start.5 = (bf16[32,1536]{1,0:T(8,128)(2,1)S(1)}, bf16[32,1536]{1,0:T(8,128)(2,1)S(1)}, u32[]{:S(2)}, u32[]{:S(2)}) collective-permute-start(bf16[32,1536]{1,0:T(8,128)(2,1)S(1)} %get-tuple-element.30), channel_id=1, source_target_pairs={{0,1},{1,0},{2,3},{3,2},{4,5},{5,4},{6,7},{7,6},{8,9},{9,8},{10,11... | collective-permute-start | bytes 294920 | tf_op jit(solution)/shard_map/ppermute | solution.py:243
  25.6 4.4 %slice-start.7 = ((s8[14680064]{0:T(1024)(128)(4,1)}), s8[2097152]{0:T(1024)(128)(4,1)S(1)}, s32[]{:S(2)}) async-start(s8[14680064]{0:T(1024)(128)(4,1)} %bitcast.3), calls=%async_computation.7 | async-start | bytes 4194304
  25.6 7.7 %slice-start.8 = ((s8[14680064]{0:T(1024)(128)(4,1)}), s8[2097152]{0:T(1024)(128)(4,1)S(1)}, s32[]{:S(2)}) async-start(s8[14680064]{0:T(1024)(128)(4,1)} %bitcast.5), calls=%async_computation.8 | async-start | bytes 4194304
  25.7 7.7 %slice-start.9 = ((s8[14680064]{0:T(1024)(128)(4,1)}), s8[4194304]{0:T(1024)(128)(4,1)S(1)}, s32[]{:S(2)}) async-start(s8[14680064]{0:T(1024)(128)(4,1)} %bitcast.5), calls=%async_computation.9 | async-start | bytes 8388608
  27.7 9.6 %collective-permute-start.13 = (bf16[32,7168]{1,0:T(8,128)(2,1)S(1)}, bf16[32,7168]{1,0:T(8,128)(2,1)S(1)}, u32[]{:S(2)}, u32[]{:S(2)}) collective-permute-start(bf16[32,7168]{1,0:T(8,128)(2,1)S(1)} %get-tuple-element.45), channel_id=1, source_target_pairs={{0,1},{1,0},{2,3},{3,2},{4,5},{5,4},{6,7},{7,6},{8,9},{9,8},{10,11... | collective-permute-start | bytes 1376264 | tf_op jit(solution)/shard_map/ppermute | solution.py:243
  27.9 4.8 %collective-permute-start.8 = (bf16[32,2048]{1,0:T(8,128)(2,1)S(1)}, bf16[32,2048]{1,0:T(8,128)(2,1)S(1)}, u32[]{:S(2)}, u32[]{:S(2)}) collective-permute-start(bf16[32,2048]{1,0:T(8,128)(2,1)S(1)} %get-tuple-element.37), channel_id=1, source_target_pairs={{0,1},{1,0},{2,3},{3,2},{4,5},{5,4},{6,7},{7,6},{8,9},{9,8},{10,11... | collective-permute-start | bytes 393224 | tf_op jit(solution)/shard_map/ppermute | solution.py:243
  28.3 5.0 %slice-start.10 = ((s8[14680064]{0:T(1024)(128)(4,1)}), s8[4194304]{0:T(1024)(128)(4,1)S(1)}, s32[]{:S(2)}) async-start(s8[14680064]{0:T(1024)(128)(4,1)} %bitcast.5), calls=%async_computation.10 | async-start | bytes 8388608
  28.4 8.2 %collective-permute-start.9 = (bf16[32,3584]{1,0:T(8,128)(2,1)S(1)}, bf16[32,3584]{1,0:T(8,128)(2,1)S(1)}, u32[]{:S(2)}, u32[]{:S(2)}) collective-permute-start(bf16[32,3584]{1,0:T(8,128)(2,1)S(1)} %shard_map.109.refs_4_), channel_id=1, source_target_pairs={{0,2},{1,3},{2,0},{3,1},{4,6},{5,7},{6,4},{7,5},{8,10},{9,11},{10,... | collective-permute-start | bytes 688136 | tf_op jit(solution)/shard_map/ppermute | solution.py:243
  30.0 3.4 %slice-start.11 = ((s8[14680064]{0:T(1024)(128)(4,1)}), s8[4194304]{0:T(1024)(128)(4,1)S(1)}, s32[]{:S(2)}) async-start(s8[14680064]{0:T(1024)(128)(4,1)} %bitcast.5), calls=%async_computation.11 | async-start | bytes 8388608
  30.0 2.7 %collective-permute-start.7 = (bf16[32,1536]{1,0:T(8,128)(2,1)S(1)}, bf16[32,1536]{1,0:T(8,128)(2,1)S(1)}, u32[]{:S(2)}, u32[]{:S(2)}) collective-permute-start(bf16[32,1536]{1,0:T(8,128)(2,1)S(1)} %get-tuple-element.36), channel_id=1, source_target_pairs={{0,1},{1,0},{2,3},{3,2},{4,5},{5,4},{6,7},{7,6},{8,9},{9,8},{10,11... | collective-permute-start | bytes 294920 | tf_op jit(solution)/shard_map/ppermute | solution.py:243
  32.1 5.1 %collective-permute-start.12 = (bf16[32,3584]{1,0:T(8,128)(2,1)S(1)}, bf16[32,3584]{1,0:T(8,128)(2,1)S(1)}, u32[]{:S(2)}, u32[]{:S(2)}) collective-permute-start(bf16[32,3584]{1,0:T(8,128)(2,1)S(1)} %get-tuple-element.44), channel_id=1, source_target_pairs={{0,1},{1,0},{2,3},{3,2},{4,5},{5,4},{6,7},{7,6},{8,9},{9,8},{10,11... | collective-permute-start | bytes 688136 | tf_op jit(solution)/shard_map/ppermute | solution.py:243
  32.7 8.6 %collective-permute-start.14 = (bf16[32,3584]{1,0:T(8,128)(2,1)S(1)}, bf16[32,3584]{1,0:T(8,128)(2,1)S(1)}, u32[]{:S(2)}, u32[]{:S(2)}) collective-permute-start(bf16[32,3584]{1,0:T(8,128)(2,1)S(1)} %shard_map.111.refs_2_), channel_id=1, source_target_pairs={{0,2},{1,3},{2,0},{3,1},{4,6},{5,7},{6,4},{7,5},{8,10},{9,11},{10,... | collective-permute-start | bytes 688136 | tf_op jit(solution)/shard_map/ppermute | solution.py:243
  36.7 4.7 %collective-permute-start.11 = (bf16[32,2048]{1,0:T(8,128)(2,1)S(1)}, bf16[32,2048]{1,0:T(8,128)(2,1)S(1)}, u32[]{:S(2)}, u32[]{:S(2)}) collective-permute-start(bf16[32,2048]{1,0:T(8,128)(2,1)S(1)} %get-tuple-element.43), channel_id=1, source_target_pairs={{0,1},{1,0},{2,3},{3,2},{4,5},{5,4},{6,7},{7,6},{8,9},{9,8},{10,11... | collective-permute-start | bytes 393224 | tf_op jit(solution)/shard_map/ppermute | solution.py:243
  36.7 4.7 %collective-permute-start.10 = (bf16[32,1536]{1,0:T(8,128)(2,1)S(1)}, bf16[32,1536]{1,0:T(8,128)(2,1)S(1)}, u32[]{:S(2)}, u32[]{:S(2)}) collective-permute-start(bf16[32,1536]{1,0:T(8,128)(2,1)S(1)} %get-tuple-element.42), channel_id=1, source_target_pairs={{0,1},{1,0},{2,3},{3,2},{4,5},{5,4},{6,7},{7,6},{8,9},{9,8},{10,11... | collective-permute-start | bytes 294920 | tf_op jit(solution)/shard_map/ppermute | solution.py:243
  37.2 8.6 %collective-permute-start.15 = (bf16[32,3584]{1,0:T(8,128)(2,1)S(1)}, bf16[32,3584]{1,0:T(8,128)(2,1)S(1)}, u32[]{:S(2)}, u32[]{:S(2)}) collective-permute-start(bf16[32,3584]{1,0:T(8,128)(2,1)S(1)} %get-tuple-element.53), channel_id=1, source_target_pairs={{0,1},{1,0},{2,3},{3,2},{4,5},{5,4},{6,7},{7,6},{8,9},{9,8},{10,11... | collective-permute-start | bytes 688136 | tf_op jit(solution)/shard_map/ppermute | solution.py:243
  37.4 8.9 %collective-permute-start.16 = (bf16[32,3584]{1,0:T(8,128)(2,1)S(1)}, bf16[32,3584]{1,0:T(8,128)(2,1)S(1)}, u32[]{:S(2)}, u32[]{:S(2)}) collective-permute-start(bf16[32,3584]{1,0:T(8,128)(2,1)S(1)} %shard_map.114.refs_3_), channel_id=1, source_target_pairs={{0,2},{1,3},{2,0},{3,1},{4,6},{5,7},{6,4},{7,5},{8,10},{9,11},{10,... | collective-permute-start | bytes 688136 | tf_op jit(solution)/shard_map/ppermute | solution.py:243
  41.4 5.1 %collective-permute-start.17 = (bf16[32,3584]{1,0:T(8,128)(2,1)S(1)}, bf16[32,3584]{1,0:T(8,128)(2,1)S(1)}, u32[]{:S(2)}, u32[]{:S(2)}) collective-permute-start(bf16[32,3584]{1,0:T(8,128)(2,1)S(1)} %get-tuple-element.55), channel_id=1, source_target_pairs={{0,1},{1,0},{2,3},{3,2},{4,5},{5,4},{6,7},{7,6},{8,9},{9,8},{10,11... | collective-permute-start | bytes 688136 | tf_op jit(solution)/shard_map/ppermute | solution.py:243
  41.5 9.4 %collective-permute-start.18 = (bf16[32,3584]{1,0:T(8,128)(2,1)S(1)}, bf16[32,3584]{1,0:T(8,128)(2,1)S(1)}, u32[]{:S(2)}, u32[]{:S(2)}) collective-permute-start(bf16[32,3584]{1,0:T(8,128)(2,1)S(1)} %shard_map.115.refs_0_), channel_id=1, source_target_pairs={{0,2},{1,3},{2,0},{3,1},{4,6},{5,7},{6,4},{7,5},{8,10},{9,11},{10,... | collective-permute-start | bytes 688136 | tf_op jit(solution)/shard_map/ppermute | solution.py:243

commit v17 on v15

--- a/solution.py
+++ b/solution.py
@@ -334,19 +334,20 @@
 
     rows, sends, own, keeps = product(target_pieces, (gate,), narrow, (), spots=target_spots)
     after = (keeps[0],)
-    _, up_sends, own, up_keeps = product(rows, (in_vmem(target_up),), narrow, after, (own,))
     target_own = exchange(own, 0, narrow)
+    _, up_sends, own, up_keeps = product(rows, (in_vmem(target_up),), narrow, after)
+    up_own = exchange(own, 0, narrow)
     sent, target_g = finish(sends, keeps, (target_own, 0), narrow, (up_keeps[0], *source_pieces[1:]))
     rows, gate_sends, own, gate_keeps = product(
         source_pieces, (in_vmem(source_gate),), narrow, (sent,), spots=source_spots, split=False
     )
     gate_own = exchange(own, 0, narrow)
     after = (gate_keeps[0],)
-    sent, target_u = finish(up_sends, up_keeps, (target_own, -width), narrow, after)
+    sent, target_u = finish(up_sends, up_keeps, (up_own, 0), narrow, after)
     _, sends, own, keeps = product(rows, (in_vmem(source_up),), narrow, (sent,))
     sends = resent(sends, (target_g[0][-1],))
     own = exchange(own, 0, narrow)
-    sent, source_g = finish(gate_sends, gate_keeps, (gate_own, 0), narrow, (keeps[0], target_own))
+    sent, source_g = finish(gate_sends, gate_keeps, (gate_own, 0), narrow, (keeps[0], target_own, up_own))
     sent, source_u = finish(sends, keeps, (own, 0), narrow, (sent, target_u[0][-1]))
     live, weight = look_up(token_ids, lengths, ratio_weight, (sent,))
     act, target_out = target_end(live, target_g, target_u)

time: 48 us -> 47.9 us (level)
  waiting for transfers between devices: 12.8 us -> 12.2 us
  starting transfers between devices: 16.1 us -> 16.6 us
    ppermute x14 -> x15, waiting for transfers between devices: 8.06 us -> 7.03 us  [exchange(): lax.ppermute(array, 'narrow', [(i, i ^ 1 << step) for i in range(size)])]
    ppermute x14 -> x15, starting transfers between devices: 7.77 us -> 8.27 us  [exchange(): lax.ppermute(array, 'narrow', [(i, i ^ 1 << step) for i in range(size)])]
  transfers between devices with their start and end apart: 20 -> 21, of which waited for: 6 -> 7; matrix products, arithmetic and copies ran while one was open for 0% -> 0% of each run, Pallas kernels for 36% -> 36%
where the time goes in v17:
time: 47.9 us; the launch traced here: 47.7 us
  Pallas kernels  17.8 us (37%)
  starting transfers between devices  16.6 us (35%)
  waiting for transfers between devices  12.2 us (25%)
  between operations  0.91 us (2%)
    pallas_call x4, Pallas kernels, product(): pl.pallas_call(functools.partial(product_kernel, len(tokens), len(matrice...  8.35 us
    ppermute x15, starting transfers between devices, exchange(): lax.ppermute(array, 'narrow', [(i, i ^ 1 << step) for i in range(size)])  8.27 us
    ppermute x15, waiting for transfers between devices, exchange(): lax.ppermute(array, 'narrow', [(i, i ^ 1 << step) for i in range(size)])  7.03 us
    ppermute x3, starting transfers between devices, gather_pieces(): lax.ppermute(source, axis, [(i, i ^ low) for i in range(size)])  5.91 us
    pallas_call x1, Pallas kernels, load(): pl.pallas_call(functools.partial(load_kernel, first), out_shape=pltpu.VME...  5.18 us
    ppermute x3, waiting for transfers between devices, gather_chained(): lax.ppermute(source, axis, [(i, i ^ low) for i in range(size)])  4.18 us
    ppermute x3, starting transfers between devices, gather_chained(): lax.ppermute(source, axis, [(i, i ^ low) for i in range(size)])  2.43 us
    pallas_call x1, Pallas kernels, look_up(): pl.pallas_call(functools.partial(look_up_kernel, ids.shape[0] // lengths....  2.16 us
  transfers between devices with their start and end apart: 21, of which 7 were waited for; matrix products, arithmetic and copies ran while one was open for 0% of the time, Pallas kernels for 36%

profile of v17, /device:TPU:0, one launch (start us, length us, event | category | flops | bytes accessed | tf_op | source)
XLA Modules:
  0.0 47.7 jit_solution(11676197103602317974)
XLA Ops:
  0.6 4.1 %collective-permute-start.4 = (bf16[32,2048]{1,0:T(8,128)(2,1)}, bf16[32,2048]{1,0:T(8,128)(2,1)S(1)}, u32[]{:S(2)}, u32[]{:S(2)}) collective-permute-start(bf16[32,2048]{1,0:T(8,128)(2,1)} %refs_0_.4), channel_id=1, source_target_pairs={{0,8},{4,12},{8,0},{12,4},{1,9},{5,13},{9,1},{13,5},{2,10},{6,14},... | collective-permute-start | bytes 393224 | tf_op jit(solution)/shard_map/ppermute | solution.py:47
  4.7 1.6 %collective-permute-start.3 = (bf16[32,2048]{1,0:T(8,128)(2,1)}, bf16[32,2048]{1,0:T(8,128)(2,1)S(1)}, u32[]{:S(2)}, u32[]{:S(2)}) collective-permute-start(bf16[32,2048]{1,0:T(8,128)(2,1)} %refs_0_.4), channel_id=1, source_target_pairs={{0,4},{4,0},{8,12},{12,8},{1,5},{5,1},{9,13},{13,9},{2,6},{6,2},{1... | collective-permute-start | bytes 393224 | tf_op jit(solution)/shard_map/ppermute | solution.py:47
  6.3 0.3 collective-permute-start
  6.6 5.2 %shard_map.105.refs_1_.refs_4_ = bf16[2048,3584]{1,0:T(8,128)(2,1)S(1)} custom-call(bf16[2048,3584]{1,0:T(8,128)(2,1)} %matrix.1), custom_call_target="tpu_custom_call" | custom-call | tf_op jit(solution)/shard_map/pallas_call | solution.py:133
  11.8 0.0 copy-start
  11.8 0.0 copy-start.1
  11.9 0.0 slice-start
  11.9 0.0 slice-start.1
  11.9 1.0 %collective-permute-done.4.refs_0_.refs_2_ = bf16[32,2048]{1,0:T(8,128)(2,1)S(1)} collective-permute-done((bf16[32,2048]{1,0:T(8,128)(2,1)}, bf16[32,2048]{1,0:T(8,128)(2,1)S(1)}, u32[]{:S(2)}, u32[]{:S(2)}) %collective-permute-start.4) | collective-permute-done | bytes 131104 | tf_op jit(solution)/shard_map/ppermute | solution.py:47
  12.9 0.0 slice-start.2
  12.9 0.2 collective-permute-start.5
  13.2 3.7 %collective-permute-done.refs_1_.refs_5_.refs_2_ = bf16[32,2048]{1,0:T(8,128)(2,1)S(1)} collective-permute-done((bf16[32,2048]{1,0:T(8,128)(2,1)}, bf16[32,2048]{1,0:T(8,128)(2,1)S(1)}, u32[]{:S(2)}, u32[]{:S(2)}) %collective-permute-start) | collective-permute-done | bytes 131104 | tf_op jit(solution)/shard_map/ppermute | solution.py:59
  16.9 0.0 slice-start.3
  16.9 0.0 slice-start.6
  16.9 0.9 %collective-permute-start.1 = (bf16[32,2048]{1,0:T(8,128)(2,1)S(1)}, bf16[32,2048]{1,0:T(8,128)(2,1)S(1)}, u32[]{:S(2)}, u32[]{:S(2)}) collective-permute-start(bf16[32,2048]{1,0:T(8,128)(2,1)S(1)} %shard_map.104), channel_id=1, source_target_pairs={{0,4},{4,0},{8,12},{12,8},{1,5},{5,1},{9,13},{13,9},{2,6},{6,2},{1... | collective-permute-start | bytes 393224 | tf_op jit(solution)/shard_map/ppermute | solution.py:59
  17.8 1.2 %collective-permute-start.2 = (bf16[32,2048]{1,0:T(8,128)(2,1)S(1)}, bf16[32,2048]{1,0:T(8,128)(2,1)S(1)}, u32[]{:S(2)}, u32[]{:S(2)}) collective-permute-start(bf16[32,2048]{1,0:T(8,128)(2,1)S(1)} %collective-permute-done.refs_1_.refs_5_.refs_2_), channel_id=1, source_target_pairs={{0,4},{4,0},{8,12},{12,8},{1,5},{5,1},{9,13},{13,9},{2,6},{6,2},{1... | collective-permute-start | bytes 393224 | tf_op jit(solution)/shard_map/ppermute | solution.py:59
  19.0 0.0 collective-permute-done.3.refs_1_
  19.0 0.0 collective-permute-done.5.refs_3_
  19.0 2.1 %shard_map.107 = (bf16[128,2048]{1,0:T(8,128)(2,1)S(1)}, bf16[32,1536]{1,0:T(8,128)(2,1)S(1)}, bf16[32,2048]{1,0:T(8,128)(2,1)S(1)}, bf16[32,3584]{1,0:T(8,128)(...) custom-call(bf16[32,2048]{1,0:T(8,128)(2,1)S(1)} %copy-done.1, ...), custom_call_target="tpu_custom_call" | custom-call | tf_op jit(solution)/shard_map/pallas_call | solution.py:204
  21.2 0.1 collective-permute-start.7
  21.2 0.5 %collective-permute-start.6 = (bf16[32,1536]{1,0:T(8,128)(2,1)S(1)}, bf16[32,1536]{1,0:T(8,128)(2,1)S(1)}, u32[]{:S(2)}, u32[]{:S(2)}) collective-permute-start(bf16[32,1536]{1,0:T(8,128)(2,1)S(1)} %get-tuple-element.30), channel_id=1, source_target_pairs={{0,1},{1,0},{2,3},{3,2},{4,5},{5,4},{6,7},{7,6},{8,9},{9,8},{10,11... | collective-permute-start | bytes 294920 | tf_op jit(solution)/shard_map/ppermute | solution.py:225
  21.8 0.0 slice-start.7
  21.8 0.0 slice-start.8
  21.8 0.0 slice-start.9
  21.8 2.1 %shard_map.108 = (bf16[32,1536]{1,0:T(8,128)(2,1)S(1)}, bf16[32,2048]{1,0:T(8,128)(2,1)S(1)}, bf16[32,3584]{1,0:T(8,128)(2,1)S(1)}, bf16[32,3584]{1,0:T(8,128)(2,1)S(1)}, bf16[32,3584]{1,0:T(8,128)(2,1)S(1)}) custom-call(bf16[128,2048]{1,0:T(8,128)(2,1)S(1)} %get-tuple-element.32.refs_0_, bf16[2048,3584]{1,0:T(8,128)(2,1)S(1)} %bitcast.2, ...), custom_call_target="tpu_custom_call" | custom-call | tf_op jit(solution)/shard_map/pallas_call | solution.py:204
  23.9 0.1 collective-permute-start.9
  24.0 0.0 collective-permute-done.1.refs_4_.refs_1_
  24.0 0.5 collective-permute-done.2.refs_6_.refs_3_
  24.5 0.0 collective-permute-done.6.refs_1_
  24.5 0.0 collective-permute-done.7.refs_2_
  24.5 0.1 shard_map.109.refs_5_
  24.5 1.5 %collective-permute-start.10 = (bf16[32,3584]{1,0:T(8,128)(2,1)S(1)}, bf16[32,3584]{1,0:T(8,128)(2,1)S(1)}, u32[]{:S(2)}, u32[]{:S(2)}) collective-permute-start(bf16[32,3584]{1,0:T(8,128)(2,1)S(1)} %shard_map.109.refs_5_), channel_id=1, source_target_pairs={{0,2},{1,3},{2,0},{3,1},{4,6},{5,7},{6,4},{7,5},{8,10},{9,11},{10,... | collective-permute-start | bytes 688136 | tf_op jit(solution)/shard_map/ppermute | solution.py:225
  26.0 0.0 collective-permute-start.8
  26.0 0.5 %collective-permute-start.15 = (bf16[32,3584]{1,0:T(8,128)(2,1)S(1)}, bf16[32,3584]{1,0:T(8,128)(2,1)S(1)}, u32[]{:S(2)}, u32[]{:S(2)}) collective-permute-start(bf16[32,3584]{1,0:T(8,128)(2,1)S(1)} %get-tuple-element.45), channel_id=1, source_target_pairs={{0,1},{1,0},{2,3},{3,2},{4,5},{5,4},{6,7},{7,6},{8,9},{9,8},{10,11... | collective-permute-start | bytes 688136 | tf_op jit(solution)/shard_map/ppermute | solution.py:225
  26.5 0.0 collective-permute-start.14
  26.6 2.1 %shard_map.110 = (bf16[128,2048]{1,0:T(8,128)(2,1)S(1)}, bf16[32,3584]{1,0:T(8,128)(2,1)S(1)}, bf16[32,3584]{1,0:T(8,128)(2,1)S(1)}, bf16[32,3584]{1,0:T(8,128)(2,1)S(1)}, bf16[32,3584]{1,0:T(8,128)(2,1)S(1)}) custom-call(bf16[32,2048]{1,0:T(8,128)(2,1)S(1)} %copy-done, bf16[32,2048]{1,0:T(8,128)(2,1)S(1)} %collective-permute-done.1.refs_4_.refs_1_, ...), custom_call_target="tpu_custom_call" | custom-call | tf_op jit(solution)/shard_map/pallas_call | solution.py:204
  28.7 0.0 collective-permute-done.8.refs_1_
  28.7 0.6 %collective-permute-start.13 = (bf16[32,3584]{1,0:T(8,128)(2,1)S(1)}, bf16[32,3584]{1,0:T(8,128)(2,1)S(1)}, u32[]{:S(2)}, u32[]{:S(2)}) collective-permute-start(bf16[32,3584]{1,0:T(8,128)(2,1)S(1)} %get-tuple-element.43), channel_id=1, source_target_pairs={{0,1},{1,0},{2,3},{3,2},{4,5},{5,4},{6,7},{7,6},{8,9},{9,8},{10,11... | collective-permute-start | bytes 688136 | tf_op jit(solution)/shard_map/ppermute | solution.py:225
  29.2 0.0 collective-permute-done.9.refs_2_
  29.2 0.1 shard_map.111.refs_2_
  29.3 0.7 %collective-permute-start.16 = (bf16[32,3584]{1,0:T(8,128)(2,1)S(1)}, bf16[32,3584]{1,0:T(8,128)(2,1)S(1)}, u32[]{:S(2)}, u32[]{:S(2)}) collective-permute-start(bf16[32,3584]{1,0:T(8,128)(2,1)S(1)} %shard_map.111.refs_2_), channel_id=1, source_target_pairs={{0,2},{1,3},{2,0},{3,1},{4,6},{5,7},{6,4},{7,5},{8,10},{9,11},{10,... | collective-permute-start | bytes 688136 | tf_op jit(solution)/shard_map/ppermute | solution.py:225
  30.0 2.1 %shard_map.112 = (bf16[32,1536]{1,0:T(8,128)(2,1)S(1)}, bf16[32,2048]{1,0:T(8,128)(2,1)S(1)}, bf16[32,3584]{1,0:T(8,128)(2,1)S(1)}, bf16[32,3584]{1,0:T(8,128)(2,1)S(1)}, bf16[32,3584]{1,0:T(8,128)(2,1)S(1)}) custom-call(bf16[128,2048]{1,0:T(8,128)(2,1)S(1)} %get-tuple-element.34.refs_0_, bf16[2048,3584]{1,0:T(8,128)(2,1)S(1)} %bitcast.6, ...), custom_call_target="tpu_custom_call" | custom-call | tf_op jit(solution)/shard_map/pallas_call | solution.py:204
  32.1 0.1 collective-permute-done.10.refs_2_
  32.2 0.1 collective-permute-start.12
  32.3 0.0 collective-permute-done.15.refs_4_
  32.3 0.5 %collective-permute-start.11 = (bf16[32,1536]{1,0:T(8,128)(2,1)S(1)}, bf16[32,1536]{1,0:T(8,128)(2,1)S(1)}, u32[]{:S(2)}, u32[]{:S(2)}) collective-permute-start(bf16[32,1536]{1,0:T(8,128)(2,1)S(1)} %get-tuple-element.41), channel_id=1, source_target_pairs={{0,1},{1,0},{2,3},{3,2},{4,5},{5,4},{6,7},{7,6},{8,9},{9,8},{10,11... | collective-permute-start | bytes 294920 | tf_op jit(solution)/shard_map/ppermute | solution.py:225
  32.8 0.0 collective-permute-done.14.refs_3_.refs_1_
  32.8 0.1 collective-permute-start.17
  32.9 0.0 collective-permute-done.13.refs_1_
  32.9 0.1 shard_map.114.refs_3_
  32.9 2.3 %collective-permute-start.18 = (bf16[32,3584]{1,0:T(8,128)(2,1)S(1)}, bf16[32,3584]{1,0:T(8,128)(2,1)S(1)}, u32[]{:S(2)}, u32[]{:S(2)}) collective-permute-start(bf16[32,3584]{1,0:T(8,128)(2,1)S(1)} %shard_map.114.refs_3_), channel_id=1, source_target_pairs={{0,2},{1,3},{2,0},{3,1},{4,6},{5,7},{6,4},{7,5},{8,10},{9,11},{10,... | collective-permute-start | bytes 688136 | tf_op jit(solution)/shard_map/ppermute | solution.py:225
  35.3 2.2 %collective-permute-done.16.refs_4_.refs_5_ = bf16[32,3584]{1,0:T(8,128)(2,1)S(1)} collective-permute-done((bf16[32,3584]{1,0:T(8,128)(2,1)S(1)}, bf16[32,3584]{1,0:T(8,128)(2,1)S(1)}, u32[]{:S(2)}, u32[]{:S(2)}) %collective-permute-start.16) | collective-permute-done | bytes 229408 | tf_op jit(solution)/shard_map/ppermute | solution.py:225
  37.4 0.0 collective-permute-start.19
  37.5 0.0 collective-permute-done.11.refs_1_
  37.5 0.0 collective-permute-done.12.refs_2_
  37.5 0.1 shard_map.115.refs_0_
  37.5 1.3 %collective-permute-start.20 = (bf16[32,3584]{1,0:T(8,128)(2,1)S(1)}, bf16[32,3584]{1,0:T(8,128)(2,1)S(1)}, u32[]{:S(2)}, u32[]{:S(2)}) collective-permute-start(bf16[32,3584]{1,0:T(8,128)(2,1)S(1)} %shard_map.115.refs_0_), channel_id=1, source_target_pairs={{0,2},{1,3},{2,0},{3,1},{4,6},{5,7},{6,4},{7,5},{8,10},{9,11},{10,... | collective-permute-start | bytes 688136 | tf_op jit(solution)/shard_map/ppermute | solution.py:225
  38.9 2.2 %shard_map.116 = (f32[32,128]{1,0:T(8,128)S(1)}, f32[32,128]{1,0:T(8,128)S(1)}) custom-call(s32[32]{0:T(128)} %ids.1, s32[2]{0:T(128)} %lengths.1, f32[1002,128]{1,0:T(8,128)} %bitcast.7, bf16[32,3584]{1,0:T(8,128)(2,1)S(1)} %shard_map.115.refs_0_), custom_call_target="tpu_custom_call" | custom-call | tf_op jit(solution)/shard_map/pallas_call | solution.py:110
  41.0 0.9 %shard_map.117 = (f32[32,3584]{1,0:T(8,128)S(1)}, bf16[32,3584]{1,0:T(8,128)(2,1)}) custom-call(f32[32,128]{1,0:T(8,128)S(1)} %get-tuple-element.46.live, bf16[32,3584]{1,0:T(8,128)(2,1)S(1)} %get-tuple-element.47.refs_0_, bf16[32,3584]{1,0:T(8,128)(2,1)S(1)} %collective-permute-done.14.refs_3_.refs_1_, ...), custom_call_target="tpu_custom_call" | custom-call | tf_op jit(solution)/shard_map/pallas_call | solution.py:283
  42.0 0.0 collective-permute-done.17.refs_1_
  42.0 0.4 collective-permute-done.18.refs_2_
  42.4 0.1 shard_map.118.gated
  42.5 4.3 %collective-permute-done.20.refs_2_ = bf16[32,3584]{1,0:T(8,128)(2,1)S(1)} collective-permute-done((bf16[32,3584]{1,0:T(8,128)(2,1)S(1)}, bf16[32,3584]{1,0:T(8,128)(2,1)S(1)}, u32[]{:S(2)}, u32[]{:S(2)}) %collective-permute-start.20) | collective-permute-done | bytes 229408 | tf_op jit(solution)/shard_map/ppermute | solution.py:225
  46.9 0.8 %shard_map.119 = bf16[32,3584]{1,0:T(8,128)(2,1)} custom-call(f32[32,3584]{1,0:T(8,128)S(1)} %get-tuple-element.50.act, f32[32,3584]{1,0:T(8,128)S(1)} %shard_map.118.gated, bf16[32,3584]{1,0:T(8,128)(2,1)S(1)} %get-tuple-element.54.refs_0_, bf16[32,3584]{1,0:T(8,128)(2,1)S(1)} %collective-permute-done.19.refs_1_, ...), custom_call_target="tpu_custom_call" | custom-call | tf_op jit(solution)/shard_map/pallas_call | solution.py:319
  (25 shorter events, 0.1 us)
Async XLA Ops:
  0.6 12.3 %collective-permute-start.4 = (bf16[32,2048]{1,0:T(8,128)(2,1)}, bf16[32,2048]{1,0:T(8,128)(2,1)S(1)}, u32[]{:S(2)}, u32[]{:S(2)}) collective-permute-start(bf16[32,2048]{1,0:T(8,128)(2,1)} %refs_0_.4), channel_id=1, source_target_pairs={{0,8},{4,12},{8,0},{12,4},{1,9},{5,13},{9,1},{13,5},{2,10},{6,14},... | collective-permute-start | bytes 393224 | tf_op jit(solution)/shard_map/ppermute | solution.py:47
  4.7 14.3 %collective-permute-start.3 = (bf16[32,2048]{1,0:T(8,128)(2,1)}, bf16[32,2048]{1,0:T(8,128)(2,1)S(1)}, u32[]{:S(2)}, u32[]{:S(2)}) collective-permute-start(bf16[32,2048]{1,0:T(8,128)(2,1)} %refs_0_.4), channel_id=1, source_target_pairs={{0,4},{4,0},{8,12},{12,8},{1,5},{5,1},{9,13},{13,9},{2,6},{6,2},{1... | collective-permute-start | bytes 393224 | tf_op jit(solution)/shard_map/ppermute | solution.py:47
  6.3 10.6 %collective-permute-start = (bf16[32,2048]{1,0:T(8,128)(2,1)}, bf16[32,2048]{1,0:T(8,128)(2,1)S(1)}, u32[]{:S(2)}, u32[]{:S(2)}) collective-permute-start(bf16[32,2048]{1,0:T(8,128)(2,1)} %refs_0_.5), channel_id=1, source_target_pairs={{0,8},{4,12},{8,0},{12,4},{1,9},{5,13},{9,1},{13,5},{2,10},{6,14},... | collective-permute-start | bytes 393224 | tf_op jit(solution)/shard_map/ppermute | solution.py:59
  11.8 5.1 %copy-start = (bf16[32,2048]{1,0:T(8,128)(2,1)S(1)}, bf16[32,2048]{1,0:T(8,128)(2,1)}, u32[]{:S(2)}) copy-start(bf16[32,2048]{1,0:T(8,128)(2,1)} %refs_0_.5) | copy-start | bytes 393220
  11.8 7.2 %copy-start.1 = (bf16[32,2048]{1,0:T(8,128)(2,1)S(1)}, bf16[32,2048]{1,0:T(8,128)(2,1)}, u32[]{:S(2)}) copy-start(bf16[32,2048]{1,0:T(8,128)(2,1)} %refs_0_.4) | copy-start | bytes 393220
  11.9 9.9 %slice-start = ((s8[14680064]{0:T(1024)(128)(4,1)}), s8[4194304]{0:T(1024)(128)(4,1)S(1)}, s32[]{:S(2)}) async-start(s8[14680064]{0:T(1024)(128)(4,1)} %bitcast.1), calls=%async_computation | async-start | bytes 8388608
  11.9 9.9 %slice-start.1 = ((s8[14680064]{0:T(1024)(128)(4,1)}), s8[4194304]{0:T(1024)(128)(4,1)S(1)}, s32[]{:S(2)}) async-start(s8[14680064]{0:T(1024)(128)(4,1)} %bitcast.1), calls=%async_computation.1 | async-start | bytes 8388608
  12.9 13.6 %slice-start.4 = ((s8[14680064]{0:T(1024)(128)(4,1)}), s8[4194304]{0:T(1024)(128)(4,1)S(1)}, s32[]{:S(2)}) async-start(s8[14680064]{0:T(1024)(128)(4,1)} %bitcast.3), calls=%async_computation.4 | async-start | bytes 8388608
  12.9 13.6 %slice-start.5 = ((s8[14680064]{0:T(1024)(128)(4,1)}), s8[4194304]{0:T(1024)(128)(4,1)S(1)}, s32[]{:S(2)}) async-start(s8[14680064]{0:T(1024)(128)(4,1)} %bitcast.3), calls=%async_computation.5 | async-start | bytes 8388608
  12.9 8.8 %slice-start.2 = ((s8[14680064]{0:T(1024)(128)(4,1)}), s8[4194304]{0:T(1024)(128)(4,1)S(1)}, s32[]{:S(2)}) async-start(s8[14680064]{0:T(1024)(128)(4,1)} %bitcast.1), calls=%async_computation.2 | async-start | bytes 8388608
  12.9 6.1 %collective-permute-start.5 = (bf16[32,2048]{1,0:T(8,128)(2,1)S(1)}, bf16[32,2048]{1,0:T(8,128)(2,1)S(1)}, u32[]{:S(2)}, u32[]{:S(2)}) collective-permute-start(bf16[32,2048]{1,0:T(8,128)(2,1)S(1)} %shard_map.106), channel_id=1, source_target_pairs={{0,4},{4,0},{8,12},{12,8},{1,5},{5,1},{9,13},{13,9},{2,6},{6,2},{1... | collective-permute-start | bytes 393224 | tf_op jit(solution)/shard_map/ppermute | solution.py:47
  16.9 4.8 %slice-start.3 = ((s8[14680064]{0:T(1024)(128)(4,1)}), s8[2097152]{0:T(1024)(128)(4,1)S(1)}, s32[]{:S(2)}) async-start(s8[14680064]{0:T(1024)(128)(4,1)} %bitcast.1), calls=%async_computation.3 | async-start | bytes 4194304
  16.9 9.6 %slice-start.6 = ((s8[14680064]{0:T(1024)(128)(4,1)}), s8[4194304]{0:T(1024)(128)(4,1)S(1)}, s32[]{:S(2)}) async-start(s8[14680064]{0:T(1024)(128)(4,1)} %bitcast.3), calls=%async_computation.6 | async-start | bytes 8388608
  16.9 7.1 %collective-permute-start.1 = (bf16[32,2048]{1,0:T(8,128)(2,1)S(1)}, bf16[32,2048]{1,0:T(8,128)(2,1)S(1)}, u32[]{:S(2)}, u32[]{:S(2)}) collective-permute-start(bf16[32,2048]{1,0:T(8,128)(2,1)S(1)} %shard_map.104), channel_id=1, source_target_pairs={{0,4},{4,0},{8,12},{12,8},{1,5},{5,1},{9,13},{13,9},{2,6},{6,2},{1... | collective-permute-start | bytes 393224 | tf_op jit(solution)/shard_map/ppermute | solution.py:59
  17.8 6.6 %collective-permute-start.2 = (bf16[32,2048]{1,0:T(8,128)(2,1)S(1)}, bf16[32,2048]{1,0:T(8,128)(2,1)S(1)}, u32[]{:S(2)}, u32[]{:S(2)}) collective-permute-start(bf16[32,2048]{1,0:T(8,128)(2,1)S(1)} %collective-permute-done.refs_1_.refs_5_.refs_2_), channel_id=1, source_target_pairs={{0,4},{4,0},{8,12},{12,8},{1,5},{5,1},{9,13},{13,9},{2,6},{6,2},{1... | collective-permute-start | bytes 393224 | tf_op jit(solution)/shard_map/ppermute | solution.py:59
  21.2 3.3 %collective-permute-start.7 = (bf16[32,2048]{1,0:T(8,128)(2,1)S(1)}, bf16[32,2048]{1,0:T(8,128)(2,1)S(1)}, u32[]{:S(2)}, u32[]{:S(2)}) collective-permute-start(bf16[32,2048]{1,0:T(8,128)(2,1)S(1)} %get-tuple-element.31), channel_id=1, source_target_pairs={{0,1},{1,0},{2,3},{3,2},{4,5},{5,4},{6,7},{7,6},{8,9},{9,8},{10,11... | collective-permute-start | bytes 393224 | tf_op jit(solution)/shard_map/ppermute | solution.py:225
  21.2 3.2 %collective-permute-start.6 = (bf16[32,1536]{1,0:T(8,128)(2,1)S(1)}, bf16[32,1536]{1,0:T(8,128)(2,1)S(1)}, u32[]{:S(2)}, u32[]{:S(2)}) collective-permute-start(bf16[32,1536]{1,0:T(8,128)(2,1)S(1)} %get-tuple-element.30), channel_id=1, source_target_pairs={{0,1},{1,0},{2,3},{3,2},{4,5},{5,4},{6,7},{7,6},{8,9},{9,8},{10,11... | collective-permute-start | bytes 294920 | tf_op jit(solution)/shard_map/ppermute | solution.py:225
  21.8 4.8 %slice-start.7 = ((s8[14680064]{0:T(1024)(128)(4,1)}), s8[2097152]{0:T(1024)(128)(4,1)S(1)}, s32[]{:S(2)}) async-start(s8[14680064]{0:T(1024)(128)(4,1)} %bitcast.3), calls=%async_computation.7 | async-start | bytes 4194304
  21.8 8.2 %slice-start.8 = ((s8[14680064]{0:T(1024)(128)(4,1)}), s8[4194304]{0:T(1024)(128)(4,1)S(1)}, s32[]{:S(2)}) async-start(s8[14680064]{0:T(1024)(128)(4,1)} %bitcast.5), calls=%async_computation.8 | async-start | bytes 8388608
  21.8 8.2 %slice-start.9 = ((s8[14680064]{0:T(1024)(128)(4,1)}), s8[4194304]{0:T(1024)(128)(4,1)S(1)}, s32[]{:S(2)}) async-start(s8[14680064]{0:T(1024)(128)(4,1)} %bitcast.5), calls=%async_computation.9 | async-start | bytes 8388608
  23.9 5.4 %collective-permute-start.9 = (bf16[32,2048]{1,0:T(8,128)(2,1)S(1)}, bf16[32,2048]{1,0:T(8,128)(2,1)S(1)}, u32[]{:S(2)}, u32[]{:S(2)}) collective-permute-start(bf16[32,2048]{1,0:T(8,128)(2,1)S(1)} %get-tuple-element.36), channel_id=1, source_target_pairs={{0,1},{1,0},{2,3},{3,2},{4,5},{5,4},{6,7},{7,6},{8,9},{9,8},{10,11... | collective-permute-start | bytes 393224 | tf_op jit(solution)/shard_map/ppermute | solution.py:225
  24.5 5.5 %slice-start.10 = ((s8[14680064]{0:T(1024)(128)(4,1)}), s8[4194304]{0:T(1024)(128)(4,1)S(1)}, s32[]{:S(2)}) async-start(s8[14680064]{0:T(1024)(128)(4,1)} %bitcast.5), calls=%async_computation.10 | async-start | bytes 8388608
  24.5 7.6 %collective-permute-start.10 = (bf16[32,3584]{1,0:T(8,128)(2,1)S(1)}, bf16[32,3584]{1,0:T(8,128)(2,1)S(1)}, u32[]{:S(2)}, u32[]{:S(2)}) collective-permute-start(bf16[32,3584]{1,0:T(8,128)(2,1)S(1)} %shard_map.109.refs_5_), channel_id=1, source_target_pairs={{0,2},{1,3},{2,0},{3,1},{4,6},{5,7},{6,4},{7,5},{8,10},{9,11},{10,... | collective-permute-start | bytes 688136 | tf_op jit(solution)/shard_map/ppermute | solution.py:225
  26.0 2.7 %collective-permute-start.8 = (bf16[32,1536]{1,0:T(8,128)(2,1)S(1)}, bf16[32,1536]{1,0:T(8,128)(2,1)S(1)}, u32[]{:S(2)}, u32[]{:S(2)}) collective-permute-start(bf16[32,1536]{1,0:T(8,128)(2,1)S(1)} %get-tuple-element.35), channel_id=1, source_target_pairs={{0,1},{1,0},{2,3},{3,2},{4,5},{5,4},{6,7},{7,6},{8,9},{9,8},{10,11... | collective-permute-start | bytes 294920 | tf_op jit(solution)/shard_map/ppermute | solution.py:225
  26.0 6.3 %collective-permute-start.15 = (bf16[32,3584]{1,0:T(8,128)(2,1)S(1)}, bf16[32,3584]{1,0:T(8,128)(2,1)S(1)}, u32[]{:S(2)}, u32[]{:S(2)}) collective-permute-start(bf16[32,3584]{1,0:T(8,128)(2,1)S(1)} %get-tuple-element.45), channel_id=1, source_target_pairs={{0,1},{1,0},{2,3},{3,2},{4,5},{5,4},{6,7},{7,6},{8,9},{9,8},{10,11... | collective-permute-start | bytes 688136 | tf_op jit(solution)/shard_map/ppermute | solution.py:225
  26.5 3.5 %slice-start.11 = ((s8[14680064]{0:T(1024)(128)(4,1)}), s8[2097152]{0:T(1024)(128)(4,1)S(1)}, s32[]{:S(2)}) async-start(s8[14680064]{0:T(1024)(128)(4,1)} %bitcast.5), calls=%async_computation.11 | async-start | bytes 4194304
  26.5 6.3 %collective-permute-start.14 = (bf16[32,3584]{1,0:T(8,128)(2,1)S(1)}, bf16[32,3584]{1,0:T(8,128)(2,1)S(1)}, u32[]{:S(2)}, u32[]{:S(2)}) collective-permute-start(bf16[32,3584]{1,0:T(8,128)(2,1)S(1)} %get-tuple-element.44), channel_id=1, source_target_pairs={{0,1},{1,0},{2,3},{3,2},{4,5},{5,4},{6,7},{7,6},{8,9},{9,8},{10,11... | collective-permute-start | bytes 688136 | tf_op jit(solution)/shard_map/ppermute | solution.py:225
  28.7 4.2 %collective-permute-start.13 = (bf16[32,3584]{1,0:T(8,128)(2,1)S(1)}, bf16[32,3584]{1,0:T(8,128)(2,1)S(1)}, u32[]{:S(2)}, u32[]{:S(2)}) collective-permute-start(bf16[32,3584]{1,0:T(8,128)(2,1)S(1)} %get-tuple-element.43), channel_id=1, source_target_pairs={{0,1},{1,0},{2,3},{3,2},{4,5},{5,4},{6,7},{7,6},{8,9},{9,8},{10,11... | collective-permute-start | bytes 688136 | tf_op jit(solution)/shard_map/ppermute | solution.py:225
  29.3 8.1 %collective-permute-start.16 = (bf16[32,3584]{1,0:T(8,128)(2,1)S(1)}, bf16[32,3584]{1,0:T(8,128)(2,1)S(1)}, u32[]{:S(2)}, u32[]{:S(2)}) collective-permute-start(bf16[32,3584]{1,0:T(8,128)(2,1)S(1)} %shard_map.111.refs_2_), channel_id=1, source_target_pairs={{0,2},{1,3},{2,0},{3,1},{4,6},{5,7},{6,4},{7,5},{8,10},{9,11},{10,... | collective-permute-start | bytes 688136 | tf_op jit(solution)/shard_map/ppermute | solution.py:225
  32.2 5.3 %collective-permute-start.12 = (bf16[32,2048]{1,0:T(8,128)(2,1)S(1)}, bf16[32,2048]{1,0:T(8,128)(2,1)S(1)}, u32[]{:S(2)}, u32[]{:S(2)}) collective-permute-start(bf16[32,2048]{1,0:T(8,128)(2,1)S(1)} %get-tuple-element.42), channel_id=1, source_target_pairs={{0,1},{1,0},{2,3},{3,2},{4,5},{5,4},{6,7},{7,6},{8,9},{9,8},{10,11... | collective-permute-start | bytes 393224 | tf_op jit(solution)/shard_map/ppermute | solution.py:225
  32.3 5.2 %collective-permute-start.11 = (bf16[32,1536]{1,0:T(8,128)(2,1)S(1)}, bf16[32,1536]{1,0:T(8,128)(2,1)S(1)}, u32[]{:S(2)}, u32[]{:S(2)}) collective-permute-start(bf16[32,1536]{1,0:T(8,128)(2,1)S(1)} %get-tuple-element.41), channel_id=1, source_target_pairs={{0,1},{1,0},{2,3},{3,2},{4,5},{5,4},{6,7},{7,6},{8,9},{9,8},{10,11... | collective-permute-start | bytes 294920 | tf_op jit(solution)/shard_map/ppermute | solution.py:225
  32.8 9.2 %collective-permute-start.17 = (bf16[32,3584]{1,0:T(8,128)(2,1)S(1)}, bf16[32,3584]{1,0:T(8,128)(2,1)S(1)}, u32[]{:S(2)}, u32[]{:S(2)}) collective-permute-start(bf16[32,3584]{1,0:T(8,128)(2,1)S(1)} %get-tuple-element.53), channel_id=1, source_target_pairs={{0,1},{1,0},{2,3},{3,2},{4,5},{5,4},{6,7},{7,6},{8,9},{9,8},{10,11... | collective-permute-start | bytes 688136 | tf_op jit(solution)/shard_map/ppermute | solution.py:225
  32.9 9.4 %collective-permute-start.18 = (bf16[32,3584]{1,0:T(8,128)(2,1)S(1)}, bf16[32,3584]{1,0:T(8,128)(2,1)S(1)}, u32[]{:S(2)}, u32[]{:S(2)}) collective-permute-start(bf16[32,3584]{1,0:T(8,128)(2,1)S(1)} %shard_map.114.refs_3_), channel_id=1, source_target_pairs={{0,2},{1,3},{2,0},{3,1},{4,6},{5,7},{6,4},{7,5},{8,10},{9,11},{10,... | collective-permute-start | bytes 688136 | tf_op jit(solution)/shard_map/ppermute | solution.py:225
  37.4 5.1 %collective-permute-start.19 = (bf16[32,3584]{1,0:T(8,128)(2,1)S(1)}, bf16[32,3584]{1,0:T(8,128)(2,1)S(1)}, u32[]{:S(2)}, u32[]{:S(2)}) collective-permute-start(bf16[32,3584]{1,0:T(8,128)(2,1)S(1)} %get-tuple-element.55), channel_id=1, source_target_pairs={{0,1},{1,0},{2,3},{3,2},{4,5},{5,4},{6,7},{7,6},{8,9},{9,8},{10,11... | collective-permute-start | bytes 688136 | tf_op jit(solution)/shard_map/ppermute | solution.py:225
  37.5 9.3 %collective-permute-start.20 = (bf16[32,3584]{1,0:T(8,128)(2,1)S(1)}, bf16[32,3584]{1,0:T(8,128)(2,1)S(1)}, u32[]{:S(2)}, u32[]{:S(2)}) collective-permute-start(bf16[32,3584]{1,0:T(8,128)(2,1)S(1)} %shard_map.115.refs_0_), channel_id=1, source_target_pairs={{0,2},{1,3},{2,0},{3,1},{4,6},{5,7},{6,4},{7,5},{8,10},{9,11},{10,... | collective-permute-start | bytes 688136 | tf_op jit(solution)/shard_map/ppermute | solution.py:225
